TPU v7x, 32 devices: a whole 2x2x4 slice. The times are simulated.
32 devices in a mesh: panel: 8 (over z, core), case: 4 (over y, x).
Axes of the slice: x: 2, y: 2, z: 4, core: 2. Of those that a mesh axis runs over, the one named last changes fastest.
Arguments:
- strengths: bfloat16 [32, 49152], P('panel', 'case'), may hold values from -6 to 6
- blocks: bfloat16 [1024, 256, 256], P(('panel', 'case')), may hold values from -0.21875 to 0.21875
- pattern: int32 [1024, 3], P(('panel', 'case')), may hold values from -1 to 191, as said below
- level_gain: float32 [8], replicated, may hold values from 0.25 to 2
Outputs:
- forward_one: bfloat16 [32, 49152], P('case', 'panel')
- adjoint_one: bfloat16 [32, 49152], P('panel', 'case')
- forward_two: bfloat16 [32, 49152], P('case', 'panel')
- adjoint_two: bfloat16 [32, 49152], P('panel', 'case')
Inputs may be any that keep to these rules, and one draw needn't show every extreme that they name: `pattern`: entries come in runs of 32, one run for each pair of a panel index p and a case index c, ordered with p slowest; a run's row blocks lie in p * 24 to (p + 1) * 24 - 1 and its column blocks in c * 48 to (c + 1) * 48 - 1; no (row block, column block) pair appears twice; levels lie in 0 to 7; an empty slot is (-1, -1, -1), a run holds its stored blocks first and its empty slots after them, every run holds at least one stored block and some run is full.
All inputs are finite; a program needn't handle non-finite values.
Results may differ from a plain program's by a relative error of at most 0.024.
Values may be sent and summed in bfloat16 or wider, within the bound.
No kernel may reach another device: no remote copies, remote signals or barrier semaphores. Data moves between devices by JAX's collectives and lax.ppermute only.
A program may use at most 64 MiB of HBM per device.

v0:
```python
import jax
import jax.numpy as jnp
from jax import lax
from jax.sharding import PartitionSpec as P

B = 256
CASES = 32
ROWB_DEV = 24


def shards(strengths, blocks, pattern, level_gain):
    col_blocks = strengths.shape[1] // B
    row_width = ROWB_DEV * B
    row_local = pattern[:, 0] - lax.axis_index("panel") * ROWB_DEV
    col_local = pattern[:, 1] - lax.axis_index("case") * col_blocks
    level_ids = jnp.arange(level_gain.shape[0], dtype=jnp.int32)
    block_scale = jnp.sum(
        jnp.where(pattern[:, 2:3] == level_ids[None, :], level_gain[None, :], jnp.float32(0.0)),
        axis=1,
    )
    row_pick = row_local[:, None] == jnp.arange(ROWB_DEV, dtype=jnp.int32)[None, :]
    col_pick = col_local[:, None] == jnp.arange(col_blocks, dtype=jnp.int32)[None, :]

    def forward_terms(portion):
        count_cases = portion.shape[0]
        tiled = portion.reshape(count_cases, col_blocks, B)
        picked = jnp.einsum(
            "sc,kcm->skm", col_pick.astype(jnp.bfloat16), tiled, preferred_element_type=jnp.float32
        ).astype(jnp.bfloat16)
        contrib = (
            jnp.einsum("skm,snm->skn", picked, blocks, preferred_element_type=jnp.float32)
            * block_scale[:, None, None]
        )
        row_terms = jnp.einsum(
            "sr,skn->krn", row_pick.astype(jnp.float32), contrib, precision=lax.Precision.HIGHEST
        )
        return row_terms.reshape(count_cases, row_width)

    def adjoint_terms(portion):
        count_cases = portion.shape[0]
        tiled = portion.reshape(count_cases, ROWB_DEV, B)
        picked = jnp.einsum(
            "sr,krn->skn", row_pick.astype(jnp.bfloat16), tiled, preferred_element_type=jnp.float32
        ).astype(jnp.bfloat16)
        contrib = (
            jnp.einsum("skn,snm->skm", picked, blocks, preferred_element_type=jnp.float32)
            * block_scale[:, None, None]
        )
        col_terms = jnp.einsum(
            "sc,skm->kcm", col_pick.astype(jnp.float32), contrib, precision=lax.Precision.HIGHEST
        )
        return col_terms.reshape(count_cases, col_blocks * B)

    first_terms = forward_terms(lax.all_gather(strengths, "panel", axis=0, tiled=True))
    case_share = CASES // lax.axis_size("case")
    panel_share = CASES // lax.axis_size("panel")

    def total_rows(partial_value):
        return lax.psum(partial_value.astype(jnp.bfloat16), "case")

    forward_full = total_rows(first_terms)
    forward_one = lax.dynamic_slice_in_dim(
        forward_full, lax.axis_index("case") * case_share, case_share, 0
    )
    adjoint_full = lax.psum(adjoint_terms(forward_full).astype(jnp.bfloat16), "panel")
    adjoint_one = lax.dynamic_slice_in_dim(
        adjoint_full, lax.axis_index("panel") * panel_share, panel_share, 0
    )
    second_full = total_rows(forward_terms(adjoint_full))
    forward_two = lax.dynamic_slice_in_dim(
        second_full, lax.axis_index("case") * case_share, case_share, 0
    )
    adjoint_two = lax.psum_scatter(
        adjoint_terms(second_full).astype(jnp.bfloat16), "panel", scatter_dimension=0, tiled=True
    )
    return (forward_one, adjoint_one, forward_two, adjoint_two)


def solution(mesh):
    in_specs = (
        P("panel", "case"),
        P(("panel", "case"), None, None),
        P(("panel", "case"), None),
        P(),
    )
    out_specs = (P("case", "panel"), P("panel", "case"), P("case", "panel"), P("panel", "case"))
    return jax.shard_map(shards, mesh=mesh, in_specs=in_specs, out_specs=out_specs, check_vma=False)
```

profile of v0, /device:TPU:0, one launch (start us, length us, event | category | flops | bytes accessed | tf_op | source)
XLA Modules:
  0.0 266.2 jit_solution(9918529612460263360)
XLA Ops:
  7.2 17.4 %all-gather = bf16[8,4,12288]{2,1,0:T(4,128)(2,1)S(1)} all-gather(bf16[1,4,12288]{2,1,0:T(4,128)(2,1)} %bitcast.60), channel_id=1, replica_groups=mesh['panel'=8,'case'=4] {'panel'}, dimensions={0}, use_global_device_ids=true | all-gather | bytes 884736 | tf_op jit(solution)/shard_map/all_gather | solution.py:54
  24.7 0.6 reshape.30
  25.2 0.8 subtract_bitcast_fusion
  26.0 0.3 convolution_convert_fusion.5
  26.4 0.7 select_reduce_fusion
  27.1 3.5 %convolution_multiply_fusion.3 = f32[32,32,256]{2,1,0:T(8,128)S(1)} fusion(bf16[32,256,256]{2,1,0:T(8,128)(2,1)} %param.5, bf16[32,32,256]{2,0,1:T(8,128)(2,1)S(1)} %convolution_convert_fusion.5, f32[32]{0:T(128)S(1)} %select_reduce_fusion), kind=kOutput, calls=%fused_computation.5 | convolution fusion | flops 134479872 | bytes 5767296 | tf_op jit(solution)/shard_map/skm,snm->skn/dot_general | solution.py:31
  30.7 1.1 convolution_convert_fusion.7
  31.8 0.8 copy.16
  32.7 0.6 dynamic-slice
  33.9 44.1 %all-reduce.6.cloned.1.call-done = bf16[32,6144]{1,0:T(8,128)(2,1)} async-done(((bf16[32,6144]{1,0:T(8,128)(2,1)}), bf16[32,6144]{1,0:T(8,128)(2,1)}) %all-reduce.6.cloned.1.call-update) | async-done | bytes 393232 | tf_op jit(solution)/shard_map/psum | solution.py:59
  78.1 1.1 copy.17
  79.1 0.3 convolution_convert_fusion.4
  79.5 3.1 %convolution_multiply_fusion.2 = f32[32,32,256]{2,1,0:T(8,128)S(1)} fusion(bf16[32,256,256]{2,1,0:T(8,128)(2,1)} %param.5, bf16[32,32,256]{2,0,1:T(8,128)(2,1)S(1)} %convolution_convert_fusion.4, f32[32]{0:T(128)S(1)} %select_reduce_fusion), kind=kOutput, calls=%fused_computation.4 | convolution fusion | flops 134479872 | bytes 5767296 | tf_op jit(solution)/shard_map/skn,snm->skm/dot_general | solution.py:46
  82.6 1.5 convolution_convert_fusion.1
  84.1 1.2 copy.18
  85.4 1.5 constant_dynamic-slice_fusion.2
  86.9 55.9 %all-reduce.8.cloned.1.call-done = bf16[32,12288]{1,0:T(8,128)(2,1)} async-done(((bf16[32,12288]{1,0:T(8,128)(2,1)}), bf16[32,12288]{1,0:T(8,128)(2,1)}) %all-reduce.8.cloned.1.call-update) | async-done | bytes 786448 | tf_op jit(solution)/shard_map/psum | solution.py:65
  142.8 1.3 copy.19
  144.1 0.3 convolution_convert_fusion.3
  144.5 3.5 %convolution_multiply_fusion.1 = f32[32,32,256]{2,1,0:T(8,128)S(1)} fusion(bf16[32,256,256]{2,1,0:T(8,128)(2,1)} %param.5, bf16[32,32,256]{2,0,1:T(8,128)(2,1)S(1)} %convolution_convert_fusion.3, f32[32]{0:T(128)S(1)} %select_reduce_fusion), kind=kOutput, calls=%fused_computation.3 | convolution fusion | flops 134479872 | bytes 5767296 | tf_op jit(solution)/shard_map/skm,snm->skn/dot_general | solution.py:31
  148.0 1.1 convolution_convert_fusion.6
  149.2 0.8 copy.20
  150.1 1.6 constant_dynamic-slice_fusion.1
  151.7 41.6 %all-reduce.10.cloned.1.call-done = bf16[32,6144]{1,0:T(8,128)(2,1)} async-done(((bf16[32,6144]{1,0:T(8,128)(2,1)}), bf16[32,6144]{1,0:T(8,128)(2,1)}) %all-reduce.10.cloned.1.call-update) | async-done | bytes 393232 | tf_op jit(solution)/shard_map/psum | solution.py:59
  193.3 1.1 copy.21
  194.4 0.3 convolution_convert_fusion.2
  194.7 3.1 %convolution_multiply_fusion = f32[32,32,256]{2,1,0:T(8,128)S(1)} fusion(bf16[32,256,256]{2,1,0:T(8,128)(2,1)} %param.5, bf16[32,32,256]{2,0,1:T(8,128)(2,1)S(1)} %convolution_convert_fusion.2, f32[32]{0:T(128)S(1)} %select_reduce_fusion), kind=kOutput, calls=%fused_computation.2 | convolution fusion | flops 134479872 | bytes 5767296 | tf_op jit(solution)/shard_map/skn,snm->skm/dot_general | solution.py:46
  197.8 1.5 convolution_convert_fusion
  199.3 1.2 copy.22
  200.5 1.5 constant_dynamic-slice_fusion
  202.1 55.9 %all-reduce.12.cloned.1.call-done = bf16[32,12288]{1,0:T(8,128)(2,1)} async-done(((bf16[32,12288]{1,0:T(8,128)(2,1)}), bf16[32,12288]{1,0:T(8,128)(2,1)}) %all-reduce.12.cloned.1.call-update) | async-done | bytes 786448
  258.0 1.6 constant_dynamic-slice_fusion.3
  (10 shorter events, 0.2 us)
Async XLA Ops:
  7.2 70.9 %all-reduce.6.cloned.1.call-start = ((), (), s32[]{:S(2)}) async-start(), calls=%async_computation | async-start | bytes 786432 | tf_op jit(solution)/shard_map/psum | solution.py:59
  27.1 5.6 %copy-start = (u32[32]{0:T(128)S(1)}, u32[32]{0:T(128)}, u32[]{:S(2)}) copy-start(u32[32]{0:T(128)} %constant.26) | copy-start | bytes 388
  32.6 110.2 %all-reduce.8.cloned.1.call-start = ((), (), s32[]{:S(2)}) async-start(), calls=%async_computation.1 | async-start | bytes 1572864 | tf_op jit(solution)/shard_map/psum | solution.py:65
  85.3 108.0 %all-reduce.10.cloned.1.call-start = ((), (), s32[]{:S(2)}) async-start(), calls=%async_computation.2 | async-start | bytes 786432 | tf_op jit(solution)/shard_map/psum | solution.py:59
  150.0 108.0 %all-reduce.12.cloned.1.call-start = ((), (), s32[]{:S(2)}) async-start(), calls=%async_computation.3 | async-start | bytes 1572864
Sparse Core Ops, SparseCore 0:
  32.8 45.2 all-reduce.5
  85.4 57.3 all-reduce.7
  150.1 43.1 all-reduce.9
  200.7 57.2 all-reduce.11
where the time goes:
time: 267 us; the launch traced here: 266 us
  waiting for transfers between devices  198 us (74%)
  matrix products  20 us (7%)
  blocking collectives  17.4 us (7%)
  local copies, waits for them, and re-layouts  14.9 us (6%)
  between operations  14.5 us (5%)
    psum x2, waiting for transfers between devices, total_rows(): return lax.psum(partial_value.astype(jnp.bfloat16), 'case')  85.7 us
    unnamed x5, waiting for transfers between devices  56 us
    psum x1, waiting for transfers between devices, shards(): lax.psum(adjoint_terms(forward_full).astype(jnp.bfloat16), 'panel')  55.9 us
    all_gather x1, blocking collectives, shards(): lax.all_gather(strengths, 'panel', axis=0, tiled=True)  17.4 us
    unnamed x11, local copies, waits for them, and re-layouts  9.58 us
    dot_general x2, matrix products, forward_terms(): jnp.einsum('skm,snm->skn', picked, blocks, preferred_element_type=jnp.flo...  7.06 us
    dot_general x2, matrix products, adjoint_terms(): jnp.einsum('skn,snm->skm', picked, blocks, preferred_element_type=jnp.flo...  6.2 us
  transfers between devices with their start and end apart: 4, of which 4 were waited for; matrix products, arithmetic and copies ran while one was open for 2% of the time, Pallas kernels for 0%

commit v1 on v0

v1 whole, which is shorter than its diff:
```python
import jax
import jax.numpy as jnp
from jax import lax
from jax.sharding import PartitionSpec as P

B = 256


def swap(value, axis, offset):
    count = lax.axis_size(axis)
    return lax.ppermute(value, axis, [(i, i ^ offset) for i in range(count)])


def pick(pieces, index):
    return lax.dynamic_index_in_dim(pieces, index, 0, keepdims=False)


def place(parts, order, offsets):
    me = order
    stacked = jnp.stack(parts)
    out = jnp.zeros_like(stacked)
    for part, offset in zip(parts, offsets):
        out = lax.dynamic_update_slice_in_dim(out, part[None], me ^ offset, 0)
    return out


def gather_direct(piece, axis):
    count = lax.axis_size(axis)
    me = lax.axis_index(axis)
    parts = [piece] + [swap(piece, axis, k) for k in range(1, count)]
    return place(parts, me, range(count))


def gather_pairs(piece, axis):
    count = lax.axis_size(axis)
    me = lax.axis_index(axis)
    same = [piece] + [swap(piece, axis, k) for k in range(2, count, 2)]
    other = [swap(part, axis, 1) for part in same]
    parts = same + other
    offsets = list(range(0, count, 2)) + [k ^ 1 for k in range(0, count, 2)]
    return place(parts, me, offsets)


def scatter_direct(pieces, axis):
    count = lax.axis_size(axis)
    me = lax.axis_index(axis)
    arrived = [swap(pick(pieces, me ^ k), axis, k) for k in range(1, count)]
    total = pick(pieces, me).astype(jnp.float32)
    for part in arrived:
        total = total + part.astype(jnp.float32)
    return total.astype(pieces.dtype)


def scatter_pairs(pieces, axis):
    count = lax.axis_size(axis)
    me = lax.axis_index(axis)
    side = me & 1
    paired = pieces.reshape(count // 2, 2, *pieces.shape[1:])
    mine = lax.dynamic_index_in_dim(paired, side, 1, keepdims=False)
    theirs = lax.dynamic_index_in_dim(paired, 1 - side, 1, keepdims=False)
    summed = (mine.astype(jnp.float32) + swap(theirs, axis, 1).astype(jnp.float32)).astype(pieces.dtype)
    place_of = me // 2
    arrived = [swap(pick(summed, place_of ^ k), axis, 2 * k) for k in range(1, count // 2)]
    total = pick(summed, place_of).astype(jnp.float32)
    for part in arrived:
        total = total + part.astype(jnp.float32)
    return total.astype(pieces.dtype)


def shards(strengths, blocks, pattern, level_gain):
    n_panel = lax.axis_size("panel")
    n_case = lax.axis_size("case")
    cases = strengths.shape[0] * n_panel
    col_blocks = strengths.shape[1] // B
    row_blocks = col_blocks * n_case // n_panel
    row_local = pattern[:, 0] - lax.axis_index("panel") * row_blocks
    col_local = pattern[:, 1] - lax.axis_index("case") * col_blocks
    level_ids = jnp.arange(level_gain.shape[0], dtype=jnp.int32)
    block_scale = jnp.sum(
        jnp.where(pattern[:, 2:3] == level_ids[None, :], level_gain[None, :], jnp.float32(0.0)),
        axis=1,
    )
    row_pick = row_local[:, None] == jnp.arange(row_blocks, dtype=jnp.int32)[None, :]
    col_pick = col_local[:, None] == jnp.arange(col_blocks, dtype=jnp.int32)[None, :]

    def forward_terms(portion):
        tiled = portion.reshape(cases, col_blocks, B)
        picked = jnp.einsum(
            "sc,kcm->skm", col_pick.astype(jnp.bfloat16), tiled, preferred_element_type=jnp.float32
        ).astype(jnp.bfloat16)
        contrib = (
            jnp.einsum("skm,snm->skn", picked, blocks, preferred_element_type=jnp.float32)
            * block_scale[:, None, None]
        )
        row_terms = jnp.einsum(
            "sr,skn->krn", row_pick.astype(jnp.float32), contrib, precision=lax.Precision.HIGHEST
        )
        return row_terms.reshape(cases, row_blocks * B).astype(jnp.bfloat16)

    def adjoint_terms(portion):
        tiled = portion.reshape(cases, row_blocks, B)
        picked = jnp.einsum(
            "sr,krn->skn", row_pick.astype(jnp.bfloat16), tiled, preferred_element_type=jnp.float32
        ).astype(jnp.bfloat16)
        contrib = (
            jnp.einsum("skn,snm->skm", picked, blocks, preferred_element_type=jnp.float32)
            * block_scale[:, None, None]
        )
        col_terms = jnp.einsum(
            "sc,skm->kcm", col_pick.astype(jnp.float32), contrib, precision=lax.Precision.HIGHEST
        )
        return col_terms.reshape(cases, col_blocks * B).astype(jnp.bfloat16)

    def by_case(terms):
        return terms.reshape(n_case, cases // n_case, -1)

    def by_panel(terms):
        return terms.reshape(n_panel, cases // n_panel, -1)

    def flat(gathered):
        return gathered.reshape(cases, -1)

    first = flat(gather_pairs(strengths, "panel"))
    forward_one = scatter_direct(by_case(forward_terms(first)), "case")
    forward_full = flat(gather_direct(forward_one, "case"))
    adjoint_one = scatter_pairs(by_panel(adjoint_terms(forward_full)), "panel")
    adjoint_full = flat(gather_pairs(adjoint_one, "panel"))
    forward_two = scatter_direct(by_case(forward_terms(adjoint_full)), "case")
    second_full = flat(gather_direct(forward_two, "case"))
    adjoint_two = scatter_pairs(by_panel(adjoint_terms(second_full)), "panel")
    return (forward_one, adjoint_one, forward_two, adjoint_two)


def solution(mesh):
    in_specs = (
        P("panel", "case"),
        P(("panel", "case"), None, None),
        P(("panel", "case"), None),
        P(),
    )
    out_specs = (P("case", "panel"), P("panel", "case"), P("case", "panel"), P("panel", "case"))
    return jax.shard_map(shards, mesh=mesh, in_specs=in_specs, out_specs=out_specs, check_vma=False)
```

time: 267 us -> 114 us (0.43)
  waiting for transfers between devices: 198 us -> 49.2 us
  starting transfers between devices: 0.16 us -> 35.1 us
  blocking collectives: 17.4 us -> 0 us
  between operations: 14.5 us -> 1.07 us
  local copies, waits for them, and re-layouts: 14.9 us -> 5.59 us
    psum x3 -> x0, waiting for transfers between devices: 142 us -> none  [the longest x2 85.7 us: total_rows(): return lax.psum(partial_value.astype(jnp.bfloat16), 'case')]
    unnamed x5 -> x0, waiting for transfers between devices: 56 us -> none
    ppermute x0 -> x34, waiting for transfers between devices: none -> 49.2 us  [swap(): return lax.ppermute(value, axis, [(i, i ^ offset) for i in range(count)])]
    ppermute x0 -> x34, starting transfers between devices: none -> 35.1 us  [swap(): return lax.ppermute(value, axis, [(i, i ^ offset) for i in range(count)])]
    all_gather x1 -> x0, blocking collectives: 17.4 us -> none  [shards(): lax.all_gather(strengths, 'panel', axis=0, tiled=True)]
    unnamed x11 -> x8, local copies, waits for them, and re-layouts: 9.58 us -> 0.17 us
    dynamic_slice x3 -> x0, local copies, waits for them, and re-layouts: 4.72 us -> none  [the longest x1 1.63 us: shards(): lax.dynamic_slice_in_dim(adjoint_full, lax.axis_index('panel') * panel_sh...]
  transfers between devices with their start and end apart: 4 -> 34, of which waited for: 4 -> 24; matrix products, arithmetic and copies ran while one was open for 2% -> 3% of each run, Pallas kernels for 0% -> 0%
where the time goes in v1:
time: 114 us
  waiting for transfers between devices  49.2 us (43%)
  starting transfers between devices  35.1 us (31%)
  matrix products  20.1 us (18%)
  local copies, waits for them, and re-layouts  5.59 us (5%)
  other arithmetic  2.96 us (3%)
    ppermute x34, waiting for transfers between devices, swap(): return lax.ppermute(value, axis, [(i, i ^ offset) for i in range(count)])  49.2 us
    ppermute x34, starting transfers between devices, swap(): return lax.ppermute(value, axis, [(i, i ^ offset) for i in range(count)])  35.1 us
    dot_general x2, matrix products, forward_terms(): jnp.einsum('skm,snm->skn', picked, blocks, preferred_element_type=jnp.flo...  7.06 us
    dot_general x2, matrix products, adjoint_terms(): jnp.einsum('skn,snm->skm', picked, blocks, preferred_element_type=jnp.flo...  6.14 us
    dot_general x2, matrix products, adjoint_terms(): jnp.einsum('sc,skm->kcm', col_pick.astype(jnp.float32), contrib, precisio...  3.02 us
    dot_general x2, matrix products, forward_terms(): jnp.einsum('sr,skn->krn', row_pick.astype(jnp.float32), contrib, precisio...  2.51 us
  transfers between devices with their start and end apart: 34, of which 24 were waited for; matrix products, arithmetic and copies ran while one was open for 3% of the time, Pallas kernels for 0%

profile of v1, /device:TPU:0, one launch (start us, length us, event | category | flops | bytes accessed | tf_op | source)
XLA Modules:
  0.0 113.9 jit_solution(14634191684664398151)
XLA Ops:
  0.6 3.1 %collective-permute-start = (bf16[4,12288]{1,0:T(4,128)(2,1)}, bf16[4,12288]{1,0:T(4,128)(2,1)S(1)}, u32[]{:S(2)}, u32[]{:S(2)}) collective-permute-start(bf16[4,12288]{1,0:T(4,128)(2,1)} %param.4), channel_id=1, source_target_pairs={{0,8},{4,12},{8,0},{12,4},{16,24},{20,28},{24,16},{28,20},{1,9},{5... | collective-permute-start | bytes 294920 | tf_op jit(solution)/shard_map/ppermute | solution.py:11
  3.7 2.6 %collective-permute-start.1 = (bf16[4,12288]{1,0:T(4,128)(2,1)}, bf16[4,12288]{1,0:T(4,128)(2,1)S(1)}, u32[]{:S(2)}, u32[]{:S(2)}) collective-permute-start(bf16[4,12288]{1,0:T(4,128)(2,1)} %param.4), channel_id=1, source_target_pairs={{0,16},{4,20},{8,24},{12,28},{16,0},{20,4},{24,8},{28,12},{1,17},{... | collective-permute-start | bytes 294920 | tf_op jit(solution)/shard_map/ppermute | solution.py:11
  9.6 4.7 %collective-permute-done.1 = bf16[4,12288]{1,0:T(4,128)(2,1)S(1)} collective-permute-done((bf16[4,12288]{1,0:T(4,128)(2,1)}, bf16[4,12288]{1,0:T(4,128)(2,1)S(1)}, u32[]{:S(2)}, u32[]{:S(2)}) %collective-permute-start.1) | collective-permute-done | bytes 98336 | tf_op jit(solution)/shard_map/ppermute | solution.py:11
  16.8 3.5 %fusion.6 = f32[32,32,256]{2,1,0:T(8,128)S(1)} fusion(bf16[32,256,256]{2,1,0:T(8,128)(2,1)} %param.5, bf16[32,32,256]{2,0,1:T(8,128)(2,1)S(1)} %fusion.31), kind=kOutput, calls=%fused_computation.20 | convolution fusion | flops 134217728 | bytes 5767168 | tf_op jit(solution)/shard_map/skm,snm->skn/dot_general | solution.py:92
  21.7 1.6 %collective-permute-start.7 = (bf16[8,6144]{1,0:T(8,128)(2,1)S(1)}, bf16[8,6144]{1,0:T(8,128)(2,1)S(1)}, u32[]{:S(2)}, u32[]{:S(2)}) collective-permute-start(bf16[8,6144]{1,0:T(8,128)(2,1)S(1)} %get-tuple-element.19), channel_id=1, source_target_pairs={{0,1},{1,0},{2,3},{3,2},{4,5},{5,4},{6,7},{7,6},{8,9},{9,8},{10,11... | collective-permute-start | bytes 294920 | tf_op jit(solution)/shard_map/ppermute | solution.py:11
  23.3 1.5 %collective-permute-start.8 = (bf16[8,6144]{1,0:T(8,128)(2,1)S(1)}, bf16[8,6144]{1,0:T(8,128)(2,1)S(1)}, u32[]{:S(2)}, u32[]{:S(2)}) collective-permute-start(bf16[8,6144]{1,0:T(8,128)(2,1)S(1)} %get-tuple-element.21), channel_id=1, source_target_pairs={{0,2},{1,3},{2,0},{3,1},{4,6},{5,7},{6,4},{7,5},{8,10},{9,11},{10,... | collective-permute-start | bytes 294920 | tf_op jit(solution)/shard_map/ppermute | solution.py:11
  25.3 1.6 %collective-permute-done.7 = bf16[8,6144]{1,0:T(8,128)(2,1)S(1)} collective-permute-done((bf16[8,6144]{1,0:T(8,128)(2,1)S(1)}, bf16[8,6144]{1,0:T(8,128)(2,1)S(1)}, u32[]{:S(2)}, u32[]{:S(2)}) %collective-permute-start.7) | collective-permute-done | bytes 98336 | tf_op jit(solution)/shard_map/ppermute | solution.py:11
  26.9 2.4 %collective-permute-done.8 = bf16[8,6144]{1,0:T(8,128)(2,1)S(1)} collective-permute-done((bf16[8,6144]{1,0:T(8,128)(2,1)S(1)}, bf16[8,6144]{1,0:T(8,128)(2,1)S(1)}, u32[]{:S(2)}, u32[]{:S(2)}) %collective-permute-start.8) | collective-permute-done | bytes 98336 | tf_op jit(solution)/shard_map/ppermute | solution.py:11
  32.4 1.6 %collective-permute-start.12 = (bf16[8,6144]{1,0:T(8,128)(2,1)S(1)}, bf16[8,6144]{1,0:T(8,128)(2,1)S(1)}, u32[]{:S(2)}, u32[]{:S(2)}) collective-permute-start(bf16[8,6144]{1,0:T(8,128)(2,1)S(1)} %get-tuple-element.9), channel_id=1, source_target_pairs={{0,3},{1,2},{2,1},{3,0},{4,7},{5,6},{6,5},{7,4},{8,11},{9,10},{10,... | collective-permute-start | bytes 294920 | tf_op jit(solution)/shard_map/ppermute | solution.py:11
  34.0 1.7 %collective-permute-done.10 = bf16[8,6144]{1,0:T(8,128)(2,1)S(1)} collective-permute-done((bf16[8,6144]{1,0:T(8,128)(2,1)S(1)}, bf16[8,6144]{1,0:T(8,128)(2,1)S(1)}, u32[]{:S(2)}, u32[]{:S(2)}) %collective-permute-start.10) | collective-permute-done | bytes 98336 | tf_op jit(solution)/shard_map/ppermute | solution.py:11
  38.4 3.1 %fusion.7 = f32[32,32,256]{2,1,0:T(8,128)S(1)} fusion(bf16[32,256,256]{2,1,0:T(8,128)(2,1)} %param.5, bf16[32,32,256]{2,0,1:T(8,128)(2,1)S(1)} %fusion.37), kind=kOutput, calls=%fused_computation.21 | convolution fusion | flops 134217728 | bytes 5767168 | tf_op jit(solution)/shard_map/skn,snm->skm/dot_general | solution.py:106
  41.4 1.5 %fusion = bf16[32,48,256]{2,1,0:T(8,128)(2,1)S(1)} fusion(f32[32,32,256]{2,1,0:T(8,128)S(1)} %fusion.7, f32[32]{0:T(128)S(1)} %select_reduce_fusion, s32[32]{0:T(128)S(1)} %get-tuple-element.23), kind=kOutput, calls=%fused_computation.2 | convolution fusion | flops 151651840 | bytes 1835264 | tf_op jit(solution)/shard_map/sc,skm->kcm/dot_general | solution.py:109
  43.8 1.7 %collective-permute-done.13 = bf16[4,4,12288]{2,1,0:T(4,128)(2,1)S(1)} collective-permute-done((bf16[4,4,12288]{2,1,0:T(4,128)(2,1)S(1)}, bf16[4,4,12288]{2,1,0:T(4,128)(2,1)S(1)}, u32[]{:S(2)}, u32[]{:S(2)}) %collective-permute-start.13) | collective-permute-done | bytes 393248 | tf_op jit(solution)/shard_map/ppermute | solution.py:11
  47.2 1.7 %collective-permute-start.15 = (bf16[4,12288]{1,0:T(4,128)(2,1)S(1)}, bf16[4,12288]{1,0:T(4,128)(2,1)S(1)}, u32[]{:S(2)}, u32[]{:S(2)}) collective-permute-start(bf16[4,12288]{1,0:T(4,128)(2,1)S(1)} %get-tuple-element.18), channel_id=1, source_target_pairs={{0,16},{4,20},{8,24},{12,28},{16,0},{20,4},{24,8},{28,12},{1,17},{... | collective-permute-start | bytes 294920 | tf_op jit(solution)/shard_map/ppermute | solution.py:11
  50.3 1.6 %collective-permute-done.14 = bf16[4,12288]{1,0:T(4,128)(2,1)S(1)} collective-permute-done((bf16[4,12288]{1,0:T(4,128)(2,1)S(1)}, bf16[4,12288]{1,0:T(4,128)(2,1)S(1)}, u32[]{:S(2)}, u32[]{:S(2)}) %collective-permute-start.14) | collective-permute-done | bytes 98336 | tf_op jit(solution)/shard_map/ppermute | solution.py:11
  51.9 6.0 %collective-permute-done.15 = bf16[4,12288]{1,0:T(4,128)(2,1)S(1)} collective-permute-done((bf16[4,12288]{1,0:T(4,128)(2,1)S(1)}, bf16[4,12288]{1,0:T(4,128)(2,1)S(1)}, u32[]{:S(2)}, u32[]{:S(2)}) %collective-permute-start.15) | collective-permute-done | bytes 98336 | tf_op jit(solution)/shard_map/ppermute | solution.py:11
  58.2 1.8 %collective-permute-start.17 = (bf16[4,12288]{1,0:T(4,128)(2,1)S(1)}, bf16[4,12288]{1,0:T(4,128)(2,1)S(1)}, u32[]{:S(2)}, u32[]{:S(2)}) collective-permute-start(bf16[4,12288]{1,0:T(4,128)(2,1)S(1)} %get-tuple-element.7), channel_id=1, source_target_pairs={{0,8},{4,12},{8,0},{12,4},{16,24},{20,28},{24,16},{28,20},{1,9},{5... | collective-permute-start | bytes 294920 | tf_op jit(solution)/shard_map/ppermute | solution.py:11
  61.0 1.7 %collective-permute-start.19 = (bf16[4,12288]{1,0:T(4,128)(2,1)S(1)}, bf16[4,12288]{1,0:T(4,128)(2,1)S(1)}, u32[]{:S(2)}, u32[]{:S(2)}) collective-permute-start(bf16[4,12288]{1,0:T(4,128)(2,1)S(1)} %get-tuple-element.7), channel_id=1, source_target_pairs={{0,24},{4,28},{8,16},{12,20},{16,8},{20,12},{24,0},{28,4},{1,25},{... | collective-permute-start | bytes 294920 | tf_op jit(solution)/shard_map/ppermute | solution.py:11
  64.0 5.8 %collective-permute-done.18 = bf16[4,12288]{1,0:T(4,128)(2,1)S(1)} collective-permute-done((bf16[4,12288]{1,0:T(4,128)(2,1)S(1)}, bf16[4,12288]{1,0:T(4,128)(2,1)S(1)}, u32[]{:S(2)}, u32[]{:S(2)}) %collective-permute-start.18) | collective-permute-done | bytes 98336 | tf_op jit(solution)/shard_map/ppermute | solution.py:11
  72.4 3.5 %fusion.8 = f32[32,32,256]{2,1,0:T(8,128)S(1)} fusion(bf16[32,256,256]{2,1,0:T(8,128)(2,1)} %param.5, bf16[32,32,256]{2,0,1:T(8,128)(2,1)S(1)} %fusion.28), kind=kOutput, calls=%fused_computation.22 | convolution fusion | flops 134217728 | bytes 5767168 | tf_op jit(solution)/shard_map/skm,snm->skn/dot_general | solution.py:92
  77.5 1.6 %collective-permute-start.24 = (bf16[8,6144]{1,0:T(8,128)(2,1)S(1)}, bf16[8,6144]{1,0:T(8,128)(2,1)S(1)}, u32[]{:S(2)}, u32[]{:S(2)}) collective-permute-start(bf16[8,6144]{1,0:T(8,128)(2,1)S(1)} %get-tuple-element.13), channel_id=1, source_target_pairs={{0,1},{1,0},{2,3},{3,2},{4,5},{5,4},{6,7},{7,6},{8,9},{9,8},{10,11... | collective-permute-start | bytes 294920 | tf_op jit(solution)/shard_map/ppermute | solution.py:11
  81.1 1.6 %collective-permute-done.24 = bf16[8,6144]{1,0:T(8,128)(2,1)S(1)} collective-permute-done((bf16[8,6144]{1,0:T(8,128)(2,1)S(1)}, bf16[8,6144]{1,0:T(8,128)(2,1)S(1)}, u32[]{:S(2)}, u32[]{:S(2)}) %collective-permute-start.24) | collective-permute-done | bytes 98336 | tf_op jit(solution)/shard_map/ppermute | solution.py:11
  82.6 3.3 %collective-permute-done.25 = bf16[8,6144]{1,0:T(8,128)(2,1)S(1)} collective-permute-done((bf16[8,6144]{1,0:T(8,128)(2,1)S(1)}, bf16[8,6144]{1,0:T(8,128)(2,1)S(1)}, u32[]{:S(2)}, u32[]{:S(2)}) %collective-permute-start.25) | collective-permute-done | bytes 98336 | tf_op jit(solution)/shard_map/ppermute | solution.py:11
  87.9 1.8 %collective-permute-start.29 = (bf16[8,6144]{1,0:T(8,128)(2,1)S(1)}, bf16[8,6144]{1,0:T(8,128)(2,1)S(1)}, u32[]{:S(2)}, u32[]{:S(2)}) collective-permute-start(bf16[8,6144]{1,0:T(8,128)(2,1)S(1)} %get-tuple-element.5), channel_id=1, source_target_pairs={{0,3},{1,2},{2,1},{3,0},{4,7},{5,6},{6,5},{7,4},{8,11},{9,10},{10,... | collective-permute-start | bytes 294920 | tf_op jit(solution)/shard_map/ppermute | solution.py:11
  89.6 2.0 %collective-permute-done.27 = bf16[8,6144]{1,0:T(8,128)(2,1)S(1)} collective-permute-done((bf16[8,6144]{1,0:T(8,128)(2,1)S(1)}, bf16[8,6144]{1,0:T(8,128)(2,1)S(1)}, u32[]{:S(2)}, u32[]{:S(2)}) %collective-permute-start.27) | collective-permute-done | bytes 98336 | tf_op jit(solution)/shard_map/ppermute | solution.py:11
  93.8 3.1 %fusion.9 = f32[32,32,256]{2,1,0:T(8,128)S(1)} fusion(bf16[32,256,256]{2,1,0:T(8,128)(2,1)} %param.5, bf16[32,32,256]{2,0,1:T(8,128)(2,1)S(1)} %fusion.34), kind=kOutput, calls=%fused_computation.23 | convolution fusion | flops 134217728 | bytes 5767168 | tf_op jit(solution)/shard_map/skn,snm->skm/dot_general | solution.py:106
  96.9 1.5 %fusion.1 = bf16[32,48,256]{2,1,0:T(8,128)(2,1)S(1)} fusion(f32[32,32,256]{2,1,0:T(8,128)S(1)} %fusion.9, f32[32]{0:T(128)S(1)} %select_reduce_fusion, s32[32]{0:T(128)S(1)} %get-tuple-element.23), kind=kOutput, calls=%fused_computation.3 | convolution fusion | flops 151651840 | bytes 1835264 | tf_op jit(solution)/shard_map/sc,skm->kcm/dot_general | solution.py:109
  99.2 1.7 %collective-permute-done.30 = bf16[4,4,12288]{2,1,0:T(4,128)(2,1)S(1)} collective-permute-done((bf16[4,4,12288]{2,1,0:T(4,128)(2,1)S(1)}, bf16[4,4,12288]{2,1,0:T(4,128)(2,1)S(1)}, u32[]{:S(2)}, u32[]{:S(2)}) %collective-permute-start.30) | collective-permute-done | bytes 393248 | tf_op jit(solution)/shard_map/ppermute | solution.py:11
  102.5 1.7 %collective-permute-start.32 = (bf16[4,12288]{1,0:T(4,128)(2,1)S(1)}, bf16[4,12288]{1,0:T(4,128)(2,1)S(1)}, u32[]{:S(2)}, u32[]{:S(2)}) collective-permute-start(bf16[4,12288]{1,0:T(4,128)(2,1)S(1)} %get-tuple-element.12), channel_id=1, source_target_pairs={{0,16},{4,20},{8,24},{12,28},{16,0},{20,4},{24,8},{28,12},{1,17},{... | collective-permute-start | bytes 294920 | tf_op jit(solution)/shard_map/ppermute | solution.py:11
  104.2 1.6 %collective-permute-start.33 = (bf16[4,12288]{1,0:T(4,128)(2,1)S(1)}, bf16[4,12288]{1,0:T(4,128)(2,1)S(1)}, u32[]{:S(2)}, u32[]{:S(2)}) collective-permute-start(bf16[4,12288]{1,0:T(4,128)(2,1)S(1)} %get-tuple-element.11), channel_id=1, source_target_pairs={{0,24},{4,28},{8,16},{12,20},{16,8},{20,12},{24,0},{28,4},{1,25},{... | collective-permute-start | bytes 294920 | tf_op jit(solution)/shard_map/ppermute | solution.py:11
  105.7 1.6 %collective-permute-done.31 = bf16[4,12288]{1,0:T(4,128)(2,1)S(1)} collective-permute-done((bf16[4,12288]{1,0:T(4,128)(2,1)S(1)}, bf16[4,12288]{1,0:T(4,128)(2,1)S(1)}, u32[]{:S(2)}, u32[]{:S(2)}) %collective-permute-start.31) | collective-permute-done | bytes 98336 | tf_op jit(solution)/shard_map/ppermute | solution.py:11
  107.4 5.8 %collective-permute-done.32 = bf16[4,12288]{1,0:T(4,128)(2,1)S(1)} collective-permute-done((bf16[4,12288]{1,0:T(4,128)(2,1)S(1)}, bf16[4,12288]{1,0:T(4,128)(2,1)S(1)}, u32[]{:S(2)}, u32[]{:S(2)}) %collective-permute-start.32) | collective-permute-done | bytes 98336 | tf_op jit(solution)/shard_map/ppermute | solution.py:11
  (101 shorter events, 33.1 us)
Async XLA Ops:
  0.6 8.4 %collective-permute-start = (bf16[4,12288]{1,0:T(4,128)(2,1)}, bf16[4,12288]{1,0:T(4,128)(2,1)S(1)}, u32[]{:S(2)}, u32[]{:S(2)}) collective-permute-start(bf16[4,12288]{1,0:T(4,128)(2,1)} %param.4), channel_id=1, source_target_pairs={{0,8},{4,12},{8,0},{12,4},{16,24},{20,28},{24,16},{28,20},{1,9},{5... | collective-permute-start | bytes 294920 | tf_op jit(solution)/shard_map/ppermute | solution.py:11
  3.7 10.6 %collective-permute-start.1 = (bf16[4,12288]{1,0:T(4,128)(2,1)}, bf16[4,12288]{1,0:T(4,128)(2,1)S(1)}, u32[]{:S(2)}, u32[]{:S(2)}) collective-permute-start(bf16[4,12288]{1,0:T(4,128)(2,1)} %param.4), channel_id=1, source_target_pairs={{0,16},{4,20},{8,24},{12,28},{16,0},{20,4},{24,8},{28,12},{1,17},{... | collective-permute-start | bytes 294920 | tf_op jit(solution)/shard_map/ppermute | solution.py:11
  6.3 8.1 %collective-permute-start.2 = (bf16[4,12288]{1,0:T(4,128)(2,1)}, bf16[4,12288]{1,0:T(4,128)(2,1)S(1)}, u32[]{:S(2)}, u32[]{:S(2)}) collective-permute-start(bf16[4,12288]{1,0:T(4,128)(2,1)} %param.4), channel_id=1, source_target_pairs={{0,24},{4,28},{8,16},{12,20},{16,8},{20,12},{24,0},{28,4},{1,25},{... | collective-permute-start | bytes 294920 | tf_op jit(solution)/shard_map/ppermute | solution.py:11
  6.3 8.7 %collective-permute-start.3 = (bf16[4,12288]{1,0:T(4,128)(2,1)}, bf16[4,12288]{1,0:T(4,128)(2,1)S(1)}, u32[]{:S(2)}, u32[]{:S(2)}) collective-permute-start(bf16[4,12288]{1,0:T(4,128)(2,1)} %param.4), channel_id=1, source_target_pairs={{0,4},{4,0},{8,12},{12,8},{16,20},{20,16},{24,28},{28,24},{1,5},{5... | collective-permute-start | bytes 294920 | tf_op jit(solution)/shard_map/ppermute | solution.py:11
  9.1 6.0 %collective-permute-start.4 = (bf16[4,12288]{1,0:T(4,128)(2,1)S(1)}, bf16[4,12288]{1,0:T(4,128)(2,1)S(1)}, u32[]{:S(2)}, u32[]{:S(2)}) collective-permute-start(bf16[4,12288]{1,0:T(4,128)(2,1)S(1)} %collective-permute-done), channel_id=1, source_target_pairs={{0,4},{4,0},{8,12},{12,8},{16,20},{20,16},{24,28},{28,24},{1,5},{5... | collective-permute-start | bytes 294920 | tf_op jit(solution)/shard_map/ppermute | solution.py:11
  14.4 1.5 %collective-permute-start.6 = (bf16[4,12288]{1,0:T(4,128)(2,1)S(1)}, bf16[4,12288]{1,0:T(4,128)(2,1)S(1)}, u32[]{:S(2)}, u32[]{:S(2)}) collective-permute-start(bf16[4,12288]{1,0:T(4,128)(2,1)S(1)} %collective-permute-done.2), channel_id=1, source_target_pairs={{0,4},{4,0},{8,12},{12,8},{16,20},{20,16},{24,28},{28,24},{1,5},{5... | collective-permute-start | bytes 294920 | tf_op jit(solution)/shard_map/ppermute | solution.py:11
  21.7 5.1 %collective-permute-start.7 = (bf16[8,6144]{1,0:T(8,128)(2,1)S(1)}, bf16[8,6144]{1,0:T(8,128)(2,1)S(1)}, u32[]{:S(2)}, u32[]{:S(2)}) collective-permute-start(bf16[8,6144]{1,0:T(8,128)(2,1)S(1)} %get-tuple-element.19), channel_id=1, source_target_pairs={{0,1},{1,0},{2,3},{3,2},{4,5},{5,4},{6,7},{7,6},{8,9},{9,8},{10,11... | collective-permute-start | bytes 294920 | tf_op jit(solution)/shard_map/ppermute | solution.py:11
  23.3 5.9 %collective-permute-start.8 = (bf16[8,6144]{1,0:T(8,128)(2,1)S(1)}, bf16[8,6144]{1,0:T(8,128)(2,1)S(1)}, u32[]{:S(2)}, u32[]{:S(2)}) collective-permute-start(bf16[8,6144]{1,0:T(8,128)(2,1)S(1)} %get-tuple-element.21), channel_id=1, source_target_pairs={{0,2},{1,3},{2,0},{3,1},{4,6},{5,7},{6,4},{7,5},{8,10},{9,11},{10,... | collective-permute-start | bytes 294920 | tf_op jit(solution)/shard_map/ppermute | solution.py:11
  24.8 5.5 %collective-permute-start.9 = (bf16[8,6144]{1,0:T(8,128)(2,1)S(1)}, bf16[8,6144]{1,0:T(8,128)(2,1)S(1)}, u32[]{:S(2)}, u32[]{:S(2)}) collective-permute-start(bf16[8,6144]{1,0:T(8,128)(2,1)S(1)} %get-tuple-element.20), channel_id=1, source_target_pairs={{0,3},{1,2},{2,1},{3,0},{4,7},{5,6},{6,5},{7,4},{8,11},{9,10},{10,... | collective-permute-start | bytes 294920 | tf_op jit(solution)/shard_map/ppermute | solution.py:11
  30.5 5.3 %collective-permute-start.10 = (bf16[8,6144]{1,0:T(8,128)(2,1)S(1)}, bf16[8,6144]{1,0:T(8,128)(2,1)S(1)}, u32[]{:S(2)}, u32[]{:S(2)}) collective-permute-start(bf16[8,6144]{1,0:T(8,128)(2,1)S(1)} %get-tuple-element.9), channel_id=1, source_target_pairs={{0,1},{1,0},{2,3},{3,2},{4,5},{5,4},{6,7},{7,6},{8,9},{9,8},{10,11... | collective-permute-start | bytes 294920 | tf_op jit(solution)/shard_map/ppermute | solution.py:11
  31.6 5.3 %collective-permute-start.11 = (bf16[8,6144]{1,0:T(8,128)(2,1)S(1)}, bf16[8,6144]{1,0:T(8,128)(2,1)S(1)}, u32[]{:S(2)}, u32[]{:S(2)}) collective-permute-start(bf16[8,6144]{1,0:T(8,128)(2,1)S(1)} %get-tuple-element.9), channel_id=1, source_target_pairs={{0,2},{1,3},{2,0},{3,1},{4,6},{5,7},{6,4},{7,5},{8,10},{9,11},{10,... | collective-permute-start | bytes 294920 | tf_op jit(solution)/shard_map/ppermute | solution.py:11
  32.4 5.5 %collective-permute-start.12 = (bf16[8,6144]{1,0:T(8,128)(2,1)S(1)}, bf16[8,6144]{1,0:T(8,128)(2,1)S(1)}, u32[]{:S(2)}, u32[]{:S(2)}) collective-permute-start(bf16[8,6144]{1,0:T(8,128)(2,1)S(1)} %get-tuple-element.9), channel_id=1, source_target_pairs={{0,3},{1,2},{2,1},{3,0},{4,7},{5,6},{6,5},{7,4},{8,11},{9,10},{10,... | collective-permute-start | bytes 294920 | tf_op jit(solution)/shard_map/ppermute | solution.py:11
  43.7 1.8 %collective-permute-start.13 = (bf16[4,4,12288]{2,1,0:T(4,128)(2,1)S(1)}, bf16[4,4,12288]{2,1,0:T(4,128)(2,1)S(1)}, u32[]{:S(2)}, u32[]{:S(2)}) collective-permute-start(bf16[4,4,12288]{2,1,0:T(4,128)(2,1)S(1)} %dynamic-slice_bitcast_fusion.1), channel_id=1, source_target_pairs={{0,4},{4,0},{8,12},{12,8},{16,20},{20,16},{24,28},{28,24},{1,5},{5... | collective-permute-start | bytes 1179656 | tf_op jit(solution)/shard_map/ppermute | solution.py:11
  45.8 6.0 %collective-permute-start.14 = (bf16[4,12288]{1,0:T(4,128)(2,1)S(1)}, bf16[4,12288]{1,0:T(4,128)(2,1)S(1)}, u32[]{:S(2)}, u32[]{:S(2)}) collective-permute-start(bf16[4,12288]{1,0:T(4,128)(2,1)S(1)} %get-tuple-element.16), channel_id=1, source_target_pairs={{0,8},{4,12},{8,0},{12,4},{16,24},{20,28},{24,16},{28,20},{1,9},{5... | collective-permute-start | bytes 294920 | tf_op jit(solution)/shard_map/ppermute | solution.py:11
  47.2 10.7 %collective-permute-start.15 = (bf16[4,12288]{1,0:T(4,128)(2,1)S(1)}, bf16[4,12288]{1,0:T(4,128)(2,1)S(1)}, u32[]{:S(2)}, u32[]{:S(2)}) collective-permute-start(bf16[4,12288]{1,0:T(4,128)(2,1)S(1)} %get-tuple-element.18), channel_id=1, source_target_pairs={{0,16},{4,20},{8,24},{12,28},{16,0},{20,4},{24,8},{28,12},{1,17},{... | collective-permute-start | bytes 294920 | tf_op jit(solution)/shard_map/ppermute | solution.py:11
  48.9 9.0 %collective-permute-start.16 = (bf16[4,12288]{1,0:T(4,128)(2,1)S(1)}, bf16[4,12288]{1,0:T(4,128)(2,1)S(1)}, u32[]{:S(2)}, u32[]{:S(2)}) collective-permute-start(bf16[4,12288]{1,0:T(4,128)(2,1)S(1)} %get-tuple-element.17), channel_id=1, source_target_pairs={{0,24},{4,28},{8,16},{12,20},{16,8},{20,12},{24,0},{28,4},{1,25},{... | collective-permute-start | bytes 294920 | tf_op jit(solution)/shard_map/ppermute | solution.py:11
  58.2 5.7 %collective-permute-start.17 = (bf16[4,12288]{1,0:T(4,128)(2,1)S(1)}, bf16[4,12288]{1,0:T(4,128)(2,1)S(1)}, u32[]{:S(2)}, u32[]{:S(2)}) collective-permute-start(bf16[4,12288]{1,0:T(4,128)(2,1)S(1)} %get-tuple-element.7), channel_id=1, source_target_pairs={{0,8},{4,12},{8,0},{12,4},{16,24},{20,28},{24,16},{28,20},{1,9},{5... | collective-permute-start | bytes 294920 | tf_op jit(solution)/shard_map/ppermute | solution.py:11
  60.0 9.8 %collective-permute-start.18 = (bf16[4,12288]{1,0:T(4,128)(2,1)S(1)}, bf16[4,12288]{1,0:T(4,128)(2,1)S(1)}, u32[]{:S(2)}, u32[]{:S(2)}) collective-permute-start(bf16[4,12288]{1,0:T(4,128)(2,1)S(1)} %get-tuple-element.7), channel_id=1, source_target_pairs={{0,16},{4,20},{8,24},{12,28},{16,0},{20,4},{24,8},{28,12},{1,17},{... | collective-permute-start | bytes 294920 | tf_op jit(solution)/shard_map/ppermute | solution.py:11
  61.0 8.9 %collective-permute-start.19 = (bf16[4,12288]{1,0:T(4,128)(2,1)S(1)}, bf16[4,12288]{1,0:T(4,128)(2,1)S(1)}, u32[]{:S(2)}, u32[]{:S(2)}) collective-permute-start(bf16[4,12288]{1,0:T(4,128)(2,1)S(1)} %get-tuple-element.7), channel_id=1, source_target_pairs={{0,24},{4,28},{8,16},{12,20},{16,8},{20,12},{24,0},{28,4},{1,25},{... | collective-permute-start | bytes 294920 | tf_op jit(solution)/shard_map/ppermute | solution.py:11
  62.7 7.8 %collective-permute-start.20 = (bf16[4,12288]{1,0:T(4,128)(2,1)S(1)}, bf16[4,12288]{1,0:T(4,128)(2,1)S(1)}, u32[]{:S(2)}, u32[]{:S(2)}) collective-permute-start(bf16[4,12288]{1,0:T(4,128)(2,1)S(1)} %get-tuple-element.7), channel_id=1, source_target_pairs={{0,4},{4,0},{8,12},{12,8},{16,20},{20,16},{24,28},{28,24},{1,5},{5... | collective-permute-start | bytes 294920 | tf_op jit(solution)/shard_map/ppermute | solution.py:11
  64.0 6.6 %collective-permute-start.21 = (bf16[4,12288]{1,0:T(4,128)(2,1)S(1)}, bf16[4,12288]{1,0:T(4,128)(2,1)S(1)}, u32[]{:S(2)}, u32[]{:S(2)}) collective-permute-start(bf16[4,12288]{1,0:T(4,128)(2,1)S(1)} %collective-permute-done.17), channel_id=1, source_target_pairs={{0,4},{4,0},{8,12},{12,8},{16,20},{20,16},{24,28},{28,24},{1,5},{5... | collective-permute-start | bytes 294920 | tf_op jit(solution)/shard_map/ppermute | solution.py:11
  69.9 1.5 %collective-permute-start.23 = (bf16[4,12288]{1,0:T(4,128)(2,1)S(1)}, bf16[4,12288]{1,0:T(4,128)(2,1)S(1)}, u32[]{:S(2)}, u32[]{:S(2)}) collective-permute-start(bf16[4,12288]{1,0:T(4,128)(2,1)S(1)} %collective-permute-done.19), channel_id=1, source_target_pairs={{0,4},{4,0},{8,12},{12,8},{16,20},{20,16},{24,28},{28,24},{1,5},{5... | collective-permute-start | bytes 294920 | tf_op jit(solution)/shard_map/ppermute | solution.py:11
  77.5 5.1 %collective-permute-start.24 = (bf16[8,6144]{1,0:T(8,128)(2,1)S(1)}, bf16[8,6144]{1,0:T(8,128)(2,1)S(1)}, u32[]{:S(2)}, u32[]{:S(2)}) collective-permute-start(bf16[8,6144]{1,0:T(8,128)(2,1)S(1)} %get-tuple-element.13), channel_id=1, source_target_pairs={{0,1},{1,0},{2,3},{3,2},{4,5},{5,4},{6,7},{7,6},{8,9},{9,8},{10,11... | collective-permute-start | bytes 294920 | tf_op jit(solution)/shard_map/ppermute | solution.py:11
  79.1 6.9 %collective-permute-start.25 = (bf16[8,6144]{1,0:T(8,128)(2,1)S(1)}, bf16[8,6144]{1,0:T(8,128)(2,1)S(1)}, u32[]{:S(2)}, u32[]{:S(2)}) collective-permute-start(bf16[8,6144]{1,0:T(8,128)(2,1)S(1)} %get-tuple-element.15), channel_id=1, source_target_pairs={{0,2},{1,3},{2,0},{3,1},{4,6},{5,7},{6,4},{7,5},{8,10},{9,11},{10,... | collective-permute-start | bytes 294920 | tf_op jit(solution)/shard_map/ppermute | solution.py:11
  79.9 6.0 %collective-permute-start.26 = (bf16[8,6144]{1,0:T(8,128)(2,1)S(1)}, bf16[8,6144]{1,0:T(8,128)(2,1)S(1)}, u32[]{:S(2)}, u32[]{:S(2)}) collective-permute-start(bf16[8,6144]{1,0:T(8,128)(2,1)S(1)} %get-tuple-element.14), channel_id=1, source_target_pairs={{0,3},{1,2},{2,1},{3,0},{4,7},{5,6},{6,5},{7,4},{8,11},{9,10},{10,... | collective-permute-start | bytes 294920 | tf_op jit(solution)/shard_map/ppermute | solution.py:11
  86.0 5.5 %collective-permute-start.27 = (bf16[8,6144]{1,0:T(8,128)(2,1)S(1)}, bf16[8,6144]{1,0:T(8,128)(2,1)S(1)}, u32[]{:S(2)}, u32[]{:S(2)}) collective-permute-start(bf16[8,6144]{1,0:T(8,128)(2,1)S(1)} %get-tuple-element.5), channel_id=1, source_target_pairs={{0,1},{1,0},{2,3},{3,2},{4,5},{5,4},{6,7},{7,6},{8,9},{9,8},{10,11... | collective-permute-start | bytes 294920 | tf_op jit(solution)/shard_map/ppermute | solution.py:11
  86.7 5.9 %collective-permute-start.28 = (bf16[8,6144]{1,0:T(8,128)(2,1)S(1)}, bf16[8,6144]{1,0:T(8,128)(2,1)S(1)}, u32[]{:S(2)}, u32[]{:S(2)}) collective-permute-start(bf16[8,6144]{1,0:T(8,128)(2,1)S(1)} %get-tuple-element.5), channel_id=1, source_target_pairs={{0,2},{1,3},{2,0},{3,1},{4,6},{5,7},{6,4},{7,5},{8,10},{9,11},{10,... | collective-permute-start | bytes 294920 | tf_op jit(solution)/shard_map/ppermute | solution.py:11
  87.9 5.5 %collective-permute-start.29 = (bf16[8,6144]{1,0:T(8,128)(2,1)S(1)}, bf16[8,6144]{1,0:T(8,128)(2,1)S(1)}, u32[]{:S(2)}, u32[]{:S(2)}) collective-permute-start(bf16[8,6144]{1,0:T(8,128)(2,1)S(1)} %get-tuple-element.5), channel_id=1, source_target_pairs={{0,3},{1,2},{2,1},{3,0},{4,7},{5,6},{6,5},{7,4},{8,11},{9,10},{10,... | collective-permute-start | bytes 294920 | tf_op jit(solution)/shard_map/ppermute | solution.py:11
  99.2 1.8 %collective-permute-start.30 = (bf16[4,4,12288]{2,1,0:T(4,128)(2,1)S(1)}, bf16[4,4,12288]{2,1,0:T(4,128)(2,1)S(1)}, u32[]{:S(2)}, u32[]{:S(2)}) collective-permute-start(bf16[4,4,12288]{2,1,0:T(4,128)(2,1)S(1)} %dynamic-slice_bitcast_fusion), channel_id=1, source_target_pairs={{0,4},{4,0},{8,12},{12,8},{16,20},{20,16},{24,28},{28,24},{1,5},{5... | collective-permute-start | bytes 1179656 | tf_op jit(solution)/shard_map/ppermute | solution.py:11
  101.3 6.1 %collective-permute-start.31 = (bf16[4,12288]{1,0:T(4,128)(2,1)S(1)}, bf16[4,12288]{1,0:T(4,128)(2,1)S(1)}, u32[]{:S(2)}, u32[]{:S(2)}) collective-permute-start(bf16[4,12288]{1,0:T(4,128)(2,1)S(1)} %get-tuple-element.10), channel_id=1, source_target_pairs={{0,8},{4,12},{8,0},{12,4},{16,24},{20,28},{24,16},{28,20},{1,9},{5... | collective-permute-start | bytes 294920 | tf_op jit(solution)/shard_map/ppermute | solution.py:11
  102.5 10.7 %collective-permute-start.32 = (bf16[4,12288]{1,0:T(4,128)(2,1)S(1)}, bf16[4,12288]{1,0:T(4,128)(2,1)S(1)}, u32[]{:S(2)}, u32[]{:S(2)}) collective-permute-start(bf16[4,12288]{1,0:T(4,128)(2,1)S(1)} %get-tuple-element.12), channel_id=1, source_target_pairs={{0,16},{4,20},{8,24},{12,28},{16,0},{20,4},{24,8},{28,12},{1,17},{... | collective-permute-start | bytes 294920 | tf_op jit(solution)/shard_map/ppermute | solution.py:11
  104.2 9.0 %collective-permute-start.33 = (bf16[4,12288]{1,0:T(4,128)(2,1)S(1)}, bf16[4,12288]{1,0:T(4,128)(2,1)S(1)}, u32[]{:S(2)}, u32[]{:S(2)}) collective-permute-start(bf16[4,12288]{1,0:T(4,128)(2,1)S(1)} %get-tuple-element.11), channel_id=1, source_target_pairs={{0,24},{4,28},{8,16},{12,20},{16,8},{20,12},{24,0},{28,4},{1,25},{... | collective-permute-start | bytes 294920 | tf_op jit(solution)/shard_map/ppermute | solution.py:11
  (5 other events, 45.2 us)

commit v2 on v1

--- a/solution.py
+++ b/solution.py
@@ -11,60 +11,47 @@
     return lax.ppermute(value, axis, [(i, i ^ offset) for i in range(count)])
 
 
-def pick(pieces, index):
-    return lax.dynamic_index_in_dim(pieces, index, 0, keepdims=False)
+def trade(pieces, axis, groups=None):
+    return lax.all_to_all(pieces, axis, 0, 0, tiled=True, axis_index_groups=groups)
 
 
-def place(parts, order, offsets):
-    me = order
-    stacked = jnp.stack(parts)
-    out = jnp.zeros_like(stacked)
-    for part, offset in zip(parts, offsets):
-        out = lax.dynamic_update_slice_in_dim(out, part[None], me ^ offset, 0)
-    return out
+def same_core(count):
+    return [list(range(core, count, 2)) for core in range(2)]
+
+
+def spread(piece, count):
+    return jnp.broadcast_to(piece[None], (count, *piece.shape))
+
+
+def add_up(parts):
+    return jnp.sum(parts.astype(jnp.float32), axis=0).astype(parts.dtype)
 
 
 def gather_direct(piece, axis):
-    count = lax.axis_size(axis)
-    me = lax.axis_index(axis)
-    parts = [piece] + [swap(piece, axis, k) for k in range(1, count)]
-    return place(parts, me, range(count))
+    return trade(spread(piece, lax.axis_size(axis)), axis)
 
 
 def gather_pairs(piece, axis):
     count = lax.axis_size(axis)
-    me = lax.axis_index(axis)
-    same = [piece] + [swap(piece, axis, k) for k in range(2, count, 2)]
-    other = [swap(part, axis, 1) for part in same]
-    parts = same + other
-    offsets = list(range(0, count, 2)) + [k ^ 1 for k in range(0, count, 2)]
-    return place(parts, me, offsets)
+    same = trade(spread(piece, count // 2), axis, same_core(count))
+    other = swap(same, axis, 1)
+    is_odd = (lax.axis_index(axis) & 1) == 1
+    pair = jnp.stack([jnp.where(is_odd, other, same), jnp.where(is_odd, same, other)], axis=1)
+    return pair.reshape(count, *piece.shape)
 
 
 def scatter_direct(pieces, axis):
-    count = lax.axis_size(axis)
-    me = lax.axis_index(axis)
-    arrived = [swap(pick(pieces, me ^ k), axis, k) for k in range(1, count)]
-    total = pick(pieces, me).astype(jnp.float32)
-    for part in arrived:
-        total = total + part.astype(jnp.float32)
-    return total.astype(pieces.dtype)
+    return add_up(trade(pieces, axis))
 
 
 def scatter_pairs(pieces, axis):
     count = lax.axis_size(axis)
-    me = lax.axis_index(axis)
-    side = me & 1
+    side = lax.axis_index(axis) & 1
     paired = pieces.reshape(count // 2, 2, *pieces.shape[1:])
     mine = lax.dynamic_index_in_dim(paired, side, 1, keepdims=False)
     theirs = lax.dynamic_index_in_dim(paired, 1 - side, 1, keepdims=False)
     summed = (mine.astype(jnp.float32) + swap(theirs, axis, 1).astype(jnp.float32)).astype(pieces.dtype)
-    place_of = me // 2
-    arrived = [swap(pick(summed, place_of ^ k), axis, 2 * k) for k in range(1, count // 2)]
-    total = pick(summed, place_of).astype(jnp.float32)
-    for part in arrived:
-        total = total + part.astype(jnp.float32)
-    return total.astype(pieces.dtype)
+    return add_up(trade(summed, axis, same_core(count)))
 
 
 def shards(strengths, blocks, pattern, level_gain):

time: 114 us -> 137 us (1.20)
  blocking collectives: 0 us -> 90.9 us
  waiting for transfers between devices: 49.2 us -> 11.2 us
  starting transfers between devices: 35.1 us -> 3.61 us
  other arithmetic: 2.96 us -> 4.87 us
    all_to_all x0 -> x7, blocking collectives: none -> 90.9 us  [trade(): lax.all_to_all(pieces, axis, 0, 0, tiled=True, axis_index_groups=groups)]
    ppermute x34 -> x4, waiting for transfers between devices: 49.2 us -> 5.32 us  [swap(): return lax.ppermute(value, axis, [(i, i ^ offset) for i in range(count)])]
    ppermute x34 -> x4, starting transfers between devices: 35.1 us -> 0.15 us  [swap(): return lax.ppermute(value, axis, [(i, i ^ offset) for i in range(count)])]
    all_to_all x0 -> x1, waiting for transfers between devices: none -> 5.84 us  [trade(): lax.all_to_all(pieces, axis, 0, 0, tiled=True, axis_index_groups=groups)]
    all_to_all x0 -> x1, starting transfers between devices: none -> 3.46 us  [trade(): lax.all_to_all(pieces, axis, 0, 0, tiled=True, axis_index_groups=groups)]
    broadcast_in_dim x0 -> x4, local copies, waits for them, and re-layouts: none -> 1.89 us  [spread(): return jnp.broadcast_to(piece[None], (count, *piece.shape))]
    dynamic_update_slice x21 -> x0, local copies, waits for them, and re-layouts: 1.74 us -> none  [place(): out = lax.dynamic_update_slice_in_dim(out, part[None], me ^ offset, 0)]
    another operation x0 -> x4, other arithmetic: none -> 1.71 us  [gather_pairs(): jnp.stack([jnp.where(is_odd, other, same), jnp.where(is_odd, same, other)...]
  transfers between devices with their start and end apart: 34 -> 5, of which waited for: 24 -> 5; matrix products, arithmetic and copies ran while one was open for 3% -> 1% of each run, Pallas kernels for 0% -> 0%
where the time goes in v2:
time: 137 us
  blocking collectives  90.9 us (66%)
  matrix products  20 us (15%)
  waiting for transfers between devices  11.2 us (8%)
  local copies, waits for them, and re-layouts  5.27 us (4%)
  other arithmetic  4.87 us (4%)
  starting transfers between devices  3.61 us (3%)
    all_to_all x7, blocking collectives, trade(): lax.all_to_all(pieces, axis, 0, 0, tiled=True, axis_index_groups=groups)  90.9 us
    dot_general x2, matrix products, forward_terms(): jnp.einsum('skm,snm->skn', picked, blocks, preferred_element_type=jnp.flo...  7.07 us
    dot_general x2, matrix products, adjoint_terms(): jnp.einsum('skn,snm->skm', picked, blocks, preferred_element_type=jnp.flo...  6.22 us
    all_to_all x1, waiting for transfers between devices, trade(): lax.all_to_all(pieces, axis, 0, 0, tiled=True, axis_index_groups=groups)  5.84 us
    ppermute x4, waiting for transfers between devices, swap(): return lax.ppermute(value, axis, [(i, i ^ offset) for i in range(count)])  5.32 us
    all_to_all x1, starting transfers between devices, trade(): lax.all_to_all(pieces, axis, 0, 0, tiled=True, axis_index_groups=groups)  3.46 us
    dot_general x2, matrix products, adjoint_terms(): jnp.einsum('sc,skm->kcm', col_pick.astype(jnp.float32), contrib, precisio...  3.06 us
  transfers between devices with their start and end apart: 5, of which 5 were waited for; matrix products, arithmetic and copies ran while one was open for 1% of the time, Pallas kernels for 0%

profile of v2, /device:TPU:0, one launch (start us, length us, event | category | flops | bytes accessed | tf_op | source)
XLA Modules:
  0.0 136.8 jit_solution(2735667974074423716)
XLA Ops:
  0.6 1.0 broadcast_in_dim.20
  1.6 17.8 %all_to_all.40 = bf16[4,4,12288]{2,1,0:T(4,128)(2,1)S(1)} all-to-all(bf16[4,4,12288]{2,1,0:T(4,128)(2,1)S(1)} %broadcast_in_dim.20), channel_id=1, replica_groups={{0,8,16,24},{4,12,20,28},{1,9,17,25},{5,13,21,29},{2,10,18,26},{6,14,22..., dimensions={0} | all-to-all | bytes 786432 | tf_op jit(solution)/shard_map/all_to_all | solution.py:15
  19.4 0.8 subtract_bitcast_fusion
  20.2 0.7 select_reduce_fusion
  21.5 0.6 pad_maximum_fusion
  22.3 0.6 reshape_reshape_reshape.6
  23.2 3.5 %convolution_multiply_fusion.3 = f32[32,32,256]{2,1,0:T(8,128)S(1)} fusion(bf16[32,256,256]{2,1,0:T(8,128)(2,1)} %param.5, bf16[32,32,256]{2,0,1:T(8,128)(2,1)S(1)} %convolution_convert_fusion.5, f32[32]{0:T(128)S(1)} %select_reduce_fusion), kind=kOutput, calls=%fused_computation.5 | convolution fusion | flops 134479872 | bytes 5767296 | tf_op jit(solution)/shard_map/skm,snm->skn/dot_general | solution.py:79
  26.8 1.2 fusion.2
  28.1 11.1 %all_to_all.41 = bf16[4,8,6144]{2,1,0:T(8,128)(2,1)S(1)} all-to-all(bf16[4,8,6144]{2,1,0:T(8,128)(2,1)S(1)} %convert_element_type.95), channel_id=1, replica_groups=mesh['panel'=8,'case'=4] {'case'}, dimensions={0} | all-to-all | bytes 786432 | tf_op jit(solution)/shard_map/all_to_all | solution.py:15
  39.3 0.8 broadcast_in_dim.23
  40.1 3.5 %all-to-all-start.2 = ((bf16[4,8,6144]{2,1,0:T(8,128)(2,1)}), bf16[4,8,6144]{2,1,0:T(8,128)(2,1)S(1)}, u32[]{:S(2)}, u32[]{:S(2)}) async-start(bf16[4,8,6144]{2,1,0:T(8,128)(2,1)} %broadcast_in_dim.23), calls=%async_computation.2 | async-start | bytes 786432 | tf_op jit(solution)/shard_map/all_to_all | solution.py:15
  43.5 5.8 %all-to-all-done.2 = bf16[4,8,6144]{2,1,0:T(8,128)(2,1)S(1)} async-done(((bf16[4,8,6144]{2,1,0:T(8,128)(2,1)}), bf16[4,8,6144]{2,1,0:T(8,128)(2,1)S(1)}, u32[]{:S(2)}, u32[]{:S(2)}) %all-to-all-start.2) | async-done | bytes 393248 | tf_op jit(solution)/shard_map/all_to_all | solution.py:15
  49.8 3.1 %convolution_multiply_fusion.2 = f32[32,32,256]{2,1,0:T(8,128)S(1)} fusion(bf16[32,256,256]{2,1,0:T(8,128)(2,1)} %param.5, bf16[32,32,256]{2,0,1:T(8,128)(2,1)S(1)} %convolution_convert_fusion.4, f32[32]{0:T(128)S(1)} %select_reduce_fusion), kind=kOutput, calls=%fused_computation.4 | convolution fusion | flops 134479872 | bytes 5767296 | tf_op jit(solution)/shard_map/skn,snm->skm/dot_general | solution.py:93
  52.9 1.5 %fusion = bf16[32,48,256]{2,1,0:T(8,128)(2,1)S(1)} fusion(f32[32,32,256]{2,1,0:T(8,128)S(1)} %convolution_multiply_fusion.2, s32[32]{0:T(128)S(1)} %get-tuple-element.9), kind=kOutput, calls=%fused_computation.6 | convolution fusion | flops 151389696 | bytes 1835136 | tf_op jit(solution)/shard_map/sc,skm->kcm/dot_general | solution.py:96
  54.5 0.6 convert_element_type.99
  55.3 1.7 %collective-permute-done.1 = bf16[4,4,12288]{2,1,0:T(4,128)(2,1)S(1)} collective-permute-done((bf16[4,4,12288]{2,1,0:T(4,128)(2,1)S(1)}, bf16[4,4,12288]{2,1,0:T(4,128)(2,1)S(1)}, u32[]{:S(2)}, u32[]{:S(2)}) %collective-permute-start.1) | collective-permute-done | bytes 393248 | tf_op jit(solution)/shard_map/ppermute | solution.py:11
  57.2 14.7 %all_to_all.42 = bf16[4,4,12288]{2,1,0:T(4,128)(2,1)S(1)} all-to-all(bf16[4,4,12288]{2,1,0:T(4,128)(2,1)S(1)} %fusion.9), channel_id=1, replica_groups={{0,8,16,24},{4,12,20,28},{1,9,17,25},{5,13,21,29},{2,10,18,26},{6,14,22..., dimensions={0} | all-to-all | bytes 786432 | tf_op jit(solution)/shard_map/all_to_all | solution.py:15
  72.2 13.8 %all_to_all.43 = bf16[4,4,12288]{2,1,0:T(4,128)(2,1)S(1)} all-to-all(bf16[4,4,12288]{2,1,0:T(4,128)(2,1)S(1)} %broadcast_in_dim.24), channel_id=1, replica_groups={{0,8,16,24},{4,12,20,28},{1,9,17,25},{5,13,21,29},{2,10,18,26},{6,14,22..., dimensions={0} | all-to-all | bytes 786432 | tf_op jit(solution)/shard_map/all_to_all | solution.py:15
  86.0 1.7 %collective-permute-done.2 = bf16[4,4,12288]{2,1,0:T(4,128)(2,1)S(1)} collective-permute-done((bf16[4,4,12288]{2,1,0:T(4,128)(2,1)S(1)}, bf16[4,4,12288]{2,1,0:T(4,128)(2,1)S(1)}, u32[]{:S(2)}, u32[]{:S(2)}) %collective-permute-start.2) | collective-permute-done | bytes 393248 | tf_op jit(solution)/shard_map/ppermute | solution.py:11
  88.0 0.5 pad_maximum_fusion.1
  88.6 0.6 reshape_reshape_reshape.7
  89.2 0.3 convolution_convert_fusion.3
  89.5 3.5 %convolution_multiply_fusion.1 = f32[32,32,256]{2,1,0:T(8,128)S(1)} fusion(bf16[32,256,256]{2,1,0:T(8,128)(2,1)} %param.5, bf16[32,32,256]{2,0,1:T(8,128)(2,1)S(1)} %convolution_convert_fusion.3, f32[32]{0:T(128)S(1)} %select_reduce_fusion), kind=kOutput, calls=%fused_computation.3 | convolution fusion | flops 134479872 | bytes 5767296 | tf_op jit(solution)/shard_map/skm,snm->skn/dot_general | solution.py:79
  93.1 1.1 fusion.3
  94.4 10.1 %all_to_all.44 = bf16[4,8,6144]{2,1,0:T(8,128)(2,1)S(1)} all-to-all(bf16[4,8,6144]{2,1,0:T(8,128)(2,1)S(1)} %convert_element_type.107), channel_id=1, replica_groups=mesh['panel'=8,'case'=4] {'case'}, dimensions={0} | all-to-all | bytes 786432 | tf_op jit(solution)/shard_map/all_to_all | solution.py:15
  104.6 8.8 %all_to_all.45 = bf16[4,8,6144]{2,1,0:T(8,128)(2,1)S(1)} all-to-all(bf16[4,8,6144]{2,1,0:T(8,128)(2,1)S(1)} %broadcast_in_dim.25), channel_id=1, replica_groups=mesh['panel'=8,'case'=4] {'case'}, dimensions={0} | all-to-all | bytes 786432 | tf_op jit(solution)/shard_map/all_to_all | solution.py:15
  113.9 3.1 %convolution_multiply_fusion = f32[32,32,256]{2,1,0:T(8,128)S(1)} fusion(bf16[32,256,256]{2,1,0:T(8,128)(2,1)} %param.5, bf16[32,32,256]{2,0,1:T(8,128)(2,1)S(1)} %convolution_convert_fusion.2, f32[32]{0:T(128)S(1)} %select_reduce_fusion), kind=kOutput, calls=%fused_computation.2 | convolution fusion | flops 134479872 | bytes 5767296 | tf_op jit(solution)/shard_map/skn,snm->skm/dot_general | solution.py:93
  117.0 1.5 %fusion.1 = bf16[32,48,256]{2,1,0:T(8,128)(2,1)S(1)} fusion(f32[32,32,256]{2,1,0:T(8,128)S(1)} %convolution_multiply_fusion, s32[32]{0:T(128)S(1)} %get-tuple-element.9), kind=kOutput, calls=%fused_computation.7 | convolution fusion | flops 151389696 | bytes 1835136 | tf_op jit(solution)/shard_map/sc,skm->kcm/dot_general | solution.py:96
  118.5 0.6 convert_element_type.111
  119.3 1.7 %collective-permute-done.3 = bf16[4,4,12288]{2,1,0:T(4,128)(2,1)S(1)} collective-permute-done((bf16[4,4,12288]{2,1,0:T(4,128)(2,1)S(1)}, bf16[4,4,12288]{2,1,0:T(4,128)(2,1)S(1)}, u32[]{:S(2)}, u32[]{:S(2)}) %collective-permute-start.3) | collective-permute-done | bytes 393248 | tf_op jit(solution)/shard_map/ppermute | solution.py:11
  121.2 14.7 %all_to_all.46 = bf16[4,4,12288]{2,1,0:T(4,128)(2,1)S(1)} all-to-all(bf16[4,4,12288]{2,1,0:T(4,128)(2,1)S(1)} %fusion.8), channel_id=1, replica_groups={{0,8,16,24},{4,12,20,28},{1,9,17,25},{5,13,21,29},{2,10,18,26},{6,14,22..., dimensions={0} | all-to-all | bytes 786432 | tf_op jit(solution)/shard_map/all_to_all | solution.py:15
  135.9 0.9 reduce_sum.61
  (30 shorter events, 4.0 us)
Async XLA Ops:
  19.4 1.7 %collective-permute-start = (bf16[4,4,12288]{2,1,0:T(4,128)(2,1)S(1)}, bf16[4,4,12288]{2,1,0:T(4,128)(2,1)S(1)}, u32[]{:S(2)}, u32[]{:S(2)}) collective-permute-start(bf16[4,4,12288]{2,1,0:T(4,128)(2,1)S(1)} %all_to_all.40), channel_id=1, source_target_pairs={{0,4},{4,0},{8,12},{12,8},{16,20},{20,16},{24,28},{28,24},{1,5},{5... | collective-permute-start | bytes 1179656 | tf_op jit(solution)/shard_map/ppermute | solution.py:11
  39.3 13.6 %copy-start = (bf16[8,6144]{1,0:T(8,128)(2,1)}, bf16[8,6144]{1,0:T(8,128)(2,1)S(1)}, u32[]{:S(2)}) copy-start(bf16[8,6144]{1,0:T(8,128)(2,1)S(1)} %reduce_sum.58) | copy-start | bytes 294916
  40.1 9.3 %all-to-all-start.2 = ((bf16[4,8,6144]{2,1,0:T(8,128)(2,1)}), bf16[4,8,6144]{2,1,0:T(8,128)(2,1)S(1)}, u32[]{:S(2)}, u32[]{:S(2)}) async-start(bf16[4,8,6144]{2,1,0:T(8,128)(2,1)} %broadcast_in_dim.23), calls=%async_computation.2 | async-start | bytes 786432 | tf_op jit(solution)/shard_map/all_to_all | solution.py:15
  55.2 1.8 %collective-permute-start.1 = (bf16[4,4,12288]{2,1,0:T(4,128)(2,1)S(1)}, bf16[4,4,12288]{2,1,0:T(4,128)(2,1)S(1)}, u32[]{:S(2)}, u32[]{:S(2)}) collective-permute-start(bf16[4,4,12288]{2,1,0:T(4,128)(2,1)S(1)} %dynamic-slice_bitcast_fusion.1), channel_id=1, source_target_pairs={{0,4},{4,0},{8,12},{12,8},{16,20},{20,16},{24,28},{28,24},{1,5},{5... | collective-permute-start | bytes 1179656 | tf_op jit(solution)/shard_map/ppermute | solution.py:11
  72.1 21.0 %copy-start.1 = (bf16[4,12288]{1,0:T(4,128)(2,1)}, bf16[4,12288]{1,0:T(4,128)(2,1)S(1)}, u32[]{:S(2)}) copy-start(bf16[4,12288]{1,0:T(4,128)(2,1)S(1)} %reduce_sum.59) | copy-start | bytes 294916
  86.0 1.7 %collective-permute-start.2 = (bf16[4,4,12288]{2,1,0:T(4,128)(2,1)S(1)}, bf16[4,4,12288]{2,1,0:T(4,128)(2,1)S(1)}, u32[]{:S(2)}, u32[]{:S(2)}) collective-permute-start(bf16[4,4,12288]{2,1,0:T(4,128)(2,1)S(1)} %all_to_all.43), channel_id=1, source_target_pairs={{0,4},{4,0},{8,12},{12,8},{16,20},{20,16},{24,28},{28,24},{1,5},{5... | collective-permute-start | bytes 1179656 | tf_op jit(solution)/shard_map/ppermute | solution.py:11
  104.6 12.4 %copy-start.2 = (bf16[8,6144]{1,0:T(8,128)(2,1)}, bf16[8,6144]{1,0:T(8,128)(2,1)S(1)}, u32[]{:S(2)}) copy-start(bf16[8,6144]{1,0:T(8,128)(2,1)S(1)} %reduce_sum.60) | copy-start | bytes 294916
  119.2 1.8 %collective-permute-start.3 = (bf16[4,4,12288]{2,1,0:T(4,128)(2,1)S(1)}, bf16[4,4,12288]{2,1,0:T(4,128)(2,1)S(1)}, u32[]{:S(2)}, u32[]{:S(2)}) collective-permute-start(bf16[4,4,12288]{2,1,0:T(4,128)(2,1)S(1)} %dynamic-slice_bitcast_fusion), channel_id=1, source_target_pairs={{0,4},{4,0},{8,12},{12,8},{16,20},{20,16},{24,28},{28,24},{1,5},{5... | collective-permute-start | bytes 1179656 | tf_op jit(solution)/shard_map/ppermute | solution.py:11

commit v3 on v0

v3 whole, which is shorter than its diff:
```python
import functools

import jax
import jax.numpy as jnp
from jax import lax
from jax.experimental import pallas as pl
from jax.experimental.pallas import tpu as pltpu
from jax.sharding import PartitionSpec as P

B = 256
LANES = 128
PER = B // LANES
COPIES = 4
VMEM_LIMIT = 32 * 1024 * 1024


def swap(value, axis, offset):
    count = lax.axis_size(axis)
    return lax.ppermute(value, axis, [(i, i ^ offset) for i in range(count)])


def add_up(*parts):
    total = parts[0].astype(jnp.float32)
    for part in parts[1:]:
        total = total + part.astype(jnp.float32)
    return total.astype(parts[0].dtype)


def start_blocks(blocks_ref, held, sems):
    share = blocks_ref.shape[0] // COPIES
    copies = []
    for i in range(COPIES):
        span = pl.ds(i * share, share)
        copies.append(pltpu.make_async_copy(blocks_ref.at[span], held.at[span], sems.at[i]))
        copies[-1].start()
    return copies


def slot_of(entry_ref, gain_ref, slot):
    level = entry_ref[slot, 2]
    scale = jnp.where(level >= 0, gain_ref[jnp.maximum(level, 0)], jnp.float32(0.0))
    return entry_ref[slot, 0], entry_ref[slot, 1], scale


def add_products(entry_ref, gain_ref, load, held, copies, total, adjoint):
    total[...] = jnp.zeros_like(total)
    slots = held.shape[0]
    share = slots // COPIES
    for slot in range(slots):
        if slot % share == 0:
            copies[slot // share].wait()
        row, col, scale = slot_of(entry_ref, gain_ref, slot)
        source, target = (row, col) if adjoint else (col, row)
        term = lax.dot_general(
            load(source),
            held[slot],
            (((1,), (0 if adjoint else 1,)), ((), ())),
            preferred_element_type=jnp.float32,
        )
        term = term * scale
        for part in range(PER):
            total[target * PER + part] += term[:, part * LANES : (part + 1) * LANES]


def first_kernel(entry_ref, gain_ref, x_ref, blocks_ref, low_ref, high_ref, held, total, sems):
    copies = start_blocks(blocks_ref, held, sems)

    def load(block):
        return x_ref[:, pl.ds(pl.multiple_of(block * B, B), B)]

    add_products(entry_ref, gain_ref, load, held, copies, total, False)
    half = low_ref.shape[0]
    low_ref[...] = total[:half].astype(low_ref.dtype)
    high_ref[...] = total[half:].astype(high_ref.dtype)


def load_from(x):
    def load(block):
        return jnp.concatenate([x[block * PER + part] for part in range(PER)], axis=1)

    return load


def forward_kernel(ways, entry_ref, gain_ref, place_ref, *refs):
    pieces = refs[: 2 * ways]
    blocks_ref, low_ref, high_ref, held, total, x, sems = refs[2 * ways :]
    copies = start_blocks(blocks_ref, held, sems)
    core, along = place_ref[0], place_ref[1]
    size = pieces[0].shape[0]
    for side in range(2):
        for way in range(ways):
            at = ((core ^ side) * ways + (along ^ way)) * size
            x[pl.ds(at, size)] = pieces[side * ways + way][...]
    add_products(entry_ref, gain_ref, load_from(x), held, copies, total, False)
    half = low_ref.shape[0]
    low_ref[...] = total[:half].astype(low_ref.dtype)
    high_ref[...] = total[half:].astype(high_ref.dtype)


def adjoint_kernel(ways, entry_ref, gain_ref, place_ref, low_ref, high_ref, blocks_ref, mine_ref, theirs_ref, held, total, x, sems):
    copies = start_blocks(blocks_ref, held, sems)
    half = low_ref.shape[0]
    x[:half] = low_ref[...]
    x[half:] = high_ref[...]
    add_products(entry_ref, gain_ref, load_from(x), held, copies, total, True)
    core, along = place_ref[0], place_ref[1]
    size = mine_ref.shape[1]
    for side, out_ref in enumerate((mine_ref, theirs_ref)):
        for way in range(ways):
            at = ((core ^ side) * ways + (along ^ way)) * size
            out_ref[way] = total[pl.ds(at, size)].astype(out_ref.dtype)


def last_kernel(ways, entry_ref, gain_ref, place_ref, low_ref, high_ref, blocks_ref, mine_ref, theirs_ref, held, total, x, sems):
    copies = start_blocks(blocks_ref, held, sems)
    half = low_ref.shape[0]
    x[:half] = low_ref[...]
    x[half:] = high_ref[...]
    add_products(entry_ref, gain_ref, load_from(x), held, copies, total, True)
    core, along = place_ref[0], place_ref[1]
    share = mine_ref.shape[1]
    groups = total.shape[0]
    for own in range(2):

        @pl.when(core == own)
        def _(own=own):
            def write(group, carry):
                lanes = pl.ds(pl.multiple_of(group * LANES, LANES), LANES)
                values = total[group].astype(mine_ref.dtype)
                for index in range(2 * ways):
                    out_ref = mine_ref if index % 2 == own else theirs_ref
                    out_ref[(index // 2) ^ along, :, lanes] = values[index * share : (index + 1) * share]
                return carry

            lax.fori_loop(0, groups, write, 0)


def shards(strengths, blocks, pattern, level_gain):
    n_panel = lax.axis_size("panel")
    n_case = lax.axis_size("case")
    ways = n_panel // 2
    share, width = strengths.shape
    cases = share * n_panel
    slots = blocks.shape[0]
    col_blocks = width // B
    row_blocks = col_blocks * n_case // n_panel
    col_groups = col_blocks * PER
    row_groups = row_blocks * PER
    panel = lax.axis_index("panel")
    case = lax.axis_index("case")
    place = jnp.stack([panel % 2, panel // 2]).astype(jnp.int32)
    first = jnp.stack([panel * row_blocks, case * col_blocks, 0]).astype(jnp.int32)
    entry = jnp.where(pattern[:, 2:3] < 0, jnp.array([0, 0, -1], jnp.int32), pattern - first)
    value = strengths.dtype

    smem = pl.BlockSpec(memory_space=pltpu.SMEM)
    vmem = pl.BlockSpec(memory_space=pltpu.VMEM)
    anywhere = pl.BlockSpec(memory_space=pl.ANY)

    def product(kernel, small, vectors, outs, total_groups, x_groups):
        scratch = [
            pltpu.VMEM(blocks.shape, blocks.dtype),
            pltpu.VMEM((total_groups, cases, LANES), jnp.float32),
        ]
        if x_groups:
            scratch.append(pltpu.VMEM((x_groups, cases, LANES), value))
        scratch.append(pltpu.SemaphoreType.DMA((COPIES,)))
        return pl.pallas_call(
            kernel,
            out_shape=[jax.ShapeDtypeStruct(shape, value) for shape in outs],
            in_specs=[smem] * len(small) + [vmem] * len(vectors) + [anywhere],
            out_specs=[vmem] * len(outs),
            scratch_shapes=scratch,
            compiler_params=pltpu.CompilerParams(vmem_limit_bytes=VMEM_LIMIT),
            cost_estimate=pl.CostEstimate(
                flops=2 * cases * slots * B * B, bytes_accessed=2 * slots * B * B, transcendentals=0
            ),
        )(*small, *vectors, blocks)

    half_rows = [(row_groups // 2, cases, LANES)] * 2
    piece = col_groups // n_panel

    def over_case(low, high):
        bits = [1 << b for b in range(n_case.bit_length() - 1)]
        for one, other in zip(bits, reversed(bits)):
            low_in, high_in = swap(low, "case", one), swap(high, "case", other)
            low, high = add_up(low, low_in), add_up(high, high_in)
        return low, high

    def scatter_panel(mine, theirs):
        summed = add_up(mine, swap(theirs, "panel", 1))
        arrived = [swap(summed[way], "panel", 2 * way) for way in range(1, ways)]
        return add_up(summed[0], *arrived)

    def gather_panel(part):
        same = [part] + [swap(part, "panel", 2 * way) for way in range(1, ways)]
        return same + [swap(one, "panel", 1) for one in same]

    def forward(pieces):
        return product(
            functools.partial(forward_kernel, ways), (entry, level_gain, place), pieces, half_rows, row_groups, col_groups
        )

    def own_cases(low, high):
        whole = jnp.concatenate([low, high])
        own = lax.dynamic_slice_in_dim(whole, case * (cases // n_case), cases // n_case, 1)
        return jnp.swapaxes(own, 0, 1).reshape(cases // n_case, row_groups * LANES)

    def own_share(pieces):
        own = jnp.stack([lax.dynamic_slice_in_dim(one, panel * share, share, 1) for one in pieces])
        own = own.reshape(2, ways, piece, share, LANES)
        own = jnp.where(panel % 2 == 1, own[::-1], own)
        bit = 1
        while bit < ways:
            flipped = own.reshape(2, ways // (2 * bit), 2, bit, piece, share, LANES)[:, :, ::-1].reshape(own.shape)
            own = jnp.where((panel // 2) & bit != 0, flipped, own)
            bit *= 2
        return jnp.moveaxis(own, 3, 0).reshape(share, width)

    same_first = [strengths] + [swap(strengths, "panel", 2 * way) for way in range(1, ways)]
    other_first = [swap(one, "panel", 1) for one in same_first]
    stacked = jnp.zeros((n_panel, share, width), value)
    for side, parts in enumerate((same_first, other_first)):
        for way, one in enumerate(parts):
            stacked = lax.dynamic_update_slice_in_dim(stacked, one[None], panel ^ (2 * way + side), 0)
    low, high = product(first_kernel, (entry, level_gain), [stacked.reshape(cases, width)], half_rows, row_groups, 0)
    low, high = over_case(low, high)
    forward_one = own_cases(low, high)

    mine, theirs = product(
        functools.partial(adjoint_kernel, ways),
        (entry, level_gain, place),
        [low, high],
        [(ways, piece, cases, LANES)] * 2,
        col_groups,
        row_groups,
    )
    pieces = gather_panel(scatter_panel(mine, theirs))
    adjoint_one = own_share(pieces)

    low, high = over_case(*forward(pieces))
    forward_two = own_cases(low, high)

    mine, theirs = product(
        functools.partial(last_kernel, ways),
        (entry, level_gain, place),
        [low, high],
        [(ways, share, width)] * 2,
        col_groups,
        row_groups,
    )
    adjoint_two = scatter_panel(mine, theirs)
    return (forward_one, adjoint_one, forward_two, adjoint_two)


def solution(mesh):
    in_specs = (
        P("panel", "case"),
        P(("panel", "case"), None, None),
        P(("panel", "case"), None),
        P(),
    )
    out_specs = (P("case", "panel"), P("panel", "case"), P("case", "panel"), P("panel", "case"))
    return jax.shard_map(shards, mesh=mesh, in_specs=in_specs, out_specs=out_specs, check_vma=False)
```

time: 267 us -> 109 us (0.41)
  waiting for transfers between devices: 198 us -> 46.2 us
  starting transfers between devices: 0.16 us -> 30.9 us
  matrix products: 20 us -> 0 us
  blocking collectives: 17.4 us -> 0 us
  between operations: 14.5 us -> 0.96 us
  Pallas kernels: 0 us -> 12 us
  other arithmetic: 1.54 us -> 5.4 us
    psum x3 -> x0, waiting for transfers between devices: 142 us -> none  [the longest x2 85.7 us: total_rows(): return lax.psum(partial_value.astype(jnp.bfloat16), 'case')]
    unnamed x5 -> x0, waiting for transfers between devices: 56 us -> none
    ppermute x0 -> x30, waiting for transfers between devices: none -> 46.2 us  [swap(): return lax.ppermute(value, axis, [(i, i ^ offset) for i in range(count)])]
    ppermute x0 -> x30, starting transfers between devices: none -> 30.9 us  [swap(): return lax.ppermute(value, axis, [(i, i ^ offset) for i in range(count)])]
    dot_general x12 -> x0, matrix products: 20 us -> none  [the longest x2 7.06 us: forward_terms(): jnp.einsum('skm,snm->skn', picked, blocks, preferred_element_type=jnp.flo...]
    all_gather x1 -> x0, blocking collectives: 17.4 us -> none  [shards(): lax.all_gather(strengths, 'panel', axis=0, tiled=True)]
    pallas_call x0 -> x4, Pallas kernels: none -> 12 us  [product(): pl.pallas_call(kernel, out_shape=[jax.ShapeDtypeStruct(shape, value) for...]
    dynamic_slice x3 -> x0, local copies, waits for them, and re-layouts: 4.72 us -> none  [the longest x1 1.63 us: shards(): lax.dynamic_slice_in_dim(adjoint_full, lax.axis_index('panel') * panel_sh...]
  transfers between devices with their start and end apart: 4 -> 30, of which waited for: 4 -> 20; matrix products, arithmetic and copies ran while one was open for 2% -> 7% of each run, Pallas kernels for 0% -> 0%
where the time goes in v3:
time: 109 us; the launch traced here: 108 us
  waiting for transfers between devices  46.2 us (42%)
  starting transfers between devices  30.9 us (28%)
  local copies, waits for them, and re-layouts  12.8 us (12%)
  Pallas kernels  12 us (11%)
  other arithmetic  5.4 us (5%)
    ppermute x30, waiting for transfers between devices, swap(): return lax.ppermute(value, axis, [(i, i ^ offset) for i in range(count)])  46.2 us
    ppermute x30, starting transfers between devices, swap(): return lax.ppermute(value, axis, [(i, i ^ offset) for i in range(count)])  30.9 us
    pallas_call x4, Pallas kernels, product(): pl.pallas_call(kernel, out_shape=[jax.ShapeDtypeStruct(shape, value) for...  12 us
    unnamed x19, local copies, waits for them, and re-layouts  9.54 us
  transfers between devices with their start and end apart: 30, of which 20 were waited for; matrix products, arithmetic and copies ran while one was open for 7% of the time, Pallas kernels for 0%

profile of v3, /device:TPU:0, one launch (start us, length us, event | category | flops | bytes accessed | tf_op | source)
XLA Modules:
  0.0 108.3 jit_solution(11470886527694347370)
XLA Ops:
  0.6 3.1 %collective-permute-start = (bf16[4,12288]{1,0:T(4,128)(2,1)}, bf16[4,12288]{1,0:T(4,128)(2,1)S(1)}, u32[]{:S(2)}, u32[]{:S(2)}) collective-permute-start(bf16[4,12288]{1,0:T(4,128)(2,1)} %param.5), channel_id=1, source_target_pairs={{0,8},{4,12},{8,0},{12,4},{16,24},{20,28},{24,16},{28,20},{1,9},{5... | collective-permute-start | bytes 294920 | tf_op jit(solution)/shard_map/ppermute | solution.py:19
  3.7 2.6 %collective-permute-start.1 = (bf16[4,12288]{1,0:T(4,128)(2,1)}, bf16[4,12288]{1,0:T(4,128)(2,1)S(1)}, u32[]{:S(2)}, u32[]{:S(2)}) collective-permute-start(bf16[4,12288]{1,0:T(4,128)(2,1)} %param.5), channel_id=1, source_target_pairs={{0,16},{4,20},{8,24},{12,28},{16,0},{20,4},{24,8},{28,12},{1,17},{... | collective-permute-start | bytes 294920 | tf_op jit(solution)/shard_map/ppermute | solution.py:19
  10.3 4.0 %collective-permute-done.1 = bf16[4,12288]{1,0:T(4,128)(2,1)S(1)} collective-permute-done((bf16[4,12288]{1,0:T(4,128)(2,1)}, bf16[4,12288]{1,0:T(4,128)(2,1)S(1)}, u32[]{:S(2)}, u32[]{:S(2)}) %collective-permute-start.1) | collective-permute-done | bytes 98336 | tf_op jit(solution)/shard_map/ppermute | solution.py:19
  16.1 2.2 %copy-done = bf16[32,256,256]{2,1,0:T(8,128)(2,1)S(1)} copy-done((bf16[32,256,256]{2,1,0:T(8,128)(2,1)S(1)}, bf16[32,256,256]{2,1,0:T(8,128)(2,1)}, u32[]{:S(2)}) %copy-start) | copy-done | bytes 4194328
  18.9 2.9 %shard_map.84 = (bf16[24,32,128]{2,1,0:T(8,128)(2,1)S(1)}, bf16[24,32,128]{2,1,0:T(8,128)(2,1)S(1)}) custom-call(s32[32,3]{1,0:T(8,128)S(1)} %broadcast_select_fusion.1.entry_ref, f32[8]{0:T(128)S(1)} %copy-done.4, bf16[32,12288]{1,0:T(8,128)(2,1)S(1)} %reshape.40.x_ref, bf16[32,256,256]{2,1,0:T(8,128)(2,1)S(1)} %copy-done), custom_call_target="tpu_custom_call" | custom-call | flops 134217728 | bytes 4194304 | tf_op jit(solution)/shard_map/pallas_call | solution.py:168
  21.9 1.6 %collective-permute-start.7 = (bf16[24,32,128]{2,1,0:T(8,128)(2,1)S(1)}, bf16[24,32,128]{2,1,0:T(8,128)(2,1)S(1)}, u32[]{:S(2)}, u32[]{:S(2)}) collective-permute-start(bf16[24,32,128]{2,1,0:T(8,128)(2,1)S(1)} %get-tuple-element.12), channel_id=1, source_target_pairs={{0,1},{1,0},{2,3},{3,2},{4,5},{5,4},{6,7},{7,6},{8,9},{9,8},{10,11... | collective-permute-start | bytes 589832 | tf_op jit(solution)/shard_map/ppermute | solution.py:19
  23.5 1.5 %collective-permute-start.9 = (bf16[24,32,128]{2,1,0:T(8,128)(2,1)S(1)}, bf16[24,32,128]{2,1,0:T(8,128)(2,1)S(1)}, u32[]{:S(2)}, u32[]{:S(2)}) collective-permute-start(bf16[24,32,128]{2,1,0:T(8,128)(2,1)S(1)} %get-tuple-element.13), channel_id=1, source_target_pairs={{0,2},{1,3},{2,0},{3,1},{4,6},{5,7},{6,4},{7,5},{8,10},{9,11},{10,... | collective-permute-start | bytes 589832 | tf_op jit(solution)/shard_map/ppermute | solution.py:19
  25.0 4.1 %collective-permute-done.7 = bf16[24,32,128]{2,1,0:T(8,128)(2,1)S(1)} collective-permute-done((bf16[24,32,128]{2,1,0:T(8,128)(2,1)S(1)}, bf16[24,32,128]{2,1,0:T(8,128)(2,1)S(1)}, u32[]{:S(2)}, u32[]{:S(2)}) %collective-permute-start.7) | collective-permute-done | bytes 196640 | tf_op jit(solution)/shard_map/ppermute | solution.py:19
  29.2 1.6 %collective-permute-start.8 = (bf16[24,32,128]{2,1,0:T(8,128)(2,1)S(1)}, bf16[24,32,128]{2,1,0:T(8,128)(2,1)S(1)}, u32[]{:S(2)}, u32[]{:S(2)}) collective-permute-start(bf16[24,32,128]{2,1,0:T(8,128)(2,1)S(1)} %add_convert_fusion.9), channel_id=1, source_target_pairs={{0,2},{1,3},{2,0},{3,1},{4,6},{5,7},{6,4},{7,5},{8,10},{9,11},{10,... | collective-permute-start | bytes 589832 | tf_op jit(solution)/shard_map/ppermute | solution.py:19
  30.8 1.6 %collective-permute-start.10 = (bf16[24,32,128]{2,1,0:T(8,128)(2,1)S(1)}, bf16[24,32,128]{2,1,0:T(8,128)(2,1)S(1)}, u32[]{:S(2)}, u32[]{:S(2)}) collective-permute-start(bf16[24,32,128]{2,1,0:T(8,128)(2,1)S(1)} %add_convert_fusion.7), channel_id=1, source_target_pairs={{0,1},{1,0},{2,3},{3,2},{4,5},{5,4},{6,7},{7,6},{8,9},{9,8},{10,11... | collective-permute-start | bytes 589832 | tf_op jit(solution)/shard_map/ppermute | solution.py:19
  32.3 3.2 %collective-permute-done.8 = bf16[24,32,128]{2,1,0:T(8,128)(2,1)S(1)} collective-permute-done((bf16[24,32,128]{2,1,0:T(8,128)(2,1)S(1)}, bf16[24,32,128]{2,1,0:T(8,128)(2,1)S(1)}, u32[]{:S(2)}, u32[]{:S(2)}) %collective-permute-start.8) | collective-permute-done | bytes 196640 | tf_op jit(solution)/shard_map/ppermute | solution.py:19
  37.0 2.2 %copy-done.1 = bf16[32,256,256]{2,1,0:T(8,128)(2,1)S(1)} copy-done((bf16[32,256,256]{2,1,0:T(8,128)(2,1)S(1)}, bf16[32,256,256]{2,1,0:T(8,128)(2,1)}, u32[]{:S(2)}) %copy-start.1) | copy-done | bytes 4194328
  39.2 2.5 %shard_map.85 = (bf16[4,12,32,128]{3,2,1,0:T(8,128)(2,1)S(1)}, bf16[4,12,32,128]{3,2,1,0:T(8,128)(2,1)S(1)}) custom-call(s32[32,3]{1,0:T(8,128)S(1)} %broadcast_select_fusion.1.entry_ref, f32[8]{0:T(128)S(1)} %copy-done.5, s32[2]{0:T(128)S(1)} %pad_add_fusion.1.place_ref, bf16[24,32,128]{2,1,0:T(8,128)(2,1)S(1)} %add_convert_fusion.8.low_ref, ...), custom_call_target="tpu_custom_call" | custom-call | flops 134217728 | bytes 4194304 | tf_op jit(solution)/shard_map/pallas_call | solution.py:168
  41.8 1.7 %collective-permute-done.11 = bf16[4,12,32,128]{3,2,1,0:T(8,128)(2,1)S(1)} collective-permute-done((bf16[4,12,32,128]{3,2,1,0:T(8,128)(2,1)S(1)}, bf16[4,12,32,128]{3,2,1,0:T(8,128)(2,1)S(1)}, u32[]{:S(2)}, u32[]{:S(2)}) %collective-permute-start.11) | collective-permute-done | bytes 393248 | tf_op jit(solution)/shard_map/ppermute | solution.py:19
  43.6 2.5 %collective-permute-start.14 = (bf16[12,32,128]{2,1,0:T(8,128)(2,1)S(1)}, bf16[12,32,128]{2,1,0:T(8,128)(2,1)S(1)}, u32[]{:S(2)}, u32[]{:S(2)}) collective-permute-start(bf16[12,32,128]{2,1,0:T(8,128)(2,1)S(1)} %get-tuple-element.24), channel_id=1, source_target_pairs={{0,24},{4,28},{8,16},{12,20},{16,8},{20,12},{24,0},{28,4},{1,25},{... | collective-permute-start | bytes 294920 | tf_op jit(solution)/shard_map/ppermute | solution.py:19
  46.2 1.9 %collective-permute-start.12 = (bf16[12,32,128]{2,1,0:T(8,128)(2,1)S(1)}, bf16[12,32,128]{2,1,0:T(8,128)(2,1)S(1)}, u32[]{:S(2)}, u32[]{:S(2)}) collective-permute-start(bf16[12,32,128]{2,1,0:T(8,128)(2,1)S(1)} %get-tuple-element.23), channel_id=1, source_target_pairs={{0,8},{4,12},{8,0},{12,4},{16,24},{20,28},{24,16},{28,20},{1,9},{5... | collective-permute-start | bytes 294920 | tf_op jit(solution)/shard_map/ppermute | solution.py:19
  48.8 2.5 %collective-permute-done.14 = bf16[12,32,128]{2,1,0:T(8,128)(2,1)S(1)} collective-permute-done((bf16[12,32,128]{2,1,0:T(8,128)(2,1)S(1)}, bf16[12,32,128]{2,1,0:T(8,128)(2,1)S(1)}, u32[]{:S(2)}, u32[]{:S(2)}) %collective-permute-start.14) | collective-permute-done | bytes 98336 | tf_op jit(solution)/shard_map/ppermute | solution.py:19
  51.2 4.1 %collective-permute-done.13 = bf16[12,32,128]{2,1,0:T(8,128)(2,1)S(1)} collective-permute-done((bf16[12,32,128]{2,1,0:T(8,128)(2,1)S(1)}, bf16[12,32,128]{2,1,0:T(8,128)(2,1)S(1)}, u32[]{:S(2)}, u32[]{:S(2)}) %collective-permute-start.13) | collective-permute-done | bytes 98336 | tf_op jit(solution)/shard_map/ppermute | solution.py:19
  55.5 3.0 %collective-permute-start.16 = (bf16[12,32,128]{2,1,0:T(8,128)(2,1)S(1)}, bf16[12,32,128]{2,1,0:T(8,128)(2,1)S(1)}, u32[]{:S(2)}, u32[]{:S(2)}) collective-permute-start(bf16[12,32,128]{2,1,0:T(8,128)(2,1)S(1)} %fusion.5.refs_0_), channel_id=1, source_target_pairs={{0,16},{4,20},{8,24},{12,28},{16,0},{20,4},{24,8},{28,12},{1,17},{... | collective-permute-start | bytes 294920 | tf_op jit(solution)/shard_map/ppermute | solution.py:19
  61.0 5.0 %collective-permute-done.16.refs_2_ = bf16[12,32,128]{2,1,0:T(8,128)(2,1)S(1)} collective-permute-done((bf16[12,32,128]{2,1,0:T(8,128)(2,1)S(1)}, bf16[12,32,128]{2,1,0:T(8,128)(2,1)S(1)}, u32[]{:S(2)}, u32[]{:S(2)}) %collective-permute-start.16) | collective-permute-done | bytes 98336 | tf_op jit(solution)/shard_map/ppermute | solution.py:19
  67.6 2.2 %copy-done.2 = bf16[32,256,256]{2,1,0:T(8,128)(2,1)S(1)} copy-done((bf16[32,256,256]{2,1,0:T(8,128)(2,1)S(1)}, bf16[32,256,256]{2,1,0:T(8,128)(2,1)}, u32[]{:S(2)}) %copy-start.2) | copy-done | bytes 4194328
  69.8 3.0 %shard_map.86 = (bf16[24,32,128]{2,1,0:T(8,128)(2,1)S(1)}, bf16[24,32,128]{2,1,0:T(8,128)(2,1)S(1)}) custom-call(s32[32,3]{1,0:T(8,128)S(1)} %broadcast_select_fusion.1.entry_ref, f32[8]{0:T(128)S(1)} %copy-done.5, s32[2]{0:T(128)S(1)} %pad_add_fusion.1.place_ref, bf16[12,32,128]{2,1,0:T(8,128)(2,1)S(1)} %fusion.5.refs_0_, ...), custom_call_target="tpu_custom_call" | custom-call | flops 134217728 | bytes 4194304 | tf_op jit(solution)/shard_map/pallas_call | solution.py:168
  72.8 1.6 %collective-permute-start.22 = (bf16[24,32,128]{2,1,0:T(8,128)(2,1)S(1)}, bf16[24,32,128]{2,1,0:T(8,128)(2,1)S(1)}, u32[]{:S(2)}, u32[]{:S(2)}) collective-permute-start(bf16[24,32,128]{2,1,0:T(8,128)(2,1)S(1)} %get-tuple-element.16), channel_id=1, source_target_pairs={{0,1},{1,0},{2,3},{3,2},{4,5},{5,4},{6,7},{7,6},{8,9},{9,8},{10,11... | collective-permute-start | bytes 589832 | tf_op jit(solution)/shard_map/ppermute | solution.py:19
  75.5 4.5 %collective-permute-done.22 = bf16[24,32,128]{2,1,0:T(8,128)(2,1)S(1)} collective-permute-done((bf16[24,32,128]{2,1,0:T(8,128)(2,1)S(1)}, bf16[24,32,128]{2,1,0:T(8,128)(2,1)S(1)}, u32[]{:S(2)}, u32[]{:S(2)}) %collective-permute-start.22) | collective-permute-done | bytes 196640 | tf_op jit(solution)/shard_map/ppermute | solution.py:19
  82.5 3.9 %collective-permute-done.23 = bf16[24,32,128]{2,1,0:T(8,128)(2,1)S(1)} collective-permute-done((bf16[24,32,128]{2,1,0:T(8,128)(2,1)S(1)}, bf16[24,32,128]{2,1,0:T(8,128)(2,1)S(1)}, u32[]{:S(2)}, u32[]{:S(2)}) %collective-permute-start.23) | collective-permute-done | bytes 196640 | tf_op jit(solution)/shard_map/ppermute | solution.py:19
  86.5 1.5 %collective-permute-done.25 = bf16[24,32,128]{2,1,0:T(8,128)(2,1)S(1)} collective-permute-done((bf16[24,32,128]{2,1,0:T(8,128)(2,1)S(1)}, bf16[24,32,128]{2,1,0:T(8,128)(2,1)S(1)}, u32[]{:S(2)}, u32[]{:S(2)}) %collective-permute-start.25) | collective-permute-done | bytes 196640 | tf_op jit(solution)/shard_map/ppermute | solution.py:19
  88.1 2.2 %copy-done.3 = bf16[32,256,256]{2,1,0:T(8,128)(2,1)S(1)} copy-done((bf16[32,256,256]{2,1,0:T(8,128)(2,1)S(1)}, bf16[32,256,256]{2,1,0:T(8,128)(2,1)}, u32[]{:S(2)}) %copy-start.3) | copy-done | bytes 4194328
  90.3 3.5 %shard_map.87 = (bf16[4,4,12288]{2,1,0:T(4,128)(2,1)S(1)}, bf16[4,4,12288]{2,1,0:T(4,128)(2,1)S(1)}) custom-call(s32[32,3]{1,0:T(8,128)S(1)} %broadcast_select_fusion.1.entry_ref, f32[8]{0:T(128)S(1)} %copy-done.5, s32[2]{0:T(128)S(1)} %pad_add_fusion.1.place_ref, bf16[24,32,128]{2,1,0:T(8,128)(2,1)S(1)} %add_convert_fusion.4.low_ref, ...), custom_call_target="tpu_custom_call" | custom-call | flops 134217728 | bytes 4194304 | tf_op jit(solution)/shard_map/pallas_call | solution.py:168
  96.0 2.3 %collective-permute-start.29 = (bf16[4,12288]{1,0:T(4,128)(2,1)S(1)}, bf16[4,12288]{1,0:T(4,128)(2,1)S(1)}, u32[]{:S(2)}, u32[]{:S(2)}) collective-permute-start(bf16[4,12288]{1,0:T(4,128)(2,1)S(1)} %get-tuple-element.21), channel_id=1, source_target_pairs={{0,24},{4,28},{8,16},{12,20},{16,8},{20,12},{24,0},{28,4},{1,25},{... | collective-permute-start | bytes 294920 | tf_op jit(solution)/shard_map/ppermute | solution.py:19
  98.4 2.0 %collective-permute-start.27 = (bf16[4,12288]{1,0:T(4,128)(2,1)S(1)}, bf16[4,12288]{1,0:T(4,128)(2,1)S(1)}, u32[]{:S(2)}, u32[]{:S(2)}) collective-permute-start(bf16[4,12288]{1,0:T(4,128)(2,1)S(1)} %get-tuple-element.20), channel_id=1, source_target_pairs={{0,8},{4,12},{8,0},{12,4},{16,24},{20,28},{24,16},{28,20},{1,9},{5... | collective-permute-start | bytes 294920 | tf_op jit(solution)/shard_map/ppermute | solution.py:19
  101.1 2.5 %collective-permute-done.29 = bf16[4,12288]{1,0:T(4,128)(2,1)S(1)} collective-permute-done((bf16[4,12288]{1,0:T(4,128)(2,1)S(1)}, bf16[4,12288]{1,0:T(4,128)(2,1)S(1)}, u32[]{:S(2)}, u32[]{:S(2)}) %collective-permute-start.29) | collective-permute-done | bytes 98336 | tf_op jit(solution)/shard_map/ppermute | solution.py:19
  103.6 4.0 %collective-permute-done.28 = bf16[4,12288]{1,0:T(4,128)(2,1)S(1)} collective-permute-done((bf16[4,12288]{1,0:T(4,128)(2,1)S(1)}, bf16[4,12288]{1,0:T(4,128)(2,1)S(1)}, u32[]{:S(2)}, u32[]{:S(2)}) %collective-permute-start.28) | collective-permute-done | bytes 98336 | tf_op jit(solution)/shard_map/ppermute | solution.py:19
  (92 shorter events, 20.4 us)
Async XLA Ops:
  0.6 9.2 %collective-permute-start = (bf16[4,12288]{1,0:T(4,128)(2,1)}, bf16[4,12288]{1,0:T(4,128)(2,1)S(1)}, u32[]{:S(2)}, u32[]{:S(2)}) collective-permute-start(bf16[4,12288]{1,0:T(4,128)(2,1)} %param.5), channel_id=1, source_target_pairs={{0,8},{4,12},{8,0},{12,4},{16,24},{20,28},{24,16},{28,20},{1,9},{5... | collective-permute-start | bytes 294920 | tf_op jit(solution)/shard_map/ppermute | solution.py:19
  3.7 10.6 %collective-permute-start.1 = (bf16[4,12288]{1,0:T(4,128)(2,1)}, bf16[4,12288]{1,0:T(4,128)(2,1)S(1)}, u32[]{:S(2)}, u32[]{:S(2)}) collective-permute-start(bf16[4,12288]{1,0:T(4,128)(2,1)} %param.5), channel_id=1, source_target_pairs={{0,16},{4,20},{8,24},{12,28},{16,0},{20,4},{24,8},{28,12},{1,17},{... | collective-permute-start | bytes 294920 | tf_op jit(solution)/shard_map/ppermute | solution.py:19
  6.3 8.1 %collective-permute-start.2 = (bf16[4,12288]{1,0:T(4,128)(2,1)}, bf16[4,12288]{1,0:T(4,128)(2,1)S(1)}, u32[]{:S(2)}, u32[]{:S(2)}) collective-permute-start(bf16[4,12288]{1,0:T(4,128)(2,1)} %param.5), channel_id=1, source_target_pairs={{0,24},{4,28},{8,16},{12,20},{16,8},{20,12},{24,0},{28,4},{1,25},{... | collective-permute-start | bytes 294920 | tf_op jit(solution)/shard_map/ppermute | solution.py:19
  6.3 8.7 %collective-permute-start.3 = (bf16[4,12288]{1,0:T(4,128)(2,1)}, bf16[4,12288]{1,0:T(4,128)(2,1)S(1)}, u32[]{:S(2)}, u32[]{:S(2)}) collective-permute-start(bf16[4,12288]{1,0:T(4,128)(2,1)} %param.5), channel_id=1, source_target_pairs={{0,4},{4,0},{8,12},{12,8},{16,20},{20,16},{24,28},{28,24},{1,5},{5... | collective-permute-start | bytes 294920 | tf_op jit(solution)/shard_map/ppermute | solution.py:19
  9.8 5.3 %collective-permute-start.4 = (bf16[4,12288]{1,0:T(4,128)(2,1)S(1)}, bf16[4,12288]{1,0:T(4,128)(2,1)S(1)}, u32[]{:S(2)}, u32[]{:S(2)}) collective-permute-start(bf16[4,12288]{1,0:T(4,128)(2,1)S(1)} %collective-permute-done), channel_id=1, source_target_pairs={{0,4},{4,0},{8,12},{12,8},{16,20},{20,16},{24,28},{28,24},{1,5},{5... | collective-permute-start | bytes 294920 | tf_op jit(solution)/shard_map/ppermute | solution.py:19
  14.4 1.3 %collective-permute-start.5 = (bf16[4,12288]{1,0:T(4,128)(2,1)S(1)}, bf16[4,12288]{1,0:T(4,128)(2,1)S(1)}, u32[]{:S(2)}, u32[]{:S(2)}) collective-permute-start(bf16[4,12288]{1,0:T(4,128)(2,1)S(1)} %collective-permute-done.1), channel_id=1, source_target_pairs={{0,4},{4,0},{8,12},{12,8},{16,20},{20,16},{24,28},{28,24},{1,5},{5... | collective-permute-start | bytes 294920 | tf_op jit(solution)/shard_map/ppermute | solution.py:19
  14.4 1.5 %collective-permute-start.6 = (bf16[4,12288]{1,0:T(4,128)(2,1)S(1)}, bf16[4,12288]{1,0:T(4,128)(2,1)S(1)}, u32[]{:S(2)}, u32[]{:S(2)}) collective-permute-start(bf16[4,12288]{1,0:T(4,128)(2,1)S(1)} %collective-permute-done.2), channel_id=1, source_target_pairs={{0,4},{4,0},{8,12},{12,8},{16,20},{20,16},{24,28},{28,24},{1,5},{5... | collective-permute-start | bytes 294920 | tf_op jit(solution)/shard_map/ppermute | solution.py:19
  15.9 21.1 %copy-start.5 = (f32[8]{0:T(128)S(1)}, f32[8]{0:T(128)}, u32[]{:S(2)}) copy-start(f32[8]{0:T(128)} %gain_ref.7) | copy-start | bytes 100
  16.1 2.2 %copy-start = (bf16[32,256,256]{2,1,0:T(8,128)(2,1)S(1)}, bf16[32,256,256]{2,1,0:T(8,128)(2,1)}, u32[]{:S(2)}) copy-start(bf16[32,256,256]{2,1,0:T(8,128)(2,1)} %blocks_ref.5) | copy-start | bytes 12582916
  21.9 7.2 %collective-permute-start.7 = (bf16[24,32,128]{2,1,0:T(8,128)(2,1)S(1)}, bf16[24,32,128]{2,1,0:T(8,128)(2,1)S(1)}, u32[]{:S(2)}, u32[]{:S(2)}) collective-permute-start(bf16[24,32,128]{2,1,0:T(8,128)(2,1)S(1)} %get-tuple-element.12), channel_id=1, source_target_pairs={{0,1},{1,0},{2,3},{3,2},{4,5},{5,4},{6,7},{7,6},{8,9},{9,8},{10,11... | collective-permute-start | bytes 589832 | tf_op jit(solution)/shard_map/ppermute | solution.py:19
  23.5 7.2 %collective-permute-start.9 = (bf16[24,32,128]{2,1,0:T(8,128)(2,1)S(1)}, bf16[24,32,128]{2,1,0:T(8,128)(2,1)S(1)}, u32[]{:S(2)}, u32[]{:S(2)}) collective-permute-start(bf16[24,32,128]{2,1,0:T(8,128)(2,1)S(1)} %get-tuple-element.13), channel_id=1, source_target_pairs={{0,2},{1,3},{2,0},{3,1},{4,6},{5,7},{6,4},{7,5},{8,10},{9,11},{10,... | collective-permute-start | bytes 589832 | tf_op jit(solution)/shard_map/ppermute | solution.py:19
  29.2 6.4 %collective-permute-start.8 = (bf16[24,32,128]{2,1,0:T(8,128)(2,1)S(1)}, bf16[24,32,128]{2,1,0:T(8,128)(2,1)S(1)}, u32[]{:S(2)}, u32[]{:S(2)}) collective-permute-start(bf16[24,32,128]{2,1,0:T(8,128)(2,1)S(1)} %add_convert_fusion.9), channel_id=1, source_target_pairs={{0,2},{1,3},{2,0},{3,1},{4,6},{5,7},{6,4},{7,5},{8,10},{9,11},{10,... | collective-permute-start | bytes 589832 | tf_op jit(solution)/shard_map/ppermute | solution.py:19
  30.8 6.1 %collective-permute-start.10 = (bf16[24,32,128]{2,1,0:T(8,128)(2,1)S(1)}, bf16[24,32,128]{2,1,0:T(8,128)(2,1)S(1)}, u32[]{:S(2)}, u32[]{:S(2)}) collective-permute-start(bf16[24,32,128]{2,1,0:T(8,128)(2,1)S(1)} %add_convert_fusion.7), channel_id=1, source_target_pairs={{0,1},{1,0},{2,3},{3,2},{4,5},{5,4},{6,7},{7,6},{8,9},{9,8},{10,11... | collective-permute-start | bytes 589832 | tf_op jit(solution)/shard_map/ppermute | solution.py:19
  41.7 1.8 %collective-permute-start.11 = (bf16[4,12,32,128]{3,2,1,0:T(8,128)(2,1)S(1)}, bf16[4,12,32,128]{3,2,1,0:T(8,128)(2,1)S(1)}, u32[]{:S(2)}, u32[]{:S(2)}) collective-permute-start(bf16[4,12,32,128]{3,2,1,0:T(8,128)(2,1)S(1)} %get-tuple-element.15), channel_id=1, source_target_pairs={{0,4},{4,0},{8,12},{12,8},{16,20},{20,16},{24,28},{28,24},{1,5},{5... | collective-permute-start | bytes 1179656 | tf_op jit(solution)/shard_map/ppermute | solution.py:19
  43.6 7.6 %collective-permute-start.14 = (bf16[12,32,128]{2,1,0:T(8,128)(2,1)S(1)}, bf16[12,32,128]{2,1,0:T(8,128)(2,1)S(1)}, u32[]{:S(2)}, u32[]{:S(2)}) collective-permute-start(bf16[12,32,128]{2,1,0:T(8,128)(2,1)S(1)} %get-tuple-element.24), channel_id=1, source_target_pairs={{0,24},{4,28},{8,16},{12,20},{16,8},{20,12},{24,0},{28,4},{1,25},{... | collective-permute-start | bytes 294920 | tf_op jit(solution)/shard_map/ppermute | solution.py:19
  46.2 9.2 %collective-permute-start.13 = (bf16[12,32,128]{2,1,0:T(8,128)(2,1)S(1)}, bf16[12,32,128]{2,1,0:T(8,128)(2,1)S(1)}, u32[]{:S(2)}, u32[]{:S(2)}) collective-permute-start(bf16[12,32,128]{2,1,0:T(8,128)(2,1)S(1)} %get-tuple-element.25), channel_id=1, source_target_pairs={{0,16},{4,20},{8,24},{12,28},{16,0},{20,4},{24,8},{28,12},{1,17},{... | collective-permute-start | bytes 294920 | tf_op jit(solution)/shard_map/ppermute | solution.py:19
  46.2 9.1 %collective-permute-start.12 = (bf16[12,32,128]{2,1,0:T(8,128)(2,1)S(1)}, bf16[12,32,128]{2,1,0:T(8,128)(2,1)S(1)}, u32[]{:S(2)}, u32[]{:S(2)}) collective-permute-start(bf16[12,32,128]{2,1,0:T(8,128)(2,1)S(1)} %get-tuple-element.23), channel_id=1, source_target_pairs={{0,8},{4,12},{8,0},{12,4},{16,24},{20,28},{24,16},{28,20},{1,9},{5... | collective-permute-start | bytes 294920 | tf_op jit(solution)/shard_map/ppermute | solution.py:19
  55.4 5.5 %collective-permute-start.15 = (bf16[12,32,128]{2,1,0:T(8,128)(2,1)S(1)}, bf16[12,32,128]{2,1,0:T(8,128)(2,1)S(1)}, u32[]{:S(2)}, u32[]{:S(2)}) collective-permute-start(bf16[12,32,128]{2,1,0:T(8,128)(2,1)S(1)} %fusion.5.refs_0_), channel_id=1, source_target_pairs={{0,8},{4,12},{8,0},{12,4},{16,24},{20,28},{24,16},{28,20},{1,9},{5... | collective-permute-start | bytes 294920 | tf_op jit(solution)/shard_map/ppermute | solution.py:19
  55.5 10.5 %collective-permute-start.16 = (bf16[12,32,128]{2,1,0:T(8,128)(2,1)S(1)}, bf16[12,32,128]{2,1,0:T(8,128)(2,1)S(1)}, u32[]{:S(2)}, u32[]{:S(2)}) collective-permute-start(bf16[12,32,128]{2,1,0:T(8,128)(2,1)S(1)} %fusion.5.refs_0_), channel_id=1, source_target_pairs={{0,16},{4,20},{8,24},{12,28},{16,0},{20,4},{24,8},{28,12},{1,17},{... | collective-permute-start | bytes 294920 | tf_op jit(solution)/shard_map/ppermute | solution.py:19
  58.5 7.6 %collective-permute-start.17 = (bf16[12,32,128]{2,1,0:T(8,128)(2,1)S(1)}, bf16[12,32,128]{2,1,0:T(8,128)(2,1)S(1)}, u32[]{:S(2)}, u32[]{:S(2)}) collective-permute-start(bf16[12,32,128]{2,1,0:T(8,128)(2,1)S(1)} %fusion.5.refs_0_), channel_id=1, source_target_pairs={{0,24},{4,28},{8,16},{12,20},{16,8},{20,12},{24,0},{28,4},{1,25},{... | collective-permute-start | bytes 294920 | tf_op jit(solution)/shard_map/ppermute | solution.py:19
  59.9 6.8 %collective-permute-start.18 = (bf16[12,32,128]{2,1,0:T(8,128)(2,1)S(1)}, bf16[12,32,128]{2,1,0:T(8,128)(2,1)S(1)}, u32[]{:S(2)}, u32[]{:S(2)}) collective-permute-start(bf16[12,32,128]{2,1,0:T(8,128)(2,1)S(1)} %fusion.5.refs_0_), channel_id=1, source_target_pairs={{0,4},{4,0},{8,12},{12,8},{16,20},{20,16},{24,28},{28,24},{1,5},{5... | collective-permute-start | bytes 294920 | tf_op jit(solution)/shard_map/ppermute | solution.py:19
  61.0 5.7 %collective-permute-start.19 = (bf16[12,32,128]{2,1,0:T(8,128)(2,1)S(1)}, bf16[12,32,128]{2,1,0:T(8,128)(2,1)S(1)}, u32[]{:S(2)}, u32[]{:S(2)}) collective-permute-start(bf16[12,32,128]{2,1,0:T(8,128)(2,1)S(1)} %collective-permute-done.15.refs_1_), channel_id=1, source_target_pairs={{0,4},{4,0},{8,12},{12,8},{16,20},{20,16},{24,28},{28,24},{1,5},{5... | collective-permute-start | bytes 294920 | tf_op jit(solution)/shard_map/ppermute | solution.py:19
  66.0 1.3 %collective-permute-start.20 = (bf16[12,32,128]{2,1,0:T(8,128)(2,1)S(1)}, bf16[12,32,128]{2,1,0:T(8,128)(2,1)S(1)}, u32[]{:S(2)}, u32[]{:S(2)}) collective-permute-start(bf16[12,32,128]{2,1,0:T(8,128)(2,1)S(1)} %collective-permute-done.16.refs_2_), channel_id=1, source_target_pairs={{0,4},{4,0},{8,12},{12,8},{16,20},{20,16},{24,28},{28,24},{1,5},{5... | collective-permute-start | bytes 294920 | tf_op jit(solution)/shard_map/ppermute | solution.py:19
  66.0 1.5 %collective-permute-start.21 = (bf16[12,32,128]{2,1,0:T(8,128)(2,1)S(1)}, bf16[12,32,128]{2,1,0:T(8,128)(2,1)S(1)}, u32[]{:S(2)}, u32[]{:S(2)}) collective-permute-start(bf16[12,32,128]{2,1,0:T(8,128)(2,1)S(1)} %collective-permute-done.17.refs_3_), channel_id=1, source_target_pairs={{0,4},{4,0},{8,12},{12,8},{16,20},{20,16},{24,28},{28,24},{1,5},{5... | collective-permute-start | bytes 294920 | tf_op jit(solution)/shard_map/ppermute | solution.py:19
  72.8 7.2 %collective-permute-start.22 = (bf16[24,32,128]{2,1,0:T(8,128)(2,1)S(1)}, bf16[24,32,128]{2,1,0:T(8,128)(2,1)S(1)}, u32[]{:S(2)}, u32[]{:S(2)}) collective-permute-start(bf16[24,32,128]{2,1,0:T(8,128)(2,1)S(1)} %get-tuple-element.16), channel_id=1, source_target_pairs={{0,1},{1,0},{2,3},{3,2},{4,5},{5,4},{6,7},{7,6},{8,9},{9,8},{10,11... | collective-permute-start | bytes 589832 | tf_op jit(solution)/shard_map/ppermute | solution.py:19
  74.9 6.9 %collective-permute-start.24 = (bf16[24,32,128]{2,1,0:T(8,128)(2,1)S(1)}, bf16[24,32,128]{2,1,0:T(8,128)(2,1)S(1)}, u32[]{:S(2)}, u32[]{:S(2)}) collective-permute-start(bf16[24,32,128]{2,1,0:T(8,128)(2,1)S(1)} %get-tuple-element.17), channel_id=1, source_target_pairs={{0,2},{1,3},{2,0},{3,1},{4,6},{5,7},{6,4},{7,5},{8,10},{9,11},{10,... | collective-permute-start | bytes 589832 | tf_op jit(solution)/shard_map/ppermute | solution.py:19
  80.1 6.4 %collective-permute-start.23 = (bf16[24,32,128]{2,1,0:T(8,128)(2,1)S(1)}, bf16[24,32,128]{2,1,0:T(8,128)(2,1)S(1)}, u32[]{:S(2)}, u32[]{:S(2)}) collective-permute-start(bf16[24,32,128]{2,1,0:T(8,128)(2,1)S(1)} %add_convert_fusion.5), channel_id=1, source_target_pairs={{0,2},{1,3},{2,0},{3,1},{4,6},{5,7},{6,4},{7,5},{8,10},{9,11},{10,... | collective-permute-start | bytes 589832 | tf_op jit(solution)/shard_map/ppermute | solution.py:19
  81.9 6.1 %collective-permute-start.25 = (bf16[24,32,128]{2,1,0:T(8,128)(2,1)S(1)}, bf16[24,32,128]{2,1,0:T(8,128)(2,1)S(1)}, u32[]{:S(2)}, u32[]{:S(2)}) collective-permute-start(bf16[24,32,128]{2,1,0:T(8,128)(2,1)S(1)} %add_convert_fusion.3), channel_id=1, source_target_pairs={{0,1},{1,0},{2,3},{3,2},{4,5},{5,4},{6,7},{7,6},{8,9},{9,8},{10,11... | collective-permute-start | bytes 589832 | tf_op jit(solution)/shard_map/ppermute | solution.py:19
  93.9 1.8 %collective-permute-start.26 = (bf16[4,4,12288]{2,1,0:T(4,128)(2,1)S(1)}, bf16[4,4,12288]{2,1,0:T(4,128)(2,1)S(1)}, u32[]{:S(2)}, u32[]{:S(2)}) collective-permute-start(bf16[4,4,12288]{2,1,0:T(4,128)(2,1)S(1)} %get-tuple-element.19), channel_id=1, source_target_pairs={{0,4},{4,0},{8,12},{12,8},{16,20},{20,16},{24,28},{28,24},{1,5},{5... | collective-permute-start | bytes 1179656 | tf_op jit(solution)/shard_map/ppermute | solution.py:19
  96.0 7.6 %collective-permute-start.29 = (bf16[4,12288]{1,0:T(4,128)(2,1)S(1)}, bf16[4,12288]{1,0:T(4,128)(2,1)S(1)}, u32[]{:S(2)}, u32[]{:S(2)}) collective-permute-start(bf16[4,12288]{1,0:T(4,128)(2,1)S(1)} %get-tuple-element.21), channel_id=1, source_target_pairs={{0,24},{4,28},{8,16},{12,20},{16,8},{20,12},{24,0},{28,4},{1,25},{... | collective-permute-start | bytes 294920 | tf_op jit(solution)/shard_map/ppermute | solution.py:19
  98.3 9.3 %collective-permute-start.28 = (bf16[4,12288]{1,0:T(4,128)(2,1)S(1)}, bf16[4,12288]{1,0:T(4,128)(2,1)S(1)}, u32[]{:S(2)}, u32[]{:S(2)}) collective-permute-start(bf16[4,12288]{1,0:T(4,128)(2,1)S(1)} %get-tuple-element.22), channel_id=1, source_target_pairs={{0,16},{4,20},{8,24},{12,28},{16,0},{20,4},{24,8},{28,12},{1,17},{... | collective-permute-start | bytes 294920 | tf_op jit(solution)/shard_map/ppermute | solution.py:19
  98.4 9.1 %collective-permute-start.27 = (bf16[4,12288]{1,0:T(4,128)(2,1)S(1)}, bf16[4,12288]{1,0:T(4,128)(2,1)S(1)}, u32[]{:S(2)}, u32[]{:S(2)}) collective-permute-start(bf16[4,12288]{1,0:T(4,128)(2,1)S(1)} %get-tuple-element.20), channel_id=1, source_target_pairs={{0,8},{4,12},{8,0},{12,4},{16,24},{20,28},{24,16},{28,20},{1,9},{5... | collective-permute-start | bytes 294920 | tf_op jit(solution)/shard_map/ppermute | solution.py:19
  (4 other events, 7.2 us)

commit v4 on v0

v4 whole, which is shorter than its diff:
```python
import functools

import jax
import jax.numpy as jnp
from jax import lax
from jax.experimental import pallas as pl
from jax.experimental.pallas import tpu as pltpu
from jax.sharding import PartitionSpec as P

B = 256
LANES = 128
PER = B // LANES
VMEM_LIMIT = 24 * 1024 * 1024


def swap(value, axis, offset):
    count = lax.axis_size(axis)
    return lax.ppermute(value, axis, [(i, i ^ offset) for i in range(count)])


def add_up(*parts):
    total = parts[0].astype(jnp.float32)
    for part in parts[1:]:
        total = total + part.astype(jnp.float32)
    return total.astype(parts[0].dtype)


def add_products(entry_ref, gain_ref, load, block_refs, total, adjoint):
    total[...] = jnp.zeros_like(total)
    slots = block_refs[0].shape[0]
    for part, block_ref in enumerate(block_refs):
        for slot in range(slots):
            at = 3 * (part * slots + slot)
            row, col, level = entry_ref[at], entry_ref[at + 1], entry_ref[at + 2]
            scale = jnp.where(level >= 0, gain_ref[jnp.maximum(level, 0)], jnp.float32(0.0))
            source, target = (row, col) if adjoint else (col, row)
            term = lax.dot_general(
                load(source),
                block_ref[slot],
                (((1,), (0 if adjoint else 1,)), ((), ())),
                preferred_element_type=jnp.float32,
            )
            term = term * scale
            for piece in range(PER):
                total[target * PER + piece] += term[:, piece * LANES : (piece + 1) * LANES]


def load_from(x):
    def load(block):
        return jnp.concatenate([x[block * PER + piece] for piece in range(PER)], axis=1)

    return load


def write_halves(total, low_ref, high_ref):
    half = low_ref.shape[0]
    low_ref[...] = total[:half].astype(low_ref.dtype)
    high_ref[...] = total[half:].astype(high_ref.dtype)


def first_kernel(entry_ref, gain_ref, x_ref, own_ref, other_ref, low_ref, high_ref, total):
    def load(block):
        return x_ref[:, pl.ds(pl.multiple_of(block * B, B), B)]

    add_products(entry_ref, gain_ref, load, (own_ref, other_ref), total, False)
    write_halves(total, low_ref, high_ref)


def forward_kernel(ways, entry_ref, gain_ref, place_ref, *refs):
    pieces = refs[:ways]
    own_ref, other_ref, low_ref, high_ref, total, x = refs[ways:]
    along = place_ref[0]
    size = pieces[0].shape[0]
    for way in range(ways):
        x[pl.ds((along ^ way) * size, size)] = pieces[way][...]
    add_products(entry_ref, gain_ref, load_from(x), (own_ref, other_ref), total, False)
    write_halves(total, low_ref, high_ref)


def adjoint_kernel(ways, entry_ref, gain_ref, place_ref, low_ref, high_ref, own_ref, other_ref, *refs):
    total, x = refs[ways:]
    half = low_ref.shape[0]
    x[:half] = low_ref[...]
    x[half:] = high_ref[...]
    add_products(entry_ref, gain_ref, load_from(x), (own_ref, other_ref), total, True)
    along = place_ref[0]
    size = refs[0].shape[0]
    for way in range(ways):
        refs[way][...] = total[pl.ds((along ^ way) * size, size)].astype(refs[way].dtype)


def last_kernel(ways, entry_ref, gain_ref, place_ref, low_ref, high_ref, own_ref, other_ref, out_ref, total, x):
    half = low_ref.shape[0]
    x[:half] = low_ref[...]
    x[half:] = high_ref[...]
    add_products(entry_ref, gain_ref, load_from(x), (own_ref, other_ref), total, True)
    along = place_ref[0]
    share = out_ref.shape[1]

    def write(group, carry):
        lanes = pl.ds(pl.multiple_of(group * LANES, LANES), LANES)
        values = total[group].astype(out_ref.dtype)
        for index in range(ways):
            out_ref[along ^ index, :, lanes] = values[index * share : (index + 1) * share]
        return carry

    lax.fori_loop(0, total.shape[0], write, 0)


def shards(strengths, blocks, pattern, level_gain):
    n_panel = lax.axis_size("panel")
    n_case = lax.axis_size("case")
    ways = n_panel // 2
    share, width = strengths.shape
    held_cases = share * ways
    slots = blocks.shape[0]
    col_blocks = width // B
    row_blocks = 2 * (col_blocks * n_case // n_panel)
    col_groups = col_blocks * PER
    row_groups = row_blocks * PER
    panel = lax.axis_index("panel")
    case = lax.axis_index("case")
    core = panel % 2
    along = panel // 2
    value = strengths.dtype

    strength_parts = [strengths] + [swap(strengths, "panel", 2 * way) for way in range(1, ways)]
    other_blocks = swap(blocks, "panel", 1)
    place = along.astype(jnp.int32)[None]
    first = jnp.stack([along * row_blocks, case * col_blocks, 0]).astype(jnp.int32)
    entry = jnp.where(pattern[:, 2:3] < 0, jnp.array([0, 0, -1], jnp.int32), pattern - first).reshape(-1)
    entry = jnp.concatenate([entry, swap(entry, "panel", 1)])

    smem = pl.BlockSpec(memory_space=pltpu.SMEM)
    vmem = pl.BlockSpec(memory_space=pltpu.VMEM)

    def product(kernel, small, vectors, outs, total_groups, x_groups):
        scratch = [pltpu.VMEM((total_groups, held_cases, LANES), jnp.float32)]
        if x_groups:
            scratch.append(pltpu.VMEM((x_groups, held_cases, LANES), value))
        return pl.pallas_call(
            kernel,
            out_shape=[jax.ShapeDtypeStruct(shape, value) for shape in outs],
            in_specs=[smem] * len(small) + [vmem] * (len(vectors) + 2),
            out_specs=[vmem] * len(outs),
            scratch_shapes=scratch,
            compiler_params=pltpu.CompilerParams(vmem_limit_bytes=VMEM_LIMIT),
            cost_estimate=pl.CostEstimate(
                flops=4 * held_cases * slots * B * B, bytes_accessed=4 * slots * B * B, transcendentals=0
            ),
        )(*small, *vectors, blocks, other_blocks)

    half_rows = [(row_groups // 2, held_cases, LANES)] * 2
    part_size = col_groups // ways

    def over_case(low, high):
        bits = [1 << b for b in range(n_case.bit_length() - 1)]
        for one, other in zip(bits, reversed(bits)):
            low_in, high_in = swap(low, "case", one), swap(high, "case", other)
            low, high = add_up(low, low_in), add_up(high, high_in)
        return low, high

    def scatter_along(parts):
        return add_up(parts[0], *[swap(parts[way], "panel", 2 * way) for way in range(1, ways)])

    def gather_along(part):
        return [part] + [swap(part, "panel", 2 * way) for way in range(1, ways)]

    def own_rows(low, high):
        count = held_cases // n_case
        mine, theirs = jnp.where(core == 0, low, high), jnp.where(core == 0, high, low)
        mine = lax.dynamic_slice_in_dim(mine, case * count, count, 1)
        theirs = swap(lax.dynamic_slice_in_dim(theirs, case * count, count, 1), "panel", 1)
        both = jnp.stack([jnp.where(core == 0, mine, theirs), jnp.where(core == 0, theirs, mine)])
        both = both.reshape(2, row_groups // 2, count // share, share, LANES)
        return jnp.transpose(both, (2, 0, 3, 1, 4)).reshape(2 * count, row_groups // 2 * LANES)

    def own_share(pieces):
        own = jnp.stack([lax.dynamic_slice_in_dim(one, along * share, share, 1) for one in pieces])
        bit = 1
        while bit < ways:
            flipped = own.reshape(ways // (2 * bit), 2, bit, part_size, share, LANES)[:, ::-1].reshape(own.shape)
            own = jnp.where(along & bit != 0, flipped, own)
            bit *= 2
        return jnp.moveaxis(own, 2, 0).reshape(share, width)

    stacked = jnp.zeros((ways, share, width), value)
    for way, one in enumerate(strength_parts):
        stacked = lax.dynamic_update_slice_in_dim(stacked, one[None], along ^ way, 0)
    low, high = product(first_kernel, (entry, level_gain), [stacked.reshape(held_cases, width)], half_rows, row_groups, 0)
    low, high = over_case(low, high)
    forward_one = own_rows(low, high)

    parts = product(
        functools.partial(adjoint_kernel, ways),
        (entry, level_gain, place),
        [low, high],
        [(part_size, held_cases, LANES)] * ways,
        col_groups,
        row_groups,
    )
    pieces = gather_along(scatter_along(parts))
    adjoint_one = own_share(pieces)

    low, high = product(
        functools.partial(forward_kernel, ways), (entry, level_gain, place), pieces, half_rows, row_groups, col_groups
    )
    low, high = over_case(low, high)
    forward_two = own_rows(low, high)

    (by_share,) = product(
        functools.partial(last_kernel, ways),
        (entry, level_gain, place),
        [low, high],
        [(ways, share, width)],
        col_groups,
        row_groups,
    )
    adjoint_two = scatter_along(by_share)
    return (forward_one, adjoint_one, forward_two, adjoint_two)


def solution(mesh):
    in_specs = (
        P("panel", "case"),
        P(("panel", "case"), None, None),
        P(("panel", "case"), None),
        P(),
    )
    out_specs = (P("case", "panel"), P("panel", "case"), P("case", "panel"), P("panel", "case"))
    return jax.shard_map(shards, mesh=mesh, in_specs=in_specs, out_specs=out_specs, check_vma=False)
```

time: 267 us -> 109 us (0.41)
  waiting for transfers between devices: 198 us -> 47.8 us
  starting transfers between devices: 0.16 us -> 28.3 us
  matrix products: 20 us -> 0 us
  blocking collectives: 17.4 us -> 0 us
  Pallas kernels: 0 us -> 17 us
  between operations: 14.5 us -> 1.01 us
  local copies, waits for them, and re-layouts: 14.9 us -> 11 us
    psum x3 -> x0, waiting for transfers between devices: 142 us -> none  [the longest x2 85.7 us: total_rows(): return lax.psum(partial_value.astype(jnp.bfloat16), 'case')]
    unnamed x5 -> x0, waiting for transfers between devices: 56 us -> none
    ppermute x0 -> x24, waiting for transfers between devices: none -> 47.8 us  [swap(): return lax.ppermute(value, axis, [(i, i ^ offset) for i in range(count)])]
    ppermute x0 -> x24, starting transfers between devices: none -> 28.3 us  [swap(): return lax.ppermute(value, axis, [(i, i ^ offset) for i in range(count)])]
    dot_general x12 -> x0, matrix products: 20 us -> none  [the longest x2 7.06 us: forward_terms(): jnp.einsum('skm,snm->skn', picked, blocks, preferred_element_type=jnp.flo...]
    all_gather x1 -> x0, blocking collectives: 17.4 us -> none  [shards(): lax.all_gather(strengths, 'panel', axis=0, tiled=True)]
    pallas_call x0 -> x4, Pallas kernels: none -> 17 us  [product(): pl.pallas_call(kernel, out_shape=[jax.ShapeDtypeStruct(shape, value) for...]
    dynamic_slice x3 -> x8, local copies, waits for them, and re-layouts: 4.72 us -> 0.11 us  [own_share(): lax.dynamic_slice_in_dim(one, along * share, share, 1)]
  transfers between devices with their start and end apart: 4 -> 24, of which waited for: 4 -> 15; matrix products, arithmetic and copies ran while one was open for 2% -> 6% of each run, Pallas kernels for 0% -> 7%
where the time goes in v4:
time: 109 us
  waiting for transfers between devices  47.8 us (44%)
  starting transfers between devices  28.3 us (26%)
  Pallas kernels  17 us (16%)
  local copies, waits for them, and re-layouts  11 us (10%)
  other arithmetic  3.36 us (3%)
    ppermute x24, waiting for transfers between devices, swap(): return lax.ppermute(value, axis, [(i, i ^ offset) for i in range(count)])  47.8 us
    ppermute x24, starting transfers between devices, swap(): return lax.ppermute(value, axis, [(i, i ^ offset) for i in range(count)])  28.3 us
    pallas_call x4, Pallas kernels, product(): pl.pallas_call(kernel, out_shape=[jax.ShapeDtypeStruct(shape, value) for...  17 us
    unnamed x13, local copies, waits for them, and re-layouts  9.24 us
  transfers between devices with their start and end apart: 24, of which 15 were waited for; matrix products, arithmetic and copies ran while one was open for 6% of the time, Pallas kernels for 7%

profile of v4, /device:TPU:0, one launch (start us, length us, event | category | flops | bytes accessed | tf_op | source)
XLA Modules:
  0.0 108.6 jit_solution(10064040986484076451)
XLA Ops:
  0.6 3.1 %collective-permute-start.1 = (bf16[4,12288]{1,0:T(4,128)(2,1)}, bf16[4,12288]{1,0:T(4,128)(2,1)S(1)}, u32[]{:S(2)}, u32[]{:S(2)}) collective-permute-start(bf16[4,12288]{1,0:T(4,128)(2,1)} %param.5), channel_id=1, source_target_pairs={{0,8},{4,12},{8,0},{12,4},{16,24},{20,28},{24,16},{28,20},{1,9},{5... | collective-permute-start | bytes 294920 | tf_op jit(solution)/shard_map/ppermute | solution.py:18
  3.7 2.5 %collective-permute-start.3 = (bf16[4,12288]{1,0:T(4,128)(2,1)}, bf16[4,12288]{1,0:T(4,128)(2,1)S(1)}, u32[]{:S(2)}, u32[]{:S(2)}) collective-permute-start(bf16[4,12288]{1,0:T(4,128)(2,1)} %param.5), channel_id=1, source_target_pairs={{0,24},{4,28},{8,16},{12,20},{16,8},{20,12},{24,0},{28,4},{1,25},{... | collective-permute-start | bytes 294920 | tf_op jit(solution)/shard_map/ppermute | solution.py:18
  9.8 5.6 %collective-permute-done.2 = bf16[4,12288]{1,0:T(4,128)(2,1)S(1)} collective-permute-done((bf16[4,12288]{1,0:T(4,128)(2,1)}, bf16[4,12288]{1,0:T(4,128)(2,1)S(1)}, u32[]{:S(2)}, u32[]{:S(2)}) %collective-permute-start.2) | collective-permute-done | bytes 98336 | tf_op jit(solution)/shard_map/ppermute | solution.py:18
  15.7 2.2 %copy-done = bf16[32,256,256]{2,1,0:T(8,128)(2,1)S(1)} copy-done((bf16[32,256,256]{2,1,0:T(8,128)(2,1)S(1)}, bf16[32,256,256]{2,1,0:T(8,128)(2,1)}, u32[]{:S(2)}) %copy-start) | copy-done | bytes 4194328
  18.6 4.6 %shard_map.84 = (bf16[48,16,128]{2,1,0:T(8,128)(2,1)S(1)}, bf16[48,16,128]{2,1,0:T(8,128)(2,1)S(1)}) custom-call(s32[192]{0:T(256)S(1)} %pad_add_fusion.entry_ref, f32[8]{0:T(128)S(1)} %copy-done.3, bf16[16,12288]{1,0:T(8,128)(2,1)S(1)} %reshape.62.x_ref, bf16[32,256,256]{2,1,0:T(8,128)(2,1)S(1)} %copy-done, ...), custom_call_target="tpu_custom_call" | custom-call | flops 134217728 | bytes 8388608 | tf_op jit(solution)/shard_map/pallas_call | solution.py:141
  23.1 1.6 %collective-permute-start.5 = (bf16[48,16,128]{2,1,0:T(8,128)(2,1)S(1)}, bf16[48,16,128]{2,1,0:T(8,128)(2,1)S(1)}, u32[]{:S(2)}, u32[]{:S(2)}) collective-permute-start(bf16[48,16,128]{2,1,0:T(8,128)(2,1)S(1)} %get-tuple-element.12), channel_id=1, source_target_pairs={{0,1},{1,0},{2,3},{3,2},{4,5},{5,4},{6,7},{7,6},{8,9},{9,8},{10,11... | collective-permute-start | bytes 589832 | tf_op jit(solution)/shard_map/ppermute | solution.py:18
  24.7 1.5 %collective-permute-start.7 = (bf16[48,16,128]{2,1,0:T(8,128)(2,1)S(1)}, bf16[48,16,128]{2,1,0:T(8,128)(2,1)S(1)}, u32[]{:S(2)}, u32[]{:S(2)}) collective-permute-start(bf16[48,16,128]{2,1,0:T(8,128)(2,1)S(1)} %get-tuple-element.13), channel_id=1, source_target_pairs={{0,2},{1,3},{2,0},{3,1},{4,6},{5,7},{6,4},{7,5},{8,10},{9,11},{10,... | collective-permute-start | bytes 589832 | tf_op jit(solution)/shard_map/ppermute | solution.py:18
  26.2 4.1 %collective-permute-done.5 = bf16[48,16,128]{2,1,0:T(8,128)(2,1)S(1)} collective-permute-done((bf16[48,16,128]{2,1,0:T(8,128)(2,1)S(1)}, bf16[48,16,128]{2,1,0:T(8,128)(2,1)S(1)}, u32[]{:S(2)}, u32[]{:S(2)}) %collective-permute-start.5) | collective-permute-done | bytes 196640 | tf_op jit(solution)/shard_map/ppermute | solution.py:18
  30.4 1.6 %collective-permute-start.6 = (bf16[48,16,128]{2,1,0:T(8,128)(2,1)S(1)}, bf16[48,16,128]{2,1,0:T(8,128)(2,1)S(1)}, u32[]{:S(2)}, u32[]{:S(2)}) collective-permute-start(bf16[48,16,128]{2,1,0:T(8,128)(2,1)S(1)} %add_convert_fusion.7), channel_id=1, source_target_pairs={{0,2},{1,3},{2,0},{3,1},{4,6},{5,7},{6,4},{7,5},{8,10},{9,11},{10,... | collective-permute-start | bytes 589832 | tf_op jit(solution)/shard_map/ppermute | solution.py:18
  32.1 1.6 %collective-permute-start.8 = (bf16[48,16,128]{2,1,0:T(8,128)(2,1)S(1)}, bf16[48,16,128]{2,1,0:T(8,128)(2,1)S(1)}, u32[]{:S(2)}, u32[]{:S(2)}) collective-permute-start(bf16[48,16,128]{2,1,0:T(8,128)(2,1)S(1)} %add_convert_fusion.5), channel_id=1, source_target_pairs={{0,1},{1,0},{2,3},{3,2},{4,5},{5,4},{6,7},{7,6},{8,9},{9,8},{10,11... | collective-permute-start | bytes 589832 | tf_op jit(solution)/shard_map/ppermute | solution.py:18
  33.7 3.2 %collective-permute-done.6 = bf16[48,16,128]{2,1,0:T(8,128)(2,1)S(1)} collective-permute-done((bf16[48,16,128]{2,1,0:T(8,128)(2,1)S(1)}, bf16[48,16,128]{2,1,0:T(8,128)(2,1)S(1)}, u32[]{:S(2)}, u32[]{:S(2)}) %collective-permute-start.6) | collective-permute-done | bytes 196640 | tf_op jit(solution)/shard_map/ppermute | solution.py:18
  36.9 1.3 %collective-permute-done.8 = bf16[48,16,128]{2,1,0:T(8,128)(2,1)S(1)} collective-permute-done((bf16[48,16,128]{2,1,0:T(8,128)(2,1)S(1)}, bf16[48,16,128]{2,1,0:T(8,128)(2,1)S(1)}, u32[]{:S(2)}, u32[]{:S(2)}) %collective-permute-start.8) | collective-permute-done | bytes 196640 | tf_op jit(solution)/shard_map/ppermute | solution.py:18
  38.5 2.2 %copy-done.1 = bf16[32,256,256]{2,1,0:T(8,128)(2,1)S(1)} copy-done((bf16[32,256,256]{2,1,0:T(8,128)(2,1)S(1)}, bf16[32,256,256]{2,1,0:T(8,128)(2,1)}, u32[]{:S(2)}) %copy-start.1) | copy-done | bytes 4194328
  40.7 3.5 %shard_map.85 = (bf16[24,16,128]{2,1,0:T(8,128)(2,1)S(1)}, bf16[24,16,128]{2,1,0:T(8,128)(2,1)S(1)}, bf16[24,16,128]{2,1,0:T(8,128)(2,1)S(1)}, bf16[24,16,128]{2,1,0:T(8,128)(2,1)S(1)}) custom-call(s32[192]{0:T(256)S(1)} %pad_add_fusion.entry_ref, f32[8]{0:T(128)S(1)} %copy-done.4, s32[1]{0:T(128)} %bitcast.11.place_ref, ...), custom_call_target="tpu_custom_call" | custom-call | flops 134217728 | bytes 8388608 | tf_op jit(solution)/shard_map/pallas_call | solution.py:141
  44.2 1.9 %collective-permute-start.10 = (bf16[24,16,128]{2,1,0:T(8,128)(2,1)S(1)}, bf16[24,16,128]{2,1,0:T(8,128)(2,1)S(1)}, u32[]{:S(2)}, u32[]{:S(2)}) collective-permute-start(bf16[24,16,128]{2,1,0:T(8,128)(2,1)S(1)} %get-tuple-element.15), channel_id=1, source_target_pairs={{0,8},{4,12},{8,0},{12,4},{16,24},{20,28},{24,16},{28,20},{1,9},{5... | collective-permute-start | bytes 294920 | tf_op jit(solution)/shard_map/ppermute | solution.py:18
  46.0 1.7 %collective-permute-start.11 = (bf16[24,16,128]{2,1,0:T(8,128)(2,1)S(1)}, bf16[24,16,128]{2,1,0:T(8,128)(2,1)S(1)}, u32[]{:S(2)}, u32[]{:S(2)}) collective-permute-start(bf16[24,16,128]{2,1,0:T(8,128)(2,1)S(1)} %get-tuple-element.16), channel_id=1, source_target_pairs={{0,16},{4,20},{8,24},{12,28},{16,0},{20,4},{24,8},{28,12},{1,17},{... | collective-permute-start | bytes 294920 | tf_op jit(solution)/shard_map/ppermute | solution.py:18
  49.5 7.3 %collective-permute-done.11 = bf16[24,16,128]{2,1,0:T(8,128)(2,1)S(1)} collective-permute-done((bf16[24,16,128]{2,1,0:T(8,128)(2,1)S(1)}, bf16[24,16,128]{2,1,0:T(8,128)(2,1)S(1)}, u32[]{:S(2)}, u32[]{:S(2)}) %collective-permute-start.11) | collective-permute-done | bytes 98336 | tf_op jit(solution)/shard_map/ppermute | solution.py:18
  56.8 2.3 %collective-permute-start.15 = (bf16[24,16,128]{2,1,0:T(8,128)(2,1)S(1)}, bf16[24,16,128]{2,1,0:T(8,128)(2,1)S(1)}, u32[]{:S(2)}, u32[]{:S(2)}) collective-permute-start(bf16[24,16,128]{2,1,0:T(8,128)(2,1)S(1)} %add_convert_fusion.8.refs_0_), channel_id=1, source_target_pairs={{0,24},{4,28},{8,16},{12,20},{16,8},{20,12},{24,0},{28,4},{1,25},{... | collective-permute-start | bytes 294920 | tf_op jit(solution)/shard_map/ppermute | solution.py:18
  61.3 2.9 %collective-permute-done.15.refs_3_ = bf16[24,16,128]{2,1,0:T(8,128)(2,1)S(1)} collective-permute-done((bf16[24,16,128]{2,1,0:T(8,128)(2,1)S(1)}, bf16[24,16,128]{2,1,0:T(8,128)(2,1)S(1)}, u32[]{:S(2)}, u32[]{:S(2)}) %collective-permute-start.15) | collective-permute-done | bytes 98336 | tf_op jit(solution)/shard_map/ppermute | solution.py:18
  64.2 4.3 %collective-permute-done.14.refs_2_ = bf16[24,16,128]{2,1,0:T(8,128)(2,1)S(1)} collective-permute-done((bf16[24,16,128]{2,1,0:T(8,128)(2,1)S(1)}, bf16[24,16,128]{2,1,0:T(8,128)(2,1)S(1)}, u32[]{:S(2)}, u32[]{:S(2)}) %collective-permute-start.14) | collective-permute-done | bytes 98336 | tf_op jit(solution)/shard_map/ppermute | solution.py:18
  68.8 2.2 %copy-done.2 = bf16[32,256,256]{2,1,0:T(8,128)(2,1)S(1)} copy-done((bf16[32,256,256]{2,1,0:T(8,128)(2,1)S(1)}, bf16[32,256,256]{2,1,0:T(8,128)(2,1)}, u32[]{:S(2)}) %copy-start.2) | copy-done | bytes 4194328
  70.9 4.5 %shard_map.86 = (bf16[48,16,128]{2,1,0:T(8,128)(2,1)S(1)}, bf16[48,16,128]{2,1,0:T(8,128)(2,1)S(1)}) custom-call(s32[192]{0:T(256)S(1)} %pad_add_fusion.entry_ref, f32[8]{0:T(128)S(1)} %copy-done.4, s32[1]{0:T(128)} %bitcast.11.place_ref, bf16[24,16,128]{2,1,0:T(8,128)(2,1)S(1)} %add_convert_fusion.8.refs_0_, ...), custom_call_target="tpu_custom_call" | custom-call | flops 134217728 | bytes 8388608 | tf_op jit(solution)/shard_map/pallas_call | solution.py:141
  75.5 1.6 %collective-permute-start.16 = (bf16[48,16,128]{2,1,0:T(8,128)(2,1)S(1)}, bf16[48,16,128]{2,1,0:T(8,128)(2,1)S(1)}, u32[]{:S(2)}, u32[]{:S(2)}) collective-permute-start(bf16[48,16,128]{2,1,0:T(8,128)(2,1)S(1)} %get-tuple-element.18), channel_id=1, source_target_pairs={{0,1},{1,0},{2,3},{3,2},{4,5},{5,4},{6,7},{7,6},{8,9},{9,8},{10,11... | collective-permute-start | bytes 589832 | tf_op jit(solution)/shard_map/ppermute | solution.py:18
  78.3 3.4 %collective-permute-done.16 = bf16[48,16,128]{2,1,0:T(8,128)(2,1)S(1)} collective-permute-done((bf16[48,16,128]{2,1,0:T(8,128)(2,1)S(1)}, bf16[48,16,128]{2,1,0:T(8,128)(2,1)S(1)}, u32[]{:S(2)}, u32[]{:S(2)}) %collective-permute-start.16) | collective-permute-done | bytes 196640 | tf_op jit(solution)/shard_map/ppermute | solution.py:18
  81.8 1.1 %collective-permute-start.17 = (bf16[48,16,128]{2,1,0:T(8,128)(2,1)S(1)}, bf16[48,16,128]{2,1,0:T(8,128)(2,1)S(1)}, u32[]{:S(2)}, u32[]{:S(2)}) collective-permute-start(bf16[48,16,128]{2,1,0:T(8,128)(2,1)S(1)} %add_convert_fusion.3), channel_id=1, source_target_pairs={{0,2},{1,3},{2,0},{3,1},{4,6},{5,7},{6,4},{7,5},{8,10},{9,11},{10,... | collective-permute-start | bytes 589832 | tf_op jit(solution)/shard_map/ppermute | solution.py:18
  82.9 1.6 %collective-permute-done.18 = bf16[48,16,128]{2,1,0:T(8,128)(2,1)S(1)} collective-permute-done((bf16[48,16,128]{2,1,0:T(8,128)(2,1)S(1)}, bf16[48,16,128]{2,1,0:T(8,128)(2,1)S(1)}, u32[]{:S(2)}, u32[]{:S(2)}) %collective-permute-start.18) | collective-permute-done | bytes 196640 | tf_op jit(solution)/shard_map/ppermute | solution.py:18
  84.6 3.3 %collective-permute-done.17 = bf16[48,16,128]{2,1,0:T(8,128)(2,1)S(1)} collective-permute-done((bf16[48,16,128]{2,1,0:T(8,128)(2,1)S(1)}, bf16[48,16,128]{2,1,0:T(8,128)(2,1)S(1)}, u32[]{:S(2)}, u32[]{:S(2)}) %collective-permute-start.17) | collective-permute-done | bytes 196640 | tf_op jit(solution)/shard_map/ppermute | solution.py:18
  88.0 2.3 %collective-permute-done.19 = bf16[48,16,128]{2,1,0:T(8,128)(2,1)S(1)} collective-permute-done((bf16[48,16,128]{2,1,0:T(8,128)(2,1)S(1)}, bf16[48,16,128]{2,1,0:T(8,128)(2,1)S(1)}, u32[]{:S(2)}, u32[]{:S(2)}) %collective-permute-start.19) | collective-permute-done | bytes 196640 | tf_op jit(solution)/shard_map/ppermute | solution.py:18
  90.5 4.4 %shard_map.87 = bf16[4,4,12288]{2,1,0:T(4,128)(2,1)S(1)} custom-call(s32[192]{0:T(256)S(1)} %pad_add_fusion.entry_ref, f32[8]{0:T(128)S(1)} %copy-done.4, s32[1]{0:T(128)} %bitcast.11.place_ref, bf16[48,16,128]{2,1,0:T(8,128)(2,1)S(1)} %add_convert_fusion.2.low_ref, bf16[48,16,128]{2,1,0:T(8,128)(2,1)S(1)} %add_convert_fusion.high_ref, ...), custom_call_target="tpu_custom_call" | custom-call | flops 134217728 | bytes 8388608 | tf_op jit(solution)/shard_map/pallas_call | solution.py:141
  95.2 2.5 %collective-permute-start.23 = (bf16[4,12288]{1,0:T(4,128)(2,1)S(1)}, bf16[4,12288]{1,0:T(4,128)(2,1)S(1)}, u32[]{:S(2)}, u32[]{:S(2)}) collective-permute-start(bf16[4,12288]{1,0:T(4,128)(2,1)S(1)} %get-tuple-element.25), channel_id=1, source_target_pairs={{0,24},{4,28},{8,16},{12,20},{16,8},{20,12},{24,0},{28,4},{1,25},{... | collective-permute-start | bytes 294920 | tf_op jit(solution)/shard_map/ppermute | solution.py:18
  100.3 3.1 %collective-permute-done.23 = bf16[4,12288]{1,0:T(4,128)(2,1)S(1)} collective-permute-done((bf16[4,12288]{1,0:T(4,128)(2,1)S(1)}, bf16[4,12288]{1,0:T(4,128)(2,1)S(1)}, u32[]{:S(2)}, u32[]{:S(2)}) %collective-permute-start.23) | collective-permute-done | bytes 98336 | tf_op jit(solution)/shard_map/ppermute | solution.py:18
  103.4 4.4 %collective-permute-done.22 = bf16[4,12288]{1,0:T(4,128)(2,1)S(1)} collective-permute-done((bf16[4,12288]{1,0:T(4,128)(2,1)S(1)}, bf16[4,12288]{1,0:T(4,128)(2,1)S(1)}, u32[]{:S(2)}, u32[]{:S(2)}) %collective-permute-start.22) | collective-permute-done | bytes 98336 | tf_op jit(solution)/shard_map/ppermute | solution.py:18
  (78 shorter events, 14.3 us)
Async XLA Ops:
  0.6 9.1 %collective-permute-start.1 = (bf16[4,12288]{1,0:T(4,128)(2,1)}, bf16[4,12288]{1,0:T(4,128)(2,1)S(1)}, u32[]{:S(2)}, u32[]{:S(2)}) collective-permute-start(bf16[4,12288]{1,0:T(4,128)(2,1)} %param.5), channel_id=1, source_target_pairs={{0,8},{4,12},{8,0},{12,4},{16,24},{20,28},{24,16},{28,20},{1,9},{5... | collective-permute-start | bytes 294920 | tf_op jit(solution)/shard_map/ppermute | solution.py:18
  3.7 11.7 %collective-permute-start.3 = (bf16[4,12288]{1,0:T(4,128)(2,1)}, bf16[4,12288]{1,0:T(4,128)(2,1)S(1)}, u32[]{:S(2)}, u32[]{:S(2)}) collective-permute-start(bf16[4,12288]{1,0:T(4,128)(2,1)} %param.5), channel_id=1, source_target_pairs={{0,24},{4,28},{8,16},{12,20},{16,8},{20,12},{24,0},{28,4},{1,25},{... | collective-permute-start | bytes 294920 | tf_op jit(solution)/shard_map/ppermute | solution.py:18
  6.2 9.2 %collective-permute-start.2 = (bf16[4,12288]{1,0:T(4,128)(2,1)}, bf16[4,12288]{1,0:T(4,128)(2,1)S(1)}, u32[]{:S(2)}, u32[]{:S(2)}) collective-permute-start(bf16[4,12288]{1,0:T(4,128)(2,1)} %param.5), channel_id=1, source_target_pairs={{0,16},{4,20},{8,24},{12,28},{16,0},{20,4},{24,8},{28,12},{1,17},{... | collective-permute-start | bytes 294920 | tf_op jit(solution)/shard_map/ppermute | solution.py:18
  8.0 1.7 %collective-permute-start = (s32[96]{0:T(128)S(1)}, s32[96]{0:T(128)S(1)}, u32[]{:S(2)}, u32[]{:S(2)}) collective-permute-start(s32[96]{0:T(128)S(1)} %reshape.61), channel_id=1, source_target_pairs={{0,4},{4,0},{8,12},{12,8},{16,20},{20,16},{24,28},{28,24},{1,5},{5... | collective-permute-start | bytes 1160 | tf_op jit(solution)/shard_map/ppermute | solution.py:18
  8.1 7.6 %collective-permute-start.4 = (bf16[32,256,256]{2,1,0:T(8,128)(2,1)}, bf16[32,256,256]{2,1,0:T(8,128)(2,1)}, u32[]{:S(2)}, u32[]{:S(2)}) collective-permute-start(bf16[32,256,256]{2,1,0:T(8,128)(2,1)} %own_ref.5), channel_id=1, source_target_pairs={{0,4},{4,0},{8,12},{12,8},{16,20},{20,16},{24,28},{28,24},{1,5},{5... | collective-permute-start | bytes 12582920 | tf_op jit(solution)/shard_map/ppermute | solution.py:18
  15.7 2.2 %copy-start = (bf16[32,256,256]{2,1,0:T(8,128)(2,1)S(1)}, bf16[32,256,256]{2,1,0:T(8,128)(2,1)}, u32[]{:S(2)}) copy-start(bf16[32,256,256]{2,1,0:T(8,128)(2,1)} %own_ref.5) | copy-start | bytes 12582916
  17.9 0.7 copy-start.3
  18.6 19.9 %copy-start.4 = (f32[8]{0:T(128)S(1)}, f32[8]{0:T(128)}, u32[]{:S(2)}) copy-start(f32[8]{0:T(128)} %gain_ref.7) | copy-start | bytes 100
  23.1 7.2 %collective-permute-start.5 = (bf16[48,16,128]{2,1,0:T(8,128)(2,1)S(1)}, bf16[48,16,128]{2,1,0:T(8,128)(2,1)S(1)}, u32[]{:S(2)}, u32[]{:S(2)}) collective-permute-start(bf16[48,16,128]{2,1,0:T(8,128)(2,1)S(1)} %get-tuple-element.12), channel_id=1, source_target_pairs={{0,1},{1,0},{2,3},{3,2},{4,5},{5,4},{6,7},{7,6},{8,9},{9,8},{10,11... | collective-permute-start | bytes 589832 | tf_op jit(solution)/shard_map/ppermute | solution.py:18
  24.7 7.3 %collective-permute-start.7 = (bf16[48,16,128]{2,1,0:T(8,128)(2,1)S(1)}, bf16[48,16,128]{2,1,0:T(8,128)(2,1)S(1)}, u32[]{:S(2)}, u32[]{:S(2)}) collective-permute-start(bf16[48,16,128]{2,1,0:T(8,128)(2,1)S(1)} %get-tuple-element.13), channel_id=1, source_target_pairs={{0,2},{1,3},{2,0},{3,1},{4,6},{5,7},{6,4},{7,5},{8,10},{9,11},{10,... | collective-permute-start | bytes 589832 | tf_op jit(solution)/shard_map/ppermute | solution.py:18
  30.4 6.4 %collective-permute-start.6 = (bf16[48,16,128]{2,1,0:T(8,128)(2,1)S(1)}, bf16[48,16,128]{2,1,0:T(8,128)(2,1)S(1)}, u32[]{:S(2)}, u32[]{:S(2)}) collective-permute-start(bf16[48,16,128]{2,1,0:T(8,128)(2,1)S(1)} %add_convert_fusion.7), channel_id=1, source_target_pairs={{0,2},{1,3},{2,0},{3,1},{4,6},{5,7},{6,4},{7,5},{8,10},{9,11},{10,... | collective-permute-start | bytes 589832 | tf_op jit(solution)/shard_map/ppermute | solution.py:18
  32.1 6.1 %collective-permute-start.8 = (bf16[48,16,128]{2,1,0:T(8,128)(2,1)S(1)}, bf16[48,16,128]{2,1,0:T(8,128)(2,1)S(1)}, u32[]{:S(2)}, u32[]{:S(2)}) collective-permute-start(bf16[48,16,128]{2,1,0:T(8,128)(2,1)S(1)} %add_convert_fusion.5), channel_id=1, source_target_pairs={{0,1},{1,0},{2,3},{3,2},{4,5},{5,4},{6,7},{7,6},{8,9},{9,8},{10,11... | collective-permute-start | bytes 589832 | tf_op jit(solution)/shard_map/ppermute | solution.py:18
  38.4 10.2 %collective-permute-start.9 = (bf16[48,4,128]{2,1,0:T(4,128)(2,1)S(1)}, bf16[48,4,128]{2,1,0:T(4,128)(2,1)S(1)}, u32[]{:S(2)}, u32[]{:S(2)}) collective-permute-start(bf16[48,4,128]{2,1,0:T(4,128)(2,1)S(1)} %broadcast_select_fusion.2), channel_id=1, source_target_pairs={{0,4},{4,0},{8,12},{12,8},{16,20},{20,16},{24,28},{28,24},{1,5},{5... | collective-permute-start | bytes 147464 | tf_op jit(solution)/shard_map/ppermute | solution.py:18
  38.5 2.2 %copy-start.1 = (bf16[32,256,256]{2,1,0:T(8,128)(2,1)S(1)}, bf16[32,256,256]{2,1,0:T(8,128)(2,1)}, u32[]{:S(2)}) copy-start(bf16[32,256,256]{2,1,0:T(8,128)(2,1)} %own_ref.5) | copy-start | bytes 12582916
  44.2 5.3 %collective-permute-start.10 = (bf16[24,16,128]{2,1,0:T(8,128)(2,1)S(1)}, bf16[24,16,128]{2,1,0:T(8,128)(2,1)S(1)}, u32[]{:S(2)}, u32[]{:S(2)}) collective-permute-start(bf16[24,16,128]{2,1,0:T(8,128)(2,1)S(1)} %get-tuple-element.15), channel_id=1, source_target_pairs={{0,8},{4,12},{8,0},{12,4},{16,24},{20,28},{24,16},{28,20},{1,9},{5... | collective-permute-start | bytes 294920 | tf_op jit(solution)/shard_map/ppermute | solution.py:18
  46.0 10.7 %collective-permute-start.11 = (bf16[24,16,128]{2,1,0:T(8,128)(2,1)S(1)}, bf16[24,16,128]{2,1,0:T(8,128)(2,1)S(1)}, u32[]{:S(2)}, u32[]{:S(2)}) collective-permute-start(bf16[24,16,128]{2,1,0:T(8,128)(2,1)S(1)} %get-tuple-element.16), channel_id=1, source_target_pairs={{0,16},{4,20},{8,24},{12,28},{16,0},{20,4},{24,8},{28,12},{1,17},{... | collective-permute-start | bytes 294920 | tf_op jit(solution)/shard_map/ppermute | solution.py:18
  47.7 9.0 %collective-permute-start.12 = (bf16[24,16,128]{2,1,0:T(8,128)(2,1)S(1)}, bf16[24,16,128]{2,1,0:T(8,128)(2,1)S(1)}, u32[]{:S(2)}, u32[]{:S(2)}) collective-permute-start(bf16[24,16,128]{2,1,0:T(8,128)(2,1)S(1)} %get-tuple-element.17), channel_id=1, source_target_pairs={{0,24},{4,28},{8,16},{12,20},{16,8},{20,12},{24,0},{28,4},{1,25},{... | collective-permute-start | bytes 294920 | tf_op jit(solution)/shard_map/ppermute | solution.py:18
  56.8 7.4 %collective-permute-start.15 = (bf16[24,16,128]{2,1,0:T(8,128)(2,1)S(1)}, bf16[24,16,128]{2,1,0:T(8,128)(2,1)S(1)}, u32[]{:S(2)}, u32[]{:S(2)}) collective-permute-start(bf16[24,16,128]{2,1,0:T(8,128)(2,1)S(1)} %add_convert_fusion.8.refs_0_), channel_id=1, source_target_pairs={{0,24},{4,28},{8,16},{12,20},{16,8},{20,12},{24,0},{28,4},{1,25},{... | collective-permute-start | bytes 294920 | tf_op jit(solution)/shard_map/ppermute | solution.py:18
  59.2 9.4 %collective-permute-start.14 = (bf16[24,16,128]{2,1,0:T(8,128)(2,1)S(1)}, bf16[24,16,128]{2,1,0:T(8,128)(2,1)S(1)}, u32[]{:S(2)}, u32[]{:S(2)}) collective-permute-start(bf16[24,16,128]{2,1,0:T(8,128)(2,1)S(1)} %add_convert_fusion.8.refs_0_), channel_id=1, source_target_pairs={{0,16},{4,20},{8,24},{12,28},{16,0},{20,4},{24,8},{28,12},{1,17},{... | collective-permute-start | bytes 294920 | tf_op jit(solution)/shard_map/ppermute | solution.py:18
  60.3 8.3 %collective-permute-start.13 = (bf16[24,16,128]{2,1,0:T(8,128)(2,1)S(1)}, bf16[24,16,128]{2,1,0:T(8,128)(2,1)S(1)}, u32[]{:S(2)}, u32[]{:S(2)}) collective-permute-start(bf16[24,16,128]{2,1,0:T(8,128)(2,1)S(1)} %add_convert_fusion.8.refs_0_), channel_id=1, source_target_pairs={{0,8},{4,12},{8,0},{12,4},{16,24},{20,28},{24,16},{28,20},{1,9},{5... | collective-permute-start | bytes 294920 | tf_op jit(solution)/shard_map/ppermute | solution.py:18
  68.7 2.2 %copy-start.2 = (bf16[32,256,256]{2,1,0:T(8,128)(2,1)S(1)}, bf16[32,256,256]{2,1,0:T(8,128)(2,1)}, u32[]{:S(2)}) copy-start(bf16[32,256,256]{2,1,0:T(8,128)(2,1)} %own_ref.5) | copy-start | bytes 12582916
  75.5 6.3 %collective-permute-start.16 = (bf16[48,16,128]{2,1,0:T(8,128)(2,1)S(1)}, bf16[48,16,128]{2,1,0:T(8,128)(2,1)S(1)}, u32[]{:S(2)}, u32[]{:S(2)}) collective-permute-start(bf16[48,16,128]{2,1,0:T(8,128)(2,1)S(1)} %get-tuple-element.18), channel_id=1, source_target_pairs={{0,1},{1,0},{2,3},{3,2},{4,5},{5,4},{6,7},{7,6},{8,9},{9,8},{10,11... | collective-permute-start | bytes 589832 | tf_op jit(solution)/shard_map/ppermute | solution.py:18
  77.8 6.7 %collective-permute-start.18 = (bf16[48,16,128]{2,1,0:T(8,128)(2,1)S(1)}, bf16[48,16,128]{2,1,0:T(8,128)(2,1)S(1)}, u32[]{:S(2)}, u32[]{:S(2)}) collective-permute-start(bf16[48,16,128]{2,1,0:T(8,128)(2,1)S(1)} %get-tuple-element.19), channel_id=1, source_target_pairs={{0,2},{1,3},{2,0},{3,1},{4,6},{5,7},{6,4},{7,5},{8,10},{9,11},{10,... | collective-permute-start | bytes 589832 | tf_op jit(solution)/shard_map/ppermute | solution.py:18
  81.8 6.2 %collective-permute-start.17 = (bf16[48,16,128]{2,1,0:T(8,128)(2,1)S(1)}, bf16[48,16,128]{2,1,0:T(8,128)(2,1)S(1)}, u32[]{:S(2)}, u32[]{:S(2)}) collective-permute-start(bf16[48,16,128]{2,1,0:T(8,128)(2,1)S(1)} %add_convert_fusion.3), channel_id=1, source_target_pairs={{0,2},{1,3},{2,0},{3,1},{4,6},{5,7},{6,4},{7,5},{8,10},{9,11},{10,... | collective-permute-start | bytes 589832 | tf_op jit(solution)/shard_map/ppermute | solution.py:18
  84.6 5.7 %collective-permute-start.19 = (bf16[48,16,128]{2,1,0:T(8,128)(2,1)S(1)}, bf16[48,16,128]{2,1,0:T(8,128)(2,1)S(1)}, u32[]{:S(2)}, u32[]{:S(2)}) collective-permute-start(bf16[48,16,128]{2,1,0:T(8,128)(2,1)S(1)} %add_convert_fusion.1), channel_id=1, source_target_pairs={{0,1},{1,0},{2,3},{3,2},{4,5},{5,4},{6,7},{7,6},{8,9},{9,8},{10,11... | collective-permute-start | bytes 589832 | tf_op jit(solution)/shard_map/ppermute | solution.py:18
  90.4 8.2 %collective-permute-start.20 = (bf16[48,4,128]{2,1,0:T(4,128)(2,1)S(1)}, bf16[48,4,128]{2,1,0:T(4,128)(2,1)S(1)}, u32[]{:S(2)}, u32[]{:S(2)}) collective-permute-start(bf16[48,4,128]{2,1,0:T(4,128)(2,1)S(1)} %broadcast_select_fusion), channel_id=1, source_target_pairs={{0,4},{4,0},{8,12},{12,8},{16,20},{20,16},{24,28},{28,24},{1,5},{5... | collective-permute-start | bytes 147464 | tf_op jit(solution)/shard_map/ppermute | solution.py:18
  95.1 5.3 %collective-permute-start.21 = (bf16[4,12288]{1,0:T(4,128)(2,1)S(1)}, bf16[4,12288]{1,0:T(4,128)(2,1)S(1)}, u32[]{:S(2)}, u32[]{:S(2)}) collective-permute-start(bf16[4,12288]{1,0:T(4,128)(2,1)S(1)} %get-tuple-element.24), channel_id=1, source_target_pairs={{0,8},{4,12},{8,0},{12,4},{16,24},{20,28},{24,16},{28,20},{1,9},{5... | collective-permute-start | bytes 294920 | tf_op jit(solution)/shard_map/ppermute | solution.py:18
  95.2 8.3 %collective-permute-start.23 = (bf16[4,12288]{1,0:T(4,128)(2,1)S(1)}, bf16[4,12288]{1,0:T(4,128)(2,1)S(1)}, u32[]{:S(2)}, u32[]{:S(2)}) collective-permute-start(bf16[4,12288]{1,0:T(4,128)(2,1)S(1)} %get-tuple-element.25), channel_id=1, source_target_pairs={{0,24},{4,28},{8,16},{12,20},{16,8},{20,12},{24,0},{28,4},{1,25},{... | collective-permute-start | bytes 294920 | tf_op jit(solution)/shard_map/ppermute | solution.py:18
  97.6 10.2 %collective-permute-start.22 = (bf16[4,12288]{1,0:T(4,128)(2,1)S(1)}, bf16[4,12288]{1,0:T(4,128)(2,1)S(1)}, u32[]{:S(2)}, u32[]{:S(2)}) collective-permute-start(bf16[4,12288]{1,0:T(4,128)(2,1)S(1)} %get-tuple-element.26), channel_id=1, source_target_pairs={{0,16},{4,20},{8,24},{12,28},{16,0},{20,4},{24,8},{28,12},{1,17},{... | collective-permute-start | bytes 294920 | tf_op jit(solution)/shard_map/ppermute | solution.py:18

commit v5 on v4

v5 whole, which is shorter than its diff:
```python
import functools

import jax
import jax.numpy as jnp
from jax import lax
from jax.experimental import pallas as pl
from jax.experimental.pallas import tpu as pltpu
from jax.sharding import PartitionSpec as P

B = 256
LANES = 128
PER = B // LANES
VMEM_LIMIT = 24 * 1024 * 1024


def swap(value, axis, offset, only=None):
    count = lax.axis_size(axis)
    pairs = [(i, i ^ offset) for i in range(count) if only is None or i % 2 == only]
    return lax.ppermute(value, axis, pairs)


def add_up(*parts):
    total = parts[0].astype(jnp.float32)
    for part in parts[1:]:
        total = total + part.astype(jnp.float32)
    return total.astype(parts[0].dtype)


def add_products(entry_ref, gain_ref, load, block_refs, total, adjoint):
    at = 0
    for block_ref in block_refs:
        for slot in range(block_ref.shape[0]):
            row, col, level = entry_ref[at], entry_ref[at + 1], entry_ref[at + 2]
            at += 3
            scale = jnp.where(level >= 0, gain_ref[jnp.maximum(level, 0)], jnp.float32(0.0))
            source, target = (row, col) if adjoint else (col, row)
            term = lax.dot_general(
                load(source),
                block_ref[slot],
                (((1,), (0 if adjoint else 1,)), ((), ())),
                preferred_element_type=jnp.float32,
            )
            term = term * scale
            for piece in range(PER):
                total[target * PER + piece] += term[:, piece * LANES : (piece + 1) * LANES]


def load_from(x):
    def load(block):
        return jnp.concatenate([x[block * PER + piece] for piece in range(PER)], axis=1)

    return load


def gate_kernel(value_ref, after_ref, out_ref):
    out_ref[...] = value_ref[...]


def first_kernel(entry_ref, gain_ref, x_ref, *refs):
    block_refs, (out_ref, total) = refs[:2], refs[-2:]
    total[...] = jnp.zeros_like(total)

    def load(block):
        return x_ref[:, pl.ds(pl.multiple_of(block * B, B), B)]

    add_products(entry_ref, gain_ref, load, block_refs, total, False)
    out_ref[...] = total[...].astype(out_ref.dtype)


def forward_kernel(ways, entry_ref, gain_ref, place_ref, *refs):
    pieces = refs[:ways]
    block_refs, (out_ref, total, x) = refs[ways : ways + 2], refs[-3:]
    total[...] = jnp.zeros_like(total)
    along = place_ref[0]
    size = pieces[0].shape[0]
    for way in range(ways):
        x[pl.ds((along ^ way) * size, size)] = pieces[way][...]
    add_products(entry_ref, gain_ref, load_from(x), block_refs, total, False)
    out_ref[...] = total[...].astype(out_ref.dtype)


def add_adjoint(entry_refs, gain_ref, own_x, other_x, block_refs, total):
    total[...] = jnp.zeros_like(total)
    add_products(entry_refs[0], gain_ref, load_from(own_x), block_refs[:2], total, True)
    add_products(entry_refs[1], gain_ref, load_from(other_x), block_refs[2:], total, True)


def adjoint_kernel(ways, own_entry, other_entry, gain_ref, place_ref, own_x, other_x, *refs):
    *block_refs, total = refs[:-ways - 1] + refs[-1:]
    outs = refs[-ways - 1 : -1]
    add_adjoint((own_entry, other_entry), gain_ref, own_x, other_x, block_refs, total)
    along = place_ref[0]
    size = outs[0].shape[0]
    for way in range(ways):
        outs[way][...] = total[pl.ds((along ^ way) * size, size)].astype(outs[way].dtype)


def last_kernel(kept, own_entry, other_entry, gain_ref, place_ref, own_x, other_x, *refs):
    total, out_ref = refs[-1], refs[-2 - kept]
    block_refs = refs[: -2 - 2 * kept]
    add_adjoint((own_entry, other_entry), gain_ref, own_x, other_x, block_refs, total)
    along = place_ref[0]
    ways, share, _ = out_ref.shape
    for group in range(total.shape[0]):
        values = total[group].astype(out_ref.dtype)
        for index in range(ways):
            out_ref[along ^ index, :, group * LANES : (group + 1) * LANES] = values[index * share : (index + 1) * share]


def shards(strengths, blocks, pattern, level_gain):
    n_panel = lax.axis_size("panel")
    n_case = lax.axis_size("case")
    ways = n_panel // 2
    share, width = strengths.shape
    held_cases = share * ways
    slots = blocks.shape[0]
    col_blocks = width // B
    row_blocks = col_blocks * n_case // n_panel
    col_groups = col_blocks * PER
    row_groups = row_blocks * PER
    part_size = col_groups // ways
    panel = lax.axis_index("panel")
    case = lax.axis_index("case")
    core = panel % 2
    along = panel // 2
    value = strengths.dtype

    smem = pl.BlockSpec(memory_space=pltpu.SMEM)
    vmem = pl.BlockSpec(memory_space=pltpu.VMEM)
    anywhere = pl.BlockSpec(memory_space=pl.ANY)
    params = pltpu.CompilerParams(vmem_limit_bytes=VMEM_LIMIT)

    def like(shape):
        return jax.ShapeDtypeStruct(shape, value)

    own_blocks = [blocks[: slots // 2], blocks[slots // 2 :]]
    other_blocks = [swap(part, "panel", 1) for part in own_blocks]
    early = [swap(strengths, "panel", 2 * way, 0) for way in range(1, ways)]
    later_strengths = pl.pallas_call(
        gate_kernel,
        out_shape=like(strengths.shape),
        in_specs=[vmem, anywhere],
        out_specs=vmem,
        compiler_params=params,
    )(strengths, other_blocks[0])
    late = [swap(later_strengths, "panel", 2 * way, 1) for way in range(1, ways)]
    place = along.astype(jnp.int32)[None]
    first = jnp.stack([panel * row_blocks, case * col_blocks, 0]).astype(jnp.int32)
    own_entry = jnp.where(pattern[:, 2:3] < 0, jnp.array([0, 0, -1], jnp.int32), pattern - first).reshape(-1)
    other_entry = swap(own_entry, "panel", 1)

    def product(kernel, small, vectors, parts, outs, total_groups, x_groups=0, kept=(), after=()):
        scratch = [pltpu.VMEM((total_groups, held_cases, LANES), jnp.float32)]
        if x_groups:
            scratch.append(pltpu.VMEM((x_groups, held_cases, LANES), value))
        held = sum(part.shape[0] for part in parts)
        before = len(small) + len(vectors) + len(parts)
        return pl.pallas_call(
            kernel,
            out_shape=[like(shape) for shape in outs] + [like(one.shape) for one in kept],
            in_specs=[smem] * len(small) + [vmem] * (len(vectors) + len(parts)) + [anywhere] * (len(kept) + len(after)),
            out_specs=[vmem] * len(outs) + [anywhere] * len(kept),
            scratch_shapes=scratch,
            input_output_aliases={before + i: len(outs) + i for i in range(len(kept))},
            compiler_params=params,
            cost_estimate=pl.CostEstimate(
                flops=2 * held_cases * held * B * B, bytes_accessed=2 * held * B * B, transcendentals=0
            ),
        )(*small, *vectors, *parts, *kept, *after)

    rows_shape = (row_groups, held_cases, LANES)

    def over_case(own, other):
        bits = [1 << b for b in range(n_case.bit_length() - 1)]
        for one, two in zip(bits, reversed(bits)):
            own_in, other_in = swap(own, "case", one), swap(other, "case", two)
            own, other = add_up(own, own_in), add_up(other, other_in)
        return own, other

    def scatter_along(parts):
        return add_up(parts[0], *[swap(parts[way], "panel", 2 * way) for way in range(1, ways)])

    def gather_along(part):
        return [part] + [swap(part, "panel", 2 * way) for way in range(1, ways)]

    def first_forward(x):
        (own,) = product(first_kernel, (own_entry, level_gain), [x], own_blocks, [rows_shape], row_groups)
        (other,) = product(
            first_kernel, (other_entry, level_gain), [x], other_blocks, [rows_shape], row_groups, after=[own]
        )
        return own, other

    def forward(pieces):
        kernel = functools.partial(forward_kernel, ways)
        (own,) = product(kernel, (own_entry, level_gain, place), pieces, own_blocks, [rows_shape], row_groups, col_groups)
        (other,) = product(
            kernel, (other_entry, level_gain, place), pieces, other_blocks, [rows_shape], row_groups, col_groups, after=[own]
        )
        return own, other

    def adjoint(kernel, own, other, outs, kept=()):
        small = (own_entry, other_entry, level_gain, place)
        return product(kernel, small, [own, other], [*own_blocks, *other_blocks], outs, col_groups, kept=kept)

    def own_rows(own, other):
        count = held_cases // n_case
        mine = lax.dynamic_slice_in_dim(own, case * count, count, 1)
        theirs = swap(lax.dynamic_slice_in_dim(other, case * count, count, 1), "panel", 1)
        both = jnp.stack([jnp.where(core == 0, mine, theirs), jnp.where(core == 0, theirs, mine)])
        both = both.reshape(2, row_groups, count // share, share, LANES)
        return jnp.transpose(both, (2, 0, 3, 1, 4)).reshape(2 * count, row_groups * LANES)

    def own_share(pieces):
        own = jnp.stack([lax.dynamic_slice_in_dim(one, along * share, share, 1) for one in pieces])
        bit = 1
        while bit < ways:
            flipped = own.reshape(ways // (2 * bit), 2, bit, part_size, share, LANES)[:, ::-1].reshape(own.shape)
            own = jnp.where(along & bit != 0, flipped, own)
            bit *= 2
        return jnp.moveaxis(own, 2, 0).reshape(share, width)

    stacked = jnp.zeros((ways, share, width), value)
    stacked = lax.dynamic_update_slice_in_dim(stacked, strengths[None], along, 0)
    for way in range(1, ways):
        one = jnp.where(core == 0, early[way - 1], late[way - 1])
        stacked = lax.dynamic_update_slice_in_dim(stacked, one[None], along ^ way, 0)
    first_sums = over_case(*first_forward(stacked.reshape(held_cases, width)))

    parts = adjoint(
        functools.partial(adjoint_kernel, ways), *first_sums, [(part_size, held_cases, LANES)] * ways
    )
    pieces = gather_along(scatter_along(parts))

    second_sums = over_case(*forward(pieces))
    kept = [*first_sums, *pieces]
    by_share, *kept = adjoint(
        functools.partial(last_kernel, len(kept)), *second_sums, [(ways, share, width)], kept
    )
    adjoint_two = scatter_along(by_share)
    forward_one = own_rows(*kept[:2])
    forward_two = own_rows(*second_sums)
    adjoint_one = own_share(kept[2:])
    return (forward_one, adjoint_one, forward_two, adjoint_two)


def solution(mesh):
    in_specs = (
        P("panel", "case"),
        P(("panel", "case"), None, None),
        P(("panel", "case"), None),
        P(),
    )
    out_specs = (P("case", "panel"), P("panel", "case"), P("case", "panel"), P("panel", "case"))
    return jax.shard_map(shards, mesh=mesh, in_specs=in_specs, out_specs=out_specs, check_vma=False)
```

time: 109 us -> 105 us (0.963)
  waiting for transfers between devices: 47.8 us -> 28.9 us
  starting transfers between devices: 28.3 us -> 44 us
  local copies, waits for them, and re-layouts: 11 us -> 8.49 us
  Pallas kernels: 17 us -> 18.6 us
    ppermute x24 -> x28, waiting for transfers between devices: 47.8 us -> 28.9 us  [swap(): return lax.ppermute(value, axis, pairs)]
    ppermute x24 -> x28, starting transfers between devices: 28.3 us -> 44 us  [swap(): return lax.ppermute(value, axis, pairs)]
    unnamed x13 -> x17, local copies, waits for them, and re-layouts: 9.24 us -> 2.31 us
    slice x0 -> x1, local copies, waits for them, and re-layouts: none -> 4.68 us  [shards(): own_blocks = [blocks[:slots // 2], blocks[slots // 2:]]]
    pallas_call x4 -> x7, Pallas kernels: 17 us -> 18.6 us  [the longest x6 18.6 us: product(): pl.pallas_call(kernel, out_shape=[like(shape) for shape in outs] + [like(...]
  transfers between devices with their start and end apart: 24 -> 28, of which waited for: 15 -> 15; matrix products, arithmetic and copies ran while one was open for 6% -> 3% of each run, Pallas kernels for 7% -> 5%
where the time goes in v5:
time: 105 us; the launch traced here: 104 us
  starting transfers between devices  44 us (42%)
  waiting for transfers between devices  28.9 us (28%)
  Pallas kernels  18.6 us (18%)
  local copies, waits for them, and re-layouts  8.49 us (8%)
  other arithmetic  2.84 us (3%)
  between operations  1.18 us (1%)
    ppermute x28, starting transfers between devices, swap(): return lax.ppermute(value, axis, pairs)  44 us
    ppermute x28, waiting for transfers between devices, swap(): return lax.ppermute(value, axis, pairs)  28.9 us
    pallas_call x6, Pallas kernels, product(): pl.pallas_call(kernel, out_shape=[like(shape) for shape in outs] + [like(...  18.6 us
    slice x1, local copies, waits for them, and re-layouts, shards(): own_blocks = [blocks[:slots // 2], blocks[slots // 2:]]  4.68 us
    unnamed x17, local copies, waits for them, and re-layouts  2.31 us
    convert_element_type x10, other arithmetic, add_up(): return total.astype(parts[0].dtype)  2.13 us
  transfers between devices with their start and end apart: 28, of which 15 were waited for; matrix products, arithmetic and copies ran while one was open for 3% of the time, Pallas kernels for 5%

profile of v5, /device:TPU:0, one launch (start us, length us, event | category | flops | bytes accessed | tf_op | source)
XLA Modules:
  0.0 104.0 jit_solution(12786481330983552745)
XLA Ops:
  0.7 4.7 %fusion.4 = (bf16[16,256,256]{2,1,0:T(8,128)(2,1)}, bf16[16,256,256]{2,1,0:T(8,128)(2,1)}) fusion(bf16[32,256,256]{2,1,0:T(8,128)(2,1)} %param.6), kind=kLoop, calls=%fused_computation.46 | loop fusion | bytes 8388608 | tf_op jit(solution)/shard_map/slice | solution.py:136
  5.8 4.5 %collective-permute-start.1 = (bf16[4,12288]{1,0:T(4,128)(2,1)S(1)}, bf16[4,12288]{1,0:T(4,128)(2,1)S(1)}, u32[]{:S(2)}, u32[]{:S(2)}) collective-permute-start(bf16[4,12288]{1,0:T(4,128)(2,1)S(1)} %copy-done.3), channel_id=1, source_target_pairs={{0,8},{8,0},{16,24},{24,16},{1,9},{9,1},{17,25},{25,17},{2,10},{10... | collective-permute-start | bytes 294920 | tf_op jit(solution)/shard_map/ppermute | solution.py:19
  10.3 4.5 %collective-permute-start.4 = (bf16[4,12288]{1,0:T(4,128)(2,1)S(1)}, bf16[4,12288]{1,0:T(4,128)(2,1)S(1)}, u32[]{:S(2)}, u32[]{:S(2)}) collective-permute-start(bf16[4,12288]{1,0:T(4,128)(2,1)S(1)} %copy-done.3), channel_id=1, source_target_pairs={{0,16},{8,24},{16,0},{24,8},{1,17},{9,25},{17,1},{25,9},{2,18},{10... | collective-permute-start | bytes 294920 | tf_op jit(solution)/shard_map/ppermute | solution.py:19
  14.8 1.9 %collective-permute-start.6 = (bf16[4,12288]{1,0:T(4,128)(2,1)S(1)}, bf16[4,12288]{1,0:T(4,128)(2,1)S(1)}, u32[]{:S(2)}, u32[]{:S(2)}) collective-permute-start(bf16[4,12288]{1,0:T(4,128)(2,1)S(1)} %copy-done.3), channel_id=1, source_target_pairs={{0,24},{8,16},{16,8},{24,0},{1,25},{9,17},{17,9},{25,1},{2,26},{10... | collective-permute-start | bytes 294920 | tf_op jit(solution)/shard_map/ppermute | solution.py:19
  18.1 2.4 %collective-permute-start.10 = (bf16[16,256,256]{2,1,0:T(8,128)(2,1)}, bf16[16,256,256]{2,1,0:T(8,128)(2,1)}, u32[]{:S(2)}, u32[]{:S(2)}) collective-permute-start(bf16[16,256,256]{2,1,0:T(8,128)(2,1)} %get-tuple-element.26.refs_1_.refs_5_), channel_id=1, source_target_pairs={{0,4},{4,0},{8,12},{12,8},{16,20},{20,16},{24,28},{28,24},{1,5},{5... | collective-permute-start | bytes 6291464 | tf_op jit(solution)/shard_map/ppermute | solution.py:19
  23.4 1.6 %copy-done = bf16[16,256,256]{2,1,0:T(8,128)(2,1)S(1)} copy-done((bf16[16,256,256]{2,1,0:T(8,128)(2,1)S(1)}, bf16[16,256,256]{2,1,0:T(8,128)(2,1)}, u32[]{:S(2)}) %copy-start) | copy-done | bytes 2097176
  25.0 2.8 %shard_map.85.refs_2_ = bf16[48,16,128]{2,1,0:T(8,128)(2,1)S(1)} custom-call(s32[96]{0:T(128)S(1)} %reshape.61.entry_ref.own_entry, f32[8]{0:T(128)S(1)} %copy-done.5, bf16[16,12288]{1,0:T(8,128)(2,1)S(1)} %reshape.62.x_ref, bf16[16,256,256]{2,1,0:T(8,128)(2,1)} %get-tuple-element.27.refs_0_.refs_4_, bf16[16,256,256]{2,1,0:T(8,128)(2,1)S(1)} %copy-done), custom_call_target="tpu_custom_call" | custom-call | flops 67108864 | bytes 4194304 | tf_op jit(solution)/shard_map/pallas_call | solution.py:158
  27.8 2.8 %shard_map.86 = bf16[48,16,128]{2,1,0:T(8,128)(2,1)S(1)} custom-call(s32[96]{0:T(128)S(1)} %collective-permute-done.entry_ref.other_entry, f32[8]{0:T(128)S(1)} %copy-done.5, bf16[16,12288]{1,0:T(8,128)(2,1)S(1)} %reshape.62.x_ref, bf16[16,256,256]{2,1,0:T(8,128)(2,1)S(1)} %collective-permute-done.2.after_ref.refs_0_.refs_2_.refs_4_, ...), custom_call_target="tpu_custom_call" | custom-call | flops 67108864 | bytes 4194304 | tf_op jit(solution)/shard_map/pallas_call | solution.py:158
  30.7 1.6 %collective-permute-start.11 = (bf16[48,16,128]{2,1,0:T(8,128)(2,1)S(1)}, bf16[48,16,128]{2,1,0:T(8,128)(2,1)S(1)}, u32[]{:S(2)}, u32[]{:S(2)}) collective-permute-start(bf16[48,16,128]{2,1,0:T(8,128)(2,1)S(1)} %shard_map.86), channel_id=1, source_target_pairs={{0,2},{1,3},{2,0},{3,1},{4,6},{5,7},{6,4},{7,5},{8,10},{9,11},{10,... | collective-permute-start | bytes 589832 | tf_op jit(solution)/shard_map/ppermute | solution.py:19
  32.3 1.5 %collective-permute-start.8 = (bf16[48,16,128]{2,1,0:T(8,128)(2,1)S(1)}, bf16[48,16,128]{2,1,0:T(8,128)(2,1)S(1)}, u32[]{:S(2)}, u32[]{:S(2)}) collective-permute-start(bf16[48,16,128]{2,1,0:T(8,128)(2,1)S(1)} %shard_map.85.refs_2_), channel_id=1, source_target_pairs={{0,1},{1,0},{2,3},{3,2},{4,5},{5,4},{6,7},{7,6},{8,9},{9,8},{10,11... | collective-permute-start | bytes 589832 | tf_op jit(solution)/shard_map/ppermute | solution.py:19
  33.8 2.7 %collective-permute-done.11 = bf16[48,16,128]{2,1,0:T(8,128)(2,1)S(1)} collective-permute-done((bf16[48,16,128]{2,1,0:T(8,128)(2,1)S(1)}, bf16[48,16,128]{2,1,0:T(8,128)(2,1)S(1)}, u32[]{:S(2)}, u32[]{:S(2)}) %collective-permute-start.11) | collective-permute-done | bytes 196640 | tf_op jit(solution)/shard_map/ppermute | solution.py:19
  36.5 1.5 %collective-permute-start.12 = (bf16[48,16,128]{2,1,0:T(8,128)(2,1)S(1)}, bf16[48,16,128]{2,1,0:T(8,128)(2,1)S(1)}, u32[]{:S(2)}, u32[]{:S(2)}) collective-permute-start(bf16[48,16,128]{2,1,0:T(8,128)(2,1)S(1)} %add_convert_fusion.5), channel_id=1, source_target_pairs={{0,1},{1,0},{2,3},{3,2},{4,5},{5,4},{6,7},{7,6},{8,9},{9,8},{10,11... | collective-permute-start | bytes 589832 | tf_op jit(solution)/shard_map/ppermute | solution.py:19
  38.1 1.6 %collective-permute-start.9 = (bf16[48,16,128]{2,1,0:T(8,128)(2,1)S(1)}, bf16[48,16,128]{2,1,0:T(8,128)(2,1)S(1)}, u32[]{:S(2)}, u32[]{:S(2)}) collective-permute-start(bf16[48,16,128]{2,1,0:T(8,128)(2,1)S(1)} %add_convert_fusion.7), channel_id=1, source_target_pairs={{0,2},{1,3},{2,0},{3,1},{4,6},{5,7},{6,4},{7,5},{8,10},{9,11},{10,... | collective-permute-start | bytes 589832 | tf_op jit(solution)/shard_map/ppermute | solution.py:19
  39.7 2.5 %collective-permute-done.12 = bf16[48,16,128]{2,1,0:T(8,128)(2,1)S(1)} collective-permute-done((bf16[48,16,128]{2,1,0:T(8,128)(2,1)S(1)}, bf16[48,16,128]{2,1,0:T(8,128)(2,1)S(1)}, u32[]{:S(2)}, u32[]{:S(2)}) %collective-permute-start.12) | collective-permute-done | bytes 196640 | tf_op jit(solution)/shard_map/ppermute | solution.py:19
  42.3 1.5 %collective-permute-done.9 = bf16[48,16,128]{2,1,0:T(8,128)(2,1)S(1)} collective-permute-done((bf16[48,16,128]{2,1,0:T(8,128)(2,1)S(1)}, bf16[48,16,128]{2,1,0:T(8,128)(2,1)S(1)}, u32[]{:S(2)}, u32[]{:S(2)}) %collective-permute-start.9) | collective-permute-done | bytes 196640 | tf_op jit(solution)/shard_map/ppermute | solution.py:19
  43.9 3.5 %shard_map.87 = (bf16[24,16,128]{2,1,0:T(8,128)(2,1)S(1)}, bf16[24,16,128]{2,1,0:T(8,128)(2,1)S(1)}, bf16[24,16,128]{2,1,0:T(8,128)(2,1)S(1)}, bf16[24,16,128]{2,1,0:T(8,128)(2,1)S(1)}) custom-call(s32[96]{0:T(128)S(1)} %reshape.61.entry_ref.own_entry, s32[96]{0:T(128)S(1)} %collective-permute-done.entry_ref.other_entry, f32[8]{0:T(128)S(1)} %copy-done.5, ...), custom_call_target="tpu_custom_call" | custom-call | flops 134217728 | bytes 8388608 | tf_op jit(solution)/shard_map/pallas_call | solution.py:158
  47.7 2.9 %collective-permute-start.14 = (bf16[24,16,128]{2,1,0:T(8,128)(2,1)S(1)}, bf16[24,16,128]{2,1,0:T(8,128)(2,1)S(1)}, u32[]{:S(2)}, u32[]{:S(2)}) collective-permute-start(bf16[24,16,128]{2,1,0:T(8,128)(2,1)S(1)} %get-tuple-element.17), channel_id=1, source_target_pairs={{0,16},{4,20},{8,24},{12,28},{16,0},{20,4},{24,8},{28,12},{1,17},{... | collective-permute-start | bytes 294920 | tf_op jit(solution)/shard_map/ppermute | solution.py:19
  53.2 3.9 %collective-permute-done.15 = bf16[24,16,128]{2,1,0:T(8,128)(2,1)S(1)} collective-permute-done((bf16[24,16,128]{2,1,0:T(8,128)(2,1)S(1)}, bf16[24,16,128]{2,1,0:T(8,128)(2,1)S(1)}, u32[]{:S(2)}, u32[]{:S(2)}) %collective-permute-start.15) | collective-permute-done | bytes 98336 | tf_op jit(solution)/shard_map/ppermute | solution.py:19
  58.4 1.4 %collective-permute-start.17 = (bf16[24,16,128]{2,1,0:T(8,128)(2,1)S(1)}, bf16[24,16,128]{2,1,0:T(8,128)(2,1)S(1)}, u32[]{:S(2)}, u32[]{:S(2)}) collective-permute-start(bf16[24,16,128]{2,1,0:T(8,128)(2,1)S(1)} %add_convert_fusion.8.refs_0_.refs_6_), channel_id=1, source_target_pairs={{0,16},{4,20},{8,24},{12,28},{16,0},{20,4},{24,8},{28,12},{1,17},{... | collective-permute-start | bytes 294920 | tf_op jit(solution)/shard_map/ppermute | solution.py:19
  59.8 1.8 %collective-permute-start.18 = (bf16[24,16,128]{2,1,0:T(8,128)(2,1)S(1)}, bf16[24,16,128]{2,1,0:T(8,128)(2,1)S(1)}, u32[]{:S(2)}, u32[]{:S(2)}) collective-permute-start(bf16[24,16,128]{2,1,0:T(8,128)(2,1)S(1)} %add_convert_fusion.8.refs_0_.refs_6_), channel_id=1, source_target_pairs={{0,24},{4,28},{8,16},{12,20},{16,8},{20,12},{24,0},{28,4},{1,25},{... | collective-permute-start | bytes 294920 | tf_op jit(solution)/shard_map/ppermute | solution.py:19
  62.5 5.6 %collective-permute-done.17.refs_2_.refs_8_ = bf16[24,16,128]{2,1,0:T(8,128)(2,1)S(1)} collective-permute-done((bf16[24,16,128]{2,1,0:T(8,128)(2,1)S(1)}, bf16[24,16,128]{2,1,0:T(8,128)(2,1)S(1)}, u32[]{:S(2)}, u32[]{:S(2)}) %collective-permute-start.17) | collective-permute-done | bytes 98336 | tf_op jit(solution)/shard_map/ppermute | solution.py:19
  68.0 2.8 %shard_map.88.refs_6_ = bf16[48,16,128]{2,1,0:T(8,128)(2,1)S(1)} custom-call(s32[96]{0:T(128)S(1)} %reshape.61.entry_ref.own_entry, f32[8]{0:T(128)S(1)} %copy-done.5, s32[1]{0:T(128)} %bitcast.3.place_ref, bf16[24,16,128]{2,1,0:T(8,128)(2,1)S(1)} %add_convert_fusion.8.refs_0_.refs_6_, bf16[24,16,128]{2,1,0:T(8,128)(2,1)S(1)} %collective-permute-done.16.refs_1_.refs_7_, ...), custom_call_target="tpu_custom_call" | custom-call | flops 67108864 | bytes 4194304 | tf_op jit(solution)/shard_map/pallas_call | solution.py:158
  70.9 1.4 %collective-permute-start.19 = (bf16[48,16,128]{2,1,0:T(8,128)(2,1)S(1)}, bf16[48,16,128]{2,1,0:T(8,128)(2,1)S(1)}, u32[]{:S(2)}, u32[]{:S(2)}) collective-permute-start(bf16[48,16,128]{2,1,0:T(8,128)(2,1)S(1)} %shard_map.88.refs_6_), channel_id=1, source_target_pairs={{0,1},{1,0},{2,3},{3,2},{4,5},{5,4},{6,7},{7,6},{8,9},{9,8},{10,11... | collective-permute-start | bytes 589832 | tf_op jit(solution)/shard_map/ppermute | solution.py:19
  72.3 2.8 %shard_map.89 = bf16[48,16,128]{2,1,0:T(8,128)(2,1)S(1)} custom-call(s32[96]{0:T(128)S(1)} %collective-permute-done.entry_ref.other_entry, f32[8]{0:T(128)S(1)} %copy-done.5, s32[1]{0:T(128)} %bitcast.3.place_ref, bf16[24,16,128]{2,1,0:T(8,128)(2,1)S(1)} %add_convert_fusion.8.refs_0_.refs_6_, ...), custom_call_target="tpu_custom_call" | custom-call | flops 67108864 | bytes 4194304 | tf_op jit(solution)/shard_map/pallas_call | solution.py:158
  76.7 1.6 %collective-permute-start.20 = (bf16[48,16,128]{2,1,0:T(8,128)(2,1)S(1)}, bf16[48,16,128]{2,1,0:T(8,128)(2,1)S(1)}, u32[]{:S(2)}, u32[]{:S(2)}) collective-permute-start(bf16[48,16,128]{2,1,0:T(8,128)(2,1)S(1)} %add_convert_fusion.3), channel_id=1, source_target_pairs={{0,2},{1,3},{2,0},{3,1},{4,6},{5,7},{6,4},{7,5},{8,10},{9,11},{10,... | collective-permute-start | bytes 589832 | tf_op jit(solution)/shard_map/ppermute | solution.py:19
  78.3 2.6 %collective-permute-done.21 = bf16[48,16,128]{2,1,0:T(8,128)(2,1)S(1)} collective-permute-done((bf16[48,16,128]{2,1,0:T(8,128)(2,1)S(1)}, bf16[48,16,128]{2,1,0:T(8,128)(2,1)S(1)}, u32[]{:S(2)}, u32[]{:S(2)}) %collective-permute-start.21) | collective-permute-done | bytes 196640 | tf_op jit(solution)/shard_map/ppermute | solution.py:19
  83.1 3.6 %collective-permute-done.22 = bf16[48,16,128]{2,1,0:T(8,128)(2,1)S(1)} collective-permute-done((bf16[48,16,128]{2,1,0:T(8,128)(2,1)S(1)}, bf16[48,16,128]{2,1,0:T(8,128)(2,1)S(1)}, u32[]{:S(2)}, u32[]{:S(2)}) %collective-permute-start.22) | collective-permute-done | bytes 196640 | tf_op jit(solution)/shard_map/ppermute | solution.py:19
  86.8 3.7 %shard_map.90 = (bf16[4,4,12288]{2,1,0:T(4,128)(2,1)S(1)}, bf16[48,16,128]{2,1,0:T(8,128)(2,1)S(1)}, bf16[48,16,128]{2,1,0:T(8,128)(2,1)S(1)}, bf16[24,16,128]{2...) custom-call(s32[96]{0:T(128)S(1)} %reshape.61.entry_ref.own_entry, ...), custom_call_target="tpu_custom_call", output_to_operand_aliasing={{1}: (10, {}), {2}: (11, {}), {3}: (12, {}), {4}: (13, {}),... | custom-call | flops 134217728 | bytes 8388608 | tf_op jit(solution)/shard_map/pallas_call | solution.py:158
  90.6 1.9 %collective-permute-start.25 = (bf16[4,12288]{1,0:T(4,128)(2,1)S(1)}, bf16[4,12288]{1,0:T(4,128)(2,1)S(1)}, u32[]{:S(2)}, u32[]{:S(2)}) collective-permute-start(bf16[4,12288]{1,0:T(4,128)(2,1)S(1)} %get-tuple-element.28), channel_id=1, source_target_pairs={{0,8},{4,12},{8,0},{12,4},{16,24},{20,28},{24,16},{28,20},{1,9},{5... | collective-permute-start | bytes 294920 | tf_op jit(solution)/shard_map/ppermute | solution.py:19
  92.6 2.5 %collective-permute-start.27 = (bf16[4,12288]{1,0:T(4,128)(2,1)S(1)}, bf16[4,12288]{1,0:T(4,128)(2,1)S(1)}, u32[]{:S(2)}, u32[]{:S(2)}) collective-permute-start(bf16[4,12288]{1,0:T(4,128)(2,1)S(1)} %get-tuple-element.29), channel_id=1, source_target_pairs={{0,24},{4,28},{8,16},{12,20},{16,8},{20,12},{24,0},{28,4},{1,25},{... | collective-permute-start | bytes 294920 | tf_op jit(solution)/shard_map/ppermute | solution.py:19
  95.4 4.1 %collective-permute-start.23 = (bf16[48,4,128]{2,1,0:T(4,128)(2,1)S(1)}, bf16[48,4,128]{2,1,0:T(4,128)(2,1)S(1)}, u32[]{:S(2)}, u32[]{:S(2)}) collective-permute-start(bf16[48,4,128]{2,1,0:T(4,128)(2,1)S(1)} %constant_dynamic-slice_fusion.5), channel_id=1, source_target_pairs={{0,4},{4,0},{8,12},{12,8},{16,20},{20,16},{24,28},{28,24},{1,5},{5... | collective-permute-start | bytes 147464 | tf_op jit(solution)/shard_map/ppermute | solution.py:19
  102.4 1.6 %fusion.2 = bf16[4,12288]{1,0:T(4,128)(2,1)} fusion(bf16[4,12288]{1,0:T(4,128)(2,1)S(1)} %collective-permute-done.27, bf16[4,12288]{1,0:T(4,128)(2,1)S(1)} %collective-permute-done.26, bf16[4,12288]{1,0:T(4,128)(2,1)S(1)} %collective-permute-done.25, bf16[4,4,12288]{2,1,0:T(4,128)(2,1)} %copy-done.4), kind=kLoop, calls=%fused_computation.11 | loop fusion | flops 393216 | bytes 491520 | tf_op jit(solution)/shard_map/convert_element_type | solution.py:26
  (92 shorter events, 16.9 us)
Async XLA Ops:
  0.6 16.2 %copy-start.7 = (s32[3]{0:T(128)S(1)}, s32[3]{0:T(128)}, u32[]{:S(2)}) copy-start(s32[3]{0:T(128)} %constant.52.clone) | copy-start | bytes 40
  0.7 16.1 %copy-start.6 = (s32[32,3]{0,1:T(4,128)S(1)}, s32[32,3]{0,1:T(4,128)}, u32[]{:S(2)}) copy-start(s32[32,3]{0,1:T(4,128)} %param.7) | copy-start | bytes 1156
  5.3 11.9 %collective-permute-start.2 = (bf16[16,256,256]{2,1,0:T(8,128)(2,1)}, bf16[16,256,256]{2,1,0:T(8,128)(2,1)S(1)}, u32[]{:S(2)}, u32[]{:S(2)}) collective-permute-start(bf16[16,256,256]{2,1,0:T(8,128)(2,1)} %get-tuple-element.27.refs_0_.refs_4_), channel_id=1, source_target_pairs={{0,4},{4,0},{8,12},{12,8},{16,20},{20,16},{24,28},{28,24},{1,5},{5... | collective-permute-start | bytes 6291464 | tf_op jit(solution)/shard_map/ppermute | solution.py:19
  5.8 12.3 %collective-permute-start.1 = (bf16[4,12288]{1,0:T(4,128)(2,1)S(1)}, bf16[4,12288]{1,0:T(4,128)(2,1)S(1)}, u32[]{:S(2)}, u32[]{:S(2)}) collective-permute-start(bf16[4,12288]{1,0:T(4,128)(2,1)S(1)} %copy-done.3), channel_id=1, source_target_pairs={{0,8},{8,0},{16,24},{24,16},{1,9},{9,1},{17,25},{25,17},{2,10},{10... | collective-permute-start | bytes 294920 | tf_op jit(solution)/shard_map/ppermute | solution.py:19
  10.3 10.9 %collective-permute-start.4 = (bf16[4,12288]{1,0:T(4,128)(2,1)S(1)}, bf16[4,12288]{1,0:T(4,128)(2,1)S(1)}, u32[]{:S(2)}, u32[]{:S(2)}) collective-permute-start(bf16[4,12288]{1,0:T(4,128)(2,1)S(1)} %copy-done.3), channel_id=1, source_target_pairs={{0,16},{8,24},{16,0},{24,8},{1,17},{9,25},{17,1},{25,9},{2,18},{10... | collective-permute-start | bytes 294920 | tf_op jit(solution)/shard_map/ppermute | solution.py:19
  14.8 8.4 %collective-permute-start.6 = (bf16[4,12288]{1,0:T(4,128)(2,1)S(1)}, bf16[4,12288]{1,0:T(4,128)(2,1)S(1)}, u32[]{:S(2)}, u32[]{:S(2)}) collective-permute-start(bf16[4,12288]{1,0:T(4,128)(2,1)S(1)} %copy-done.3), channel_id=1, source_target_pairs={{0,24},{8,16},{16,8},{24,0},{1,25},{9,17},{17,9},{25,1},{2,26},{10... | collective-permute-start | bytes 294920 | tf_op jit(solution)/shard_map/ppermute | solution.py:19
  17.1 10.7 %collective-permute-start = (s32[96]{0:T(128)S(1)}, s32[96]{0:T(128)S(1)}, u32[]{:S(2)}, u32[]{:S(2)}) collective-permute-start(s32[96]{0:T(128)S(1)} %reshape.61.entry_ref.own_entry), channel_id=1, source_target_pairs={{0,4},{4,0},{8,12},{12,8},{16,20},{20,16},{24,28},{28,24},{1,5},{5... | collective-permute-start | bytes 1160 | tf_op jit(solution)/shard_map/ppermute | solution.py:19
  17.2 3.3 %collective-permute-start.3 = (bf16[4,12288]{1,0:T(4,128)(2,1)S(1)}, bf16[4,12288]{1,0:T(4,128)(2,1)S(1)}, u32[]{:S(2)}, u32[]{:S(2)}) collective-permute-start(bf16[4,12288]{1,0:T(4,128)(2,1)S(1)} %shard_map.84), channel_id=1, source_target_pairs={{4,12},{12,4},{20,28},{28,20},{5,13},{13,5},{21,29},{29,21},{6,14}... | collective-permute-start | bytes 294920 | tf_op jit(solution)/shard_map/ppermute | solution.py:19
  18.1 9.7 %collective-permute-start.10 = (bf16[16,256,256]{2,1,0:T(8,128)(2,1)}, bf16[16,256,256]{2,1,0:T(8,128)(2,1)}, u32[]{:S(2)}, u32[]{:S(2)}) collective-permute-start(bf16[16,256,256]{2,1,0:T(8,128)(2,1)} %get-tuple-element.26.refs_1_.refs_5_), channel_id=1, source_target_pairs={{0,4},{4,0},{8,12},{12,8},{16,20},{20,16},{24,28},{28,24},{1,5},{5... | collective-permute-start | bytes 6291464 | tf_op jit(solution)/shard_map/ppermute | solution.py:19
  20.5 1.4 %collective-permute-start.5 = (bf16[4,12288]{1,0:T(4,128)(2,1)S(1)}, bf16[4,12288]{1,0:T(4,128)(2,1)S(1)}, u32[]{:S(2)}, u32[]{:S(2)}) collective-permute-start(bf16[4,12288]{1,0:T(4,128)(2,1)S(1)} %shard_map.84), channel_id=1, source_target_pairs={{4,20},{12,28},{20,4},{28,12},{5,21},{13,29},{21,5},{29,13},{6,22}... | collective-permute-start | bytes 294920 | tf_op jit(solution)/shard_map/ppermute | solution.py:19
  21.2 2.0 %collective-permute-start.7 = (bf16[4,12288]{1,0:T(4,128)(2,1)S(1)}, bf16[4,12288]{1,0:T(4,128)(2,1)S(1)}, u32[]{:S(2)}, u32[]{:S(2)}) collective-permute-start(bf16[4,12288]{1,0:T(4,128)(2,1)S(1)} %shard_map.84), channel_id=1, source_target_pairs={{4,28},{12,20},{20,12},{28,4},{5,29},{13,21},{21,13},{29,5},{6,30}... | collective-permute-start | bytes 294920 | tf_op jit(solution)/shard_map/ppermute | solution.py:19
  30.7 13.2 %copy-start.1 = (bf16[16,256,256]{2,1,0:T(8,128)(2,1)S(1)}, bf16[16,256,256]{2,1,0:T(8,128)(2,1)}, u32[]{:S(2)}) copy-start(bf16[16,256,256]{2,1,0:T(8,128)(2,1)} %get-tuple-element.26.refs_1_.refs_5_) | copy-start | bytes 6291460
  30.7 5.7 %collective-permute-start.11 = (bf16[48,16,128]{2,1,0:T(8,128)(2,1)S(1)}, bf16[48,16,128]{2,1,0:T(8,128)(2,1)S(1)}, u32[]{:S(2)}, u32[]{:S(2)}) collective-permute-start(bf16[48,16,128]{2,1,0:T(8,128)(2,1)S(1)} %shard_map.86), channel_id=1, source_target_pairs={{0,2},{1,3},{2,0},{3,1},{4,6},{5,7},{6,4},{7,5},{8,10},{9,11},{10,... | collective-permute-start | bytes 589832 | tf_op jit(solution)/shard_map/ppermute | solution.py:19
  32.3 5.8 %collective-permute-start.8 = (bf16[48,16,128]{2,1,0:T(8,128)(2,1)S(1)}, bf16[48,16,128]{2,1,0:T(8,128)(2,1)S(1)}, u32[]{:S(2)}, u32[]{:S(2)}) collective-permute-start(bf16[48,16,128]{2,1,0:T(8,128)(2,1)S(1)} %shard_map.85.refs_2_), channel_id=1, source_target_pairs={{0,1},{1,0},{2,3},{3,2},{4,5},{5,4},{6,7},{7,6},{8,9},{9,8},{10,11... | collective-permute-start | bytes 589832 | tf_op jit(solution)/shard_map/ppermute | solution.py:19
  36.5 5.7 %collective-permute-start.12 = (bf16[48,16,128]{2,1,0:T(8,128)(2,1)S(1)}, bf16[48,16,128]{2,1,0:T(8,128)(2,1)S(1)}, u32[]{:S(2)}, u32[]{:S(2)}) collective-permute-start(bf16[48,16,128]{2,1,0:T(8,128)(2,1)S(1)} %add_convert_fusion.5), channel_id=1, source_target_pairs={{0,1},{1,0},{2,3},{3,2},{4,5},{5,4},{6,7},{7,6},{8,9},{9,8},{10,11... | collective-permute-start | bytes 589832 | tf_op jit(solution)/shard_map/ppermute | solution.py:19
  38.1 5.7 %collective-permute-start.9 = (bf16[48,16,128]{2,1,0:T(8,128)(2,1)S(1)}, bf16[48,16,128]{2,1,0:T(8,128)(2,1)S(1)}, u32[]{:S(2)}, u32[]{:S(2)}) collective-permute-start(bf16[48,16,128]{2,1,0:T(8,128)(2,1)S(1)} %add_convert_fusion.7), channel_id=1, source_target_pairs={{0,2},{1,3},{2,0},{3,1},{4,6},{5,7},{6,4},{7,5},{8,10},{9,11},{10,... | collective-permute-start | bytes 589832 | tf_op jit(solution)/shard_map/ppermute | solution.py:19
  47.4 4.7 %collective-permute-start.13 = (bf16[24,16,128]{2,1,0:T(8,128)(2,1)S(1)}, bf16[24,16,128]{2,1,0:T(8,128)(2,1)S(1)}, u32[]{:S(2)}, u32[]{:S(2)}) collective-permute-start(bf16[24,16,128]{2,1,0:T(8,128)(2,1)S(1)} %get-tuple-element.16), channel_id=1, source_target_pairs={{0,8},{4,12},{8,0},{12,4},{16,24},{20,28},{24,16},{28,20},{1,9},{5... | collective-permute-start | bytes 294920 | tf_op jit(solution)/shard_map/ppermute | solution.py:19
  47.7 5.5 %collective-permute-start.14 = (bf16[24,16,128]{2,1,0:T(8,128)(2,1)S(1)}, bf16[24,16,128]{2,1,0:T(8,128)(2,1)S(1)}, u32[]{:S(2)}, u32[]{:S(2)}) collective-permute-start(bf16[24,16,128]{2,1,0:T(8,128)(2,1)S(1)} %get-tuple-element.17), channel_id=1, source_target_pairs={{0,16},{4,20},{8,24},{12,28},{16,0},{20,4},{24,8},{28,12},{1,17},{... | collective-permute-start | bytes 294920 | tf_op jit(solution)/shard_map/ppermute | solution.py:19
  50.6 6.5 %collective-permute-start.15 = (bf16[24,16,128]{2,1,0:T(8,128)(2,1)S(1)}, bf16[24,16,128]{2,1,0:T(8,128)(2,1)S(1)}, u32[]{:S(2)}, u32[]{:S(2)}) collective-permute-start(bf16[24,16,128]{2,1,0:T(8,128)(2,1)S(1)} %get-tuple-element.18), channel_id=1, source_target_pairs={{0,24},{4,28},{8,16},{12,20},{16,8},{20,12},{24,0},{28,4},{1,25},{... | collective-permute-start | bytes 294920 | tf_op jit(solution)/shard_map/ppermute | solution.py:19
  57.1 5.4 %collective-permute-start.16 = (bf16[24,16,128]{2,1,0:T(8,128)(2,1)S(1)}, bf16[24,16,128]{2,1,0:T(8,128)(2,1)S(1)}, u32[]{:S(2)}, u32[]{:S(2)}) collective-permute-start(bf16[24,16,128]{2,1,0:T(8,128)(2,1)S(1)} %add_convert_fusion.8.refs_0_.refs_6_), channel_id=1, source_target_pairs={{0,8},{4,12},{8,0},{12,4},{16,24},{20,28},{24,16},{28,20},{1,9},{5... | collective-permute-start | bytes 294920 | tf_op jit(solution)/shard_map/ppermute | solution.py:19
  58.4 9.6 %collective-permute-start.17 = (bf16[24,16,128]{2,1,0:T(8,128)(2,1)S(1)}, bf16[24,16,128]{2,1,0:T(8,128)(2,1)S(1)}, u32[]{:S(2)}, u32[]{:S(2)}) collective-permute-start(bf16[24,16,128]{2,1,0:T(8,128)(2,1)S(1)} %add_convert_fusion.8.refs_0_.refs_6_), channel_id=1, source_target_pairs={{0,16},{4,20},{8,24},{12,28},{16,0},{20,4},{24,8},{28,12},{1,17},{... | collective-permute-start | bytes 294920 | tf_op jit(solution)/shard_map/ppermute | solution.py:19
  59.8 8.2 %collective-permute-start.18 = (bf16[24,16,128]{2,1,0:T(8,128)(2,1)S(1)}, bf16[24,16,128]{2,1,0:T(8,128)(2,1)S(1)}, u32[]{:S(2)}, u32[]{:S(2)}) collective-permute-start(bf16[24,16,128]{2,1,0:T(8,128)(2,1)S(1)} %add_convert_fusion.8.refs_0_.refs_6_), channel_id=1, source_target_pairs={{0,24},{4,28},{8,16},{12,20},{16,8},{20,12},{24,0},{28,4},{1,25},{... | collective-permute-start | bytes 294920 | tf_op jit(solution)/shard_map/ppermute | solution.py:19
  70.9 5.7 %collective-permute-start.19 = (bf16[48,16,128]{2,1,0:T(8,128)(2,1)S(1)}, bf16[48,16,128]{2,1,0:T(8,128)(2,1)S(1)}, u32[]{:S(2)}, u32[]{:S(2)}) collective-permute-start(bf16[48,16,128]{2,1,0:T(8,128)(2,1)S(1)} %shard_map.88.refs_6_), channel_id=1, source_target_pairs={{0,1},{1,0},{2,3},{3,2},{4,5},{5,4},{6,7},{7,6},{8,9},{9,8},{10,11... | collective-permute-start | bytes 589832 | tf_op jit(solution)/shard_map/ppermute | solution.py:19
  75.2 11.6 %copy-start.2 = (bf16[16,256,256]{2,1,0:T(8,128)(2,1)S(1)}, bf16[16,256,256]{2,1,0:T(8,128)(2,1)}, u32[]{:S(2)}) copy-start(bf16[16,256,256]{2,1,0:T(8,128)(2,1)} %get-tuple-element.26.refs_1_.refs_5_) | copy-start | bytes 6291460
  75.2 5.7 %collective-permute-start.21 = (bf16[48,16,128]{2,1,0:T(8,128)(2,1)S(1)}, bf16[48,16,128]{2,1,0:T(8,128)(2,1)S(1)}, u32[]{:S(2)}, u32[]{:S(2)}) collective-permute-start(bf16[48,16,128]{2,1,0:T(8,128)(2,1)S(1)} %shard_map.89), channel_id=1, source_target_pairs={{0,2},{1,3},{2,0},{3,1},{4,6},{5,7},{6,4},{7,5},{8,10},{9,11},{10,... | collective-permute-start | bytes 589832 | tf_op jit(solution)/shard_map/ppermute | solution.py:19
  76.7 6.3 %collective-permute-start.20 = (bf16[48,16,128]{2,1,0:T(8,128)(2,1)S(1)}, bf16[48,16,128]{2,1,0:T(8,128)(2,1)S(1)}, u32[]{:S(2)}, u32[]{:S(2)}) collective-permute-start(bf16[48,16,128]{2,1,0:T(8,128)(2,1)S(1)} %add_convert_fusion.3), channel_id=1, source_target_pairs={{0,2},{1,3},{2,0},{3,1},{4,6},{5,7},{6,4},{7,5},{8,10},{9,11},{10,... | collective-permute-start | bytes 589832 | tf_op jit(solution)/shard_map/ppermute | solution.py:19
  81.0 5.7 %collective-permute-start.22 = (bf16[48,16,128]{2,1,0:T(8,128)(2,1)S(1)}, bf16[48,16,128]{2,1,0:T(8,128)(2,1)S(1)}, u32[]{:S(2)}, u32[]{:S(2)}) collective-permute-start(bf16[48,16,128]{2,1,0:T(8,128)(2,1)S(1)} %add_convert_fusion.1), channel_id=1, source_target_pairs={{0,1},{1,0},{2,3},{3,2},{4,5},{5,4},{6,7},{7,6},{8,9},{9,8},{10,11... | collective-permute-start | bytes 589832 | tf_op jit(solution)/shard_map/ppermute | solution.py:19
  90.6 11.8 %collective-permute-start.25 = (bf16[4,12288]{1,0:T(4,128)(2,1)S(1)}, bf16[4,12288]{1,0:T(4,128)(2,1)S(1)}, u32[]{:S(2)}, u32[]{:S(2)}) collective-permute-start(bf16[4,12288]{1,0:T(4,128)(2,1)S(1)} %get-tuple-element.28), channel_id=1, source_target_pairs={{0,8},{4,12},{8,0},{12,4},{16,24},{20,28},{24,16},{28,20},{1,9},{5... | collective-permute-start | bytes 294920 | tf_op jit(solution)/shard_map/ppermute | solution.py:19
  92.4 9.9 %collective-permute-start.26 = (bf16[4,12288]{1,0:T(4,128)(2,1)S(1)}, bf16[4,12288]{1,0:T(4,128)(2,1)S(1)}, u32[]{:S(2)}, u32[]{:S(2)}) collective-permute-start(bf16[4,12288]{1,0:T(4,128)(2,1)S(1)} %get-tuple-element.30), channel_id=1, source_target_pairs={{0,16},{4,20},{8,24},{12,28},{16,0},{20,4},{24,8},{28,12},{1,17},{... | collective-permute-start | bytes 294920 | tf_op jit(solution)/shard_map/ppermute | solution.py:19
  92.6 9.8 %collective-permute-start.27 = (bf16[4,12288]{1,0:T(4,128)(2,1)S(1)}, bf16[4,12288]{1,0:T(4,128)(2,1)S(1)}, u32[]{:S(2)}, u32[]{:S(2)}) collective-permute-start(bf16[4,12288]{1,0:T(4,128)(2,1)S(1)} %get-tuple-element.29), channel_id=1, source_target_pairs={{0,24},{4,28},{8,16},{12,20},{16,8},{20,12},{24,0},{28,4},{1,25},{... | collective-permute-start | bytes 294920 | tf_op jit(solution)/shard_map/ppermute | solution.py:19
  95.4 5.0 %collective-permute-start.23 = (bf16[48,4,128]{2,1,0:T(4,128)(2,1)S(1)}, bf16[48,4,128]{2,1,0:T(4,128)(2,1)S(1)}, u32[]{:S(2)}, u32[]{:S(2)}) collective-permute-start(bf16[48,4,128]{2,1,0:T(4,128)(2,1)S(1)} %constant_dynamic-slice_fusion.5), channel_id=1, source_target_pairs={{0,4},{4,0},{8,12},{12,8},{16,20},{20,16},{24,28},{28,24},{1,5},{5... | collective-permute-start | bytes 147464 | tf_op jit(solution)/shard_map/ppermute | solution.py:19
  100.2 1.2 %collective-permute-start.24 = (bf16[48,4,128]{2,1,0:T(4,128)(2,1)S(1)}, bf16[48,4,128]{2,1,0:T(4,128)(2,1)S(1)}, u32[]{:S(2)}, u32[]{:S(2)}) collective-permute-start(bf16[48,4,128]{2,1,0:T(4,128)(2,1)S(1)} %constant_dynamic-slice_fusion), channel_id=1, source_target_pairs={{0,4},{4,0},{8,12},{12,8},{16,20},{20,16},{24,28},{28,24},{1,5},{5... | collective-permute-start | bytes 147464 | tf_op jit(solution)/shard_map/ppermute | solution.py:19
  (4 other events, 17.6 us)

commit v6 on v4

v6 whole, which is shorter than its diff:
```python
import functools

import jax
import jax.numpy as jnp
from jax import lax
from jax.experimental import pallas as pl
from jax.experimental.pallas import tpu as pltpu
from jax.sharding import PartitionSpec as P

B = 256
LANES = 128
PER = B // LANES
HELD_PARTS = 2
ROW_PARTS = 4
COL_PARTS = 2
VMEM_LIMIT = 24 * 1024 * 1024


def swap(value, axis, offset):
    count = lax.axis_size(axis)
    return lax.ppermute(value, axis, [(i, i ^ offset) for i in range(count)])


def add_up(*parts):
    total = parts[0].astype(jnp.float32)
    for part in parts[1:]:
        total = total + part.astype(jnp.float32)
    return total.astype(parts[0].dtype)


def spans(size, count):
    edges = [size * i // count for i in range(count + 1)]
    return [(a, b - a) for a, b in zip(edges, edges[1:])]


def add_products(entry_ref, gain_ref, load, block_refs, total, adjoint):
    total[...] = jnp.zeros_like(total)
    at = 0
    for block_ref in block_refs:
        for slot in range(block_ref.shape[0]):
            row, col, level = entry_ref[at], entry_ref[at + 1], entry_ref[at + 2]
            at += 3
            scale = jnp.where(level >= 0, gain_ref[jnp.maximum(level, 0)], jnp.float32(0.0))
            source, target = (row, col) if adjoint else (col, row)
            term = lax.dot_general(
                load(source),
                block_ref[slot],
                (((1,), (0 if adjoint else 1,)), ((), ())),
                preferred_element_type=jnp.float32,
            )
            term = term * scale
            for piece in range(PER):
                total[target * PER + piece] += term[:, piece * LANES : (piece + 1) * LANES]


def load_from(x):
    def load(block):
        return jnp.concatenate([x[block * PER + piece] for piece in range(PER)], axis=1)

    return load


def write_parts(total, outs):
    at = 0
    for out_ref in outs:
        size = out_ref.shape[0]
        out_ref[...] = total[at : at + size].astype(out_ref.dtype)
        at += size


def join_parts(x, parts):
    at = 0
    for part in parts:
        size = part.shape[0]
        x[at : at + size] = part[...]
        at += size


def first_kernel(entry_ref, gain_ref, x_ref, *refs):
    block_refs, outs, total = refs[:HELD_PARTS], refs[HELD_PARTS:-1], refs[-1]

    def load(block):
        return x_ref[:, pl.ds(pl.multiple_of(block * B, B), B)]

    add_products(entry_ref, gain_ref, load, block_refs, total, False)
    write_parts(total, outs)


def forward_kernel(ways, cuts, entry_ref, gain_ref, place_ref, *refs):
    count = len(cuts) * 2 * ways
    pieces, block_refs, outs = refs[:count], refs[count : count + HELD_PARTS], refs[count + HELD_PARTS : -2]
    total, x = refs[-2:]
    core, along = place_ref[0], place_ref[1]
    whole = sum(size for _, size in cuts)
    for cut, (start, size) in enumerate(cuts):
        for side in range(2):
            for way in range(ways):
                at = ((core ^ side) * ways + (along ^ way)) * whole + start
                x[pl.ds(at, size)] = pieces[(cut * 2 + side) * ways + way][...]
    add_products(entry_ref, gain_ref, load_from(x), block_refs, total, False)
    write_parts(total, outs)


def adjoint_kernel(ways, cuts, entry_ref, gain_ref, place_ref, *refs):
    parts, block_refs = refs[:ROW_PARTS], refs[ROW_PARTS : ROW_PARTS + HELD_PARTS]
    outs = refs[ROW_PARTS + HELD_PARTS : -2]
    total, x = refs[-2:]
    join_parts(x, parts)
    add_products(entry_ref, gain_ref, load_from(x), block_refs, total, True)
    core, along = place_ref[0], place_ref[1]
    whole = sum(size for _, size in cuts)
    for cut, (start, size) in enumerate(cuts):
        for side in range(2):
            out_ref = outs[cut * 2 + side]
            for way in range(ways):
                at = ((core ^ side) * ways + (along ^ way)) * whole + start
                out_ref[way] = total[pl.ds(at, size)].astype(out_ref.dtype)


def last_kernel(entry_ref, gain_ref, place_ref, *refs):
    parts, block_refs = refs[:ROW_PARTS], refs[ROW_PARTS : ROW_PARTS + HELD_PARTS]
    total, x = refs[-2:]
    kept = (len(refs) - 2 - ROW_PARTS - HELD_PARTS - COL_PARTS) // 2
    outs = refs[ROW_PARTS + HELD_PARTS + kept :][:COL_PARTS]
    join_parts(x, parts)
    add_products(entry_ref, gain_ref, load_from(x), block_refs, total, True)
    core, along = place_ref[0], place_ref[1]
    group = 0
    for out_ref in outs:
        _, ways, share, width = out_ref.shape
        for lane in range(0, width, LANES):
            values = total[group].astype(out_ref.dtype)
            group += 1
            for index in range(2 * ways):
                piece = values[index * share : (index + 1) * share]
                out_ref[core ^ (index % 2), along ^ (index // 2), :, lane : lane + LANES] = piece


def shards(strengths, blocks, pattern, level_gain):
    n_panel = lax.axis_size("panel")
    n_case = lax.axis_size("case")
    ways = n_panel // 2
    share, width = strengths.shape
    cases = share * n_panel
    slots = blocks.shape[0]
    col_blocks = width // B
    row_blocks = col_blocks * n_case // n_panel
    col_groups = col_blocks * PER
    row_groups = row_blocks * PER
    panel = lax.axis_index("panel")
    case = lax.axis_index("case")
    core = panel % 2
    along = panel // 2
    value = strengths.dtype
    row_cuts = spans(row_groups, ROW_PARTS)
    cuts = spans(col_groups // n_panel, COL_PARTS)

    place = jnp.stack([core, along]).astype(jnp.int32)
    first = jnp.stack([panel * row_blocks, case * col_blocks, 0]).astype(jnp.int32)
    entry = jnp.where(pattern[:, 2:3] < 0, jnp.array([0, 0, -1], jnp.int32), pattern - first).reshape(-1)
    held = [blocks[a : a + n] for a, n in spans(slots, HELD_PARTS)]

    smem = pl.BlockSpec(memory_space=pltpu.SMEM)
    vmem = pl.BlockSpec(memory_space=pltpu.VMEM)
    anywhere = pl.BlockSpec(memory_space=pl.ANY)

    def product(kernel, small, vectors, outs, total_groups, x_groups=0, kept=()):
        scratch = [pltpu.VMEM((total_groups, cases, LANES), jnp.float32)]
        if x_groups:
            scratch.append(pltpu.VMEM((x_groups, cases, LANES), value))
        before = len(small) + len(vectors) + len(held)
        return pl.pallas_call(
            kernel,
            out_shape=[jax.ShapeDtypeStruct(shape, value) for shape in (*outs, *(one.shape for one in kept))],
            in_specs=[smem] * len(small) + [vmem] * (len(vectors) + len(held)) + [anywhere] * len(kept),
            out_specs=[vmem] * len(outs) + [anywhere] * len(kept),
            scratch_shapes=scratch,
            input_output_aliases={before + i: len(outs) + i for i in range(len(kept))},
            compiler_params=pltpu.CompilerParams(vmem_limit_bytes=VMEM_LIMIT),
            cost_estimate=pl.CostEstimate(
                flops=2 * cases * slots * B * B, bytes_accessed=2 * slots * B * B, transcendentals=0
            ),
        )(*small, *vectors, *held, *kept)

    row_shapes = [(size, cases, LANES) for _, size in row_cuts]

    def over_case(parts):
        bits = [1 << b for b in range(n_case.bit_length() - 1)]
        parts = list(parts)
        for step in range(len(bits)):
            arrived = [swap(part, "case", bits[(step + i) % len(bits)]) for i, part in enumerate(parts)]
            parts = [add_up(part, one) for part, one in zip(parts, arrived)]
        return parts

    def scatter_panel(mine, theirs):
        return scatter_along(add_up(mine, swap(theirs, "panel", 1)))

    def scatter_along(summed):
        return add_up(summed[0], *[swap(summed[way], "panel", 2 * way) for way in range(1, ways)])

    def gather_panel(part):
        same = [part] + [swap(part, "panel", 2 * way) for way in range(1, ways)]
        return same + [swap(one, "panel", 1) for one in same]

    def own_cases(parts):
        whole = jnp.concatenate(parts)
        own = lax.dynamic_slice_in_dim(whole, case * (cases // n_case), cases // n_case, 1)
        return jnp.swapaxes(own, 0, 1).reshape(cases // n_case, row_groups * LANES)

    def own_share(pieces):
        picked = [lax.dynamic_slice_in_dim(one, panel * share, share, 1) for one in pieces]
        count = 2 * ways
        joined = [jnp.concatenate([picked[cut * count + i] for cut in range(len(cuts))]) for i in range(count)]
        own = jnp.stack(joined).reshape(2, ways, col_groups // n_panel, share, LANES)
        own = jnp.where(core == 1, own[::-1], own)
        bit = 1
        while bit < ways:
            flipped = own.reshape(2, ways // (2 * bit), 2, bit, *own.shape[2:])[:, :, ::-1].reshape(own.shape)
            own = jnp.where(along & bit != 0, flipped, own)
            bit *= 2
        return jnp.moveaxis(own, 3, 0).reshape(share, width)

    same_first = [strengths] + [swap(strengths, "panel", 2 * way) for way in range(1, ways)]
    other_first = [swap(one, "panel", 1) for one in same_first]
    stacked = jnp.zeros((n_panel, share, width), value)
    for side, parts in enumerate((same_first, other_first)):
        for way, one in enumerate(parts):
            stacked = lax.dynamic_update_slice_in_dim(stacked, one[None], panel ^ (2 * way + side), 0)
    x = stacked.reshape(cases, width)
    first_sums = over_case(product(first_kernel, (entry, level_gain), [x], row_shapes, row_groups))

    small = (entry, level_gain, place)
    outs = [(ways, size, cases, LANES) for _, size in cuts for _ in range(2)]
    halves = product(functools.partial(adjoint_kernel, ways, cuts), small, first_sums, outs, col_groups, row_groups)
    pieces = []
    for part in [scatter_panel(*halves[2 * cut : 2 * cut + 2]) for cut in range(len(cuts))]:
        pieces += gather_panel(part)

    kernel = functools.partial(forward_kernel, ways, cuts)
    second_sums = over_case(product(kernel, small, pieces, row_shapes, row_groups, col_groups))

    outs = [(2, ways, share, width // COL_PARTS)] * COL_PARTS
    kept = [*first_sums, *pieces]
    result = product(last_kernel, small, second_sums, outs, col_groups, row_groups, kept)
    by_share, kept = result[:COL_PARTS], result[COL_PARTS:]
    summed = [add_up(one[0], swap(one[1], "panel", 1)) for one in by_share]
    summed, kept, second_sums = lax.optimization_barrier((summed, kept, second_sums))
    adjoint_two = jnp.concatenate([scatter_along(one) for one in summed], axis=1)
    forward_one = own_cases(kept[:ROW_PARTS])
    forward_two = own_cases(second_sums)
    adjoint_one = own_share(kept[ROW_PARTS:])
    return (forward_one, adjoint_one, forward_two, adjoint_two)


def solution(mesh):
    in_specs = (
        P("panel", "case"),
        P(("panel", "case"), None, None),
        P(("panel", "case"), None),
        P(),
    )
    out_specs = (P("case", "panel"), P("panel", "case"), P("case", "panel"), P("panel", "case"))
    return jax.shard_map(shards, mesh=mesh, in_specs=in_specs, out_specs=out_specs, check_vma=False)
```

time: 109 us -> 104 us (0.954)
  waiting for transfers between devices: 47.8 us -> 21.4 us
  starting transfers between devices: 28.3 us -> 54.4 us
  Pallas kernels: 17 us -> 7.09 us
  local copies, waits for them, and re-layouts: 11 us -> 15 us
    ppermute x24 -> x53, waiting for transfers between devices: 47.8 us -> 21.4 us  [swap(): return lax.ppermute(value, axis, [(i, i ^ offset) for i in range(count)])]
    ppermute x24 -> x53, starting transfers between devices: 28.3 us -> 54.4 us  [swap(): return lax.ppermute(value, axis, [(i, i ^ offset) for i in range(count)])]
    pallas_call x4, Pallas kernels: 17 us -> 7.09 us  [product(): pl.pallas_call(kernel, out_shape=[jax.ShapeDtypeStruct(shape, value) for...]
    unnamed x13 -> x24, local copies, waits for them, and re-layouts: 9.24 us -> 1.62 us
    dynamic_update_slice x4 -> x8, local copies, waits for them, and re-layouts: 1.1 us -> 5.42 us  [shards(): lax.dynamic_update_slice_in_dim(stacked, one[None], panel ^ 2 * way + sid...]
    slice x0 -> x1, local copies, waits for them, and re-layouts: none -> 3.93 us  [shards(): held = [blocks[a:a + n] for a, n in spans(slots, HELD_PARTS)]]
    reshape x1 -> x3, local copies, waits for them, and re-layouts: 0.09 us -> 2.3 us  [the longest x1 1.58 us: shards(): x = stacked.reshape(cases, width)]
  transfers between devices with their start and end apart: 24 -> 53, of which waited for: 15 -> 26; matrix products, arithmetic and copies ran while one was open for 6% -> 14% of each run, Pallas kernels for 7% -> 0%
where the time goes in v6:
time: 104 us
  starting transfers between devices  54.4 us (52%)
  waiting for transfers between devices  21.4 us (21%)
  local copies, waits for them, and re-layouts  15 us (14%)
  Pallas kernels  7.09 us (7%)
  other arithmetic  4.38 us (4%)
  between operations  1.22 us (1%)
    ppermute x53, starting transfers between devices, swap(): return lax.ppermute(value, axis, [(i, i ^ offset) for i in range(count)])  54.4 us
    ppermute x53, waiting for transfers between devices, swap(): return lax.ppermute(value, axis, [(i, i ^ offset) for i in range(count)])  21.4 us
    pallas_call x4, Pallas kernels, product(): pl.pallas_call(kernel, out_shape=[jax.ShapeDtypeStruct(shape, value) for...  7.09 us
    dynamic_update_slice x8, local copies, waits for them, and re-layouts, shards(): lax.dynamic_update_slice_in_dim(stacked, one[None], panel ^ 2 * way + sid...  5.42 us
    slice x1, local copies, waits for them, and re-layouts, shards(): held = [blocks[a:a + n] for a, n in spans(slots, HELD_PARTS)]  3.93 us
  transfers between devices with their start and end apart: 53, of which 26 were waited for; matrix products, arithmetic and copies ran while one was open for 14% of the time, Pallas kernels for 0%

profile of v6, /device:TPU:0, one launch (start us, length us, event | category | flops | bytes accessed | tf_op | source)
XLA Modules:
  0.0 103.6 jit_solution(433597243549803670)
XLA Ops:
  0.6 3.1 %collective-permute-start = (bf16[4,12288]{1,0:T(4,128)(2,1)}, bf16[4,12288]{1,0:T(4,128)(2,1)S(1)}, u32[]{:S(2)}, u32[]{:S(2)}) collective-permute-start(bf16[4,12288]{1,0:T(4,128)(2,1)} %param.5), channel_id=1, source_target_pairs={{0,8},{4,12},{8,0},{12,4},{16,24},{20,28},{24,16},{28,20},{1,9},{5... | collective-permute-start | bytes 294920 | tf_op jit(solution)/shard_map/ppermute | solution.py:21
  3.7 2.6 %collective-permute-start.1 = (bf16[4,12288]{1,0:T(4,128)(2,1)}, bf16[4,12288]{1,0:T(4,128)(2,1)S(1)}, u32[]{:S(2)}, u32[]{:S(2)}) collective-permute-start(bf16[4,12288]{1,0:T(4,128)(2,1)} %param.5), channel_id=1, source_target_pairs={{0,16},{4,20},{8,24},{12,28},{16,0},{20,4},{24,8},{28,12},{1,17},{... | collective-permute-start | bytes 294920 | tf_op jit(solution)/shard_map/ppermute | solution.py:21
  7.0 3.9 %fusion.22 = (bf16[16,256,256]{2,1,0:T(8,128)(2,1)S(1)}, bf16[16,256,256]{2,1,0:T(8,128)(2,1)}) fusion(bf16[32,256,256]{2,1,0:T(8,128)(2,1)} %param.6), kind=kLoop, calls=%fused_computation.118 | loop fusion | bytes 8388608 | tf_op jit(solution)/shard_map/slice | solution.py:161
  19.6 1.6 %reshape.52.x_ref = bf16[32,12288]{1,0:T(8,128)(2,1)S(1)} reshape(bf16[8,4,12288]{2,1,0:T(4,128)(2,1)} %bitcast_dynamic-update-slice_fusion) | data formatting | bytes 1572864 | tf_op jit(solution)/shard_map/reshape | solution.py:229
  21.2 1.6 %copy-done = bf16[16,256,256]{2,1,0:T(8,128)(2,1)S(1)} copy-done((bf16[16,256,256]{2,1,0:T(8,128)(2,1)S(1)}, bf16[16,256,256]{2,1,0:T(8,128)(2,1)}, u32[]{:S(2)}) %copy-start) | copy-done | bytes 2097176
  22.8 1.9 %shard_map.84 = (bf16[12,32,128]{2,1,0:T(8,128)(2,1)S(1)}, bf16[12,32,128]{2,1,0:T(8,128)(2,1)S(1)}, bf16[12,32,128]{2,1,0:T(8,128)(2,1)S(1)}, bf16[12,32,128]{2,1,0:T(8,128)(2,1)S(1)}) custom-call(s32[96]{0:T(128)S(1)} %reshape.51.entry_ref, f32[8]{0:T(128)S(1)} %copy-done.8, bf16[32,12288]{1,0:T(8,128)(2,1)S(1)} %reshape.52.x_ref, ...), custom_call_target="tpu_custom_call" | custom-call | flops 134217728 | bytes 4194304 | tf_op jit(solution)/shard_map/pallas_call | solution.py:172
  24.8 1.6 %collective-permute-start.13 = (bf16[12,32,128]{2,1,0:T(8,128)(2,1)S(1)}, bf16[12,32,128]{2,1,0:T(8,128)(2,1)S(1)}, u32[]{:S(2)}, u32[]{:S(2)}) collective-permute-start(bf16[12,32,128]{2,1,0:T(8,128)(2,1)S(1)} %get-tuple-element.67), channel_id=1, source_target_pairs={{0,2},{1,3},{2,0},{3,1},{4,6},{5,7},{6,4},{7,5},{8,10},{9,11},{10,... | collective-permute-start | bytes 294920 | tf_op jit(solution)/shard_map/ppermute | solution.py:21
  26.4 1.5 %collective-permute-start.11 = (bf16[12,32,128]{2,1,0:T(8,128)(2,1)S(1)}, bf16[12,32,128]{2,1,0:T(8,128)(2,1)S(1)}, u32[]{:S(2)}, u32[]{:S(2)}) collective-permute-start(bf16[12,32,128]{2,1,0:T(8,128)(2,1)S(1)} %get-tuple-element.66), channel_id=1, source_target_pairs={{0,1},{1,0},{2,3},{3,2},{4,5},{5,4},{6,7},{7,6},{8,9},{9,8},{10,11... | collective-permute-start | bytes 294920 | tf_op jit(solution)/shard_map/ppermute | solution.py:21
  29.6 2.1 %collective-permute-start.14 = (bf16[12,32,128]{2,1,0:T(8,128)(2,1)S(1)}, bf16[12,32,128]{2,1,0:T(8,128)(2,1)S(1)}, u32[]{:S(2)}, u32[]{:S(2)}) collective-permute-start(bf16[12,32,128]{2,1,0:T(8,128)(2,1)S(1)} %add_convert_fusion.11), channel_id=1, source_target_pairs={{0,1},{1,0},{2,3},{3,2},{4,5},{5,4},{6,7},{7,6},{8,9},{9,8},{10,11... | collective-permute-start | bytes 294920 | tf_op jit(solution)/shard_map/ppermute | solution.py:21
  31.9 1.8 %collective-permute-start.12 = (bf16[12,32,128]{2,1,0:T(8,128)(2,1)S(1)}, bf16[12,32,128]{2,1,0:T(8,128)(2,1)S(1)}, u32[]{:S(2)}, u32[]{:S(2)}) collective-permute-start(bf16[12,32,128]{2,1,0:T(8,128)(2,1)S(1)} %add_convert_fusion.13), channel_id=1, source_target_pairs={{0,2},{1,3},{2,0},{3,1},{4,6},{5,7},{6,4},{7,5},{8,10},{9,11},{10,... | collective-permute-start | bytes 294920 | tf_op jit(solution)/shard_map/ppermute | solution.py:21
  34.2 1.8 %collective-permute-start.8 = (bf16[12,32,128]{2,1,0:T(8,128)(2,1)S(1)}, bf16[12,32,128]{2,1,0:T(8,128)(2,1)S(1)}, u32[]{:S(2)}, u32[]{:S(2)}) collective-permute-start(bf16[12,32,128]{2,1,0:T(8,128)(2,1)S(1)} %add_convert_fusion.17), channel_id=1, source_target_pairs={{0,2},{1,3},{2,0},{3,1},{4,6},{5,7},{6,4},{7,5},{8,10},{9,11},{10,... | collective-permute-start | bytes 294920 | tf_op jit(solution)/shard_map/ppermute | solution.py:21
  38.9 1.5 %shard_map.85 = (bf16[4,6,32,128]{3,2,1,0:T(8,128)(2,1)S(1)}, bf16[4,6,32,128]{3,2,1,0:T(8,128)(2,1)S(1)}, bf16[4,6,32,128]{3,2,1,0:T(8,128)(2,1)S(1)}, bf16[4,6,32,128]{3,2,1,0:T(8,128)(2,1)S(1)}) custom-call(s32[96]{0:T(128)S(1)} %reshape.51.entry_ref, f32[8]{0:T(128)S(1)} %copy-done.8, s32[2]{0:T(128)S(1)} %pad_add_fusion.1.place_ref, ...), custom_call_target="tpu_custom_call" | custom-call | flops 134217728 | bytes 4194304 | tf_op jit(solution)/shard_map/pallas_call | solution.py:172
  43.3 2.5 %collective-permute-start.28 = (bf16[6,32,128]{2,1,0:T(8,128)(2,1)S(1)}, bf16[6,32,128]{2,1,0:T(8,128)(2,1)S(1)}, u32[]{:S(2)}, u32[]{:S(2)}) collective-permute-start(bf16[6,32,128]{2,1,0:T(8,128)(2,1)S(1)} %get-tuple-element.134), channel_id=1, source_target_pairs={{0,16},{4,20},{8,24},{12,28},{16,0},{20,4},{24,8},{28,12},{1,17},{... | collective-permute-start | bytes 147464 | tf_op jit(solution)/shard_map/ppermute | solution.py:21
  47.0 3.4 %collective-permute-start.17 = (bf16[6,32,128]{2,1,0:T(8,128)(2,1)S(1)}, bf16[6,32,128]{2,1,0:T(8,128)(2,1)S(1)}, u32[]{:S(2)}, u32[]{:S(2)}) collective-permute-start(bf16[6,32,128]{2,1,0:T(8,128)(2,1)S(1)} %get-tuple-element.137), channel_id=1, source_target_pairs={{0,16},{4,20},{8,24},{12,28},{16,0},{20,4},{24,8},{28,12},{1,17},{... | collective-permute-start | bytes 147464 | tf_op jit(solution)/shard_map/ppermute | solution.py:21
  52.0 2.8 %collective-permute-start.31 = (bf16[6,32,128]{2,1,0:T(8,128)(2,1)S(1)}, bf16[6,32,128]{2,1,0:T(8,128)(2,1)S(1)}, u32[]{:S(2)}, u32[]{:S(2)}) collective-permute-start(bf16[6,32,128]{2,1,0:T(8,128)(2,1)S(1)} %fusion.18.refs_8_.refs_18_), channel_id=1, source_target_pairs={{0,16},{4,20},{8,24},{12,28},{16,0},{20,4},{24,8},{28,12},{1,17},{... | collective-permute-start | bytes 147464 | tf_op jit(solution)/shard_map/ppermute | solution.py:21
  54.8 1.5 %collective-permute-start.32 = (bf16[6,32,128]{2,1,0:T(8,128)(2,1)S(1)}, bf16[6,32,128]{2,1,0:T(8,128)(2,1)S(1)}, u32[]{:S(2)}, u32[]{:S(2)}) collective-permute-start(bf16[6,32,128]{2,1,0:T(8,128)(2,1)S(1)} %fusion.18.refs_8_.refs_18_), channel_id=1, source_target_pairs={{0,24},{4,28},{8,16},{12,20},{16,8},{20,12},{24,0},{28,4},{1,25},{... | collective-permute-start | bytes 147464 | tf_op jit(solution)/shard_map/ppermute | solution.py:21
  56.7 2.7 %collective-permute-start.20 = (bf16[6,32,128]{2,1,0:T(8,128)(2,1)S(1)}, bf16[6,32,128]{2,1,0:T(8,128)(2,1)S(1)}, u32[]{:S(2)}, u32[]{:S(2)}) collective-permute-start(bf16[6,32,128]{2,1,0:T(8,128)(2,1)S(1)} %fusion.21.refs_0_.refs_10_), channel_id=1, source_target_pairs={{0,16},{4,20},{8,24},{12,28},{16,0},{20,4},{24,8},{28,12},{1,17},{... | collective-permute-start | bytes 147464 | tf_op jit(solution)/shard_map/ppermute | solution.py:21
  59.4 1.7 %collective-permute-start.21 = (bf16[6,32,128]{2,1,0:T(8,128)(2,1)S(1)}, bf16[6,32,128]{2,1,0:T(8,128)(2,1)S(1)}, u32[]{:S(2)}, u32[]{:S(2)}) collective-permute-start(bf16[6,32,128]{2,1,0:T(8,128)(2,1)S(1)} %fusion.21.refs_0_.refs_10_), channel_id=1, source_target_pairs={{0,24},{4,28},{8,16},{12,20},{16,8},{20,12},{24,0},{28,4},{1,25},{... | collective-permute-start | bytes 147464 | tf_op jit(solution)/shard_map/ppermute | solution.py:21
  63.3 2.0 %collective-permute-done.21.refs_3_.refs_13_ = bf16[6,32,128]{2,1,0:T(8,128)(2,1)S(1)} collective-permute-done((bf16[6,32,128]{2,1,0:T(8,128)(2,1)S(1)}, bf16[6,32,128]{2,1,0:T(8,128)(2,1)S(1)}, u32[]{:S(2)}, u32[]{:S(2)}) %collective-permute-start.21) | collective-permute-done | bytes 49184 | tf_op jit(solution)/shard_map/ppermute | solution.py:21
  67.0 2.0 %shard_map.86 = (bf16[12,32,128]{2,1,0:T(8,128)(2,1)S(1)}, bf16[12,32,128]{2,1,0:T(8,128)(2,1)S(1)}, bf16[12,32,128]{2,1,0:T(8,128)(2,1)S(1)}, bf16[12,32,128]{2,1,0:T(8,128)(2,1)S(1)}) custom-call(s32[96]{0:T(128)S(1)} %reshape.51.entry_ref, f32[8]{0:T(128)S(1)} %copy-done.8, s32[2]{0:T(128)S(1)} %pad_add_fusion.1.place_ref, ...), custom_call_target="tpu_custom_call" | custom-call | flops 134217728 | bytes 4194304 | tf_op jit(solution)/shard_map/pallas_call | solution.py:172
  69.0 1.8 %collective-permute-start.43 = (bf16[12,32,128]{2,1,0:T(8,128)(2,1)S(1)}, bf16[12,32,128]{2,1,0:T(8,128)(2,1)}, u32[]{:S(2)}, u32[]{:S(2)}) collective-permute-start(bf16[12,32,128]{2,1,0:T(8,128)(2,1)S(1)} %get-tuple-element.75), channel_id=1, source_target_pairs={{0,2},{1,3},{2,0},{3,1},{4,6},{5,7},{6,4},{7,5},{8,10},{9,11},{10,... | collective-permute-start | bytes 294920 | tf_op jit(solution)/shard_map/ppermute | solution.py:21
  71.1 1.8 %collective-permute-start.39 = (bf16[12,32,128]{2,1,0:T(8,128)(2,1)S(1)}, bf16[12,32,128]{2,1,0:T(8,128)(2,1)S(1)}, u32[]{:S(2)}, u32[]{:S(2)}) collective-permute-start(bf16[12,32,128]{2,1,0:T(8,128)(2,1)S(1)} %get-tuple-element.73), channel_id=1, source_target_pairs={{0,2},{1,3},{2,0},{3,1},{4,6},{5,7},{6,4},{7,5},{8,10},{9,11},{10,... | collective-permute-start | bytes 294920 | tf_op jit(solution)/shard_map/ppermute | solution.py:21
  75.5 1.7 %collective-permute-start.44 = (bf16[12,32,128]{2,1,0:T(8,128)(2,1)S(1)}, bf16[12,32,128]{2,1,0:T(8,128)(2,1)S(1)}, u32[]{:S(2)}, u32[]{:S(2)}) collective-permute-start(bf16[12,32,128]{2,1,0:T(8,128)(2,1)S(1)} %add_convert_fusion.3), channel_id=1, source_target_pairs={{0,1},{1,0},{2,3},{3,2},{4,5},{5,4},{6,7},{7,6},{8,9},{9,8},{10,11... | collective-permute-start | bytes 294920 | tf_op jit(solution)/shard_map/ppermute | solution.py:21
  77.6 1.9 %collective-permute-start.40 = (bf16[12,32,128]{2,1,0:T(8,128)(2,1)S(1)}, bf16[12,32,128]{2,1,0:T(8,128)(2,1)S(1)}, u32[]{:S(2)}, u32[]{:S(2)}) collective-permute-start(bf16[12,32,128]{2,1,0:T(8,128)(2,1)S(1)} %add_convert_fusion.7), channel_id=1, source_target_pairs={{0,1},{1,0},{2,3},{3,2},{4,5},{5,4},{6,7},{7,6},{8,9},{9,8},{10,11... | collective-permute-start | bytes 294920 | tf_op jit(solution)/shard_map/ppermute | solution.py:21
  80.8 1.5 %collective-permute-done.42 = bf16[12,32,128]{2,1,0:T(8,128)(2,1)S(1)} collective-permute-done((bf16[12,32,128]{2,1,0:T(8,128)(2,1)S(1)}, bf16[12,32,128]{2,1,0:T(8,128)(2,1)S(1)}, u32[]{:S(2)}, u32[]{:S(2)}) %collective-permute-start.42) | collective-permute-done | bytes 98336 | tf_op jit(solution)/shard_map/ppermute | solution.py:21
  82.4 1.9 %collective-permute-done.38 = bf16[12,32,128]{2,1,0:T(8,128)(2,1)S(1)} collective-permute-done((bf16[12,32,128]{2,1,0:T(8,128)(2,1)S(1)}, bf16[12,32,128]{2,1,0:T(8,128)(2,1)S(1)}, u32[]{:S(2)}, u32[]{:S(2)}) %collective-permute-start.38) | collective-permute-done | bytes 98336 | tf_op jit(solution)/shard_map/ppermute | solution.py:21
  84.4 1.7 %shard_map.87 = (bf16[2,4,4,6144]{3,2,1,0:T(4,128)(2,1)S(1)}, bf16[2,4,4,6144]{3,2,1,0:T(4,128)(2,1)S(1)}, bf16[12,32,128]{2,1,0:T(8,128)(2,1)S(1)}, bf16[12,32,...) custom-call(s32[96]{0:T(128)S(1)} %reshape.51.entry_ref, ...), custom_call_target="tpu_custom_call", output_to_operand_aliasing={{2}: (9, {}), {3}: (10, {}), {4}: (11, {}), {5}: (12, {}), ... | custom-call | flops 134217728 | bytes 4194304 | tf_op jit(solution)/shard_map/pallas_call | solution.py:172
  88.2 2.3 %collective-permute-start.48 = (bf16[4,6144]{1,0:T(4,128)(2,1)S(1)}, bf16[4,6144]{1,0:T(4,128)(2,1)S(1)}, u32[]{:S(2)}, u32[]{:S(2)}) collective-permute-start(bf16[4,6144]{1,0:T(4,128)(2,1)S(1)} %get-tuple-element.128), channel_id=1, source_target_pairs={{0,16},{4,20},{8,24},{12,28},{16,0},{20,4},{24,8},{28,12},{1,17},{... | collective-permute-start | bytes 147464 | tf_op jit(solution)/shard_map/ppermute | solution.py:21
  90.4 2.1 %collective-permute-start.49 = (bf16[4,6144]{1,0:T(4,128)(2,1)S(1)}, bf16[4,6144]{1,0:T(4,128)(2,1)S(1)}, u32[]{:S(2)}, u32[]{:S(2)}) collective-permute-start(bf16[4,6144]{1,0:T(4,128)(2,1)S(1)} %get-tuple-element.127), channel_id=1, source_target_pairs={{0,24},{4,28},{8,16},{12,20},{16,8},{20,12},{24,0},{28,4},{1,25},{... | collective-permute-start | bytes 147464 | tf_op jit(solution)/shard_map/ppermute | solution.py:21
  92.7 2.2 %collective-permute-start.51 = (bf16[4,6144]{1,0:T(4,128)(2,1)S(1)}, bf16[4,6144]{1,0:T(4,128)(2,1)S(1)}, u32[]{:S(2)}, u32[]{:S(2)}) collective-permute-start(bf16[4,6144]{1,0:T(4,128)(2,1)S(1)} %get-tuple-element.131), channel_id=1, source_target_pairs={{0,16},{4,20},{8,24},{12,28},{16,0},{20,4},{24,8},{28,12},{1,17},{... | collective-permute-start | bytes 147464 | tf_op jit(solution)/shard_map/ppermute | solution.py:21
  96.9 2.1 %collective-permute-start.52 = (bf16[4,6144]{1,0:T(4,128)(2,1)S(1)}, bf16[4,6144]{1,0:T(4,128)(2,1)S(1)}, u32[]{:S(2)}, u32[]{:S(2)}) collective-permute-start(bf16[4,6144]{1,0:T(4,128)(2,1)S(1)} %get-tuple-element.130), channel_id=1, source_target_pairs={{0,24},{4,28},{8,16},{12,20},{16,8},{20,12},{24,0},{28,4},{1,25},{... | collective-permute-start | bytes 147464 | tf_op jit(solution)/shard_map/ppermute | solution.py:21
  99.1 3.7 %collective-permute-done.52 = bf16[4,6144]{1,0:T(4,128)(2,1)S(1)} collective-permute-done((bf16[4,6144]{1,0:T(4,128)(2,1)S(1)}, bf16[4,6144]{1,0:T(4,128)(2,1)S(1)}, u32[]{:S(2)}, u32[]{:S(2)}) %collective-permute-start.52) | collective-permute-done | bytes 49184 | tf_op jit(solution)/shard_map/ppermute | solution.py:21
  (174 shorter events, 34.0 us)
Async XLA Ops:
  0.6 12.5 %collective-permute-start = (bf16[4,12288]{1,0:T(4,128)(2,1)}, bf16[4,12288]{1,0:T(4,128)(2,1)S(1)}, u32[]{:S(2)}, u32[]{:S(2)}) collective-permute-start(bf16[4,12288]{1,0:T(4,128)(2,1)} %param.5), channel_id=1, source_target_pairs={{0,8},{4,12},{8,0},{12,4},{16,24},{20,28},{24,16},{28,20},{1,9},{5... | collective-permute-start | bytes 294920 | tf_op jit(solution)/shard_map/ppermute | solution.py:21
  3.7 10.6 %collective-permute-start.1 = (bf16[4,12288]{1,0:T(4,128)(2,1)}, bf16[4,12288]{1,0:T(4,128)(2,1)S(1)}, u32[]{:S(2)}, u32[]{:S(2)}) collective-permute-start(bf16[4,12288]{1,0:T(4,128)(2,1)} %param.5), channel_id=1, source_target_pairs={{0,16},{4,20},{8,24},{12,28},{16,0},{20,4},{24,8},{28,12},{1,17},{... | collective-permute-start | bytes 294920 | tf_op jit(solution)/shard_map/ppermute | solution.py:21
  6.3 8.1 %collective-permute-start.2 = (bf16[4,12288]{1,0:T(4,128)(2,1)}, bf16[4,12288]{1,0:T(4,128)(2,1)S(1)}, u32[]{:S(2)}, u32[]{:S(2)}) collective-permute-start(bf16[4,12288]{1,0:T(4,128)(2,1)} %param.5), channel_id=1, source_target_pairs={{0,24},{4,28},{8,16},{12,20},{16,8},{20,12},{24,0},{28,4},{1,25},{... | collective-permute-start | bytes 294920 | tf_op jit(solution)/shard_map/ppermute | solution.py:21
  6.3 10.6 %collective-permute-start.3 = (bf16[4,12288]{1,0:T(4,128)(2,1)}, bf16[4,12288]{1,0:T(4,128)(2,1)S(1)}, u32[]{:S(2)}, u32[]{:S(2)}) collective-permute-start(bf16[4,12288]{1,0:T(4,128)(2,1)} %param.5), channel_id=1, source_target_pairs={{0,4},{4,0},{8,12},{12,8},{16,20},{20,16},{24,28},{28,24},{1,5},{5... | collective-permute-start | bytes 294920 | tf_op jit(solution)/shard_map/ppermute | solution.py:21
  26.4 5.5 %collective-permute-start.11 = (bf16[12,32,128]{2,1,0:T(8,128)(2,1)S(1)}, bf16[12,32,128]{2,1,0:T(8,128)(2,1)S(1)}, u32[]{:S(2)}, u32[]{:S(2)}) collective-permute-start(bf16[12,32,128]{2,1,0:T(8,128)(2,1)S(1)} %get-tuple-element.66), channel_id=1, source_target_pairs={{0,1},{1,0},{2,3},{3,2},{4,5},{5,4},{6,7},{7,6},{8,9},{9,8},{10,11... | collective-permute-start | bytes 294920 | tf_op jit(solution)/shard_map/ppermute | solution.py:21
  27.9 5.8 %collective-permute-start.9 = (bf16[12,32,128]{2,1,0:T(8,128)(2,1)S(1)}, bf16[12,32,128]{2,1,0:T(8,128)(2,1)S(1)}, u32[]{:S(2)}, u32[]{:S(2)}) collective-permute-start(bf16[12,32,128]{2,1,0:T(8,128)(2,1)S(1)} %get-tuple-element.65), channel_id=1, source_target_pairs={{0,2},{1,3},{2,0},{3,1},{4,6},{5,7},{6,4},{7,5},{8,10},{9,11},{10,... | collective-permute-start | bytes 294920 | tf_op jit(solution)/shard_map/ppermute | solution.py:21
  28.4 5.7 %collective-permute-start.7 = (bf16[12,32,128]{2,1,0:T(8,128)(2,1)S(1)}, bf16[12,32,128]{2,1,0:T(8,128)(2,1)S(1)}, u32[]{:S(2)}, u32[]{:S(2)}) collective-permute-start(bf16[12,32,128]{2,1,0:T(8,128)(2,1)S(1)} %get-tuple-element.64), channel_id=1, source_target_pairs={{0,1},{1,0},{2,3},{3,2},{4,5},{5,4},{6,7},{7,6},{8,9},{9,8},{10,11... | collective-permute-start | bytes 294920 | tf_op jit(solution)/shard_map/ppermute | solution.py:21
  29.6 6.7 %collective-permute-start.14 = (bf16[12,32,128]{2,1,0:T(8,128)(2,1)S(1)}, bf16[12,32,128]{2,1,0:T(8,128)(2,1)S(1)}, u32[]{:S(2)}, u32[]{:S(2)}) collective-permute-start(bf16[12,32,128]{2,1,0:T(8,128)(2,1)S(1)} %add_convert_fusion.11), channel_id=1, source_target_pairs={{0,1},{1,0},{2,3},{3,2},{4,5},{5,4},{6,7},{7,6},{8,9},{9,8},{10,11... | collective-permute-start | bytes 294920 | tf_op jit(solution)/shard_map/ppermute | solution.py:21
  31.9 5.1 %collective-permute-start.12 = (bf16[12,32,128]{2,1,0:T(8,128)(2,1)S(1)}, bf16[12,32,128]{2,1,0:T(8,128)(2,1)S(1)}, u32[]{:S(2)}, u32[]{:S(2)}) collective-permute-start(bf16[12,32,128]{2,1,0:T(8,128)(2,1)S(1)} %add_convert_fusion.13), channel_id=1, source_target_pairs={{0,2},{1,3},{2,0},{3,1},{4,6},{5,7},{6,4},{7,5},{8,10},{9,11},{10,... | collective-permute-start | bytes 294920 | tf_op jit(solution)/shard_map/ppermute | solution.py:21
  40.5 6.0 %collective-permute-start.15 = (bf16[4,6,32,128]{3,2,1,0:T(8,128)(2,1)S(1)}, bf16[4,6,32,128]{3,2,1,0:T(8,128)(2,1)S(1)}, u32[]{:S(2)}, u32[]{:S(2)}) collective-permute-start(bf16[4,6,32,128]{3,2,1,0:T(8,128)(2,1)S(1)} %get-tuple-element.69), channel_id=1, source_target_pairs={{0,4},{4,0},{8,12},{12,8},{16,20},{20,16},{24,28},{28,24},{1,5},{5... | collective-permute-start | bytes 589832 | tf_op jit(solution)/shard_map/ppermute | solution.py:21
  42.0 8.4 %collective-permute-start.27 = (bf16[6,32,128]{2,1,0:T(8,128)(2,1)S(1)}, bf16[6,32,128]{2,1,0:T(8,128)(2,1)S(1)}, u32[]{:S(2)}, u32[]{:S(2)}) collective-permute-start(bf16[6,32,128]{2,1,0:T(8,128)(2,1)S(1)} %get-tuple-element.132), channel_id=1, source_target_pairs={{0,8},{4,12},{8,0},{12,4},{16,24},{20,28},{24,16},{28,20},{1,9},{5... | collective-permute-start | bytes 147464 | tf_op jit(solution)/shard_map/ppermute | solution.py:21
  43.3 7.7 %collective-permute-start.28 = (bf16[6,32,128]{2,1,0:T(8,128)(2,1)S(1)}, bf16[6,32,128]{2,1,0:T(8,128)(2,1)S(1)}, u32[]{:S(2)}, u32[]{:S(2)}) collective-permute-start(bf16[6,32,128]{2,1,0:T(8,128)(2,1)S(1)} %get-tuple-element.134), channel_id=1, source_target_pairs={{0,16},{4,20},{8,24},{12,28},{16,0},{20,4},{24,8},{28,12},{1,17},{... | collective-permute-start | bytes 147464 | tf_op jit(solution)/shard_map/ppermute | solution.py:21
  45.8 6.1 %collective-permute-start.29 = (bf16[6,32,128]{2,1,0:T(8,128)(2,1)S(1)}, bf16[6,32,128]{2,1,0:T(8,128)(2,1)S(1)}, u32[]{:S(2)}, u32[]{:S(2)}) collective-permute-start(bf16[6,32,128]{2,1,0:T(8,128)(2,1)S(1)} %get-tuple-element.133), channel_id=1, source_target_pairs={{0,24},{4,28},{8,16},{12,20},{16,8},{20,12},{24,0},{28,4},{1,25},{... | collective-permute-start | bytes 147464 | tf_op jit(solution)/shard_map/ppermute | solution.py:21
  46.5 8.3 %collective-permute-start.16 = (bf16[6,32,128]{2,1,0:T(8,128)(2,1)S(1)}, bf16[6,32,128]{2,1,0:T(8,128)(2,1)S(1)}, u32[]{:S(2)}, u32[]{:S(2)}) collective-permute-start(bf16[6,32,128]{2,1,0:T(8,128)(2,1)S(1)} %get-tuple-element.135), channel_id=1, source_target_pairs={{0,8},{4,12},{8,0},{12,4},{16,24},{20,28},{24,16},{28,20},{1,9},{5... | collective-permute-start | bytes 147464 | tf_op jit(solution)/shard_map/ppermute | solution.py:21
  47.0 9.4 %collective-permute-start.17 = (bf16[6,32,128]{2,1,0:T(8,128)(2,1)S(1)}, bf16[6,32,128]{2,1,0:T(8,128)(2,1)S(1)}, u32[]{:S(2)}, u32[]{:S(2)}) collective-permute-start(bf16[6,32,128]{2,1,0:T(8,128)(2,1)S(1)} %get-tuple-element.137), channel_id=1, source_target_pairs={{0,16},{4,20},{8,24},{12,28},{16,0},{20,4},{24,8},{28,12},{1,17},{... | collective-permute-start | bytes 147464 | tf_op jit(solution)/shard_map/ppermute | solution.py:21
  50.3 6.0 %collective-permute-start.18 = (bf16[6,32,128]{2,1,0:T(8,128)(2,1)S(1)}, bf16[6,32,128]{2,1,0:T(8,128)(2,1)S(1)}, u32[]{:S(2)}, u32[]{:S(2)}) collective-permute-start(bf16[6,32,128]{2,1,0:T(8,128)(2,1)S(1)} %get-tuple-element.136), channel_id=1, source_target_pairs={{0,24},{4,28},{8,16},{12,20},{16,8},{20,12},{24,0},{28,4},{1,25},{... | collective-permute-start | bytes 147464 | tf_op jit(solution)/shard_map/ppermute | solution.py:21
  52.0 7.4 %collective-permute-start.31 = (bf16[6,32,128]{2,1,0:T(8,128)(2,1)S(1)}, bf16[6,32,128]{2,1,0:T(8,128)(2,1)S(1)}, u32[]{:S(2)}, u32[]{:S(2)}) collective-permute-start(bf16[6,32,128]{2,1,0:T(8,128)(2,1)S(1)} %fusion.18.refs_8_.refs_18_), channel_id=1, source_target_pairs={{0,16},{4,20},{8,24},{12,28},{16,0},{20,4},{24,8},{28,12},{1,17},{... | collective-permute-start | bytes 147464 | tf_op jit(solution)/shard_map/ppermute | solution.py:21
  54.8 6.4 %collective-permute-start.32 = (bf16[6,32,128]{2,1,0:T(8,128)(2,1)S(1)}, bf16[6,32,128]{2,1,0:T(8,128)(2,1)S(1)}, u32[]{:S(2)}, u32[]{:S(2)}) collective-permute-start(bf16[6,32,128]{2,1,0:T(8,128)(2,1)S(1)} %fusion.18.refs_8_.refs_18_), channel_id=1, source_target_pairs={{0,24},{4,28},{8,16},{12,20},{16,8},{20,12},{24,0},{28,4},{1,25},{... | collective-permute-start | bytes 147464 | tf_op jit(solution)/shard_map/ppermute | solution.py:21
  56.4 5.6 %collective-permute-start.19 = (bf16[6,32,128]{2,1,0:T(8,128)(2,1)S(1)}, bf16[6,32,128]{2,1,0:T(8,128)(2,1)S(1)}, u32[]{:S(2)}, u32[]{:S(2)}) collective-permute-start(bf16[6,32,128]{2,1,0:T(8,128)(2,1)S(1)} %fusion.21.refs_0_.refs_10_), channel_id=1, source_target_pairs={{0,8},{4,12},{8,0},{12,4},{16,24},{20,28},{24,16},{28,20},{1,9},{5... | collective-permute-start | bytes 147464 | tf_op jit(solution)/shard_map/ppermute | solution.py:21
  56.7 6.6 %collective-permute-start.20 = (bf16[6,32,128]{2,1,0:T(8,128)(2,1)S(1)}, bf16[6,32,128]{2,1,0:T(8,128)(2,1)S(1)}, u32[]{:S(2)}, u32[]{:S(2)}) collective-permute-start(bf16[6,32,128]{2,1,0:T(8,128)(2,1)S(1)} %fusion.21.refs_0_.refs_10_), channel_id=1, source_target_pairs={{0,16},{4,20},{8,24},{12,28},{16,0},{20,4},{24,8},{28,12},{1,17},{... | collective-permute-start | bytes 147464 | tf_op jit(solution)/shard_map/ppermute | solution.py:21
  59.4 5.9 %collective-permute-start.21 = (bf16[6,32,128]{2,1,0:T(8,128)(2,1)S(1)}, bf16[6,32,128]{2,1,0:T(8,128)(2,1)S(1)}, u32[]{:S(2)}, u32[]{:S(2)}) collective-permute-start(bf16[6,32,128]{2,1,0:T(8,128)(2,1)S(1)} %fusion.21.refs_0_.refs_10_), channel_id=1, source_target_pairs={{0,24},{4,28},{8,16},{12,20},{16,8},{20,12},{24,0},{28,4},{1,25},{... | collective-permute-start | bytes 147464 | tf_op jit(solution)/shard_map/ppermute | solution.py:21
  69.0 5.6 %collective-permute-start.43 = (bf16[12,32,128]{2,1,0:T(8,128)(2,1)S(1)}, bf16[12,32,128]{2,1,0:T(8,128)(2,1)}, u32[]{:S(2)}, u32[]{:S(2)}) collective-permute-start(bf16[12,32,128]{2,1,0:T(8,128)(2,1)S(1)} %get-tuple-element.75), channel_id=1, source_target_pairs={{0,2},{1,3},{2,0},{3,1},{4,6},{5,7},{6,4},{7,5},{8,10},{9,11},{10,... | collective-permute-start | bytes 294920 | tf_op jit(solution)/shard_map/ppermute | solution.py:21
  70.8 6.5 %collective-permute-start.41 = (bf16[12,32,128]{2,1,0:T(8,128)(2,1)S(1)}, bf16[12,32,128]{2,1,0:T(8,128)(2,1)S(1)}, u32[]{:S(2)}, u32[]{:S(2)}) collective-permute-start(bf16[12,32,128]{2,1,0:T(8,128)(2,1)S(1)} %get-tuple-element.74), channel_id=1, source_target_pairs={{0,1},{1,0},{2,3},{3,2},{4,5},{5,4},{6,7},{7,6},{8,9},{9,8},{10,11... | collective-permute-start | bytes 294920 | tf_op jit(solution)/shard_map/ppermute | solution.py:21
  71.1 6.5 %collective-permute-start.39 = (bf16[12,32,128]{2,1,0:T(8,128)(2,1)S(1)}, bf16[12,32,128]{2,1,0:T(8,128)(2,1)S(1)}, u32[]{:S(2)}, u32[]{:S(2)}) collective-permute-start(bf16[12,32,128]{2,1,0:T(8,128)(2,1)S(1)} %get-tuple-element.73), channel_id=1, source_target_pairs={{0,2},{1,3},{2,0},{3,1},{4,6},{5,7},{6,4},{7,5},{8,10},{9,11},{10,... | collective-permute-start | bytes 294920 | tf_op jit(solution)/shard_map/ppermute | solution.py:21
  72.8 6.7 %collective-permute-start.37 = (bf16[12,32,128]{2,1,0:T(8,128)(2,1)S(1)}, bf16[12,32,128]{2,1,0:T(8,128)(2,1)S(1)}, u32[]{:S(2)}, u32[]{:S(2)}) collective-permute-start(bf16[12,32,128]{2,1,0:T(8,128)(2,1)S(1)} %get-tuple-element.72), channel_id=1, source_target_pairs={{0,1},{1,0},{2,3},{3,2},{4,5},{5,4},{6,7},{7,6},{8,9},{9,8},{10,11... | collective-permute-start | bytes 294920 | tf_op jit(solution)/shard_map/ppermute | solution.py:21
  75.5 5.2 %collective-permute-start.44 = (bf16[12,32,128]{2,1,0:T(8,128)(2,1)S(1)}, bf16[12,32,128]{2,1,0:T(8,128)(2,1)S(1)}, u32[]{:S(2)}, u32[]{:S(2)}) collective-permute-start(bf16[12,32,128]{2,1,0:T(8,128)(2,1)S(1)} %add_convert_fusion.3), channel_id=1, source_target_pairs={{0,1},{1,0},{2,3},{3,2},{4,5},{5,4},{6,7},{7,6},{8,9},{9,8},{10,11... | collective-permute-start | bytes 294920 | tf_op jit(solution)/shard_map/ppermute | solution.py:21
  88.1 8.8 %collective-permute-start.47 = (bf16[4,6144]{1,0:T(4,128)(2,1)S(1)}, bf16[4,6144]{1,0:T(4,128)(2,1)S(1)}, u32[]{:S(2)}, u32[]{:S(2)}) collective-permute-start(bf16[4,6144]{1,0:T(4,128)(2,1)S(1)} %get-tuple-element.126), channel_id=1, source_target_pairs={{0,8},{4,12},{8,0},{12,4},{16,24},{20,28},{24,16},{28,20},{1,9},{5... | collective-permute-start | bytes 147464 | tf_op jit(solution)/shard_map/ppermute | solution.py:21
  88.2 10.9 %collective-permute-start.48 = (bf16[4,6144]{1,0:T(4,128)(2,1)S(1)}, bf16[4,6144]{1,0:T(4,128)(2,1)S(1)}, u32[]{:S(2)}, u32[]{:S(2)}) collective-permute-start(bf16[4,6144]{1,0:T(4,128)(2,1)S(1)} %get-tuple-element.128), channel_id=1, source_target_pairs={{0,16},{4,20},{8,24},{12,28},{16,0},{20,4},{24,8},{28,12},{1,17},{... | collective-permute-start | bytes 147464 | tf_op jit(solution)/shard_map/ppermute | solution.py:21
  90.4 8.6 %collective-permute-start.49 = (bf16[4,6144]{1,0:T(4,128)(2,1)S(1)}, bf16[4,6144]{1,0:T(4,128)(2,1)S(1)}, u32[]{:S(2)}, u32[]{:S(2)}) collective-permute-start(bf16[4,6144]{1,0:T(4,128)(2,1)S(1)} %get-tuple-element.127), channel_id=1, source_target_pairs={{0,24},{4,28},{8,16},{12,20},{16,8},{20,12},{24,0},{28,4},{1,25},{... | collective-permute-start | bytes 147464 | tf_op jit(solution)/shard_map/ppermute | solution.py:21
  92.6 6.5 %collective-permute-start.50 = (bf16[4,6144]{1,0:T(4,128)(2,1)S(1)}, bf16[4,6144]{1,0:T(4,128)(2,1)S(1)}, u32[]{:S(2)}, u32[]{:S(2)}) collective-permute-start(bf16[4,6144]{1,0:T(4,128)(2,1)S(1)} %get-tuple-element.129), channel_id=1, source_target_pairs={{0,8},{4,12},{8,0},{12,4},{16,24},{20,28},{24,16},{28,20},{1,9},{5... | collective-permute-start | bytes 147464 | tf_op jit(solution)/shard_map/ppermute | solution.py:21
  92.7 6.4 %collective-permute-start.51 = (bf16[4,6144]{1,0:T(4,128)(2,1)S(1)}, bf16[4,6144]{1,0:T(4,128)(2,1)S(1)}, u32[]{:S(2)}, u32[]{:S(2)}) collective-permute-start(bf16[4,6144]{1,0:T(4,128)(2,1)S(1)} %get-tuple-element.131), channel_id=1, source_target_pairs={{0,16},{4,20},{8,24},{12,28},{16,0},{20,4},{24,8},{28,12},{1,17},{... | collective-permute-start | bytes 147464 | tf_op jit(solution)/shard_map/ppermute | solution.py:21
  96.9 5.9 %collective-permute-start.52 = (bf16[4,6144]{1,0:T(4,128)(2,1)S(1)}, bf16[4,6144]{1,0:T(4,128)(2,1)S(1)}, u32[]{:S(2)}, u32[]{:S(2)}) collective-permute-start(bf16[4,6144]{1,0:T(4,128)(2,1)S(1)} %get-tuple-element.130), channel_id=1, source_target_pairs={{0,24},{4,28},{8,16},{12,20},{16,8},{20,12},{24,0},{28,4},{1,25},{... | collective-permute-start | bytes 147464 | tf_op jit(solution)/shard_map/ppermute | solution.py:21
  (33 other events, 164.0 us)

commit v7 on v5

v7 whole, which is shorter than its diff:
```python
import functools

import jax
import jax.numpy as jnp
from jax import lax
from jax.experimental import pallas as pl
from jax.experimental.pallas import tpu as pltpu
from jax.sharding import PartitionSpec as P

B = 256
LANES = 128
PER = B // LANES
VMEM_LIMIT = 12 * 1024 * 1024
CHUNK = 1536


def swap(value, axis, offset, only=None):
    count = lax.axis_size(axis)
    pairs = [(i, i ^ offset) for i in range(count) if only is None or i % 2 == only]
    return lax.ppermute(value, axis, pairs)


def add_up(*parts):
    total = parts[0].astype(jnp.float32)
    for part in parts[1:]:
        total = total + part.astype(jnp.float32)
    return total.astype(parts[0].dtype)


def add_products(entry_ref, gain_ref, load, block_refs, add, adjoint):
    at = 0
    for block_ref in block_refs:
        for slot in range(block_ref.shape[0]):
            row, col, level = entry_ref[at], entry_ref[at + 1], entry_ref[at + 2]
            at += 3
            scale = jnp.where(level >= 0, gain_ref[jnp.maximum(level, 0)], jnp.float32(0.0))
            source, target = (row, col) if adjoint else (col, row)
            term = lax.dot_general(
                load(source),
                block_ref[slot],
                (((1,), (0 if adjoint else 1,)), ((), ())),
                preferred_element_type=jnp.float32,
            )
            term = term * scale
            for piece in range(PER):
                add[target * PER + piece] += term[:, piece * LANES : (piece + 1) * LANES]


def load_from(x):
    def load(block):
        return jnp.concatenate([x[block * PER + piece] for piece in range(PER)], axis=1)

    return load


def gate_kernel(value_ref, after_ref, out_ref):
    out_ref[...] = value_ref[...]


def add_forward(own_entry, other_entry, gain_ref, load, block_refs, outs, totals):
    for total in totals:
        total[...] = jnp.zeros_like(total)
    add_products(own_entry, gain_ref, load, block_refs[:2], totals[0], False)
    add_products(other_entry, gain_ref, load, block_refs[2:], totals[1], False)
    for out_ref, total in zip(outs, totals):
        out_ref[...] = total[...].astype(out_ref.dtype)


def first_kernel(ways, own_entry, other_entry, gain_ref, place_ref, mine_ref, *refs):
    early, late = refs[: ways - 1], refs[ways - 1 : 2 * ways - 2]
    *block_refs, own_out, other_out, own_total, other_total, wide, x = refs[2 * ways - 2 :]
    along, is_even = place_ref[0], place_ref[1] == 0
    share, width = mine_ref.shape
    for start in range(0, width, CHUNK):
        lanes = slice(start, min(start + CHUNK, width))
        rows = [mine_ref[:, lanes].astype(jnp.float32)]
        for a, b in zip(early, late):
            rows.append(jnp.where(is_even, a[:, lanes].astype(jnp.float32), b[:, lanes].astype(jnp.float32)))
        bit = 1
        while bit < ways:
            flip = (along & bit) != 0
            rows = [jnp.where(flip, rows[i ^ bit], rows[i]) for i in range(ways)]
            bit *= 2
        for i, row in enumerate(rows):
            wide[i * share : (i + 1) * share, lanes] = row
        x[:, lanes] = wide[:, lanes].astype(x.dtype)

    def load(block):
        return x[:, pl.ds(pl.multiple_of(block * B, B), B)]

    outs, totals = (own_out, other_out), (own_total, other_total)
    add_forward(own_entry, other_entry, gain_ref, load, block_refs, outs, totals)


def forward_kernel(ways, own_entry, other_entry, gain_ref, place_ref, *refs):
    pieces = refs[:ways]
    *block_refs, own_out, other_out, own_total, other_total, x = refs[ways:]
    along = place_ref[0]
    size = pieces[0].shape[0]
    for way in range(ways):
        x[pl.ds((along ^ way) * size, size)] = pieces[way][...]
    outs, totals = (own_out, other_out), (own_total, other_total)
    add_forward(own_entry, other_entry, gain_ref, load_from(x), block_refs, outs, totals)


def add_adjoint(entry_refs, gain_ref, own_x, other_x, block_refs, total):
    total[...] = jnp.zeros_like(total)
    add_products(entry_refs[0], gain_ref, load_from(own_x), block_refs[:2], total, True)
    add_products(entry_refs[1], gain_ref, load_from(other_x), block_refs[2:], total, True)


def adjoint_kernel(ways, own_entry, other_entry, gain_ref, place_ref, own_x, other_x, *refs):
    block_refs, total = refs[: -ways - 1], refs[-1]
    outs = refs[-ways - 1 : -1]
    add_adjoint((own_entry, other_entry), gain_ref, own_x, other_x, block_refs, total)
    along = place_ref[0]
    size = outs[0].shape[0]
    for way in range(ways):
        outs[way][...] = total[pl.ds((along ^ way) * size, size)].astype(outs[way].dtype)


def last_kernel(ways, own_entry, other_entry, gain_ref, place_ref, own_x, other_x, *refs):
    block_refs, total = refs[:3], refs[-1]
    out_ref = refs[3 + (len(refs) - 5) // 2]
    add_adjoint((own_entry, other_entry), gain_ref, own_x, other_x, block_refs, total)
    along = place_ref[0]
    share = out_ref.shape[1]
    for group in range(total.shape[0]):
        values = total[group].astype(out_ref.dtype)
        for index in range(ways):
            out_ref[along ^ index, :, group * LANES : (group + 1) * LANES] = values[index * share : (index + 1) * share]


def shards(strengths, blocks, pattern, level_gain):
    n_panel = lax.axis_size("panel")
    n_case = lax.axis_size("case")
    ways = n_panel // 2
    share, width = strengths.shape
    held_cases = share * ways
    slots = blocks.shape[0]
    col_blocks = width // B
    row_blocks = col_blocks * n_case // n_panel
    col_groups = col_blocks * PER
    row_groups = row_blocks * PER
    part_size = col_groups // ways
    panel = lax.axis_index("panel")
    case = lax.axis_index("case")
    core = panel % 2
    along = panel // 2
    value = strengths.dtype

    smem = pl.BlockSpec(memory_space=pltpu.SMEM)
    vmem = pl.BlockSpec(memory_space=pltpu.VMEM)
    anywhere = pl.BlockSpec(memory_space=pl.ANY)
    params = pltpu.CompilerParams(vmem_limit_bytes=VMEM_LIMIT)

    def like(shape):
        return jax.ShapeDtypeStruct(shape, value)

    place = jnp.stack([along, core]).astype(jnp.int32)
    first = jnp.stack([panel * row_blocks, case * col_blocks, 0]).astype(jnp.int32)
    own_entry = jnp.where(pattern[:, 2:3] < 0, jnp.array([0, 0, -1], jnp.int32), pattern - first).reshape(-1)
    early = [swap(strengths, "panel", 2 * way, 0) for way in range(1, ways)]
    other_entry = swap(own_entry, "panel", 1)
    other_blocks = swap(lax.optimization_barrier((blocks, other_entry))[0], "panel", 1)
    later_strengths = pl.pallas_call(
        gate_kernel,
        out_shape=like(strengths.shape),
        in_specs=[vmem, anywhere],
        out_specs=vmem,
        compiler_params=params,
    )(strengths, other_entry)
    late = [swap(later_strengths, "panel", 2 * way, 1) for way in range(1, ways)]
    later_blocks = lax.optimization_barrier((blocks, later_strengths))[0]
    own_blocks = [later_blocks[: slots // 2], later_blocks[slots // 2 :]]

    def product(kernel, vectors, outs, scratch, kept=()):
        small = (own_entry, other_entry, level_gain, place)
        parts = (*own_blocks, other_blocks)
        before = len(small) + len(vectors) + len(parts)
        return pl.pallas_call(
            functools.partial(kernel, ways),
            out_shape=[like(shape) for shape in outs] + [like(one.shape) for one in kept],
            in_specs=[smem] * len(small) + [vmem] * (len(vectors) + len(parts)) + [anywhere] * len(kept),
            out_specs=[vmem] * len(outs) + [anywhere] * len(kept),
            scratch_shapes=scratch,
            input_output_aliases={before + i: len(outs) + i for i in range(len(kept))},
            compiler_params=params,
            cost_estimate=pl.CostEstimate(
                flops=4 * held_cases * slots * B * B, bytes_accessed=4 * slots * B * B, transcendentals=0
            ),
        )(*small, *vectors, *parts, *kept)

    rows_total = pltpu.VMEM((row_groups, held_cases, LANES), jnp.float32)
    cols_total = pltpu.VMEM((col_groups, held_cases, LANES), jnp.float32)
    cols_held = pltpu.VMEM((col_groups, held_cases, LANES), value)
    rows_shape = (row_groups, held_cases, LANES)

    def over_case(own, other):
        bits = [1 << b for b in range(n_case.bit_length() - 1)]
        for one, two in zip(bits, reversed(bits)):
            own_in, other_in = swap(own, "case", one), swap(other, "case", two)
            own, other = add_up(own, own_in), add_up(other, other_in)
        return own, other

    def scatter_along(parts):
        return add_up(parts[0], *[swap(parts[way], "panel", 2 * way) for way in range(1, ways)])

    def gather_along(part):
        return [part] + [swap(part, "panel", 2 * way) for way in range(1, ways)]

    def own_rows(own, other):
        count = held_cases // n_case
        mine = lax.dynamic_slice_in_dim(own, case * count, count, 1)
        theirs = swap(lax.dynamic_slice_in_dim(other, case * count, count, 1), "panel", 1)
        both = jnp.stack([jnp.where(core == 0, mine, theirs), jnp.where(core == 0, theirs, mine)])
        both = both.reshape(2, row_groups, count // share, share, LANES)
        return jnp.transpose(both, (2, 0, 3, 1, 4)).reshape(2 * count, row_groups * LANES)

    def own_share(pieces):
        own = jnp.stack([lax.dynamic_slice_in_dim(one, along * share, share, 1) for one in pieces])
        bit = 1
        while bit < ways:
            flipped = own.reshape(ways // (2 * bit), 2, bit, part_size, share, LANES)[:, ::-1].reshape(own.shape)
            own = jnp.where(along & bit != 0, flipped, own)
            bit *= 2
        return jnp.moveaxis(own, 2, 0).reshape(share, width)

    flat = [pltpu.VMEM((held_cases, width), kind) for kind in (jnp.float32, value)]
    sums = product(first_kernel, [strengths, *early, *late], [rows_shape] * 2, [rows_total] * 2 + flat)
    first_sums = over_case(*sums)

    parts = product(adjoint_kernel, first_sums, [(part_size, held_cases, LANES)] * ways, [cols_total])
    pieces = gather_along(scatter_along(parts))

    sums = product(forward_kernel, pieces, [rows_shape] * 2, [rows_total] * 2 + [cols_held])
    second_sums = over_case(*sums)
    kept = [*first_sums, *pieces]
    by_share, *kept = product(last_kernel, second_sums, [(ways, share, width)], [cols_total], kept)
    adjoint_two = scatter_along(by_share)
    forward_one = own_rows(*kept[:2])
    forward_two = own_rows(*second_sums)
    adjoint_one = own_share(kept[2:])
    return (forward_one, adjoint_one, forward_two, adjoint_two)


def solution(mesh):
    in_specs = (
        P("panel", "case"),
        P(("panel", "case"), None, None),
        P(("panel", "case"), None),
        P(),
    )
    out_specs = (P("case", "panel"), P("panel", "case"), P("case", "panel"), P("panel", "case"))
    return jax.shard_map(shards, mesh=mesh, in_specs=in_specs, out_specs=out_specs, check_vma=False)
```

time: 105 us -> 102 us (0.971)
  waiting for transfers between devices: 28.9 us -> 37.2 us
  starting transfers between devices: 44 us -> 37.4 us
  local copies, waits for them, and re-layouts: 8.49 us -> 5.39 us
  Pallas kernels: 18.6 us -> 16.5 us
  other arithmetic: 2.84 us -> 4.09 us
    ppermute x28 -> x27, waiting for transfers between devices: 28.9 us -> 37.2 us  [swap(): return lax.ppermute(value, axis, pairs)]
    ppermute x28 -> x27, starting transfers between devices: 44 us -> 37.4 us  [swap(): return lax.ppermute(value, axis, pairs)]
    slice x1, local copies, waits for them, and re-layouts: 4.68 us -> 2.54 us  [shards(): own_blocks = [later_blocks[:slots // 2], later_blocks[slots // 2:]]]
    pallas_call x6 -> x4, Pallas kernels: 18.6 us -> 16.5 us  [product(): pl.pallas_call(functools.partial(kernel, ways), out_shape=[like(shape) fo...]
    unnamed x17 -> x13, local copies, waits for them, and re-layouts: 2.31 us -> 1.61 us
  transfers between devices with their start and end apart: 28 -> 27, of which waited for: 15 -> 16; matrix products, arithmetic and copies ran while one was open for 3% -> 5% of each run, Pallas kernels for 5% -> 0%
where the time goes in v7:
time: 102 us
  starting transfers between devices  37.4 us (37%)
  waiting for transfers between devices  37.2 us (36%)
  Pallas kernels  16.5 us (16%)
  local copies, waits for them, and re-layouts  5.39 us (5%)
  other arithmetic  4.09 us (4%)
  between operations  1.06 us (1%)
    ppermute x27, starting transfers between devices, swap(): return lax.ppermute(value, axis, pairs)  37.4 us
    ppermute x27, waiting for transfers between devices, swap(): return lax.ppermute(value, axis, pairs)  37.2 us
    pallas_call x4, Pallas kernels, product(): pl.pallas_call(functools.partial(kernel, ways), out_shape=[like(shape) fo...  16.5 us
    slice x1, local copies, waits for them, and re-layouts, shards(): own_blocks = [later_blocks[:slots // 2], later_blocks[slots // 2:]]  2.54 us
    convert_element_type x10, other arithmetic, add_up(): return total.astype(parts[0].dtype)  2.14 us
  transfers between devices with their start and end apart: 27, of which 16 were waited for; matrix products, arithmetic and copies ran while one was open for 5% of the time, Pallas kernels for 0%

profile of v7, /device:TPU:0, one launch (start us, length us, event | category | flops | bytes accessed | tf_op | source)
XLA Modules:
  0.0 101.6 jit_solution(8999361623907809259)
XLA Ops:
  4.0 4.7 %collective-permute-start.1 = (bf16[4,12288]{1,0:T(4,128)(2,1)}, bf16[4,12288]{1,0:T(4,128)(2,1)S(1)}, u32[]{:S(2)}, u32[]{:S(2)}) collective-permute-start(bf16[4,12288]{1,0:T(4,128)(2,1)} %mine_ref.1), channel_id=1, source_target_pairs={{0,8},{8,0},{16,24},{24,16},{1,9},{9,1},{17,25},{25,17},{2,10},{10... | collective-permute-start | bytes 294920 | tf_op jit(solution)/shard_map/ppermute | solution.py:20
  8.7 4.5 %collective-permute-start.2 = (bf16[4,12288]{1,0:T(4,128)(2,1)}, bf16[4,12288]{1,0:T(4,128)(2,1)S(1)}, u32[]{:S(2)}, u32[]{:S(2)}) collective-permute-start(bf16[4,12288]{1,0:T(4,128)(2,1)} %mine_ref.1), channel_id=1, source_target_pairs={{0,16},{8,24},{16,0},{24,8},{1,17},{9,25},{17,1},{25,9},{2,18},{10... | collective-permute-start | bytes 294920 | tf_op jit(solution)/shard_map/ppermute | solution.py:20
  13.2 1.9 %collective-permute-start.3 = (bf16[4,12288]{1,0:T(4,128)(2,1)}, bf16[4,12288]{1,0:T(4,128)(2,1)S(1)}, u32[]{:S(2)}, u32[]{:S(2)}) collective-permute-start(bf16[4,12288]{1,0:T(4,128)(2,1)} %mine_ref.1), channel_id=1, source_target_pairs={{0,24},{8,16},{16,8},{24,0},{1,25},{9,17},{17,9},{25,1},{2,26},{10... | collective-permute-start | bytes 294920 | tf_op jit(solution)/shard_map/ppermute | solution.py:20
  18.3 2.5 %fusion.4 = (bf16[16,256,256]{2,1,0:T(8,128)(2,1)S(1)}, bf16[16,256,256]{2,1,0:T(8,128)(2,1)S(1)}) fusion(bf16[32,256,256]{2,1,0:T(8,128)(2,1)} %param.6), kind=kLoop, calls=%fused_computation.43 | loop fusion | bytes 8388608 | tf_op jit(solution)/shard_map/slice | solution.py:175
  21.9 4.8 %shard_map.85 = (bf16[48,16,128]{2,1,0:T(8,128)(2,1)S(1)}, bf16[48,16,128]{2,1,0:T(8,128)(2,1)S(1)}) custom-call(s32[96]{0:T(128)S(1)} %reshape.58.own_entry, s32[96]{0:T(128)S(1)} %collective-permute-done.after_ref.other_entry, f32[8]{0:T(128)S(1)} %copy-done.5, s32[2]{0:T(128)S(1)} %pad_add_fusion.1.place_ref, bf16[4,12288]{1,0:T(4,128)(2,1)S(1)} %copy-done.3, ...), custom_call_target="tpu_custom_call" | custom-call | flops 134217728 | bytes 8388608 | tf_op jit(solution)/shard_map/pallas_call | solution.py:181
  26.6 1.6 %collective-permute-start.10 = (bf16[48,16,128]{2,1,0:T(8,128)(2,1)S(1)}, bf16[48,16,128]{2,1,0:T(8,128)(2,1)S(1)}, u32[]{:S(2)}, u32[]{:S(2)}) collective-permute-start(bf16[48,16,128]{2,1,0:T(8,128)(2,1)S(1)} %get-tuple-element.24), channel_id=1, source_target_pairs={{0,2},{1,3},{2,0},{3,1},{4,6},{5,7},{6,4},{7,5},{8,10},{9,11},{10,... | collective-permute-start | bytes 589832 | tf_op jit(solution)/shard_map/ppermute | solution.py:20
  28.2 1.5 %collective-permute-start.8 = (bf16[48,16,128]{2,1,0:T(8,128)(2,1)S(1)}, bf16[48,16,128]{2,1,0:T(8,128)(2,1)S(1)}, u32[]{:S(2)}, u32[]{:S(2)}) collective-permute-start(bf16[48,16,128]{2,1,0:T(8,128)(2,1)S(1)} %get-tuple-element.23), channel_id=1, source_target_pairs={{0,1},{1,0},{2,3},{3,2},{4,5},{5,4},{6,7},{7,6},{8,9},{9,8},{10,11... | collective-permute-start | bytes 589832 | tf_op jit(solution)/shard_map/ppermute | solution.py:20
  29.7 4.3 %collective-permute-done.10 = bf16[48,16,128]{2,1,0:T(8,128)(2,1)S(1)} collective-permute-done((bf16[48,16,128]{2,1,0:T(8,128)(2,1)S(1)}, bf16[48,16,128]{2,1,0:T(8,128)(2,1)S(1)}, u32[]{:S(2)}, u32[]{:S(2)}) %collective-permute-start.10) | collective-permute-done | bytes 196640 | tf_op jit(solution)/shard_map/ppermute | solution.py:20
  34.0 1.5 %collective-permute-start.11 = (bf16[48,16,128]{2,1,0:T(8,128)(2,1)S(1)}, bf16[48,16,128]{2,1,0:T(8,128)(2,1)S(1)}, u32[]{:S(2)}, u32[]{:S(2)}) collective-permute-start(bf16[48,16,128]{2,1,0:T(8,128)(2,1)S(1)} %add_convert_fusion.5), channel_id=1, source_target_pairs={{0,1},{1,0},{2,3},{3,2},{4,5},{5,4},{6,7},{7,6},{8,9},{9,8},{10,11... | collective-permute-start | bytes 589832 | tf_op jit(solution)/shard_map/ppermute | solution.py:20
  35.7 1.5 %collective-permute-start.9 = (bf16[48,16,128]{2,1,0:T(8,128)(2,1)S(1)}, bf16[48,16,128]{2,1,0:T(8,128)(2,1)S(1)}, u32[]{:S(2)}, u32[]{:S(2)}) collective-permute-start(bf16[48,16,128]{2,1,0:T(8,128)(2,1)S(1)} %add_convert_fusion.7), channel_id=1, source_target_pairs={{0,2},{1,3},{2,0},{3,1},{4,6},{5,7},{6,4},{7,5},{8,10},{9,11},{10,... | collective-permute-start | bytes 589832 | tf_op jit(solution)/shard_map/ppermute | solution.py:20
  37.2 4.3 %collective-permute-done.11 = bf16[48,16,128]{2,1,0:T(8,128)(2,1)S(1)} collective-permute-done((bf16[48,16,128]{2,1,0:T(8,128)(2,1)S(1)}, bf16[48,16,128]{2,1,0:T(8,128)(2,1)S(1)}, u32[]{:S(2)}, u32[]{:S(2)}) %collective-permute-start.11) | collective-permute-done | bytes 196640 | tf_op jit(solution)/shard_map/ppermute | solution.py:20
  41.6 1.3 %collective-permute-done.9 = bf16[48,16,128]{2,1,0:T(8,128)(2,1)S(1)} collective-permute-done((bf16[48,16,128]{2,1,0:T(8,128)(2,1)S(1)}, bf16[48,16,128]{2,1,0:T(8,128)(2,1)S(1)}, u32[]{:S(2)}, u32[]{:S(2)}) %collective-permute-start.9) | collective-permute-done | bytes 196640 | tf_op jit(solution)/shard_map/ppermute | solution.py:20
  42.9 3.5 %shard_map.86 = (bf16[24,16,128]{2,1,0:T(8,128)(2,1)S(1)}, bf16[24,16,128]{2,1,0:T(8,128)(2,1)S(1)}, bf16[24,16,128]{2,1,0:T(8,128)(2,1)S(1)}, bf16[24,16,128]{2,1,0:T(8,128)(2,1)S(1)}) custom-call(s32[96]{0:T(128)S(1)} %reshape.58.own_entry, s32[96]{0:T(128)S(1)} %collective-permute-done.after_ref.other_entry, f32[8]{0:T(128)S(1)} %copy-done.5, ...), custom_call_target="tpu_custom_call" | custom-call | flops 134217728 | bytes 8388608 | tf_op jit(solution)/shard_map/pallas_call | solution.py:181
  47.4 1.2 %collective-permute-start.13 = (bf16[24,16,128]{2,1,0:T(8,128)(2,1)S(1)}, bf16[24,16,128]{2,1,0:T(8,128)(2,1)S(1)}, u32[]{:S(2)}, u32[]{:S(2)}) collective-permute-start(bf16[24,16,128]{2,1,0:T(8,128)(2,1)S(1)} %get-tuple-element.27), channel_id=1, source_target_pairs={{0,16},{4,20},{8,24},{12,28},{16,0},{20,4},{24,8},{28,12},{1,17},{... | collective-permute-start | bytes 294920 | tf_op jit(solution)/shard_map/ppermute | solution.py:20
  48.6 2.3 %collective-permute-start.14 = (bf16[24,16,128]{2,1,0:T(8,128)(2,1)S(1)}, bf16[24,16,128]{2,1,0:T(8,128)(2,1)S(1)}, u32[]{:S(2)}, u32[]{:S(2)}) collective-permute-start(bf16[24,16,128]{2,1,0:T(8,128)(2,1)S(1)} %get-tuple-element.28), channel_id=1, source_target_pairs={{0,24},{4,28},{8,16},{12,20},{16,8},{20,12},{24,0},{28,4},{1,25},{... | collective-permute-start | bytes 294920 | tf_op jit(solution)/shard_map/ppermute | solution.py:20
  51.8 5.4 %collective-permute-done.13 = bf16[24,16,128]{2,1,0:T(8,128)(2,1)S(1)} collective-permute-done((bf16[24,16,128]{2,1,0:T(8,128)(2,1)S(1)}, bf16[24,16,128]{2,1,0:T(8,128)(2,1)S(1)}, u32[]{:S(2)}, u32[]{:S(2)}) %collective-permute-start.13) | collective-permute-done | bytes 98336 | tf_op jit(solution)/shard_map/ppermute | solution.py:20
  57.2 1.8 %collective-permute-start.15 = (bf16[24,16,128]{2,1,0:T(8,128)(2,1)S(1)}, bf16[24,16,128]{2,1,0:T(8,128)(2,1)S(1)}, u32[]{:S(2)}, u32[]{:S(2)}) collective-permute-start(bf16[24,16,128]{2,1,0:T(8,128)(2,1)S(1)} %add_convert_fusion.8.refs_0_.refs_5_), channel_id=1, source_target_pairs={{0,8},{4,12},{8,0},{12,4},{16,24},{20,28},{24,16},{28,20},{1,9},{5... | collective-permute-start | bytes 294920 | tf_op jit(solution)/shard_map/ppermute | solution.py:20
  59.9 1.8 %collective-permute-start.17 = (bf16[24,16,128]{2,1,0:T(8,128)(2,1)S(1)}, bf16[24,16,128]{2,1,0:T(8,128)(2,1)S(1)}, u32[]{:S(2)}, u32[]{:S(2)}) collective-permute-start(bf16[24,16,128]{2,1,0:T(8,128)(2,1)S(1)} %add_convert_fusion.8.refs_0_.refs_5_), channel_id=1, source_target_pairs={{0,24},{4,28},{8,16},{12,20},{16,8},{20,12},{24,0},{28,4},{1,25},{... | collective-permute-start | bytes 294920 | tf_op jit(solution)/shard_map/ppermute | solution.py:20
  62.2 5.9 %collective-permute-done.16.refs_2_.refs_7_ = bf16[24,16,128]{2,1,0:T(8,128)(2,1)S(1)} collective-permute-done((bf16[24,16,128]{2,1,0:T(8,128)(2,1)S(1)}, bf16[24,16,128]{2,1,0:T(8,128)(2,1)S(1)}, u32[]{:S(2)}, u32[]{:S(2)}) %collective-permute-start.16) | collective-permute-done | bytes 98336 | tf_op jit(solution)/shard_map/ppermute | solution.py:20
  68.1 4.6 %shard_map.87 = (bf16[48,16,128]{2,1,0:T(8,128)(2,1)S(1)}, bf16[48,16,128]{2,1,0:T(8,128)(2,1)S(1)}) custom-call(s32[96]{0:T(128)S(1)} %reshape.58.own_entry, s32[96]{0:T(128)S(1)} %collective-permute-done.after_ref.other_entry, f32[8]{0:T(128)S(1)} %copy-done.5, s32[2]{0:T(128)S(1)} %pad_add_fusion.1.place_ref, ...), custom_call_target="tpu_custom_call" | custom-call | flops 134217728 | bytes 8388608 | tf_op jit(solution)/shard_map/pallas_call | solution.py:181
  72.7 1.8 %collective-permute-start.18 = (bf16[48,16,128]{2,1,0:T(8,128)(2,1)S(1)}, bf16[48,16,128]{2,1,0:T(8,128)(2,1)S(1)}, u32[]{:S(2)}, u32[]{:S(2)}) collective-permute-start(bf16[48,16,128]{2,1,0:T(8,128)(2,1)S(1)} %get-tuple-element.29), channel_id=1, source_target_pairs={{0,1},{1,0},{2,3},{3,2},{4,5},{5,4},{6,7},{7,6},{8,9},{9,8},{10,11... | collective-permute-start | bytes 589832 | tf_op jit(solution)/shard_map/ppermute | solution.py:20
  74.7 3.7 %collective-permute-done.18 = bf16[48,16,128]{2,1,0:T(8,128)(2,1)S(1)} collective-permute-done((bf16[48,16,128]{2,1,0:T(8,128)(2,1)S(1)}, bf16[48,16,128]{2,1,0:T(8,128)(2,1)S(1)}, u32[]{:S(2)}, u32[]{:S(2)}) %collective-permute-start.18) | collective-permute-done | bytes 196640 | tf_op jit(solution)/shard_map/ppermute | solution.py:20
  78.5 1.3 %collective-permute-start.19 = (bf16[48,16,128]{2,1,0:T(8,128)(2,1)S(1)}, bf16[48,16,128]{2,1,0:T(8,128)(2,1)S(1)}, u32[]{:S(2)}, u32[]{:S(2)}) collective-permute-start(bf16[48,16,128]{2,1,0:T(8,128)(2,1)S(1)} %add_convert_fusion.3), channel_id=1, source_target_pairs={{0,2},{1,3},{2,0},{3,1},{4,6},{5,7},{6,4},{7,5},{8,10},{9,11},{10,... | collective-permute-start | bytes 589832 | tf_op jit(solution)/shard_map/ppermute | solution.py:20
  79.8 1.6 %collective-permute-done.20 = bf16[48,16,128]{2,1,0:T(8,128)(2,1)S(1)} collective-permute-done((bf16[48,16,128]{2,1,0:T(8,128)(2,1)S(1)}, bf16[48,16,128]{2,1,0:T(8,128)(2,1)S(1)}, u32[]{:S(2)}, u32[]{:S(2)}) %collective-permute-start.20) | collective-permute-done | bytes 196640 | tf_op jit(solution)/shard_map/ppermute | solution.py:20
  81.5 2.8 %collective-permute-done.19 = bf16[48,16,128]{2,1,0:T(8,128)(2,1)S(1)} collective-permute-done((bf16[48,16,128]{2,1,0:T(8,128)(2,1)S(1)}, bf16[48,16,128]{2,1,0:T(8,128)(2,1)S(1)}, u32[]{:S(2)}, u32[]{:S(2)}) %collective-permute-start.19) | collective-permute-done | bytes 196640 | tf_op jit(solution)/shard_map/ppermute | solution.py:20
  84.4 2.8 %collective-permute-done.21 = bf16[48,16,128]{2,1,0:T(8,128)(2,1)S(1)} collective-permute-done((bf16[48,16,128]{2,1,0:T(8,128)(2,1)S(1)}, bf16[48,16,128]{2,1,0:T(8,128)(2,1)S(1)}, u32[]{:S(2)}, u32[]{:S(2)}) %collective-permute-start.21) | collective-permute-done | bytes 196640 | tf_op jit(solution)/shard_map/ppermute | solution.py:20
  87.2 3.7 %shard_map.88 = (bf16[4,4,12288]{2,1,0:T(4,128)(2,1)S(1)}, bf16[48,16,128]{2,1,0:T(8,128)(2,1)S(1)}, bf16[48,16,128]{2,1,0:T(8,128)(2,1)S(1)}, bf16[24,16,128]{2...) custom-call(s32[96]{0:T(128)S(1)} %reshape.58.own_entry, ...), custom_call_target="tpu_custom_call", output_to_operand_aliasing={{1}: (9, {}), {2}: (10, {}), {3}: (11, {}), {4}: (12, {}), ... | custom-call | flops 134217728 | bytes 8388608 | tf_op jit(solution)/shard_map/pallas_call | solution.py:181
  91.1 1.1 %collective-permute-start.24 = (bf16[4,12288]{1,0:T(4,128)(2,1)S(1)}, bf16[4,12288]{1,0:T(4,128)(2,1)S(1)}, u32[]{:S(2)}, u32[]{:S(2)}) collective-permute-start(bf16[4,12288]{1,0:T(4,128)(2,1)S(1)} %get-tuple-element.40), channel_id=1, source_target_pairs={{0,8},{4,12},{8,0},{12,4},{16,24},{20,28},{24,16},{28,20},{1,9},{5... | collective-permute-start | bytes 294920 | tf_op jit(solution)/shard_map/ppermute | solution.py:20
  92.2 1.1 %collective-permute-start.25 = (bf16[4,12288]{1,0:T(4,128)(2,1)S(1)}, bf16[4,12288]{1,0:T(4,128)(2,1)S(1)}, u32[]{:S(2)}, u32[]{:S(2)}) collective-permute-start(bf16[4,12288]{1,0:T(4,128)(2,1)S(1)} %get-tuple-element.42), channel_id=1, source_target_pairs={{0,16},{4,20},{8,24},{12,28},{16,0},{20,4},{24,8},{28,12},{1,17},{... | collective-permute-start | bytes 294920 | tf_op jit(solution)/shard_map/ppermute | solution.py:20
  93.3 2.3 %collective-permute-start.26 = (bf16[4,12288]{1,0:T(4,128)(2,1)S(1)}, bf16[4,12288]{1,0:T(4,128)(2,1)S(1)}, u32[]{:S(2)}, u32[]{:S(2)}) collective-permute-start(bf16[4,12288]{1,0:T(4,128)(2,1)S(1)} %get-tuple-element.41), channel_id=1, source_target_pairs={{0,24},{4,28},{8,16},{12,20},{16,8},{20,12},{24,0},{28,4},{1,25},{... | collective-permute-start | bytes 294920 | tf_op jit(solution)/shard_map/ppermute | solution.py:20
  98.9 1.0 %collective-permute-done.25 = bf16[4,12288]{1,0:T(4,128)(2,1)S(1)} collective-permute-done((bf16[4,12288]{1,0:T(4,128)(2,1)S(1)}, bf16[4,12288]{1,0:T(4,128)(2,1)S(1)}, u32[]{:S(2)}, u32[]{:S(2)}) %collective-permute-start.25) | collective-permute-done | bytes 98336 | tf_op jit(solution)/shard_map/ppermute | solution.py:20
  100.0 1.6 %fusion.2 = bf16[4,12288]{1,0:T(4,128)(2,1)} fusion(bf16[4,12288]{1,0:T(4,128)(2,1)S(1)} %collective-permute-done.26, bf16[4,12288]{1,0:T(4,128)(2,1)S(1)} %collective-permute-done.25, bf16[4,12288]{1,0:T(4,128)(2,1)S(1)} %collective-permute-done.24, bf16[4,4,12288]{2,1,0:T(4,128)(2,1)} %copy-done.4), kind=kLoop, calls=%fused_computation.11 | loop fusion | flops 393216 | bytes 491520 | tf_op jit(solution)/shard_map/convert_element_type | solution.py:27
  (79 shorter events, 15.1 us)
Async XLA Ops:
  2.4 1.3 %collective-permute-start = (s32[96]{0:T(128)S(1)}, s32[96]{0:T(128)S(1)}, u32[]{:S(2)}, u32[]{:S(2)}) collective-permute-start(s32[96]{0:T(128)S(1)} %reshape.58.own_entry), channel_id=1, source_target_pairs={{0,4},{4,0},{8,12},{12,8},{16,20},{20,16},{24,28},{28,24},{1,5},{5... | collective-permute-start | bytes 1160 | tf_op jit(solution)/shard_map/ppermute | solution.py:20
  3.7 18.1 %collective-permute-start.7 = (bf16[32,256,256]{2,1,0:T(8,128)(2,1)}, bf16[32,256,256]{2,1,0:T(8,128)(2,1)}, u32[]{:S(2)}, u32[]{:S(2)}) collective-permute-start(bf16[32,256,256]{2,1,0:T(8,128)(2,1)} %param.6), channel_id=1, source_target_pairs={{0,4},{4,0},{8,12},{12,8},{16,20},{20,16},{24,28},{28,24},{1,5},{5... | collective-permute-start | bytes 12582920 | tf_op jit(solution)/shard_map/ppermute | solution.py:20
  4.0 12.9 %collective-permute-start.1 = (bf16[4,12288]{1,0:T(4,128)(2,1)}, bf16[4,12288]{1,0:T(4,128)(2,1)S(1)}, u32[]{:S(2)}, u32[]{:S(2)}) collective-permute-start(bf16[4,12288]{1,0:T(4,128)(2,1)} %mine_ref.1), channel_id=1, source_target_pairs={{0,8},{8,0},{16,24},{24,16},{1,9},{9,1},{17,25},{25,17},{2,10},{10... | collective-permute-start | bytes 294920 | tf_op jit(solution)/shard_map/ppermute | solution.py:20
  8.7 8.9 %collective-permute-start.2 = (bf16[4,12288]{1,0:T(4,128)(2,1)}, bf16[4,12288]{1,0:T(4,128)(2,1)S(1)}, u32[]{:S(2)}, u32[]{:S(2)}) collective-permute-start(bf16[4,12288]{1,0:T(4,128)(2,1)} %mine_ref.1), channel_id=1, source_target_pairs={{0,16},{8,24},{16,0},{24,8},{1,17},{9,25},{17,1},{25,9},{2,18},{10... | collective-permute-start | bytes 294920 | tf_op jit(solution)/shard_map/ppermute | solution.py:20
  13.2 8.6 %collective-permute-start.3 = (bf16[4,12288]{1,0:T(4,128)(2,1)}, bf16[4,12288]{1,0:T(4,128)(2,1)S(1)}, u32[]{:S(2)}, u32[]{:S(2)}) collective-permute-start(bf16[4,12288]{1,0:T(4,128)(2,1)} %mine_ref.1), channel_id=1, source_target_pairs={{0,24},{8,16},{16,8},{24,0},{1,25},{9,17},{17,9},{25,1},{2,26},{10... | collective-permute-start | bytes 294920 | tf_op jit(solution)/shard_map/ppermute | solution.py:20
  16.1 5.7 %copy-start.3 = (bf16[4,12288]{1,0:T(4,128)(2,1)S(1)}, bf16[4,12288]{1,0:T(4,128)(2,1)}, u32[]{:S(2)}) copy-start(bf16[4,12288]{1,0:T(4,128)(2,1)} %mine_ref.1) | copy-start | bytes 294916
  16.1 5.7 %copy-start.5 = (f32[8]{0:T(128)S(1)}, f32[8]{0:T(128)}, u32[]{:S(2)}) copy-start(f32[8]{0:T(128)} %gain_ref.7) | copy-start | bytes 100
  16.1 5.7 %collective-permute-start.4 = (bf16[4,12288]{1,0:T(4,128)(2,1)S(1)}, bf16[4,12288]{1,0:T(4,128)(2,1)S(1)}, u32[]{:S(2)}, u32[]{:S(2)}) collective-permute-start(bf16[4,12288]{1,0:T(4,128)(2,1)S(1)} %shard_map.84), channel_id=1, source_target_pairs={{4,12},{12,4},{20,28},{28,20},{5,13},{13,5},{21,29},{29,21},{6,14}... | collective-permute-start | bytes 294920 | tf_op jit(solution)/shard_map/ppermute | solution.py:20
  17.0 4.9 %collective-permute-start.5 = (bf16[4,12288]{1,0:T(4,128)(2,1)S(1)}, bf16[4,12288]{1,0:T(4,128)(2,1)S(1)}, u32[]{:S(2)}, u32[]{:S(2)}) collective-permute-start(bf16[4,12288]{1,0:T(4,128)(2,1)S(1)} %shard_map.84), channel_id=1, source_target_pairs={{4,20},{12,28},{20,4},{28,12},{5,21},{13,29},{21,5},{29,13},{6,22}... | collective-permute-start | bytes 294920 | tf_op jit(solution)/shard_map/ppermute | solution.py:20
  17.6 4.2 %collective-permute-start.6 = (bf16[4,12288]{1,0:T(4,128)(2,1)S(1)}, bf16[4,12288]{1,0:T(4,128)(2,1)S(1)}, u32[]{:S(2)}, u32[]{:S(2)}) collective-permute-start(bf16[4,12288]{1,0:T(4,128)(2,1)S(1)} %shard_map.84), channel_id=1, source_target_pairs={{4,28},{12,20},{20,12},{28,4},{5,29},{13,21},{21,13},{29,5},{6,30}... | collective-permute-start | bytes 294920 | tf_op jit(solution)/shard_map/ppermute | solution.py:20
  20.9 47.3 %copy-start = (bf16[16,256,256]{2,1,0:T(8,128)(2,1)}, bf16[16,256,256]{2,1,0:T(8,128)(2,1)S(1)}, u32[]{:S(2)}) copy-start(bf16[16,256,256]{2,1,0:T(8,128)(2,1)S(1)} %get-tuple-element.39.refs_6_.refs_0_.refs_4_) | copy-start | bytes 6291460
  26.6 7.3 %collective-permute-start.10 = (bf16[48,16,128]{2,1,0:T(8,128)(2,1)S(1)}, bf16[48,16,128]{2,1,0:T(8,128)(2,1)S(1)}, u32[]{:S(2)}, u32[]{:S(2)}) collective-permute-start(bf16[48,16,128]{2,1,0:T(8,128)(2,1)S(1)} %get-tuple-element.24), channel_id=1, source_target_pairs={{0,2},{1,3},{2,0},{3,1},{4,6},{5,7},{6,4},{7,5},{8,10},{9,11},{10,... | collective-permute-start | bytes 589832 | tf_op jit(solution)/shard_map/ppermute | solution.py:20
  28.2 7.5 %collective-permute-start.8 = (bf16[48,16,128]{2,1,0:T(8,128)(2,1)S(1)}, bf16[48,16,128]{2,1,0:T(8,128)(2,1)S(1)}, u32[]{:S(2)}, u32[]{:S(2)}) collective-permute-start(bf16[48,16,128]{2,1,0:T(8,128)(2,1)S(1)} %get-tuple-element.23), channel_id=1, source_target_pairs={{0,1},{1,0},{2,3},{3,2},{4,5},{5,4},{6,7},{7,6},{8,9},{9,8},{10,11... | collective-permute-start | bytes 589832 | tf_op jit(solution)/shard_map/ppermute | solution.py:20
  34.0 7.5 %collective-permute-start.11 = (bf16[48,16,128]{2,1,0:T(8,128)(2,1)S(1)}, bf16[48,16,128]{2,1,0:T(8,128)(2,1)S(1)}, u32[]{:S(2)}, u32[]{:S(2)}) collective-permute-start(bf16[48,16,128]{2,1,0:T(8,128)(2,1)S(1)} %add_convert_fusion.5), channel_id=1, source_target_pairs={{0,1},{1,0},{2,3},{3,2},{4,5},{5,4},{6,7},{7,6},{8,9},{9,8},{10,11... | collective-permute-start | bytes 589832 | tf_op jit(solution)/shard_map/ppermute | solution.py:20
  35.7 7.1 %collective-permute-start.9 = (bf16[48,16,128]{2,1,0:T(8,128)(2,1)S(1)}, bf16[48,16,128]{2,1,0:T(8,128)(2,1)S(1)}, u32[]{:S(2)}, u32[]{:S(2)}) collective-permute-start(bf16[48,16,128]{2,1,0:T(8,128)(2,1)S(1)} %add_convert_fusion.7), channel_id=1, source_target_pairs={{0,2},{1,3},{2,0},{3,1},{4,6},{5,7},{6,4},{7,5},{8,10},{9,11},{10,... | collective-permute-start | bytes 589832 | tf_op jit(solution)/shard_map/ppermute | solution.py:20
  46.4 5.3 %collective-permute-start.12 = (bf16[24,16,128]{2,1,0:T(8,128)(2,1)S(1)}, bf16[24,16,128]{2,1,0:T(8,128)(2,1)S(1)}, u32[]{:S(2)}, u32[]{:S(2)}) collective-permute-start(bf16[24,16,128]{2,1,0:T(8,128)(2,1)S(1)} %get-tuple-element.26), channel_id=1, source_target_pairs={{0,8},{4,12},{8,0},{12,4},{16,24},{20,28},{24,16},{28,20},{1,9},{5... | collective-permute-start | bytes 294920 | tf_op jit(solution)/shard_map/ppermute | solution.py:20
  47.4 9.7 %collective-permute-start.13 = (bf16[24,16,128]{2,1,0:T(8,128)(2,1)S(1)}, bf16[24,16,128]{2,1,0:T(8,128)(2,1)S(1)}, u32[]{:S(2)}, u32[]{:S(2)}) collective-permute-start(bf16[24,16,128]{2,1,0:T(8,128)(2,1)S(1)} %get-tuple-element.27), channel_id=1, source_target_pairs={{0,16},{4,20},{8,24},{12,28},{16,0},{20,4},{24,8},{28,12},{1,17},{... | collective-permute-start | bytes 294920 | tf_op jit(solution)/shard_map/ppermute | solution.py:20
  48.6 8.6 %collective-permute-start.14 = (bf16[24,16,128]{2,1,0:T(8,128)(2,1)S(1)}, bf16[24,16,128]{2,1,0:T(8,128)(2,1)S(1)}, u32[]{:S(2)}, u32[]{:S(2)}) collective-permute-start(bf16[24,16,128]{2,1,0:T(8,128)(2,1)S(1)} %get-tuple-element.28), channel_id=1, source_target_pairs={{0,24},{4,28},{8,16},{12,20},{16,8},{20,12},{24,0},{28,4},{1,25},{... | collective-permute-start | bytes 294920 | tf_op jit(solution)/shard_map/ppermute | solution.py:20
  57.2 5.1 %collective-permute-start.15 = (bf16[24,16,128]{2,1,0:T(8,128)(2,1)S(1)}, bf16[24,16,128]{2,1,0:T(8,128)(2,1)S(1)}, u32[]{:S(2)}, u32[]{:S(2)}) collective-permute-start(bf16[24,16,128]{2,1,0:T(8,128)(2,1)S(1)} %add_convert_fusion.8.refs_0_.refs_5_), channel_id=1, source_target_pairs={{0,8},{4,12},{8,0},{12,4},{16,24},{20,28},{24,16},{28,20},{1,9},{5... | collective-permute-start | bytes 294920 | tf_op jit(solution)/shard_map/ppermute | solution.py:20
  59.0 9.1 %collective-permute-start.16 = (bf16[24,16,128]{2,1,0:T(8,128)(2,1)S(1)}, bf16[24,16,128]{2,1,0:T(8,128)(2,1)S(1)}, u32[]{:S(2)}, u32[]{:S(2)}) collective-permute-start(bf16[24,16,128]{2,1,0:T(8,128)(2,1)S(1)} %add_convert_fusion.8.refs_0_.refs_5_), channel_id=1, source_target_pairs={{0,16},{4,20},{8,24},{12,28},{16,0},{20,4},{24,8},{28,12},{1,17},{... | collective-permute-start | bytes 294920 | tf_op jit(solution)/shard_map/ppermute | solution.py:20
  59.9 8.2 %collective-permute-start.17 = (bf16[24,16,128]{2,1,0:T(8,128)(2,1)S(1)}, bf16[24,16,128]{2,1,0:T(8,128)(2,1)S(1)}, u32[]{:S(2)}, u32[]{:S(2)}) collective-permute-start(bf16[24,16,128]{2,1,0:T(8,128)(2,1)S(1)} %add_convert_fusion.8.refs_0_.refs_5_), channel_id=1, source_target_pairs={{0,24},{4,28},{8,16},{12,20},{16,8},{20,12},{24,0},{28,4},{1,25},{... | collective-permute-start | bytes 294920 | tf_op jit(solution)/shard_map/ppermute | solution.py:20
  72.7 5.8 %collective-permute-start.18 = (bf16[48,16,128]{2,1,0:T(8,128)(2,1)S(1)}, bf16[48,16,128]{2,1,0:T(8,128)(2,1)S(1)}, u32[]{:S(2)}, u32[]{:S(2)}) collective-permute-start(bf16[48,16,128]{2,1,0:T(8,128)(2,1)S(1)} %get-tuple-element.29), channel_id=1, source_target_pairs={{0,1},{1,0},{2,3},{3,2},{4,5},{5,4},{6,7},{7,6},{8,9},{9,8},{10,11... | collective-permute-start | bytes 589832 | tf_op jit(solution)/shard_map/ppermute | solution.py:20
  74.4 12.8 %copy-start.1 = (bf16[16,256,256]{2,1,0:T(8,128)(2,1)S(1)}, bf16[16,256,256]{2,1,0:T(8,128)(2,1)}, u32[]{:S(2)}) copy-start(bf16[16,256,256]{2,1,0:T(8,128)(2,1)} %copy-done) | copy-start | bytes 6291460
  74.5 6.9 %collective-permute-start.20 = (bf16[48,16,128]{2,1,0:T(8,128)(2,1)S(1)}, bf16[48,16,128]{2,1,0:T(8,128)(2,1)S(1)}, u32[]{:S(2)}, u32[]{:S(2)}) collective-permute-start(bf16[48,16,128]{2,1,0:T(8,128)(2,1)S(1)} %get-tuple-element.30), channel_id=1, source_target_pairs={{0,2},{1,3},{2,0},{3,1},{4,6},{5,7},{6,4},{7,5},{8,10},{9,11},{10,... | collective-permute-start | bytes 589832 | tf_op jit(solution)/shard_map/ppermute | solution.py:20
  78.5 5.8 %collective-permute-start.19 = (bf16[48,16,128]{2,1,0:T(8,128)(2,1)S(1)}, bf16[48,16,128]{2,1,0:T(8,128)(2,1)S(1)}, u32[]{:S(2)}, u32[]{:S(2)}) collective-permute-start(bf16[48,16,128]{2,1,0:T(8,128)(2,1)S(1)} %add_convert_fusion.3), channel_id=1, source_target_pairs={{0,2},{1,3},{2,0},{3,1},{4,6},{5,7},{6,4},{7,5},{8,10},{9,11},{10,... | collective-permute-start | bytes 589832 | tf_op jit(solution)/shard_map/ppermute | solution.py:20
  81.4 5.7 %collective-permute-start.21 = (bf16[48,16,128]{2,1,0:T(8,128)(2,1)S(1)}, bf16[48,16,128]{2,1,0:T(8,128)(2,1)S(1)}, u32[]{:S(2)}, u32[]{:S(2)}) collective-permute-start(bf16[48,16,128]{2,1,0:T(8,128)(2,1)S(1)} %add_convert_fusion.1), channel_id=1, source_target_pairs={{0,1},{1,0},{2,3},{3,2},{4,5},{5,4},{6,7},{7,6},{8,9},{9,8},{10,11... | collective-permute-start | bytes 589832 | tf_op jit(solution)/shard_map/ppermute | solution.py:20
  90.9 4.7 %copy-start.4 = (bf16[4,4,12288]{2,1,0:T(4,128)(2,1)}, bf16[4,4,12288]{2,1,0:T(4,128)(2,1)S(1)}, u32[]{:S(2)}) copy-start(bf16[4,4,12288]{2,1,0:T(4,128)(2,1)S(1)} %get-tuple-element.37) | copy-start | bytes 1179652
  91.1 7.9 %collective-permute-start.24 = (bf16[4,12288]{1,0:T(4,128)(2,1)S(1)}, bf16[4,12288]{1,0:T(4,128)(2,1)S(1)}, u32[]{:S(2)}, u32[]{:S(2)}) collective-permute-start(bf16[4,12288]{1,0:T(4,128)(2,1)S(1)} %get-tuple-element.40), channel_id=1, source_target_pairs={{0,8},{4,12},{8,0},{12,4},{16,24},{20,28},{24,16},{28,20},{1,9},{5... | collective-permute-start | bytes 294920 | tf_op jit(solution)/shard_map/ppermute | solution.py:20
  92.2 7.8 %collective-permute-start.25 = (bf16[4,12288]{1,0:T(4,128)(2,1)S(1)}, bf16[4,12288]{1,0:T(4,128)(2,1)S(1)}, u32[]{:S(2)}, u32[]{:S(2)}) collective-permute-start(bf16[4,12288]{1,0:T(4,128)(2,1)S(1)} %get-tuple-element.42), channel_id=1, source_target_pairs={{0,16},{4,20},{8,24},{12,28},{16,0},{20,4},{24,8},{28,12},{1,17},{... | collective-permute-start | bytes 294920 | tf_op jit(solution)/shard_map/ppermute | solution.py:20
  93.3 6.7 %collective-permute-start.26 = (bf16[4,12288]{1,0:T(4,128)(2,1)S(1)}, bf16[4,12288]{1,0:T(4,128)(2,1)S(1)}, u32[]{:S(2)}, u32[]{:S(2)}) collective-permute-start(bf16[4,12288]{1,0:T(4,128)(2,1)S(1)} %get-tuple-element.41), channel_id=1, source_target_pairs={{0,24},{4,28},{8,16},{12,20},{16,8},{20,12},{24,0},{28,4},{1,25},{... | collective-permute-start | bytes 294920 | tf_op jit(solution)/shard_map/ppermute | solution.py:20
  95.9 1.3 %collective-permute-start.22 = (bf16[48,4,128]{2,1,0:T(4,128)(2,1)S(1)}, bf16[48,4,128]{2,1,0:T(4,128)(2,1)S(1)}, u32[]{:S(2)}, u32[]{:S(2)}) collective-permute-start(bf16[48,4,128]{2,1,0:T(4,128)(2,1)S(1)} %constant_dynamic-slice_fusion.5), channel_id=1, source_target_pairs={{0,4},{4,0},{8,12},{12,8},{16,20},{20,16},{24,28},{28,24},{1,5},{5... | collective-permute-start | bytes 147464 | tf_op jit(solution)/shard_map/ppermute | solution.py:20
  96.7 1.4 %collective-permute-start.23 = (bf16[48,4,128]{2,1,0:T(4,128)(2,1)S(1)}, bf16[48,4,128]{2,1,0:T(4,128)(2,1)S(1)}, u32[]{:S(2)}, u32[]{:S(2)}) collective-permute-start(bf16[48,4,128]{2,1,0:T(4,128)(2,1)S(1)} %constant_dynamic-slice_fusion), channel_id=1, source_target_pairs={{0,4},{4,0},{8,12},{12,8},{16,20},{20,16},{24,28},{28,24},{1,5},{5... | collective-permute-start | bytes 147464 | tf_op jit(solution)/shard_map/ppermute | solution.py:20
  (1 other events, 0.9 us)

commit v8 on v6

v8 whole, which is shorter than its diff:
```python
import functools
import math

import jax
import jax.numpy as jnp
from jax import lax
from jax.experimental import pallas as pl
from jax.experimental.pallas import tpu as pltpu
from jax.sharding import PartitionSpec as P

B = 256
LANES = 128
PER = B // LANES
HELD_PARTS = 2
ROW_PARTS = 2
CHUNK = 1536
VMEM_LIMIT = 12 * 1024 * 1024


def swap(value, axis, offset):
    count = lax.axis_size(axis)
    return lax.ppermute(value, axis, [(i, i ^ offset) for i in range(count)])


def add_up(*parts):
    total = parts[0].astype(jnp.float32)
    for part in parts[1:]:
        total = total + part.astype(jnp.float32)
    return total.astype(parts[0].dtype)


def spans(size, count):
    edges = [size * i // count for i in range(count + 1)]
    return [(a, b - a) for a, b in zip(edges, edges[1:])]


def add_products(entry_ref, gain_ref, load, block_refs, total, adjoint):
    total[...] = jnp.zeros_like(total)
    at = 0
    for block_ref in block_refs:
        for slot in range(block_ref.shape[0]):
            row, col, level = entry_ref[at], entry_ref[at + 1], entry_ref[at + 2]
            at += 3
            scale = jnp.where(level >= 0, gain_ref[jnp.maximum(level, 0)], jnp.float32(0.0))
            source, target = (row, col) if adjoint else (col, row)
            term = lax.dot_general(
                load(source),
                block_ref[slot],
                (((1,), (0 if adjoint else 1,)), ((), ())),
                preferred_element_type=jnp.float32,
            )
            term = term * scale
            for piece in range(PER):
                total[target * PER + piece] += term[:, piece * LANES : (piece + 1) * LANES]


def load_from(x):
    def load(block):
        return jnp.concatenate([x[block * PER + piece] for piece in range(PER)], axis=1)

    return load


def write_parts(total, outs):
    at = 0
    for out_ref in outs:
        size = out_ref.shape[0]
        out_ref[...] = total[at : at + size].astype(out_ref.dtype)
        at += size


def join_parts(x, parts):
    at = 0
    for part in parts:
        size = part.shape[0]
        x[at : at + size] = part[...]
        at += size


def first_kernel(ways, entry_ref, gain_ref, place_ref, *refs):
    count = 2 * ways
    pieces, block_refs, outs = refs[:count], refs[count : count + HELD_PARTS], refs[count + HELD_PARTS : -3]
    total, wide, x = refs[-3:]
    core, along = place_ref[0], place_ref[1]
    share, width = pieces[0].shape
    chunk = math.gcd(width, CHUNK)

    def assemble(step, carry):
        lanes = pl.ds(pl.multiple_of(step * chunk, chunk), chunk)
        rows = [piece[:, lanes].astype(jnp.float32) for piece in pieces]
        bit, place = 1, along + core * ways
        while bit < count:
            flip = (place & bit) != 0
            rows = [jnp.where(flip, rows[i ^ bit], rows[i]) for i in range(count)]
            bit *= 2
        for side in range(2):
            for way in range(ways):
                at = (2 * way + side) * share
                wide[at : at + share, lanes] = rows[side * ways + way]
        x[:, lanes] = wide[:, lanes].astype(x.dtype)
        return carry

    lax.fori_loop(0, width // chunk, assemble, 0)

    def load(block):
        return x[:, pl.ds(pl.multiple_of(block * B, B), B)]

    add_products(entry_ref, gain_ref, load, block_refs, total, False)
    write_parts(total, outs)


def forward_kernel(ways, entry_ref, gain_ref, place_ref, *refs):
    count = 2 * ways
    pieces, block_refs, outs = refs[:count], refs[count : count + HELD_PARTS], refs[count + HELD_PARTS : -2]
    total, x = refs[-2:]
    core, along = place_ref[0], place_ref[1]
    size = pieces[0].shape[0]
    for side in range(2):
        for way in range(ways):
            at = ((core ^ side) * ways + (along ^ way)) * size
            x[pl.ds(at, size)] = pieces[side * ways + way][...]
    add_products(entry_ref, gain_ref, load_from(x), block_refs, total, False)
    write_parts(total, outs)


def adjoint_kernel(ways, entry_ref, gain_ref, place_ref, *refs):
    parts, block_refs = refs[:ROW_PARTS], refs[ROW_PARTS : ROW_PARTS + HELD_PARTS]
    outs = refs[ROW_PARTS + HELD_PARTS : -2]
    total, x = refs[-2:]
    join_parts(x, parts)
    add_products(entry_ref, gain_ref, load_from(x), block_refs, total, True)
    core, along = place_ref[0], place_ref[1]
    size = outs[0].shape[1]
    for side, out_ref in enumerate(outs):
        for way in range(ways):
            at = ((core ^ side) * ways + (along ^ way)) * size
            out_ref[way] = total[pl.ds(at, size)].astype(out_ref.dtype)


def last_kernel(ways, entry_ref, gain_ref, place_ref, *refs):
    parts, block_refs = refs[:ROW_PARTS], refs[ROW_PARTS : ROW_PARTS + HELD_PARTS]
    out_ref, total, x = refs[ROW_PARTS + HELD_PARTS :]
    join_parts(x, parts)
    add_products(entry_ref, gain_ref, load_from(x), block_refs, total, True)
    core, along = place_ref[0], place_ref[1]
    share = out_ref.shape[2]
    for group in range(total.shape[0]):
        values = total[group].astype(out_ref.dtype)
        for index in range(2 * ways):
            piece = values[index * share : (index + 1) * share]
            out_ref[core ^ (index % 2), along ^ (index // 2), :, group * LANES : (group + 1) * LANES] = piece


def shards(strengths, blocks, pattern, level_gain):
    n_panel = lax.axis_size("panel")
    n_case = lax.axis_size("case")
    ways = n_panel // 2
    share, width = strengths.shape
    cases = share * n_panel
    slots = blocks.shape[0]
    col_blocks = width // B
    row_blocks = col_blocks * n_case // n_panel
    col_groups = col_blocks * PER
    row_groups = row_blocks * PER
    panel = lax.axis_index("panel")
    case = lax.axis_index("case")
    core = panel % 2
    along = panel // 2
    value = strengths.dtype
    row_cuts = spans(row_groups, ROW_PARTS)
    part_size = col_groups // n_panel

    place = jnp.stack([core, along]).astype(jnp.int32)
    first = jnp.stack([panel * row_blocks, case * col_blocks, 0]).astype(jnp.int32)
    entry = jnp.where(pattern[:, 2:3] < 0, jnp.array([0, 0, -1], jnp.int32), pattern - first).reshape(-1)
    held = [blocks[a : a + n] for a, n in spans(slots, HELD_PARTS)]

    smem = pl.BlockSpec(memory_space=pltpu.SMEM)
    vmem = pl.BlockSpec(memory_space=pltpu.VMEM)

    def product(kernel, vectors, outs, scratch):
        small = (entry, level_gain, place)
        return pl.pallas_call(
            functools.partial(kernel, ways),
            out_shape=[jax.ShapeDtypeStruct(shape, value) for shape in outs],
            in_specs=[smem] * len(small) + [vmem] * (len(vectors) + len(held)),
            out_specs=[vmem] * len(outs),
            scratch_shapes=scratch,
            compiler_params=pltpu.CompilerParams(vmem_limit_bytes=VMEM_LIMIT),
            cost_estimate=pl.CostEstimate(
                flops=2 * cases * slots * B * B, bytes_accessed=2 * slots * B * B, transcendentals=0
            ),
        )(*small, *vectors, *held)

    def scratch(groups, kind):
        return pltpu.VMEM((groups, cases, LANES), kind)

    rows_total, rows_held = scratch(row_groups, jnp.float32), scratch(row_groups, value)
    cols_total, cols_held = scratch(col_groups, jnp.float32), scratch(col_groups, value)
    flat = [pltpu.VMEM((cases, width), kind) for kind in (jnp.float32, value)]
    row_shapes = [(size, cases, LANES) for _, size in row_cuts]

    def over_case(parts):
        bits = [1 << b for b in range(n_case.bit_length() - 1)]
        parts = list(parts)
        for step in range(len(bits)):
            arrived = [swap(part, "case", bits[(step + i) % len(bits)]) for i, part in enumerate(parts)]
            parts = [add_up(part, one) for part, one in zip(parts, arrived)]
        return parts

    def scatter_panel(mine, theirs):
        return scatter_along(add_up(mine, swap(theirs, "panel", 1)))

    def scatter_along(summed):
        return add_up(summed[0], *[swap(summed[way], "panel", 2 * way) for way in range(1, ways)])

    def gather_panel(part):
        same = [part] + [swap(part, "panel", 2 * way) for way in range(1, ways)]
        return same + [swap(one, "panel", 1) for one in same]

    def own_cases(parts):
        whole = jnp.concatenate(parts)
        own = lax.dynamic_slice_in_dim(whole, case * (cases // n_case), cases // n_case, 1)
        return jnp.swapaxes(own, 0, 1).reshape(cases // n_case, row_groups * LANES)

    def own_share(pieces):
        own = jnp.stack([lax.dynamic_slice_in_dim(one, panel * share, share, 1) for one in pieces])
        own = own.reshape(2, ways, part_size, share, LANES)
        own = jnp.where(core == 1, own[::-1], own)
        bit = 1
        while bit < ways:
            flipped = own.reshape(2, ways // (2 * bit), 2, bit, *own.shape[2:])[:, :, ::-1].reshape(own.shape)
            own = jnp.where(along & bit != 0, flipped, own)
            bit *= 2
        return jnp.moveaxis(own, 3, 0).reshape(share, width)

    first_sums = over_case(product(first_kernel, gather_panel(strengths), row_shapes, [rows_total, *flat]))
    outs = [(ways, part_size, cases, LANES)] * 2
    pieces = gather_panel(scatter_panel(*product(adjoint_kernel, first_sums, outs, [cols_total, rows_held])))
    second_sums = over_case(product(forward_kernel, pieces, row_shapes, [rows_total, cols_held]))
    (by_share,) = product(last_kernel, second_sums, [(2, ways, share, width)], [cols_total, rows_held])
    summed = add_up(by_share[0], swap(by_share[1], "panel", 1))

    summed, first_sums, pieces, second_sums = lax.optimization_barrier((summed, first_sums, pieces, second_sums))
    adjoint_two = scatter_along(summed)
    forward_one = own_cases(first_sums)
    forward_two = own_cases(second_sums)
    adjoint_one = own_share(pieces)
    return (forward_one, adjoint_one, forward_two, adjoint_two)


def solution(mesh):
    in_specs = (
        P("panel", "case"),
        P(("panel", "case"), None, None),
        P(("panel", "case"), None),
        P(),
    )
    out_specs = (P("case", "panel"), P("panel", "case"), P("case", "panel"), P("panel", "case"))
    return jax.shard_map(shards, mesh=mesh, in_specs=in_specs, out_specs=out_specs, check_vma=False)
```

time: 104 us -> 98.4 us (0.946)
  starting transfers between devices: 54.4 us -> 31.2 us
  waiting for transfers between devices: 21.4 us -> 40.9 us
  local copies, waits for them, and re-layouts: 15 us -> 13.5 us
    ppermute x53 -> x30, starting transfers between devices: 54.4 us -> 31.2 us  [swap(): return lax.ppermute(value, axis, [(i, i ^ offset) for i in range(count)])]
    ppermute x53 -> x30, waiting for transfers between devices: 21.4 us -> 40.9 us  [swap(): return lax.ppermute(value, axis, [(i, i ^ offset) for i in range(count)])]
    dynamic_update_slice x8 -> x0, local copies, waits for them, and re-layouts: 5.42 us -> none  [shards(): lax.dynamic_update_slice_in_dim(stacked, one[None], panel ^ 2 * way + sid...]
    unnamed x24 -> x37, local copies, waits for them, and re-layouts: 1.62 us -> 6.96 us
    reshape x2 -> x0, local copies, waits for them, and re-layouts: 1.61 us -> none  [the longest x1 1.58 us: shards(): x = stacked.reshape(cases, width)]
    broadcast_in_dim x1 -> x0, local copies, waits for them, and re-layouts: 1.09 us -> none  [shards(): stacked = jnp.zeros((n_panel, share, width), value)]
  transfers between devices with their start and end apart: 53 -> 30, of which waited for: 26 -> 18; matrix products, arithmetic and copies ran while one was open for 14% -> 14% of each run, Pallas kernels for 0% -> 0%
where the time goes in v8:
time: 98.4 us; the launch traced here: 97.8 us
  waiting for transfers between devices  40.9 us (42%)
  starting transfers between devices  31.2 us (32%)
  local copies, waits for them, and re-layouts  13.5 us (14%)
  Pallas kernels  7.72 us (8%)
  other arithmetic  3.38 us (3%)
  between operations  1.02 us (1%)
    ppermute x30, waiting for transfers between devices, swap(): return lax.ppermute(value, axis, [(i, i ^ offset) for i in range(count)])  40.9 us
    ppermute x30, starting transfers between devices, swap(): return lax.ppermute(value, axis, [(i, i ^ offset) for i in range(count)])  31.2 us
    pallas_call x4, Pallas kernels, product(): pl.pallas_call(functools.partial(kernel, ways), out_shape=[jax.ShapeDtype...  7.72 us
    unnamed x37, local copies, waits for them, and re-layouts  6.96 us
    slice x1, local copies, waits for them, and re-layouts, shards(): held = [blocks[a:a + n] for a, n in spans(slots, HELD_PARTS)]  4 us
  transfers between devices with their start and end apart: 30, of which 18 were waited for; matrix products, arithmetic and copies ran while one was open for 14% of the time, Pallas kernels for 0%

profile of v8, /device:TPU:0, one launch (start us, length us, event | category | flops | bytes accessed | tf_op | source)
XLA Modules:
  0.0 97.8 jit_solution(7520958650604972039)
XLA Ops:
  0.6 3.1 %collective-permute-start = (bf16[4,12288]{1,0:T(4,128)(2,1)}, bf16[4,12288]{1,0:T(4,128)(2,1)S(1)}, u32[]{:S(2)}, u32[]{:S(2)}) collective-permute-start(bf16[4,12288]{1,0:T(4,128)(2,1)} %refs_0_.1), channel_id=1, source_target_pairs={{0,8},{4,12},{8,0},{12,4},{16,24},{20,28},{24,16},{28,20},{1,9},{5... | collective-permute-start | bytes 294920 | tf_op jit(solution)/shard_map/ppermute | solution.py:22
  3.7 2.6 %collective-permute-start.1 = (bf16[4,12288]{1,0:T(4,128)(2,1)}, bf16[4,12288]{1,0:T(4,128)(2,1)S(1)}, u32[]{:S(2)}, u32[]{:S(2)}) collective-permute-start(bf16[4,12288]{1,0:T(4,128)(2,1)} %refs_0_.1), channel_id=1, source_target_pairs={{0,16},{4,20},{8,24},{12,28},{16,0},{20,4},{24,8},{28,12},{1,17},{... | collective-permute-start | bytes 294920 | tf_op jit(solution)/shard_map/ppermute | solution.py:22
  7.0 4.0 %fusion.11 = (bf16[16,256,256]{2,1,0:T(8,128)(2,1)S(1)}, bf16[16,256,256]{2,1,0:T(8,128)(2,1)}) fusion(bf16[32,256,256]{2,1,0:T(8,128)(2,1)} %param.6), kind=kLoop, calls=%fused_computation.51 | loop fusion | bytes 8388608 | tf_op jit(solution)/shard_map/slice | solution.py:176
  12.0 2.4 %collective-permute-done.1.refs_2_ = bf16[4,12288]{1,0:T(4,128)(2,1)S(1)} collective-permute-done((bf16[4,12288]{1,0:T(4,128)(2,1)}, bf16[4,12288]{1,0:T(4,128)(2,1)S(1)}, u32[]{:S(2)}, u32[]{:S(2)}) %collective-permute-start.1) | collective-permute-done | bytes 98336 | tf_op jit(solution)/shard_map/ppermute | solution.py:22
  15.8 1.6 %copy-done = bf16[16,256,256]{2,1,0:T(8,128)(2,1)S(1)} copy-done((bf16[16,256,256]{2,1,0:T(8,128)(2,1)S(1)}, bf16[16,256,256]{2,1,0:T(8,128)(2,1)}, u32[]{:S(2)}) %copy-start) | copy-done | bytes 2097176
  17.4 2.5 %shard_map.84 = (bf16[24,32,128]{2,1,0:T(8,128)(2,1)S(1)}, bf16[24,32,128]{2,1,0:T(8,128)(2,1)S(1)}) custom-call(s32[96]{0:T(128)S(1)} %reshape.42.entry_ref, f32[8]{0:T(128)S(1)} %copy-done.12, s32[2]{0:T(128)S(1)} %pad_add_fusion.1.place_ref, bf16[4,12288]{1,0:T(4,128)(2,1)S(1)} %copy-done.11, bf16[4,12288]{1,0:T(4,128)(2,1)S(1)} %collective-permute-done.refs_1_, ...), custom_call_target="tpu_custom_call" | custom-call | flops 134217728 | bytes 4194304 | tf_op jit(solution)/shard_map/pallas_call | solution.py:183
  19.9 1.6 %collective-permute-start.9 = (bf16[24,32,128]{2,1,0:T(8,128)(2,1)S(1)}, bf16[24,32,128]{2,1,0:T(8,128)(2,1)S(1)}, u32[]{:S(2)}, u32[]{:S(2)}) collective-permute-start(bf16[24,32,128]{2,1,0:T(8,128)(2,1)S(1)} %get-tuple-element.24), channel_id=1, source_target_pairs={{0,2},{1,3},{2,0},{3,1},{4,6},{5,7},{6,4},{7,5},{8,10},{9,11},{10,... | collective-permute-start | bytes 589832 | tf_op jit(solution)/shard_map/ppermute | solution.py:22
  21.5 1.5 %collective-permute-start.7 = (bf16[24,32,128]{2,1,0:T(8,128)(2,1)S(1)}, bf16[24,32,128]{2,1,0:T(8,128)(2,1)S(1)}, u32[]{:S(2)}, u32[]{:S(2)}) collective-permute-start(bf16[24,32,128]{2,1,0:T(8,128)(2,1)S(1)} %get-tuple-element.23), channel_id=1, source_target_pairs={{0,1},{1,0},{2,3},{3,2},{4,5},{5,4},{6,7},{7,6},{8,9},{9,8},{10,11... | collective-permute-start | bytes 589832 | tf_op jit(solution)/shard_map/ppermute | solution.py:22
  23.0 4.1 %collective-permute-done.9 = bf16[24,32,128]{2,1,0:T(8,128)(2,1)S(1)} collective-permute-done((bf16[24,32,128]{2,1,0:T(8,128)(2,1)S(1)}, bf16[24,32,128]{2,1,0:T(8,128)(2,1)S(1)}, u32[]{:S(2)}, u32[]{:S(2)}) %collective-permute-start.9) | collective-permute-done | bytes 196640 | tf_op jit(solution)/shard_map/ppermute | solution.py:22
  27.2 1.6 %collective-permute-start.10 = (bf16[24,32,128]{2,1,0:T(8,128)(2,1)S(1)}, bf16[24,32,128]{2,1,0:T(8,128)(2,1)S(1)}, u32[]{:S(2)}, u32[]{:S(2)}) collective-permute-start(bf16[24,32,128]{2,1,0:T(8,128)(2,1)S(1)} %add_convert_fusion.6), channel_id=1, source_target_pairs={{0,1},{1,0},{2,3},{3,2},{4,5},{5,4},{6,7},{7,6},{8,9},{9,8},{10,11... | collective-permute-start | bytes 589832 | tf_op jit(solution)/shard_map/ppermute | solution.py:22
  28.8 1.6 %collective-permute-start.8 = (bf16[24,32,128]{2,1,0:T(8,128)(2,1)S(1)}, bf16[24,32,128]{2,1,0:T(8,128)(2,1)S(1)}, u32[]{:S(2)}, u32[]{:S(2)}) collective-permute-start(bf16[24,32,128]{2,1,0:T(8,128)(2,1)S(1)} %add_convert_fusion.8), channel_id=1, source_target_pairs={{0,2},{1,3},{2,0},{3,1},{4,6},{5,7},{6,4},{7,5},{8,10},{9,11},{10,... | collective-permute-start | bytes 589832 | tf_op jit(solution)/shard_map/ppermute | solution.py:22
  30.4 3.2 %collective-permute-done.10 = bf16[24,32,128]{2,1,0:T(8,128)(2,1)S(1)} collective-permute-done((bf16[24,32,128]{2,1,0:T(8,128)(2,1)S(1)}, bf16[24,32,128]{2,1,0:T(8,128)(2,1)S(1)}, u32[]{:S(2)}, u32[]{:S(2)}) %collective-permute-start.10) | collective-permute-done | bytes 196640 | tf_op jit(solution)/shard_map/ppermute | solution.py:22
  33.7 1.3 %collective-permute-done.8 = bf16[24,32,128]{2,1,0:T(8,128)(2,1)S(1)} collective-permute-done((bf16[24,32,128]{2,1,0:T(8,128)(2,1)S(1)}, bf16[24,32,128]{2,1,0:T(8,128)(2,1)S(1)}, u32[]{:S(2)}, u32[]{:S(2)}) %collective-permute-start.8) | collective-permute-done | bytes 196640 | tf_op jit(solution)/shard_map/ppermute | solution.py:22
  35.1 1.5 %shard_map.85 = (bf16[4,12,32,128]{3,2,1,0:T(8,128)(2,1)S(1)}, bf16[4,12,32,128]{3,2,1,0:T(8,128)(2,1)S(1)}) custom-call(s32[96]{0:T(128)S(1)} %reshape.42.entry_ref, f32[8]{0:T(128)S(1)} %copy-done.12, s32[2]{0:T(128)S(1)} %pad_add_fusion.1.place_ref, bf16[24,32,128]{2,1,0:T(8,128)(2,1)S(1)} %add_convert_fusion.7.refs_0_, ...), custom_call_target="tpu_custom_call" | custom-call | flops 134217728 | bytes 4194304 | tf_op jit(solution)/shard_map/pallas_call | solution.py:183
  36.6 1.7 %collective-permute-done.11 = bf16[4,12,32,128]{3,2,1,0:T(8,128)(2,1)S(1)} collective-permute-done((bf16[4,12,32,128]{3,2,1,0:T(8,128)(2,1)S(1)}, bf16[4,12,32,128]{3,2,1,0:T(8,128)(2,1)S(1)}, u32[]{:S(2)}, u32[]{:S(2)}) %collective-permute-start.11) | collective-permute-done | bytes 393248 | tf_op jit(solution)/shard_map/ppermute | solution.py:22
  39.6 2.0 %collective-permute-start.13 = (bf16[12,32,128]{2,1,0:T(8,128)(2,1)S(1)}, bf16[12,32,128]{2,1,0:T(8,128)(2,1)S(1)}, u32[]{:S(2)}, u32[]{:S(2)}) collective-permute-start(bf16[12,32,128]{2,1,0:T(8,128)(2,1)S(1)} %get-tuple-element.49), channel_id=1, source_target_pairs={{0,16},{4,20},{8,24},{12,28},{16,0},{20,4},{24,8},{28,12},{1,17},{... | collective-permute-start | bytes 294920 | tf_op jit(solution)/shard_map/ppermute | solution.py:22
  41.5 1.4 %collective-permute-start.14 = (bf16[12,32,128]{2,1,0:T(8,128)(2,1)S(1)}, bf16[12,32,128]{2,1,0:T(8,128)(2,1)S(1)}, u32[]{:S(2)}, u32[]{:S(2)}) collective-permute-start(bf16[12,32,128]{2,1,0:T(8,128)(2,1)S(1)} %get-tuple-element.48), channel_id=1, source_target_pairs={{0,24},{4,28},{8,16},{12,20},{16,8},{20,12},{24,0},{28,4},{1,25},{... | collective-permute-start | bytes 294920 | tf_op jit(solution)/shard_map/ppermute | solution.py:22
  42.9 1.7 %collective-permute-done.12 = bf16[12,32,128]{2,1,0:T(8,128)(2,1)S(1)} collective-permute-done((bf16[12,32,128]{2,1,0:T(8,128)(2,1)S(1)}, bf16[12,32,128]{2,1,0:T(8,128)(2,1)S(1)}, u32[]{:S(2)}, u32[]{:S(2)}) %collective-permute-start.12) | collective-permute-done | bytes 98336 | tf_op jit(solution)/shard_map/ppermute | solution.py:22
  44.6 5.6 %collective-permute-done.13 = bf16[12,32,128]{2,1,0:T(8,128)(2,1)S(1)} collective-permute-done((bf16[12,32,128]{2,1,0:T(8,128)(2,1)S(1)}, bf16[12,32,128]{2,1,0:T(8,128)(2,1)S(1)}, u32[]{:S(2)}, u32[]{:S(2)}) %collective-permute-start.13) | collective-permute-done | bytes 98336 | tf_op jit(solution)/shard_map/ppermute | solution.py:22
  50.3 1.8 %collective-permute-start.15 = (bf16[12,32,128]{2,1,0:T(8,128)(2,1)S(1)}, bf16[12,32,128]{2,1,0:T(8,128)(2,1)S(1)}, u32[]{:S(2)}, u32[]{:S(2)}) collective-permute-start(bf16[12,32,128]{2,1,0:T(8,128)(2,1)S(1)} %fusion.6.refs_0_), channel_id=1, source_target_pairs={{0,8},{4,12},{8,0},{12,4},{16,24},{20,28},{24,16},{28,20},{1,9},{5... | collective-permute-start | bytes 294920 | tf_op jit(solution)/shard_map/ppermute | solution.py:22
  53.1 1.6 %collective-permute-start.17 = (bf16[12,32,128]{2,1,0:T(8,128)(2,1)S(1)}, bf16[12,32,128]{2,1,0:T(8,128)(2,1)S(1)}, u32[]{:S(2)}, u32[]{:S(2)}) collective-permute-start(bf16[12,32,128]{2,1,0:T(8,128)(2,1)S(1)} %fusion.6.refs_0_), channel_id=1, source_target_pairs={{0,24},{4,28},{8,16},{12,20},{16,8},{20,12},{24,0},{28,4},{1,25},{... | collective-permute-start | bytes 294920 | tf_op jit(solution)/shard_map/ppermute | solution.py:22
  54.8 1.3 %collective-permute-done.15.refs_1_ = bf16[12,32,128]{2,1,0:T(8,128)(2,1)S(1)} collective-permute-done((bf16[12,32,128]{2,1,0:T(8,128)(2,1)S(1)}, bf16[12,32,128]{2,1,0:T(8,128)(2,1)S(1)}, u32[]{:S(2)}, u32[]{:S(2)}) %collective-permute-start.15) | collective-permute-done | bytes 98336 | tf_op jit(solution)/shard_map/ppermute | solution.py:22
  56.1 5.8 %collective-permute-done.16.refs_2_ = bf16[12,32,128]{2,1,0:T(8,128)(2,1)S(1)} collective-permute-done((bf16[12,32,128]{2,1,0:T(8,128)(2,1)S(1)}, bf16[12,32,128]{2,1,0:T(8,128)(2,1)S(1)}, u32[]{:S(2)}, u32[]{:S(2)}) %collective-permute-start.16) | collective-permute-done | bytes 98336 | tf_op jit(solution)/shard_map/ppermute | solution.py:22
  63.3 1.9 %shard_map.86 = (bf16[24,32,128]{2,1,0:T(8,128)(2,1)S(1)}, bf16[24,32,128]{2,1,0:T(8,128)(2,1)S(1)}) custom-call(s32[96]{0:T(128)S(1)} %reshape.42.entry_ref, f32[8]{0:T(128)S(1)} %copy-done.12, s32[2]{0:T(128)S(1)} %pad_add_fusion.1.place_ref, bf16[12,32,128]{2,1,0:T(8,128)(2,1)S(1)} %fusion.6.refs_0_, ...), custom_call_target="tpu_custom_call" | custom-call | flops 134217728 | bytes 4194304 | tf_op jit(solution)/shard_map/pallas_call | solution.py:183
  65.4 1.6 %collective-permute-start.24 = (bf16[24,32,128]{2,1,0:T(8,128)(2,1)S(1)}, bf16[24,32,128]{2,1,0:T(8,128)(2,1)S(1)}, u32[]{:S(2)}, u32[]{:S(2)}) collective-permute-start(bf16[24,32,128]{2,1,0:T(8,128)(2,1)S(1)} %get-tuple-element.28), channel_id=1, source_target_pairs={{0,2},{1,3},{2,0},{3,1},{4,6},{5,7},{6,4},{7,5},{8,10},{9,11},{10,... | collective-permute-start | bytes 589832 | tf_op jit(solution)/shard_map/ppermute | solution.py:22
  67.5 5.1 %collective-permute-done.24 = bf16[24,32,128]{2,1,0:T(8,128)(2,1)S(1)} collective-permute-done((bf16[24,32,128]{2,1,0:T(8,128)(2,1)S(1)}, bf16[24,32,128]{2,1,0:T(8,128)(2,1)S(1)}, u32[]{:S(2)}, u32[]{:S(2)}) %collective-permute-start.24) | collective-permute-done | bytes 196640 | tf_op jit(solution)/shard_map/ppermute | solution.py:22
  72.6 1.1 %collective-permute-start.25 = (bf16[24,32,128]{2,1,0:T(8,128)(2,1)S(1)}, bf16[24,32,128]{2,1,0:T(8,128)(2,1)S(1)}, u32[]{:S(2)}, u32[]{:S(2)}) collective-permute-start(bf16[24,32,128]{2,1,0:T(8,128)(2,1)S(1)} %add_convert_fusion.2), channel_id=1, source_target_pairs={{0,1},{1,0},{2,3},{3,2},{4,5},{5,4},{6,7},{7,6},{8,9},{9,8},{10,11... | collective-permute-start | bytes 589832 | tf_op jit(solution)/shard_map/ppermute | solution.py:22
  74.9 4.2 %collective-permute-done.25 = bf16[24,32,128]{2,1,0:T(8,128)(2,1)S(1)} collective-permute-done((bf16[24,32,128]{2,1,0:T(8,128)(2,1)S(1)}, bf16[24,32,128]{2,1,0:T(8,128)(2,1)S(1)}, u32[]{:S(2)}, u32[]{:S(2)}) %collective-permute-start.25) | collective-permute-done | bytes 196640 | tf_op jit(solution)/shard_map/ppermute | solution.py:22
  80.0 1.8 %shard_map.87 = bf16[2,4,4,12288]{3,2,1,0:T(4,128)(2,1)S(1)} custom-call(s32[96]{0:T(128)S(1)} %reshape.42.entry_ref, f32[8]{0:T(128)S(1)} %copy-done.12, s32[2]{0:T(128)S(1)} %pad_add_fusion.1.place_ref, bf16[24,32,128]{2,1,0:T(8,128)(2,1)S(1)} %add_convert_fusion.3.refs_0_, bf16[24,32,128]{2,1,0:T(8,128)(2,1)S(1)} %add_convert_fusion.1.refs_1_, ...), custom_call_target="tpu_custom_call" | custom-call | flops 134217728 | bytes 4194304 | tf_op jit(solution)/shard_map/pallas_call | solution.py:183
  82.1 1.7 %collective-permute-done.26 = bf16[4,4,12288]{2,1,0:T(4,128)(2,1)S(1)} collective-permute-done((bf16[4,4,12288]{2,1,0:T(4,128)(2,1)S(1)}, bf16[4,4,12288]{2,1,0:T(4,128)(2,1)S(1)}, u32[]{:S(2)}, u32[]{:S(2)}) %collective-permute-start.26) | collective-permute-done | bytes 393248 | tf_op jit(solution)/shard_map/ppermute | solution.py:22
  85.2 1.7 %collective-permute-start.28 = (bf16[4,12288]{1,0:T(4,128)(2,1)S(1)}, bf16[4,12288]{1,0:T(4,128)(2,1)S(1)}, u32[]{:S(2)}, u32[]{:S(2)}) collective-permute-start(bf16[4,12288]{1,0:T(4,128)(2,1)S(1)} %get-tuple-element.46), channel_id=1, source_target_pairs={{0,16},{4,20},{8,24},{12,28},{16,0},{20,4},{24,8},{28,12},{1,17},{... | collective-permute-start | bytes 294920 | tf_op jit(solution)/shard_map/ppermute | solution.py:22
  86.9 1.7 %collective-permute-start.29 = (bf16[4,12288]{1,0:T(4,128)(2,1)S(1)}, bf16[4,12288]{1,0:T(4,128)(2,1)S(1)}, u32[]{:S(2)}, u32[]{:S(2)}) collective-permute-start(bf16[4,12288]{1,0:T(4,128)(2,1)S(1)} %get-tuple-element.45), channel_id=1, source_target_pairs={{0,24},{4,28},{8,16},{12,20},{16,8},{20,12},{24,0},{28,4},{1,25},{... | collective-permute-start | bytes 294920 | tf_op jit(solution)/shard_map/ppermute | solution.py:22
  (101 shorter events, 20.6 us)
Async XLA Ops:
  0.6 10.8 %collective-permute-start = (bf16[4,12288]{1,0:T(4,128)(2,1)}, bf16[4,12288]{1,0:T(4,128)(2,1)S(1)}, u32[]{:S(2)}, u32[]{:S(2)}) collective-permute-start(bf16[4,12288]{1,0:T(4,128)(2,1)} %refs_0_.1), channel_id=1, source_target_pairs={{0,8},{4,12},{8,0},{12,4},{16,24},{20,28},{24,16},{28,20},{1,9},{5... | collective-permute-start | bytes 294920 | tf_op jit(solution)/shard_map/ppermute | solution.py:22
  3.7 10.6 %collective-permute-start.1 = (bf16[4,12288]{1,0:T(4,128)(2,1)}, bf16[4,12288]{1,0:T(4,128)(2,1)S(1)}, u32[]{:S(2)}, u32[]{:S(2)}) collective-permute-start(bf16[4,12288]{1,0:T(4,128)(2,1)} %refs_0_.1), channel_id=1, source_target_pairs={{0,16},{4,20},{8,24},{12,28},{16,0},{20,4},{24,8},{28,12},{1,17},{... | collective-permute-start | bytes 294920 | tf_op jit(solution)/shard_map/ppermute | solution.py:22
  6.3 8.1 %collective-permute-start.2 = (bf16[4,12288]{1,0:T(4,128)(2,1)}, bf16[4,12288]{1,0:T(4,128)(2,1)S(1)}, u32[]{:S(2)}, u32[]{:S(2)}) collective-permute-start(bf16[4,12288]{1,0:T(4,128)(2,1)} %refs_0_.1), channel_id=1, source_target_pairs={{0,24},{4,28},{8,16},{12,20},{16,8},{20,12},{24,0},{28,4},{1,25},{... | collective-permute-start | bytes 294920 | tf_op jit(solution)/shard_map/ppermute | solution.py:22
  6.3 8.6 %collective-permute-start.3 = (bf16[4,12288]{1,0:T(4,128)(2,1)}, bf16[4,12288]{1,0:T(4,128)(2,1)S(1)}, u32[]{:S(2)}, u32[]{:S(2)}) collective-permute-start(bf16[4,12288]{1,0:T(4,128)(2,1)} %refs_0_.1), channel_id=1, source_target_pairs={{0,4},{4,0},{8,12},{12,8},{16,20},{20,16},{24,28},{28,24},{1,5},{5... | collective-permute-start | bytes 294920 | tf_op jit(solution)/shard_map/ppermute | solution.py:22
  11.4 3.6 %collective-permute-start.4 = (bf16[4,12288]{1,0:T(4,128)(2,1)S(1)}, bf16[4,12288]{1,0:T(4,128)(2,1)S(1)}, u32[]{:S(2)}, u32[]{:S(2)}) collective-permute-start(bf16[4,12288]{1,0:T(4,128)(2,1)S(1)} %collective-permute-done.refs_1_), channel_id=1, source_target_pairs={{0,4},{4,0},{8,12},{12,8},{16,20},{20,16},{24,28},{28,24},{1,5},{5... | collective-permute-start | bytes 294920 | tf_op jit(solution)/shard_map/ppermute | solution.py:22
  14.4 1.3 %collective-permute-start.5 = (bf16[4,12288]{1,0:T(4,128)(2,1)S(1)}, bf16[4,12288]{1,0:T(4,128)(2,1)S(1)}, u32[]{:S(2)}, u32[]{:S(2)}) collective-permute-start(bf16[4,12288]{1,0:T(4,128)(2,1)S(1)} %collective-permute-done.1.refs_2_), channel_id=1, source_target_pairs={{0,4},{4,0},{8,12},{12,8},{16,20},{20,16},{24,28},{28,24},{1,5},{5... | collective-permute-start | bytes 294920 | tf_op jit(solution)/shard_map/ppermute | solution.py:22
  14.4 1.5 %collective-permute-start.6 = (bf16[4,12288]{1,0:T(4,128)(2,1)S(1)}, bf16[4,12288]{1,0:T(4,128)(2,1)S(1)}, u32[]{:S(2)}, u32[]{:S(2)}) collective-permute-start(bf16[4,12288]{1,0:T(4,128)(2,1)S(1)} %collective-permute-done.2.refs_3_), channel_id=1, source_target_pairs={{0,4},{4,0},{8,12},{12,8},{16,20},{20,16},{24,28},{28,24},{1,5},{5... | collective-permute-start | bytes 294920 | tf_op jit(solution)/shard_map/ppermute | solution.py:22
  19.9 7.2 %collective-permute-start.9 = (bf16[24,32,128]{2,1,0:T(8,128)(2,1)S(1)}, bf16[24,32,128]{2,1,0:T(8,128)(2,1)S(1)}, u32[]{:S(2)}, u32[]{:S(2)}) collective-permute-start(bf16[24,32,128]{2,1,0:T(8,128)(2,1)S(1)} %get-tuple-element.24), channel_id=1, source_target_pairs={{0,2},{1,3},{2,0},{3,1},{4,6},{5,7},{6,4},{7,5},{8,10},{9,11},{10,... | collective-permute-start | bytes 589832 | tf_op jit(solution)/shard_map/ppermute | solution.py:22
  21.5 7.3 %collective-permute-start.7 = (bf16[24,32,128]{2,1,0:T(8,128)(2,1)S(1)}, bf16[24,32,128]{2,1,0:T(8,128)(2,1)S(1)}, u32[]{:S(2)}, u32[]{:S(2)}) collective-permute-start(bf16[24,32,128]{2,1,0:T(8,128)(2,1)S(1)} %get-tuple-element.23), channel_id=1, source_target_pairs={{0,1},{1,0},{2,3},{3,2},{4,5},{5,4},{6,7},{7,6},{8,9},{9,8},{10,11... | collective-permute-start | bytes 589832 | tf_op jit(solution)/shard_map/ppermute | solution.py:22
  27.2 6.4 %collective-permute-start.10 = (bf16[24,32,128]{2,1,0:T(8,128)(2,1)S(1)}, bf16[24,32,128]{2,1,0:T(8,128)(2,1)S(1)}, u32[]{:S(2)}, u32[]{:S(2)}) collective-permute-start(bf16[24,32,128]{2,1,0:T(8,128)(2,1)S(1)} %add_convert_fusion.6), channel_id=1, source_target_pairs={{0,1},{1,0},{2,3},{3,2},{4,5},{5,4},{6,7},{7,6},{8,9},{9,8},{10,11... | collective-permute-start | bytes 589832 | tf_op jit(solution)/shard_map/ppermute | solution.py:22
  28.8 6.1 %collective-permute-start.8 = (bf16[24,32,128]{2,1,0:T(8,128)(2,1)S(1)}, bf16[24,32,128]{2,1,0:T(8,128)(2,1)S(1)}, u32[]{:S(2)}, u32[]{:S(2)}) collective-permute-start(bf16[24,32,128]{2,1,0:T(8,128)(2,1)S(1)} %add_convert_fusion.8), channel_id=1, source_target_pairs={{0,2},{1,3},{2,0},{3,1},{4,6},{5,7},{6,4},{7,5},{8,10},{9,11},{10,... | collective-permute-start | bytes 589832 | tf_op jit(solution)/shard_map/ppermute | solution.py:22
  36.5 1.8 %collective-permute-start.11 = (bf16[4,12,32,128]{3,2,1,0:T(8,128)(2,1)S(1)}, bf16[4,12,32,128]{3,2,1,0:T(8,128)(2,1)S(1)}, u32[]{:S(2)}, u32[]{:S(2)}) collective-permute-start(bf16[4,12,32,128]{3,2,1,0:T(8,128)(2,1)S(1)} %get-tuple-element.26), channel_id=1, source_target_pairs={{0,4},{4,0},{8,12},{12,8},{16,20},{20,16},{24,28},{28,24},{1,5},{5... | collective-permute-start | bytes 1179656 | tf_op jit(solution)/shard_map/ppermute | solution.py:22
  38.5 6.2 %collective-permute-start.12 = (bf16[12,32,128]{2,1,0:T(8,128)(2,1)S(1)}, bf16[12,32,128]{2,1,0:T(8,128)(2,1)S(1)}, u32[]{:S(2)}, u32[]{:S(2)}) collective-permute-start(bf16[12,32,128]{2,1,0:T(8,128)(2,1)S(1)} %get-tuple-element.47), channel_id=1, source_target_pairs={{0,8},{4,12},{8,0},{12,4},{16,24},{20,28},{24,16},{28,20},{1,9},{5... | collective-permute-start | bytes 294920 | tf_op jit(solution)/shard_map/ppermute | solution.py:22
  39.6 10.7 %collective-permute-start.13 = (bf16[12,32,128]{2,1,0:T(8,128)(2,1)S(1)}, bf16[12,32,128]{2,1,0:T(8,128)(2,1)S(1)}, u32[]{:S(2)}, u32[]{:S(2)}) collective-permute-start(bf16[12,32,128]{2,1,0:T(8,128)(2,1)S(1)} %get-tuple-element.49), channel_id=1, source_target_pairs={{0,16},{4,20},{8,24},{12,28},{16,0},{20,4},{24,8},{28,12},{1,17},{... | collective-permute-start | bytes 294920 | tf_op jit(solution)/shard_map/ppermute | solution.py:22
  41.5 8.7 %collective-permute-start.14 = (bf16[12,32,128]{2,1,0:T(8,128)(2,1)S(1)}, bf16[12,32,128]{2,1,0:T(8,128)(2,1)S(1)}, u32[]{:S(2)}, u32[]{:S(2)}) collective-permute-start(bf16[12,32,128]{2,1,0:T(8,128)(2,1)S(1)} %get-tuple-element.48), channel_id=1, source_target_pairs={{0,24},{4,28},{8,16},{12,20},{16,8},{20,12},{24,0},{28,4},{1,25},{... | collective-permute-start | bytes 294920 | tf_op jit(solution)/shard_map/ppermute | solution.py:22
  50.3 15.0 %copy-start.3 = (bf16[12,32,128]{2,1,0:T(8,128)(2,1)}, bf16[12,32,128]{2,1,0:T(8,128)(2,1)S(1)}, u32[]{:S(2)}) copy-start(bf16[12,32,128]{2,1,0:T(8,128)(2,1)S(1)} %fusion.6.refs_0_) | copy-start | bytes 294916
  50.3 5.7 %collective-permute-start.15 = (bf16[12,32,128]{2,1,0:T(8,128)(2,1)S(1)}, bf16[12,32,128]{2,1,0:T(8,128)(2,1)S(1)}, u32[]{:S(2)}, u32[]{:S(2)}) collective-permute-start(bf16[12,32,128]{2,1,0:T(8,128)(2,1)S(1)} %fusion.6.refs_0_), channel_id=1, source_target_pairs={{0,8},{4,12},{8,0},{12,4},{16,24},{20,28},{24,16},{28,20},{1,9},{5... | collective-permute-start | bytes 294920 | tf_op jit(solution)/shard_map/ppermute | solution.py:22
  52.1 9.8 %collective-permute-start.16 = (bf16[12,32,128]{2,1,0:T(8,128)(2,1)S(1)}, bf16[12,32,128]{2,1,0:T(8,128)(2,1)S(1)}, u32[]{:S(2)}, u32[]{:S(2)}) collective-permute-start(bf16[12,32,128]{2,1,0:T(8,128)(2,1)S(1)} %fusion.6.refs_0_), channel_id=1, source_target_pairs={{0,16},{4,20},{8,24},{12,28},{16,0},{20,4},{24,8},{28,12},{1,17},{... | collective-permute-start | bytes 294920 | tf_op jit(solution)/shard_map/ppermute | solution.py:22
  53.1 8.7 %collective-permute-start.17 = (bf16[12,32,128]{2,1,0:T(8,128)(2,1)S(1)}, bf16[12,32,128]{2,1,0:T(8,128)(2,1)S(1)}, u32[]{:S(2)}, u32[]{:S(2)}) collective-permute-start(bf16[12,32,128]{2,1,0:T(8,128)(2,1)S(1)} %fusion.6.refs_0_), channel_id=1, source_target_pairs={{0,24},{4,28},{8,16},{12,20},{16,8},{20,12},{24,0},{28,4},{1,25},{... | collective-permute-start | bytes 294920 | tf_op jit(solution)/shard_map/ppermute | solution.py:22
  54.8 7.6 %collective-permute-start.18 = (bf16[12,32,128]{2,1,0:T(8,128)(2,1)S(1)}, bf16[12,32,128]{2,1,0:T(8,128)(2,1)S(1)}, u32[]{:S(2)}, u32[]{:S(2)}) collective-permute-start(bf16[12,32,128]{2,1,0:T(8,128)(2,1)S(1)} %fusion.6.refs_0_), channel_id=1, source_target_pairs={{0,4},{4,0},{8,12},{12,8},{16,20},{20,16},{24,28},{28,24},{1,5},{5... | collective-permute-start | bytes 294920 | tf_op jit(solution)/shard_map/ppermute | solution.py:22
  56.1 6.3 %collective-permute-start.19 = (bf16[12,32,128]{2,1,0:T(8,128)(2,1)S(1)}, bf16[12,32,128]{2,1,0:T(8,128)(2,1)S(1)}, u32[]{:S(2)}, u32[]{:S(2)}) collective-permute-start(bf16[12,32,128]{2,1,0:T(8,128)(2,1)S(1)} %collective-permute-done.15.refs_1_), channel_id=1, source_target_pairs={{0,4},{4,0},{8,12},{12,8},{16,20},{20,16},{24,28},{28,24},{1,5},{5... | collective-permute-start | bytes 294920 | tf_op jit(solution)/shard_map/ppermute | solution.py:22
  61.9 1.3 %collective-permute-start.20 = (bf16[12,32,128]{2,1,0:T(8,128)(2,1)S(1)}, bf16[12,32,128]{2,1,0:T(8,128)(2,1)S(1)}, u32[]{:S(2)}, u32[]{:S(2)}) collective-permute-start(bf16[12,32,128]{2,1,0:T(8,128)(2,1)S(1)} %collective-permute-done.16.refs_2_), channel_id=1, source_target_pairs={{0,4},{4,0},{8,12},{12,8},{16,20},{20,16},{24,28},{28,24},{1,5},{5... | collective-permute-start | bytes 294920 | tf_op jit(solution)/shard_map/ppermute | solution.py:22
  61.9 1.4 %collective-permute-start.21 = (bf16[12,32,128]{2,1,0:T(8,128)(2,1)S(1)}, bf16[12,32,128]{2,1,0:T(8,128)(2,1)S(1)}, u32[]{:S(2)}, u32[]{:S(2)}) collective-permute-start(bf16[12,32,128]{2,1,0:T(8,128)(2,1)S(1)} %collective-permute-done.17.refs_3_), channel_id=1, source_target_pairs={{0,4},{4,0},{8,12},{12,8},{16,20},{20,16},{24,28},{28,24},{1,5},{5... | collective-permute-start | bytes 294920 | tf_op jit(solution)/shard_map/ppermute | solution.py:22
  65.4 7.2 %collective-permute-start.24 = (bf16[24,32,128]{2,1,0:T(8,128)(2,1)S(1)}, bf16[24,32,128]{2,1,0:T(8,128)(2,1)S(1)}, u32[]{:S(2)}, u32[]{:S(2)}) collective-permute-start(bf16[24,32,128]{2,1,0:T(8,128)(2,1)S(1)} %get-tuple-element.28), channel_id=1, source_target_pairs={{0,2},{1,3},{2,0},{3,1},{4,6},{5,7},{6,4},{7,5},{8,10},{9,11},{10,... | collective-permute-start | bytes 589832 | tf_op jit(solution)/shard_map/ppermute | solution.py:22
  66.9 6.9 %collective-permute-start.22 = (bf16[24,32,128]{2,1,0:T(8,128)(2,1)S(1)}, bf16[24,32,128]{2,1,0:T(8,128)(2,1)S(1)}, u32[]{:S(2)}, u32[]{:S(2)}) collective-permute-start(bf16[24,32,128]{2,1,0:T(8,128)(2,1)S(1)} %get-tuple-element.27), channel_id=1, source_target_pairs={{0,1},{1,0},{2,3},{3,2},{4,5},{5,4},{6,7},{7,6},{8,9},{9,8},{10,11... | collective-permute-start | bytes 589832 | tf_op jit(solution)/shard_map/ppermute | solution.py:22
  72.6 6.4 %collective-permute-start.25 = (bf16[24,32,128]{2,1,0:T(8,128)(2,1)S(1)}, bf16[24,32,128]{2,1,0:T(8,128)(2,1)S(1)}, u32[]{:S(2)}, u32[]{:S(2)}) collective-permute-start(bf16[24,32,128]{2,1,0:T(8,128)(2,1)S(1)} %add_convert_fusion.2), channel_id=1, source_target_pairs={{0,1},{1,0},{2,3},{3,2},{4,5},{5,4},{6,7},{7,6},{8,9},{9,8},{10,11... | collective-permute-start | bytes 589832 | tf_op jit(solution)/shard_map/ppermute | solution.py:22
  73.9 6.1 %collective-permute-start.23 = (bf16[24,32,128]{2,1,0:T(8,128)(2,1)S(1)}, bf16[24,32,128]{2,1,0:T(8,128)(2,1)S(1)}, u32[]{:S(2)}, u32[]{:S(2)}) collective-permute-start(bf16[24,32,128]{2,1,0:T(8,128)(2,1)S(1)} %add_convert_fusion.4), channel_id=1, source_target_pairs={{0,2},{1,3},{2,0},{3,1},{4,6},{5,7},{6,4},{7,5},{8,10},{9,11},{10,... | collective-permute-start | bytes 589832 | tf_op jit(solution)/shard_map/ppermute | solution.py:22
  81.9 13.6 %copy-start.2 = (bf16[24,32,128]{2,1,0:T(8,128)(2,1)S(1)}, bf16[24,32,128]{2,1,0:T(8,128)(2,1)}, u32[]{:S(2)}) copy-start(bf16[24,32,128]{2,1,0:T(8,128)(2,1)} %copy-done.1) | copy-start | bytes 589828
  82.0 1.8 %collective-permute-start.26 = (bf16[4,4,12288]{2,1,0:T(4,128)(2,1)S(1)}, bf16[4,4,12288]{2,1,0:T(4,128)(2,1)S(1)}, u32[]{:S(2)}, u32[]{:S(2)}) collective-permute-start(bf16[4,4,12288]{2,1,0:T(4,128)(2,1)S(1)} %slice_bitcast_fusion), channel_id=1, source_target_pairs={{0,4},{4,0},{8,12},{12,8},{16,20},{20,16},{24,28},{28,24},{1,5},{5... | collective-permute-start | bytes 1179656 | tf_op jit(solution)/shard_map/ppermute | solution.py:22
  84.1 12.9 %collective-permute-start.27 = (bf16[4,12288]{1,0:T(4,128)(2,1)S(1)}, bf16[4,12288]{1,0:T(4,128)(2,1)S(1)}, u32[]{:S(2)}, u32[]{:S(2)}) collective-permute-start(bf16[4,12288]{1,0:T(4,128)(2,1)S(1)} %get-tuple-element.44), channel_id=1, source_target_pairs={{0,8},{4,12},{8,0},{12,4},{16,24},{20,28},{24,16},{28,20},{1,9},{5... | collective-permute-start | bytes 294920 | tf_op jit(solution)/shard_map/ppermute | solution.py:22
  85.2 11.8 %collective-permute-start.28 = (bf16[4,12288]{1,0:T(4,128)(2,1)S(1)}, bf16[4,12288]{1,0:T(4,128)(2,1)S(1)}, u32[]{:S(2)}, u32[]{:S(2)}) collective-permute-start(bf16[4,12288]{1,0:T(4,128)(2,1)S(1)} %get-tuple-element.46), channel_id=1, source_target_pairs={{0,16},{4,20},{8,24},{12,28},{16,0},{20,4},{24,8},{28,12},{1,17},{... | collective-permute-start | bytes 294920 | tf_op jit(solution)/shard_map/ppermute | solution.py:22
  86.9 10.1 %collective-permute-start.29 = (bf16[4,12288]{1,0:T(4,128)(2,1)S(1)}, bf16[4,12288]{1,0:T(4,128)(2,1)S(1)}, u32[]{:S(2)}, u32[]{:S(2)}) collective-permute-start(bf16[4,12288]{1,0:T(4,128)(2,1)S(1)} %get-tuple-element.45), channel_id=1, source_target_pairs={{0,24},{4,28},{8,16},{12,20},{16,8},{20,12},{24,0},{28,4},{1,25},{... | collective-permute-start | bytes 294920 | tf_op jit(solution)/shard_map/ppermute | solution.py:22
  (13 other events, 55.1 us)

commit v9 on v8

--- a/solution.py
+++ b/solution.py
@@ -11,7 +11,7 @@
 B = 256
 LANES = 128
 PER = B // LANES
-HELD_PARTS = 2
+COPIES = 4
 ROW_PARTS = 2
 CHUNK = 1536
 VMEM_LIMIT = 12 * 1024 * 1024
@@ -32,6 +32,53 @@
 def spans(size, count):
     edges = [size * i // count for i in range(count + 1)]
     return [(a, b - a) for a, b in zip(edges, edges[1:])]
+
+
+def hold_kernel(blocks_ref, held_ref, sems):
+    copies = []
+    for i, (start, size) in enumerate(spans(blocks_ref.shape[0], COPIES)):
+        span = pl.ds(start, size)
+        copies.append(pltpu.make_async_copy(blocks_ref.at[span], held_ref.at[span], sems.at[i]))
+    for copy in copies:
+        copy.start()
+    for copy in copies:
+        copy.wait()
+
+
+def pick_rows(values, index, size):
+    values = values.astype(jnp.float32)
+    picked = values[:size]
+    for i in range(1, values.shape[0] // size):
+        picked = jnp.where(index == i, values[i * size : (i + 1) * size], picked)
+    return picked
+
+
+def cut_rows(place_ref, parts, out_ref):
+    at = 0
+    for part in parts:
+        for group in range(part.shape[0]):
+            picked = pick_rows(part[group], place_ref[2], out_ref.shape[0])
+            out_ref[:, at : at + LANES] = picked.astype(out_ref.dtype)
+            at += LANES
+
+
+def cut_kernel(ways, place_ref, *refs):
+    parts, pieces, (rows_ref, share_ref) = refs[:ROW_PARTS], refs[ROW_PARTS:-2], refs[-2:]
+    cut_rows(place_ref, parts, rows_ref)
+    core, along = place_ref[0], place_ref[1]
+    panel = along * 2 + core
+    for side in range(2):
+        for way in range(ways):
+            piece = pieces[side * ways + way]
+            at = ((core ^ side) * ways + (along ^ way)) * piece.shape[0]
+            for group in range(piece.shape[0]):
+                lanes = pl.ds(pl.multiple_of((at + group) * LANES, LANES), LANES)
+                picked = pick_rows(piece[group], panel, share_ref.shape[0])
+                share_ref[:, lanes] = picked.astype(share_ref.dtype)
+
+
+def cut_last_kernel(ways, place_ref, *refs):
+    cut_rows(place_ref, refs[:-1], refs[-1])
 
 
 def add_products(entry_ref, gain_ref, load, block_refs, total, adjoint):
@@ -79,7 +126,7 @@
 
 def first_kernel(ways, entry_ref, gain_ref, place_ref, *refs):
     count = 2 * ways
-    pieces, block_refs, outs = refs[:count], refs[count : count + HELD_PARTS], refs[count + HELD_PARTS : -3]
+    pieces, block_refs, outs = refs[:count], refs[count : count + 1], refs[count + 1 : -3]
     total, wide, x = refs[-3:]
     core, along = place_ref[0], place_ref[1]
     share, width = pieces[0].shape
@@ -111,7 +158,7 @@
 
 def forward_kernel(ways, entry_ref, gain_ref, place_ref, *refs):
     count = 2 * ways
-    pieces, block_refs, outs = refs[:count], refs[count : count + HELD_PARTS], refs[count + HELD_PARTS : -2]
+    pieces, block_refs, outs = refs[:count], refs[count : count + 1], refs[count + 1 : -2]
     total, x = refs[-2:]
     core, along = place_ref[0], place_ref[1]
     size = pieces[0].shape[0]
@@ -124,8 +171,8 @@
 
 
 def adjoint_kernel(ways, entry_ref, gain_ref, place_ref, *refs):
-    parts, block_refs = refs[:ROW_PARTS], refs[ROW_PARTS : ROW_PARTS + HELD_PARTS]
-    outs = refs[ROW_PARTS + HELD_PARTS : -2]
+    parts, block_refs = refs[:ROW_PARTS], refs[ROW_PARTS : ROW_PARTS + 1]
+    outs = refs[ROW_PARTS + 1 : -2]
     total, x = refs[-2:]
     join_parts(x, parts)
     add_products(entry_ref, gain_ref, load_from(x), block_refs, total, True)
@@ -138,8 +185,8 @@
 
 
 def last_kernel(ways, entry_ref, gain_ref, place_ref, *refs):
-    parts, block_refs = refs[:ROW_PARTS], refs[ROW_PARTS : ROW_PARTS + HELD_PARTS]
-    out_ref, total, x = refs[ROW_PARTS + HELD_PARTS :]
+    parts, block_refs = refs[:ROW_PARTS], refs[ROW_PARTS : ROW_PARTS + 1]
+    out_ref, total, x = refs[ROW_PARTS + 1 :]
     join_parts(x, parts)
     add_products(entry_ref, gain_ref, load_from(x), block_refs, total, True)
     core, along = place_ref[0], place_ref[1]
@@ -170,27 +217,47 @@
     row_cuts = spans(row_groups, ROW_PARTS)
     part_size = col_groups // n_panel
 
-    place = jnp.stack([core, along]).astype(jnp.int32)
+    place = jnp.stack([core, along, case]).astype(jnp.int32)
     first = jnp.stack([panel * row_blocks, case * col_blocks, 0]).astype(jnp.int32)
     entry = jnp.where(pattern[:, 2:3] < 0, jnp.array([0, 0, -1], jnp.int32), pattern - first).reshape(-1)
-    held = [blocks[a : a + n] for a, n in spans(slots, HELD_PARTS)]
 
     smem = pl.BlockSpec(memory_space=pltpu.SMEM)
     vmem = pl.BlockSpec(memory_space=pltpu.VMEM)
+
+    params = pltpu.CompilerParams(vmem_limit_bytes=VMEM_LIMIT)
+    held = pl.pallas_call(
+        hold_kernel,
+        out_shape=jax.ShapeDtypeStruct(blocks.shape, blocks.dtype),
+        in_specs=[pl.BlockSpec(memory_space=pl.ANY)],
+        out_specs=vmem,
+        scratch_shapes=[pltpu.SemaphoreType.DMA((COPIES,))],
+        compiler_params=params,
+        cost_estimate=pl.CostEstimate(flops=0, bytes_accessed=2 * slots * B * B, transcendentals=0),
+    )(blocks)
+
+    def cut(kernel, vectors, outs):
+        return pl.pallas_call(
+            functools.partial(kernel, ways),
+            out_shape=[jax.ShapeDtypeStruct(shape, value) for shape in outs],
+            in_specs=[smem] + [vmem] * len(vectors),
+            out_specs=[vmem] * len(outs),
+            compiler_params=params,
+            cost_estimate=pl.CostEstimate(flops=0, bytes_accessed=8 * share * width, transcendentals=0),
+        )(place, *vectors)
 
     def product(kernel, vectors, outs, scratch):
         small = (entry, level_gain, place)
         return pl.pallas_call(
             functools.partial(kernel, ways),
             out_shape=[jax.ShapeDtypeStruct(shape, value) for shape in outs],
-            in_specs=[smem] * len(small) + [vmem] * (len(vectors) + len(held)),
+            in_specs=[smem] * len(small) + [vmem] * (len(vectors) + 1),
             out_specs=[vmem] * len(outs),
             scratch_shapes=scratch,
-            compiler_params=pltpu.CompilerParams(vmem_limit_bytes=VMEM_LIMIT),
+            compiler_params=params,
             cost_estimate=pl.CostEstimate(
                 flops=2 * cases * slots * B * B, bytes_accessed=2 * slots * B * B, transcendentals=0
             ),
-        )(*small, *vectors, *held)
+        )(*small, *vectors, held)
 
     def scratch(groups, kind):
         return pltpu.VMEM((groups, cases, LANES), kind)
@@ -211,41 +278,32 @@
     def scatter_panel(mine, theirs):
         return scatter_along(add_up(mine, swap(theirs, "panel", 1)))
 
+    far_first = sorted(range(1, ways), key=lambda way: way & (ways // 2) == 0)
+
+    def along_swaps(part_of):
+        arrived = {way: swap(part_of(way), "panel", 2 * way) for way in far_first}
+        return [arrived[way] for way in range(1, ways)]
+
     def scatter_along(summed):
-        return add_up(summed[0], *[swap(summed[way], "panel", 2 * way) for way in range(1, ways)])
+        return add_up(summed[0], *along_swaps(lambda way: summed[way]))
 
     def gather_panel(part):
-        same = [part] + [swap(part, "panel", 2 * way) for way in range(1, ways)]
+        same = [part, *along_swaps(lambda way: part)]
         return same + [swap(one, "panel", 1) for one in same]
-
-    def own_cases(parts):
-        whole = jnp.concatenate(parts)
-        own = lax.dynamic_slice_in_dim(whole, case * (cases // n_case), cases // n_case, 1)
-        return jnp.swapaxes(own, 0, 1).reshape(cases // n_case, row_groups * LANES)
-
-    def own_share(pieces):
-        own = jnp.stack([lax.dynamic_slice_in_dim(one, panel * share, share, 1) for one in pieces])
-        own = own.reshape(2, ways, part_size, share, LANES)
-        own = jnp.where(core == 1, own[::-1], own)
-        bit = 1
-        while bit < ways:
-            flipped = own.reshape(2, ways // (2 * bit), 2, bit, *own.shape[2:])[:, :, ::-1].reshape(own.shape)
-            own = jnp.where(along & bit != 0, flipped, own)
-            bit *= 2
-        return jnp.moveaxis(own, 3, 0).reshape(share, width)
 
     first_sums = over_case(product(first_kernel, gather_panel(strengths), row_shapes, [rows_total, *flat]))
     outs = [(ways, part_size, cases, LANES)] * 2
     pieces = gather_panel(scatter_panel(*product(adjoint_kernel, first_sums, outs, [cols_total, rows_held])))
-    second_sums = over_case(product(forward_kernel, pieces, row_shapes, [rows_total, cols_held]))
+    sums = product(forward_kernel, pieces, row_shapes, [rows_total, cols_held])
+    rows_out, share_out = (cases // n_case, row_groups * LANES), (share, width)
+    sums, first_sums, pieces = lax.optimization_barrier((sums, first_sums, pieces))
+    forward_one, adjoint_one = cut(cut_kernel, [*first_sums, *pieces], [rows_out, share_out])
+    second_sums = over_case(sums)
     (by_share,) = product(last_kernel, second_sums, [(2, ways, share, width)], [cols_total, rows_held])
     summed = add_up(by_share[0], swap(by_share[1], "panel", 1))
-
-    summed, first_sums, pieces, second_sums = lax.optimization_barrier((summed, first_sums, pieces, second_sums))
+    summed, second_sums = lax.optimization_barrier((summed, second_sums))
     adjoint_two = scatter_along(summed)
-    forward_one = own_cases(first_sums)
-    forward_two = own_cases(second_sums)
-    adjoint_one = own_share(pieces)
+    (forward_two,) = cut(cut_last_kernel, second_sums, [rows_out])
     return (forward_one, adjoint_one, forward_two, adjoint_two)
 
 

time: 98.4 us -> 97.5 us (level)
  local copies, waits for them, and re-layouts: 13.5 us -> 6.81 us
  waiting for transfers between devices: 40.9 us -> 46.3 us
  Pallas kernels: 7.72 us -> 10.8 us
  starting transfers between devices: 31.2 us -> 29.3 us
    ppermute x30, waiting for transfers between devices: 40.9 us -> 46.3 us  [swap(): return lax.ppermute(value, axis, [(i, i ^ offset) for i in range(count)])]
    slice x1 -> x0, local copies, waits for them, and re-layouts: 4 us -> none  [shards(): held = [blocks[a:a + n] for a, n in spans(slots, HELD_PARTS)]]
    pallas_call x0 -> x3, Pallas kernels: none -> 3.1 us  [the longest x2 2.77 us: cut(): pl.pallas_call(functools.partial(kernel, ways), out_shape=[jax.ShapeDtype...]
    ppermute x30, starting transfers between devices: 31.2 us -> 29.3 us  [swap(): return lax.ppermute(value, axis, [(i, i ^ offset) for i in range(count)])]
    unnamed x37 -> x12, local copies, waits for them, and re-layouts: 6.96 us -> 6.35 us
  transfers between devices with their start and end apart: 30 -> 30, of which waited for: 18 -> 21; matrix products, arithmetic and copies ran while one was open for 14% -> 2% of each run, Pallas kernels for 0% -> 3%
where the time goes in v9:
time: 97.5 us; the launch traced here: 97.3 us
  waiting for transfers between devices  46.3 us (47%)
  starting transfers between devices  29.3 us (30%)
  Pallas kernels  10.8 us (11%)
  local copies, waits for them, and re-layouts  6.81 us (7%)
  other arithmetic  3.15 us (3%)
    ppermute x30, waiting for transfers between devices, swap(): return lax.ppermute(value, axis, [(i, i ^ offset) for i in range(count)])  46.3 us
    ppermute x30, starting transfers between devices, swap(): return lax.ppermute(value, axis, [(i, i ^ offset) for i in range(count)])  29.3 us
    pallas_call x4, Pallas kernels, product(): pl.pallas_call(functools.partial(kernel, ways), out_shape=[jax.ShapeDtype...  7.73 us
    unnamed x12, local copies, waits for them, and re-layouts  6.35 us
    pallas_call x2, Pallas kernels, cut(): pl.pallas_call(functools.partial(kernel, ways), out_shape=[jax.ShapeDtype...  2.77 us
  transfers between devices with their start and end apart: 30, of which 21 were waited for; matrix products, arithmetic and copies ran while one was open for 2% of the time, Pallas kernels for 3%

profile of v9, /device:TPU:0, one launch (start us, length us, event | category | flops | bytes accessed | tf_op | source)
XLA Modules:
  0.0 97.3 jit_solution(1426266322555334002)
XLA Ops:
  0.6 5.1 %collective-permute-start.2 = (bf16[4,12288]{1,0:T(4,128)(2,1)}, bf16[4,12288]{1,0:T(4,128)(2,1)S(1)}, u32[]{:S(2)}, u32[]{:S(2)}) collective-permute-start(bf16[4,12288]{1,0:T(4,128)(2,1)} %refs_0_.1), channel_id=1, source_target_pairs={{0,24},{4,28},{8,16},{12,20},{16,8},{20,12},{24,0},{28,4},{1,25},{... | collective-permute-start | bytes 294920 | tf_op jit(solution)/shard_map/ppermute | solution.py:22
  8.1 2.2 %copy-done.3 = bf16[32,256,256]{2,1,0:T(8,128)(2,1)S(1)} copy-done((bf16[32,256,256]{2,1,0:T(8,128)(2,1)S(1)}, bf16[32,256,256]{2,1,0:T(8,128)(2,1)}, u32[]{:S(2)}) %copy-start.3) | copy-done | bytes 4194328
  10.6 2.0 %copy-done = bf16[32,256,256]{2,1,0:T(8,128)(2,1)} copy-done((bf16[32,256,256]{2,1,0:T(8,128)(2,1)}, bf16[32,256,256]{2,1,0:T(8,128)(2,1)S(1)}, u32[]{:S(2)}) %copy-start) | copy-done | bytes 4194328
  15.7 2.2 %copy-done.1 = bf16[32,256,256]{2,1,0:T(8,128)(2,1)S(1)} copy-done((bf16[32,256,256]{2,1,0:T(8,128)(2,1)S(1)}, bf16[32,256,256]{2,1,0:T(8,128)(2,1)}, u32[]{:S(2)}) %copy-start.1) | copy-done | bytes 4194328
  17.9 2.5 %shard_map.85 = (bf16[24,32,128]{2,1,0:T(8,128)(2,1)S(1)}, bf16[24,32,128]{2,1,0:T(8,128)(2,1)S(1)}) custom-call(s32[96]{0:T(128)S(1)} %reshape.18.entry_ref, f32[8]{0:T(128)S(1)} %copy-done.5, s32[3]{0:T(128)S(1)} %pad_add_fusion.place_ref, bf16[4,12288]{1,0:T(4,128)(2,1)S(1)} %copy-done.4, bf16[4,12288]{1,0:T(4,128)(2,1)S(1)} %collective-permute-done.refs_1_, ...), custom_call_target="tpu_custom_call" | custom-call | flops 134217728 | bytes 4194304 | tf_op jit(solution)/shard_map/pallas_call | solution.py:250
  20.4 1.6 %collective-permute-start.7 = (bf16[24,32,128]{2,1,0:T(8,128)(2,1)S(1)}, bf16[24,32,128]{2,1,0:T(8,128)(2,1)S(1)}, u32[]{:S(2)}, u32[]{:S(2)}) collective-permute-start(bf16[24,32,128]{2,1,0:T(8,128)(2,1)S(1)} %get-tuple-element.27), channel_id=1, source_target_pairs={{0,1},{1,0},{2,3},{3,2},{4,5},{5,4},{6,7},{7,6},{8,9},{9,8},{10,11... | collective-permute-start | bytes 589832 | tf_op jit(solution)/shard_map/ppermute | solution.py:22
  21.9 1.5 %collective-permute-start.9 = (bf16[24,32,128]{2,1,0:T(8,128)(2,1)S(1)}, bf16[24,32,128]{2,1,0:T(8,128)(2,1)S(1)}, u32[]{:S(2)}, u32[]{:S(2)}) collective-permute-start(bf16[24,32,128]{2,1,0:T(8,128)(2,1)S(1)} %get-tuple-element.28), channel_id=1, source_target_pairs={{0,2},{1,3},{2,0},{3,1},{4,6},{5,7},{6,4},{7,5},{8,10},{9,11},{10,... | collective-permute-start | bytes 589832 | tf_op jit(solution)/shard_map/ppermute | solution.py:22
  23.4 4.2 %collective-permute-done.7 = bf16[24,32,128]{2,1,0:T(8,128)(2,1)S(1)} collective-permute-done((bf16[24,32,128]{2,1,0:T(8,128)(2,1)S(1)}, bf16[24,32,128]{2,1,0:T(8,128)(2,1)S(1)}, u32[]{:S(2)}, u32[]{:S(2)}) %collective-permute-start.7) | collective-permute-done | bytes 196640 | tf_op jit(solution)/shard_map/ppermute | solution.py:22
  27.7 1.6 %collective-permute-start.8 = (bf16[24,32,128]{2,1,0:T(8,128)(2,1)S(1)}, bf16[24,32,128]{2,1,0:T(8,128)(2,1)S(1)}, u32[]{:S(2)}, u32[]{:S(2)}) collective-permute-start(bf16[24,32,128]{2,1,0:T(8,128)(2,1)S(1)} %add_convert_fusion.8), channel_id=1, source_target_pairs={{0,2},{1,3},{2,0},{3,1},{4,6},{5,7},{6,4},{7,5},{8,10},{9,11},{10,... | collective-permute-start | bytes 589832 | tf_op jit(solution)/shard_map/ppermute | solution.py:22
  29.3 1.5 %collective-permute-start.10 = (bf16[24,32,128]{2,1,0:T(8,128)(2,1)S(1)}, bf16[24,32,128]{2,1,0:T(8,128)(2,1)S(1)}, u32[]{:S(2)}, u32[]{:S(2)}) collective-permute-start(bf16[24,32,128]{2,1,0:T(8,128)(2,1)S(1)} %add_convert_fusion.6), channel_id=1, source_target_pairs={{0,1},{1,0},{2,3},{3,2},{4,5},{5,4},{6,7},{7,6},{8,9},{9,8},{10,11... | collective-permute-start | bytes 589832 | tf_op jit(solution)/shard_map/ppermute | solution.py:22
  30.9 3.2 %collective-permute-done.8 = bf16[24,32,128]{2,1,0:T(8,128)(2,1)S(1)} collective-permute-done((bf16[24,32,128]{2,1,0:T(8,128)(2,1)S(1)}, bf16[24,32,128]{2,1,0:T(8,128)(2,1)S(1)}, u32[]{:S(2)}, u32[]{:S(2)}) %collective-permute-start.8) | collective-permute-done | bytes 196640 | tf_op jit(solution)/shard_map/ppermute | solution.py:22
  34.1 1.3 %collective-permute-done.10 = bf16[24,32,128]{2,1,0:T(8,128)(2,1)S(1)} collective-permute-done((bf16[24,32,128]{2,1,0:T(8,128)(2,1)S(1)}, bf16[24,32,128]{2,1,0:T(8,128)(2,1)S(1)}, u32[]{:S(2)}, u32[]{:S(2)}) %collective-permute-start.10) | collective-permute-done | bytes 196640 | tf_op jit(solution)/shard_map/ppermute | solution.py:22
  35.5 1.5 %shard_map.86 = (bf16[4,12,32,128]{3,2,1,0:T(8,128)(2,1)S(1)}, bf16[4,12,32,128]{3,2,1,0:T(8,128)(2,1)S(1)}) custom-call(s32[96]{0:T(128)S(1)} %reshape.18.entry_ref, f32[8]{0:T(128)S(1)} %copy-done.5, s32[3]{0:T(128)S(1)} %pad_add_fusion.place_ref, bf16[24,32,128]{2,1,0:T(8,128)(2,1)S(1)} %add_convert_fusion.7.refs_0_, ...), custom_call_target="tpu_custom_call" | custom-call | flops 134217728 | bytes 4194304 | tf_op jit(solution)/shard_map/pallas_call | solution.py:250
  37.1 1.7 %collective-permute-done.11 = bf16[4,12,32,128]{3,2,1,0:T(8,128)(2,1)S(1)} collective-permute-done((bf16[4,12,32,128]{3,2,1,0:T(8,128)(2,1)S(1)}, bf16[4,12,32,128]{3,2,1,0:T(8,128)(2,1)S(1)}, u32[]{:S(2)}, u32[]{:S(2)}) %collective-permute-start.11) | collective-permute-done | bytes 393248 | tf_op jit(solution)/shard_map/ppermute | solution.py:22
  39.2 2.5 %collective-permute-start.14 = (bf16[12,32,128]{2,1,0:T(8,128)(2,1)S(1)}, bf16[12,32,128]{2,1,0:T(8,128)(2,1)S(1)}, u32[]{:S(2)}, u32[]{:S(2)}) collective-permute-start(bf16[12,32,128]{2,1,0:T(8,128)(2,1)S(1)} %get-tuple-element.54), channel_id=1, source_target_pairs={{0,24},{4,28},{8,16},{12,20},{16,8},{20,12},{24,0},{28,4},{1,25},{... | collective-permute-start | bytes 294920 | tf_op jit(solution)/shard_map/ppermute | solution.py:22
  42.5 1.3 %collective-permute-done.12 = bf16[12,32,128]{2,1,0:T(8,128)(2,1)S(1)} collective-permute-done((bf16[12,32,128]{2,1,0:T(8,128)(2,1)S(1)}, bf16[12,32,128]{2,1,0:T(8,128)(2,1)S(1)}, u32[]{:S(2)}, u32[]{:S(2)}) %collective-permute-start.12) | collective-permute-done | bytes 98336 | tf_op jit(solution)/shard_map/ppermute | solution.py:22
  43.8 3.6 %collective-permute-done.14 = bf16[12,32,128]{2,1,0:T(8,128)(2,1)S(1)} collective-permute-done((bf16[12,32,128]{2,1,0:T(8,128)(2,1)S(1)}, bf16[12,32,128]{2,1,0:T(8,128)(2,1)S(1)}, u32[]{:S(2)}, u32[]{:S(2)}) %collective-permute-start.14) | collective-permute-done | bytes 98336 | tf_op jit(solution)/shard_map/ppermute | solution.py:22
  47.4 4.0 %collective-permute-done.13 = bf16[12,32,128]{2,1,0:T(8,128)(2,1)S(1)} collective-permute-done((bf16[12,32,128]{2,1,0:T(8,128)(2,1)S(1)}, bf16[12,32,128]{2,1,0:T(8,128)(2,1)S(1)}, u32[]{:S(2)}, u32[]{:S(2)}) %collective-permute-start.13) | collective-permute-done | bytes 98336 | tf_op jit(solution)/shard_map/ppermute | solution.py:22
  51.4 2.7 %collective-permute-start.17 = (bf16[12,32,128]{2,1,0:T(8,128)(2,1)S(1)}, bf16[12,32,128]{2,1,0:T(8,128)(2,1)S(1)}, u32[]{:S(2)}, u32[]{:S(2)}) collective-permute-start(bf16[12,32,128]{2,1,0:T(8,128)(2,1)S(1)} %fusion.6.refs_0_.refs_2_), channel_id=1, source_target_pairs={{0,24},{4,28},{8,16},{12,20},{16,8},{20,12},{24,0},{28,4},{1,25},{... | collective-permute-start | bytes 294920 | tf_op jit(solution)/shard_map/ppermute | solution.py:22
  54.1 1.8 %collective-permute-start.15 = (bf16[12,32,128]{2,1,0:T(8,128)(2,1)S(1)}, bf16[12,32,128]{2,1,0:T(8,128)(2,1)S(1)}, u32[]{:S(2)}, u32[]{:S(2)}) collective-permute-start(bf16[12,32,128]{2,1,0:T(8,128)(2,1)S(1)} %fusion.6.refs_0_.refs_2_), channel_id=1, source_target_pairs={{0,8},{4,12},{8,0},{12,4},{16,24},{20,28},{24,16},{28,20},{1,9},{5... | collective-permute-start | bytes 294920 | tf_op jit(solution)/shard_map/ppermute | solution.py:22
  55.9 3.2 %collective-permute-done.17.refs_3_.refs_5_ = bf16[12,32,128]{2,1,0:T(8,128)(2,1)S(1)} collective-permute-done((bf16[12,32,128]{2,1,0:T(8,128)(2,1)S(1)}, bf16[12,32,128]{2,1,0:T(8,128)(2,1)S(1)}, u32[]{:S(2)}, u32[]{:S(2)}) %collective-permute-start.17) | collective-permute-done | bytes 98336 | tf_op jit(solution)/shard_map/ppermute | solution.py:22
  59.1 2.8 %collective-permute-done.16.refs_2_.refs_4_ = bf16[12,32,128]{2,1,0:T(8,128)(2,1)S(1)} collective-permute-done((bf16[12,32,128]{2,1,0:T(8,128)(2,1)S(1)}, bf16[12,32,128]{2,1,0:T(8,128)(2,1)S(1)}, u32[]{:S(2)}, u32[]{:S(2)}) %collective-permute-start.16) | collective-permute-done | bytes 98336 | tf_op jit(solution)/shard_map/ppermute | solution.py:22
  63.4 2.0 %shard_map.87 = (bf16[24,32,128]{2,1,0:T(8,128)(2,1)S(1)}, bf16[24,32,128]{2,1,0:T(8,128)(2,1)S(1)}) custom-call(s32[96]{0:T(128)S(1)} %reshape.18.entry_ref, f32[8]{0:T(128)S(1)} %copy-done.5, s32[3]{0:T(128)S(1)} %pad_add_fusion.place_ref, bf16[12,32,128]{2,1,0:T(8,128)(2,1)S(1)} %fusion.6.refs_0_.refs_2_, ...), custom_call_target="tpu_custom_call" | custom-call | flops 134217728 | bytes 4194304 | tf_op jit(solution)/shard_map/pallas_call | solution.py:250
  65.4 1.6 %collective-permute-start.22 = (bf16[24,32,128]{2,1,0:T(8,128)(2,1)S(1)}, bf16[24,32,128]{2,1,0:T(8,128)(2,1)S(1)}, u32[]{:S(2)}, u32[]{:S(2)}) collective-permute-start(bf16[24,32,128]{2,1,0:T(8,128)(2,1)S(1)} %get-tuple-element.45), channel_id=1, source_target_pairs={{0,1},{1,0},{2,3},{3,2},{4,5},{5,4},{6,7},{7,6},{8,9},{9,8},{10,11... | collective-permute-start | bytes 589832 | tf_op jit(solution)/shard_map/ppermute | solution.py:22
  67.4 5.2 %collective-permute-done.22 = bf16[24,32,128]{2,1,0:T(8,128)(2,1)S(1)} collective-permute-done((bf16[24,32,128]{2,1,0:T(8,128)(2,1)S(1)}, bf16[24,32,128]{2,1,0:T(8,128)(2,1)S(1)}, u32[]{:S(2)}, u32[]{:S(2)}) %collective-permute-start.22) | collective-permute-done | bytes 196640 | tf_op jit(solution)/shard_map/ppermute | solution.py:22
  74.8 4.2 %collective-permute-done.23 = bf16[24,32,128]{2,1,0:T(8,128)(2,1)S(1)} collective-permute-done((bf16[24,32,128]{2,1,0:T(8,128)(2,1)S(1)}, bf16[24,32,128]{2,1,0:T(8,128)(2,1)S(1)}, u32[]{:S(2)}, u32[]{:S(2)}) %collective-permute-start.23) | collective-permute-done | bytes 196640 | tf_op jit(solution)/shard_map/ppermute | solution.py:22
  80.0 1.8 %shard_map.89 = bf16[2,4,4,12288]{3,2,1,0:T(4,128)(2,1)S(1)} custom-call(s32[96]{0:T(128)S(1)} %reshape.18.entry_ref, f32[8]{0:T(128)S(1)} %copy-done.5, s32[3]{0:T(128)S(1)} %pad_add_fusion.place_ref, bf16[24,32,128]{2,1,0:T(8,128)(2,1)S(1)} %add_convert_fusion.3.refs_0_, bf16[24,32,128]{2,1,0:T(8,128)(2,1)S(1)} %add_convert_fusion.1.refs_1_, ...), custom_call_target="tpu_custom_call" | custom-call | flops 134217728 | bytes 4194304 | tf_op jit(solution)/shard_map/pallas_call | solution.py:250
  82.1 1.7 %collective-permute-done.26 = bf16[4,4,12288]{2,1,0:T(4,128)(2,1)S(1)} collective-permute-done((bf16[4,4,12288]{2,1,0:T(4,128)(2,1)S(1)}, bf16[4,4,12288]{2,1,0:T(4,128)(2,1)S(1)}, u32[]{:S(2)}, u32[]{:S(2)}) %collective-permute-start.26) | collective-permute-done | bytes 393248 | tf_op jit(solution)/shard_map/ppermute | solution.py:22
  84.2 2.3 %collective-permute-start.29 = (bf16[4,12288]{1,0:T(4,128)(2,1)S(1)}, bf16[4,12288]{1,0:T(4,128)(2,1)S(1)}, u32[]{:S(2)}, u32[]{:S(2)}) collective-permute-start(bf16[4,12288]{1,0:T(4,128)(2,1)S(1)} %get-tuple-element.51), channel_id=1, source_target_pairs={{0,24},{4,28},{8,16},{12,20},{16,8},{20,12},{24,0},{28,4},{1,25},{... | collective-permute-start | bytes 294920 | tf_op jit(solution)/shard_map/ppermute | solution.py:22
  87.7 1.5 %shard_map.88 = (bf16[8,6144]{1,0:T(8,128)(2,1)}, bf16[4,12288]{1,0:T(4,128)(2,1)}) custom-call(s32[3]{0:T(128)S(1)} %pad_add_fusion.place_ref, bf16[24,32,128]{2,1,0:T(8,128)(2,1)S(1)} %add_convert_fusion.7.refs_0_, bf16[24,32,128]{2,1,0:T(8,128)(2,1)S(1)} %add_convert_fusion.5.refs_1_, bf16[12,32,128]{2,1,0:T(8,128)(2,1)S(1)} %fusion.6.refs_0_.refs_2_, ...), custom_call_target="tpu_custom_call" | custom-call | bytes 393216 | tf_op jit(solution)/shard_map/pallas_call | solution.py:239
  90.4 1.7 %collective-permute-done.29 = bf16[4,12288]{1,0:T(4,128)(2,1)S(1)} collective-permute-done((bf16[4,12288]{1,0:T(4,128)(2,1)S(1)}, bf16[4,12288]{1,0:T(4,128)(2,1)S(1)}, u32[]{:S(2)}, u32[]{:S(2)}) %collective-permute-start.29) | collective-permute-done | bytes 98336 | tf_op jit(solution)/shard_map/ppermute | solution.py:22
  92.1 4.4 %collective-permute-done.28 = bf16[4,12288]{1,0:T(4,128)(2,1)S(1)} collective-permute-done((bf16[4,12288]{1,0:T(4,128)(2,1)S(1)}, bf16[4,12288]{1,0:T(4,128)(2,1)S(1)}, u32[]{:S(2)}, u32[]{:S(2)}) %collective-permute-start.28) | collective-permute-done | bytes 98336 | tf_op jit(solution)/shard_map/ppermute | solution.py:22
  (68 shorter events, 16.2 us)
Async XLA Ops:
  0.6 12.0 %collective-permute-start.2 = (bf16[4,12288]{1,0:T(4,128)(2,1)}, bf16[4,12288]{1,0:T(4,128)(2,1)S(1)}, u32[]{:S(2)}, u32[]{:S(2)}) collective-permute-start(bf16[4,12288]{1,0:T(4,128)(2,1)} %refs_0_.1), channel_id=1, source_target_pairs={{0,24},{4,28},{8,16},{12,20},{16,8},{20,12},{24,0},{28,4},{1,25},{... | collective-permute-start | bytes 294920 | tf_op jit(solution)/shard_map/ppermute | solution.py:22
  5.7 8.5 %collective-permute-start.1 = (bf16[4,12288]{1,0:T(4,128)(2,1)}, bf16[4,12288]{1,0:T(4,128)(2,1)S(1)}, u32[]{:S(2)}, u32[]{:S(2)}) collective-permute-start(bf16[4,12288]{1,0:T(4,128)(2,1)} %refs_0_.1), channel_id=1, source_target_pairs={{0,16},{4,20},{8,24},{12,28},{16,0},{20,4},{24,8},{28,12},{1,17},{... | collective-permute-start | bytes 294920 | tf_op jit(solution)/shard_map/ppermute | solution.py:22
  5.7 8.5 %collective-permute-start = (bf16[4,12288]{1,0:T(4,128)(2,1)}, bf16[4,12288]{1,0:T(4,128)(2,1)S(1)}, u32[]{:S(2)}, u32[]{:S(2)}) collective-permute-start(bf16[4,12288]{1,0:T(4,128)(2,1)} %refs_0_.1), channel_id=1, source_target_pairs={{0,8},{4,12},{8,0},{12,4},{16,24},{20,28},{24,16},{28,20},{1,9},{5... | collective-permute-start | bytes 294920 | tf_op jit(solution)/shard_map/ppermute | solution.py:22
  6.4 8.4 %collective-permute-start.3 = (bf16[4,12288]{1,0:T(4,128)(2,1)}, bf16[4,12288]{1,0:T(4,128)(2,1)S(1)}, u32[]{:S(2)}, u32[]{:S(2)}) collective-permute-start(bf16[4,12288]{1,0:T(4,128)(2,1)} %refs_0_.1), channel_id=1, source_target_pairs={{0,4},{4,0},{8,12},{12,8},{16,20},{20,16},{24,28},{28,24},{1,5},{5... | collective-permute-start | bytes 294920 | tf_op jit(solution)/shard_map/ppermute | solution.py:22
  10.3 5.4 %copy-start.5 = (f32[8]{0:T(128)S(1)}, f32[8]{0:T(128)}, u32[]{:S(2)}) copy-start(f32[8]{0:T(128)} %gain_ref.7) | copy-start | bytes 100
  12.6 2.2 %collective-permute-start.6 = (bf16[4,12288]{1,0:T(4,128)(2,1)S(1)}, bf16[4,12288]{1,0:T(4,128)(2,1)S(1)}, u32[]{:S(2)}, u32[]{:S(2)}) collective-permute-start(bf16[4,12288]{1,0:T(4,128)(2,1)S(1)} %collective-permute-done.2.refs_3_), channel_id=1, source_target_pairs={{0,4},{4,0},{8,12},{12,8},{16,20},{20,16},{24,28},{28,24},{1,5},{5... | collective-permute-start | bytes 294920 | tf_op jit(solution)/shard_map/ppermute | solution.py:22
  14.2 1.3 %collective-permute-start.5 = (bf16[4,12288]{1,0:T(4,128)(2,1)S(1)}, bf16[4,12288]{1,0:T(4,128)(2,1)S(1)}, u32[]{:S(2)}, u32[]{:S(2)}) collective-permute-start(bf16[4,12288]{1,0:T(4,128)(2,1)S(1)} %collective-permute-done.1.refs_2_), channel_id=1, source_target_pairs={{0,4},{4,0},{8,12},{12,8},{16,20},{20,16},{24,28},{28,24},{1,5},{5... | collective-permute-start | bytes 294920 | tf_op jit(solution)/shard_map/ppermute | solution.py:22
  14.2 1.5 %collective-permute-start.4 = (bf16[4,12288]{1,0:T(4,128)(2,1)S(1)}, bf16[4,12288]{1,0:T(4,128)(2,1)S(1)}, u32[]{:S(2)}, u32[]{:S(2)}) collective-permute-start(bf16[4,12288]{1,0:T(4,128)(2,1)S(1)} %collective-permute-done.refs_1_), channel_id=1, source_target_pairs={{0,4},{4,0},{8,12},{12,8},{16,20},{20,16},{24,28},{28,24},{1,5},{5... | collective-permute-start | bytes 294920 | tf_op jit(solution)/shard_map/ppermute | solution.py:22
  20.4 7.2 %collective-permute-start.7 = (bf16[24,32,128]{2,1,0:T(8,128)(2,1)S(1)}, bf16[24,32,128]{2,1,0:T(8,128)(2,1)S(1)}, u32[]{:S(2)}, u32[]{:S(2)}) collective-permute-start(bf16[24,32,128]{2,1,0:T(8,128)(2,1)S(1)} %get-tuple-element.27), channel_id=1, source_target_pairs={{0,1},{1,0},{2,3},{3,2},{4,5},{5,4},{6,7},{7,6},{8,9},{9,8},{10,11... | collective-permute-start | bytes 589832 | tf_op jit(solution)/shard_map/ppermute | solution.py:22
  21.9 7.3 %collective-permute-start.9 = (bf16[24,32,128]{2,1,0:T(8,128)(2,1)S(1)}, bf16[24,32,128]{2,1,0:T(8,128)(2,1)S(1)}, u32[]{:S(2)}, u32[]{:S(2)}) collective-permute-start(bf16[24,32,128]{2,1,0:T(8,128)(2,1)S(1)} %get-tuple-element.28), channel_id=1, source_target_pairs={{0,2},{1,3},{2,0},{3,1},{4,6},{5,7},{6,4},{7,5},{8,10},{9,11},{10,... | collective-permute-start | bytes 589832 | tf_op jit(solution)/shard_map/ppermute | solution.py:22
  27.7 35.7 %copy-start.2 = (bf16[32,256,256]{2,1,0:T(8,128)(2,1)S(1)}, bf16[32,256,256]{2,1,0:T(8,128)(2,1)}, u32[]{:S(2)}) copy-start(bf16[32,256,256]{2,1,0:T(8,128)(2,1)} %copy-done) | copy-start | bytes 12582916
  27.7 6.4 %collective-permute-start.8 = (bf16[24,32,128]{2,1,0:T(8,128)(2,1)S(1)}, bf16[24,32,128]{2,1,0:T(8,128)(2,1)S(1)}, u32[]{:S(2)}, u32[]{:S(2)}) collective-permute-start(bf16[24,32,128]{2,1,0:T(8,128)(2,1)S(1)} %add_convert_fusion.8), channel_id=1, source_target_pairs={{0,2},{1,3},{2,0},{3,1},{4,6},{5,7},{6,4},{7,5},{8,10},{9,11},{10,... | collective-permute-start | bytes 589832 | tf_op jit(solution)/shard_map/ppermute | solution.py:22
  29.3 6.1 %collective-permute-start.10 = (bf16[24,32,128]{2,1,0:T(8,128)(2,1)S(1)}, bf16[24,32,128]{2,1,0:T(8,128)(2,1)S(1)}, u32[]{:S(2)}, u32[]{:S(2)}) collective-permute-start(bf16[24,32,128]{2,1,0:T(8,128)(2,1)S(1)} %add_convert_fusion.6), channel_id=1, source_target_pairs={{0,1},{1,0},{2,3},{3,2},{4,5},{5,4},{6,7},{7,6},{8,9},{9,8},{10,11... | collective-permute-start | bytes 589832 | tf_op jit(solution)/shard_map/ppermute | solution.py:22
  37.0 1.8 %collective-permute-start.11 = (bf16[4,12,32,128]{3,2,1,0:T(8,128)(2,1)S(1)}, bf16[4,12,32,128]{3,2,1,0:T(8,128)(2,1)S(1)}, u32[]{:S(2)}, u32[]{:S(2)}) collective-permute-start(bf16[4,12,32,128]{3,2,1,0:T(8,128)(2,1)S(1)} %get-tuple-element.30), channel_id=1, source_target_pairs={{0,4},{4,0},{8,12},{12,8},{16,20},{20,16},{24,28},{28,24},{1,5},{5... | collective-permute-start | bytes 1179656 | tf_op jit(solution)/shard_map/ppermute | solution.py:22
  38.9 4.9 %collective-permute-start.12 = (bf16[12,32,128]{2,1,0:T(8,128)(2,1)S(1)}, bf16[12,32,128]{2,1,0:T(8,128)(2,1)S(1)}, u32[]{:S(2)}, u32[]{:S(2)}) collective-permute-start(bf16[12,32,128]{2,1,0:T(8,128)(2,1)S(1)} %get-tuple-element.53), channel_id=1, source_target_pairs={{0,8},{4,12},{8,0},{12,4},{16,24},{20,28},{24,16},{28,20},{1,9},{5... | collective-permute-start | bytes 294920 | tf_op jit(solution)/shard_map/ppermute | solution.py:22
  39.2 8.2 %collective-permute-start.14 = (bf16[12,32,128]{2,1,0:T(8,128)(2,1)S(1)}, bf16[12,32,128]{2,1,0:T(8,128)(2,1)S(1)}, u32[]{:S(2)}, u32[]{:S(2)}) collective-permute-start(bf16[12,32,128]{2,1,0:T(8,128)(2,1)S(1)} %get-tuple-element.54), channel_id=1, source_target_pairs={{0,24},{4,28},{8,16},{12,20},{16,8},{20,12},{24,0},{28,4},{1,25},{... | collective-permute-start | bytes 294920 | tf_op jit(solution)/shard_map/ppermute | solution.py:22
  41.7 9.7 %collective-permute-start.13 = (bf16[12,32,128]{2,1,0:T(8,128)(2,1)S(1)}, bf16[12,32,128]{2,1,0:T(8,128)(2,1)S(1)}, u32[]{:S(2)}, u32[]{:S(2)}) collective-permute-start(bf16[12,32,128]{2,1,0:T(8,128)(2,1)S(1)} %get-tuple-element.55), channel_id=1, source_target_pairs={{0,16},{4,20},{8,24},{12,28},{16,0},{20,4},{24,8},{28,12},{1,17},{... | collective-permute-start | bytes 294920 | tf_op jit(solution)/shard_map/ppermute | solution.py:22
  51.4 7.6 %collective-permute-start.17 = (bf16[12,32,128]{2,1,0:T(8,128)(2,1)S(1)}, bf16[12,32,128]{2,1,0:T(8,128)(2,1)S(1)}, u32[]{:S(2)}, u32[]{:S(2)}) collective-permute-start(bf16[12,32,128]{2,1,0:T(8,128)(2,1)S(1)} %fusion.6.refs_0_.refs_2_), channel_id=1, source_target_pairs={{0,24},{4,28},{8,16},{12,20},{16,8},{20,12},{24,0},{28,4},{1,25},{... | collective-permute-start | bytes 294920 | tf_op jit(solution)/shard_map/ppermute | solution.py:22
  54.1 7.8 %collective-permute-start.16 = (bf16[12,32,128]{2,1,0:T(8,128)(2,1)S(1)}, bf16[12,32,128]{2,1,0:T(8,128)(2,1)S(1)}, u32[]{:S(2)}, u32[]{:S(2)}) collective-permute-start(bf16[12,32,128]{2,1,0:T(8,128)(2,1)S(1)} %fusion.6.refs_0_.refs_2_), channel_id=1, source_target_pairs={{0,16},{4,20},{8,24},{12,28},{16,0},{20,4},{24,8},{28,12},{1,17},{... | collective-permute-start | bytes 294920 | tf_op jit(solution)/shard_map/ppermute | solution.py:22
  54.1 7.8 %collective-permute-start.15 = (bf16[12,32,128]{2,1,0:T(8,128)(2,1)S(1)}, bf16[12,32,128]{2,1,0:T(8,128)(2,1)S(1)}, u32[]{:S(2)}, u32[]{:S(2)}) collective-permute-start(bf16[12,32,128]{2,1,0:T(8,128)(2,1)S(1)} %fusion.6.refs_0_.refs_2_), channel_id=1, source_target_pairs={{0,8},{4,12},{8,0},{12,4},{16,24},{20,28},{24,16},{28,20},{1,9},{5... | collective-permute-start | bytes 294920 | tf_op jit(solution)/shard_map/ppermute | solution.py:22
  55.9 6.6 %collective-permute-start.18 = (bf16[12,32,128]{2,1,0:T(8,128)(2,1)S(1)}, bf16[12,32,128]{2,1,0:T(8,128)(2,1)S(1)}, u32[]{:S(2)}, u32[]{:S(2)}) collective-permute-start(bf16[12,32,128]{2,1,0:T(8,128)(2,1)S(1)} %fusion.6.refs_0_.refs_2_), channel_id=1, source_target_pairs={{0,4},{4,0},{8,12},{12,8},{16,20},{20,16},{24,28},{28,24},{1,5},{5... | collective-permute-start | bytes 294920 | tf_op jit(solution)/shard_map/ppermute | solution.py:22
  59.1 3.4 %collective-permute-start.21 = (bf16[12,32,128]{2,1,0:T(8,128)(2,1)S(1)}, bf16[12,32,128]{2,1,0:T(8,128)(2,1)S(1)}, u32[]{:S(2)}, u32[]{:S(2)}) collective-permute-start(bf16[12,32,128]{2,1,0:T(8,128)(2,1)S(1)} %collective-permute-done.17.refs_3_.refs_5_), channel_id=1, source_target_pairs={{0,4},{4,0},{8,12},{12,8},{16,20},{20,16},{24,28},{28,24},{1,5},{5... | collective-permute-start | bytes 294920 | tf_op jit(solution)/shard_map/ppermute | solution.py:22
  61.9 1.3 %collective-permute-start.20 = (bf16[12,32,128]{2,1,0:T(8,128)(2,1)S(1)}, bf16[12,32,128]{2,1,0:T(8,128)(2,1)S(1)}, u32[]{:S(2)}, u32[]{:S(2)}) collective-permute-start(bf16[12,32,128]{2,1,0:T(8,128)(2,1)S(1)} %collective-permute-done.16.refs_2_.refs_4_), channel_id=1, source_target_pairs={{0,4},{4,0},{8,12},{12,8},{16,20},{20,16},{24,28},{28,24},{1,5},{5... | collective-permute-start | bytes 294920 | tf_op jit(solution)/shard_map/ppermute | solution.py:22
  62.0 1.4 %collective-permute-start.19 = (bf16[12,32,128]{2,1,0:T(8,128)(2,1)S(1)}, bf16[12,32,128]{2,1,0:T(8,128)(2,1)S(1)}, u32[]{:S(2)}, u32[]{:S(2)}) collective-permute-start(bf16[12,32,128]{2,1,0:T(8,128)(2,1)S(1)} %collective-permute-done.15.refs_1_.refs_3_), channel_id=1, source_target_pairs={{0,4},{4,0},{8,12},{12,8},{16,20},{20,16},{24,28},{28,24},{1,5},{5... | collective-permute-start | bytes 294920 | tf_op jit(solution)/shard_map/ppermute | solution.py:22
  65.4 7.2 %collective-permute-start.22 = (bf16[24,32,128]{2,1,0:T(8,128)(2,1)S(1)}, bf16[24,32,128]{2,1,0:T(8,128)(2,1)S(1)}, u32[]{:S(2)}, u32[]{:S(2)}) collective-permute-start(bf16[24,32,128]{2,1,0:T(8,128)(2,1)S(1)} %get-tuple-element.45), channel_id=1, source_target_pairs={{0,1},{1,0},{2,3},{3,2},{4,5},{5,4},{6,7},{7,6},{8,9},{9,8},{10,11... | collective-permute-start | bytes 589832 | tf_op jit(solution)/shard_map/ppermute | solution.py:22
  66.9 6.9 %collective-permute-start.24 = (bf16[24,32,128]{2,1,0:T(8,128)(2,1)S(1)}, bf16[24,32,128]{2,1,0:T(8,128)(2,1)S(1)}, u32[]{:S(2)}, u32[]{:S(2)}) collective-permute-start(bf16[24,32,128]{2,1,0:T(8,128)(2,1)S(1)} %get-tuple-element.46), channel_id=1, source_target_pairs={{0,2},{1,3},{2,0},{3,1},{4,6},{5,7},{6,4},{7,5},{8,10},{9,11},{10,... | collective-permute-start | bytes 589832 | tf_op jit(solution)/shard_map/ppermute | solution.py:22
  72.7 6.4 %collective-permute-start.23 = (bf16[24,32,128]{2,1,0:T(8,128)(2,1)S(1)}, bf16[24,32,128]{2,1,0:T(8,128)(2,1)S(1)}, u32[]{:S(2)}, u32[]{:S(2)}) collective-permute-start(bf16[24,32,128]{2,1,0:T(8,128)(2,1)S(1)} %add_convert_fusion.4), channel_id=1, source_target_pairs={{0,2},{1,3},{2,0},{3,1},{4,6},{5,7},{6,4},{7,5},{8,10},{9,11},{10,... | collective-permute-start | bytes 589832 | tf_op jit(solution)/shard_map/ppermute | solution.py:22
  73.9 6.1 %collective-permute-start.25 = (bf16[24,32,128]{2,1,0:T(8,128)(2,1)S(1)}, bf16[24,32,128]{2,1,0:T(8,128)(2,1)S(1)}, u32[]{:S(2)}, u32[]{:S(2)}) collective-permute-start(bf16[24,32,128]{2,1,0:T(8,128)(2,1)S(1)} %add_convert_fusion.2), channel_id=1, source_target_pairs={{0,1},{1,0},{2,3},{3,2},{4,5},{5,4},{6,7},{7,6},{8,9},{9,8},{10,11... | collective-permute-start | bytes 589832 | tf_op jit(solution)/shard_map/ppermute | solution.py:22
  82.0 1.8 %collective-permute-start.26 = (bf16[4,4,12288]{2,1,0:T(4,128)(2,1)S(1)}, bf16[4,4,12288]{2,1,0:T(4,128)(2,1)S(1)}, u32[]{:S(2)}, u32[]{:S(2)}) collective-permute-start(bf16[4,4,12288]{2,1,0:T(4,128)(2,1)S(1)} %slice_bitcast_fusion), channel_id=1, source_target_pairs={{0,4},{4,0},{8,12},{12,8},{16,20},{20,16},{24,28},{28,24},{1,5},{5... | collective-permute-start | bytes 1179656 | tf_op jit(solution)/shard_map/ppermute | solution.py:22
  84.1 6.3 %collective-permute-start.27 = (bf16[4,12288]{1,0:T(4,128)(2,1)S(1)}, bf16[4,12288]{1,0:T(4,128)(2,1)S(1)}, u32[]{:S(2)}, u32[]{:S(2)}) collective-permute-start(bf16[4,12288]{1,0:T(4,128)(2,1)S(1)} %get-tuple-element.50), channel_id=1, source_target_pairs={{0,8},{4,12},{8,0},{12,4},{16,24},{20,28},{24,16},{28,20},{1,9},{5... | collective-permute-start | bytes 294920 | tf_op jit(solution)/shard_map/ppermute | solution.py:22
  84.2 8.0 %collective-permute-start.29 = (bf16[4,12288]{1,0:T(4,128)(2,1)S(1)}, bf16[4,12288]{1,0:T(4,128)(2,1)S(1)}, u32[]{:S(2)}, u32[]{:S(2)}) collective-permute-start(bf16[4,12288]{1,0:T(4,128)(2,1)S(1)} %get-tuple-element.51), channel_id=1, source_target_pairs={{0,24},{4,28},{8,16},{12,20},{16,8},{20,12},{24,0},{28,4},{1,25},{... | collective-permute-start | bytes 294920 | tf_op jit(solution)/shard_map/ppermute | solution.py:22
  86.4 10.1 %collective-permute-start.28 = (bf16[4,12288]{1,0:T(4,128)(2,1)S(1)}, bf16[4,12288]{1,0:T(4,128)(2,1)S(1)}, u32[]{:S(2)}, u32[]{:S(2)}) collective-permute-start(bf16[4,12288]{1,0:T(4,128)(2,1)S(1)} %get-tuple-element.52), channel_id=1, source_target_pairs={{0,16},{4,20},{8,24},{12,28},{16,0},{20,4},{24,8},{28,12},{1,17},{... | collective-permute-start | bytes 294920 | tf_op jit(solution)/shard_map/ppermute | solution.py:22
  (4 other events, 11.7 us)

commit v10 on v9

--- a/solution.py
+++ b/solution.py
@@ -13,8 +13,9 @@
 PER = B // LANES
 COPIES = 4
 ROW_PARTS = 2
-CHUNK = 1536
+CHUNK = 768
 VMEM_LIMIT = 12 * 1024 * 1024
+FIRST_LIMIT = 50 * 1024 * 1024
 
 
 def swap(value, axis, offset):
@@ -34,15 +35,13 @@
     return [(a, b - a) for a, b in zip(edges, edges[1:])]
 
 
-def hold_kernel(blocks_ref, held_ref, sems):
+def start_hold(blocks_ref, held_ref, sems):
     copies = []
     for i, (start, size) in enumerate(spans(blocks_ref.shape[0], COPIES)):
         span = pl.ds(start, size)
         copies.append(pltpu.make_async_copy(blocks_ref.at[span], held_ref.at[span], sems.at[i]))
-    for copy in copies:
-        copy.start()
-    for copy in copies:
-        copy.wait()
+        copies[-1].start()
+    return [(start, copy) for (start, _), copy in zip(spans(blocks_ref.shape[0], COPIES), copies)]
 
 
 def pick_rows(values, index, size):
@@ -81,11 +80,14 @@
     cut_rows(place_ref, refs[:-1], refs[-1])
 
 
-def add_products(entry_ref, gain_ref, load, block_refs, total, adjoint):
+def add_products(entry_ref, gain_ref, load, block_refs, total, adjoint, copies=()):
     total[...] = jnp.zeros_like(total)
     at = 0
     for block_ref in block_refs:
         for slot in range(block_ref.shape[0]):
+            for start, copy in copies:
+                if start == slot:
+                    copy.wait()
             row, col, level = entry_ref[at], entry_ref[at + 1], entry_ref[at + 2]
             at += 3
             scale = jnp.where(level >= 0, gain_ref[jnp.maximum(level, 0)], jnp.float32(0.0))
@@ -126,8 +128,9 @@
 
 def first_kernel(ways, entry_ref, gain_ref, place_ref, *refs):
     count = 2 * ways
-    pieces, block_refs, outs = refs[:count], refs[count : count + 1], refs[count + 1 : -3]
-    total, wide, x = refs[-3:]
+    pieces, blocks_ref, outs = refs[:count], refs[count], refs[count + 1 : -5]
+    total, wide, x, held_ref, sems = refs[-5:]
+    copies = start_hold(blocks_ref, held_ref, sems)
     core, along = place_ref[0], place_ref[1]
     share, width = pieces[0].shape
     chunk = math.gcd(width, CHUNK)
@@ -152,7 +155,7 @@
     def load(block):
         return x[:, pl.ds(pl.multiple_of(block * B, B), B)]
 
-    add_products(entry_ref, gain_ref, load, block_refs, total, False)
+    add_products(entry_ref, gain_ref, load, [held_ref], total, False, copies)
     write_parts(total, outs)
 
 
@@ -225,16 +228,6 @@
     vmem = pl.BlockSpec(memory_space=pltpu.VMEM)
 
     params = pltpu.CompilerParams(vmem_limit_bytes=VMEM_LIMIT)
-    held = pl.pallas_call(
-        hold_kernel,
-        out_shape=jax.ShapeDtypeStruct(blocks.shape, blocks.dtype),
-        in_specs=[pl.BlockSpec(memory_space=pl.ANY)],
-        out_specs=vmem,
-        scratch_shapes=[pltpu.SemaphoreType.DMA((COPIES,))],
-        compiler_params=params,
-        cost_estimate=pl.CostEstimate(flops=0, bytes_accessed=2 * slots * B * B, transcendentals=0),
-    )(blocks)
-
     def cut(kernel, vectors, outs):
         return pl.pallas_call(
             functools.partial(kernel, ways),
@@ -245,19 +238,19 @@
             cost_estimate=pl.CostEstimate(flops=0, bytes_accessed=8 * share * width, transcendentals=0),
         )(place, *vectors)
 
-    def product(kernel, vectors, outs, scratch):
+    def product(kernel, vectors, outs, scratch, limit=VMEM_LIMIT, space=pltpu.VMEM):
         small = (entry, level_gain, place)
         return pl.pallas_call(
             functools.partial(kernel, ways),
             out_shape=[jax.ShapeDtypeStruct(shape, value) for shape in outs],
-            in_specs=[smem] * len(small) + [vmem] * (len(vectors) + 1),
+            in_specs=[smem] * len(small) + [vmem] * len(vectors) + [pl.BlockSpec(memory_space=space)],
             out_specs=[vmem] * len(outs),
             scratch_shapes=scratch,
-            compiler_params=params,
+            compiler_params=pltpu.CompilerParams(vmem_limit_bytes=limit),
             cost_estimate=pl.CostEstimate(
                 flops=2 * cases * slots * B * B, bytes_accessed=2 * slots * B * B, transcendentals=0
             ),
-        )(*small, *vectors, held)
+        )(*small, *vectors, blocks)
 
     def scratch(groups, kind):
         return pltpu.VMEM((groups, cases, LANES), kind)
@@ -291,7 +284,11 @@
         same = [part, *along_swaps(lambda way: part)]
         return same + [swap(one, "panel", 1) for one in same]
 
-    first_sums = over_case(product(first_kernel, gather_panel(strengths), row_shapes, [rows_total, *flat]))
+    own_copy = [pltpu.VMEM(blocks.shape, blocks.dtype), pltpu.SemaphoreType.DMA((COPIES,))]
+    scratches = [rows_total, *flat, *own_copy]
+    first_sums = over_case(
+        product(first_kernel, gather_panel(strengths), row_shapes, scratches, FIRST_LIMIT, pl.ANY)
+    )
     outs = [(ways, part_size, cases, LANES)] * 2
     pieces = gather_panel(scatter_panel(*product(adjoint_kernel, first_sums, outs, [cols_total, rows_held])))
     sums = product(forward_kernel, pieces, row_shapes, [rows_total, cols_held])

time: 97.5 us -> 97.7 us (level)
  waiting for transfers between devices: 46.3 us -> 51.1 us
  local copies, waits for them, and re-layouts: 6.81 us -> 2.01 us
    unnamed x12 -> x6, local copies, waits for them, and re-layouts: 6.35 us -> 1.55 us
    ppermute x30, waiting for transfers between devices: 46.3 us -> 51.1 us  [swap(): return lax.ppermute(value, axis, [(i, i ^ offset) for i in range(count)])]
    pallas_call x4, Pallas kernels: 7.73 us -> 8.82 us  [product(): pl.pallas_call(functools.partial(kernel, ways), out_shape=[jax.ShapeDtype...]
where the time goes in v10:
time: 97.7 us; the launch traced here: 97.5 us
  waiting for transfers between devices  51.1 us (52%)
  starting transfers between devices  28.9 us (30%)
  Pallas kernels  11.6 us (12%)
  other arithmetic  3.15 us (3%)
  local copies, waits for them, and re-layouts  2.01 us (2%)
    ppermute x30, waiting for transfers between devices, swap(): return lax.ppermute(value, axis, [(i, i ^ offset) for i in range(count)])  51.1 us
    ppermute x30, starting transfers between devices, swap(): return lax.ppermute(value, axis, [(i, i ^ offset) for i in range(count)])  28.9 us
    pallas_call x4, Pallas kernels, product(): pl.pallas_call(functools.partial(kernel, ways), out_shape=[jax.ShapeDtype...  8.82 us
    pallas_call x2, Pallas kernels, cut(): pl.pallas_call(functools.partial(kernel, ways), out_shape=[jax.ShapeDtype...  2.77 us
  transfers between devices with their start and end apart: 30, of which 21 were waited for; matrix products, arithmetic and copies ran while one was open for 2% of the time, Pallas kernels for 3%

profile of v10, /device:TPU:0, one launch (start us, length us, event | category | flops | bytes accessed | tf_op | source)
XLA Modules:
  0.0 97.5 jit_solution(5106675993999110753)
XLA Ops:
  0.6 5.1 %collective-permute-start.2 = (bf16[4,12288]{1,0:T(4,128)(2,1)}, bf16[4,12288]{1,0:T(4,128)(2,1)S(1)}, u32[]{:S(2)}, u32[]{:S(2)}) collective-permute-start(bf16[4,12288]{1,0:T(4,128)(2,1)} %refs_0_.1), channel_id=1, source_target_pairs={{0,24},{4,28},{8,16},{12,20},{16,8},{20,12},{24,0},{28,4},{1,25},{... | collective-permute-start | bytes 294920 | tf_op jit(solution)/shard_map/ppermute | solution.py:23
  8.1 1.5 %collective-permute-done.2.refs_3_ = bf16[4,12288]{1,0:T(4,128)(2,1)S(1)} collective-permute-done((bf16[4,12288]{1,0:T(4,128)(2,1)}, bf16[4,12288]{1,0:T(4,128)(2,1)S(1)}, u32[]{:S(2)}, u32[]{:S(2)}) %collective-permute-start.2) | collective-permute-done | bytes 98336 | tf_op jit(solution)/shard_map/ppermute | solution.py:23
  9.7 4.6 %collective-permute-done.1.refs_2_ = bf16[4,12288]{1,0:T(4,128)(2,1)S(1)} collective-permute-done((bf16[4,12288]{1,0:T(4,128)(2,1)}, bf16[4,12288]{1,0:T(4,128)(2,1)S(1)}, u32[]{:S(2)}, u32[]{:S(2)}) %collective-permute-start.1) | collective-permute-done | bytes 98336 | tf_op jit(solution)/shard_map/ppermute | solution.py:23
  17.2 3.6 %shard_map.84 = (bf16[24,32,128]{2,1,0:T(8,128)(2,1)S(1)}, bf16[24,32,128]{2,1,0:T(8,128)(2,1)S(1)}) custom-call(s32[96]{0:T(128)S(1)} %reshape.18.entry_ref, f32[8]{0:T(128)S(1)} %copy-done.2, s32[3]{0:T(128)S(1)} %pad_add_fusion.place_ref, bf16[4,12288]{1,0:T(4,128)(2,1)S(1)} %copy-done.1, bf16[4,12288]{1,0:T(4,128)(2,1)S(1)} %collective-permute-done.refs_1_, ...), custom_call_target="tpu_custom_call" | custom-call | flops 134217728 | bytes 4194304 | tf_op jit(solution)/shard_map/pallas_call | solution.py:243
  20.8 1.6 %collective-permute-start.7 = (bf16[24,32,128]{2,1,0:T(8,128)(2,1)S(1)}, bf16[24,32,128]{2,1,0:T(8,128)(2,1)S(1)}, u32[]{:S(2)}, u32[]{:S(2)}) collective-permute-start(bf16[24,32,128]{2,1,0:T(8,128)(2,1)S(1)} %get-tuple-element.27), channel_id=1, source_target_pairs={{0,1},{1,0},{2,3},{3,2},{4,5},{5,4},{6,7},{7,6},{8,9},{9,8},{10,11... | collective-permute-start | bytes 589832 | tf_op jit(solution)/shard_map/ppermute | solution.py:23
  22.4 1.5 %collective-permute-start.9 = (bf16[24,32,128]{2,1,0:T(8,128)(2,1)S(1)}, bf16[24,32,128]{2,1,0:T(8,128)(2,1)S(1)}, u32[]{:S(2)}, u32[]{:S(2)}) collective-permute-start(bf16[24,32,128]{2,1,0:T(8,128)(2,1)S(1)} %get-tuple-element.28), channel_id=1, source_target_pairs={{0,2},{1,3},{2,0},{3,1},{4,6},{5,7},{6,4},{7,5},{8,10},{9,11},{10,... | collective-permute-start | bytes 589832 | tf_op jit(solution)/shard_map/ppermute | solution.py:23
  23.9 4.1 %collective-permute-done.7 = bf16[24,32,128]{2,1,0:T(8,128)(2,1)S(1)} collective-permute-done((bf16[24,32,128]{2,1,0:T(8,128)(2,1)S(1)}, bf16[24,32,128]{2,1,0:T(8,128)(2,1)S(1)}, u32[]{:S(2)}, u32[]{:S(2)}) %collective-permute-start.7) | collective-permute-done | bytes 196640 | tf_op jit(solution)/shard_map/ppermute | solution.py:23
  28.1 1.6 %collective-permute-start.8 = (bf16[24,32,128]{2,1,0:T(8,128)(2,1)S(1)}, bf16[24,32,128]{2,1,0:T(8,128)(2,1)S(1)}, u32[]{:S(2)}, u32[]{:S(2)}) collective-permute-start(bf16[24,32,128]{2,1,0:T(8,128)(2,1)S(1)} %add_convert_fusion.8), channel_id=1, source_target_pairs={{0,2},{1,3},{2,0},{3,1},{4,6},{5,7},{6,4},{7,5},{8,10},{9,11},{10,... | collective-permute-start | bytes 589832 | tf_op jit(solution)/shard_map/ppermute | solution.py:23
  29.7 1.6 %collective-permute-start.10 = (bf16[24,32,128]{2,1,0:T(8,128)(2,1)S(1)}, bf16[24,32,128]{2,1,0:T(8,128)(2,1)S(1)}, u32[]{:S(2)}, u32[]{:S(2)}) collective-permute-start(bf16[24,32,128]{2,1,0:T(8,128)(2,1)S(1)} %add_convert_fusion.6), channel_id=1, source_target_pairs={{0,1},{1,0},{2,3},{3,2},{4,5},{5,4},{6,7},{7,6},{8,9},{9,8},{10,11... | collective-permute-start | bytes 589832 | tf_op jit(solution)/shard_map/ppermute | solution.py:23
  31.3 3.2 %collective-permute-done.8 = bf16[24,32,128]{2,1,0:T(8,128)(2,1)S(1)} collective-permute-done((bf16[24,32,128]{2,1,0:T(8,128)(2,1)S(1)}, bf16[24,32,128]{2,1,0:T(8,128)(2,1)S(1)}, u32[]{:S(2)}, u32[]{:S(2)}) %collective-permute-start.8) | collective-permute-done | bytes 196640 | tf_op jit(solution)/shard_map/ppermute | solution.py:23
  34.6 1.3 %collective-permute-done.10 = bf16[24,32,128]{2,1,0:T(8,128)(2,1)S(1)} collective-permute-done((bf16[24,32,128]{2,1,0:T(8,128)(2,1)S(1)}, bf16[24,32,128]{2,1,0:T(8,128)(2,1)S(1)}, u32[]{:S(2)}, u32[]{:S(2)}) %collective-permute-start.10) | collective-permute-done | bytes 196640 | tf_op jit(solution)/shard_map/ppermute | solution.py:23
  35.9 1.5 %shard_map.85 = (bf16[4,12,32,128]{3,2,1,0:T(8,128)(2,1)S(1)}, bf16[4,12,32,128]{3,2,1,0:T(8,128)(2,1)S(1)}) custom-call(s32[96]{0:T(128)S(1)} %reshape.18.entry_ref, f32[8]{0:T(128)S(1)} %copy-done.2, s32[3]{0:T(128)S(1)} %pad_add_fusion.place_ref, bf16[24,32,128]{2,1,0:T(8,128)(2,1)S(1)} %add_convert_fusion.7.refs_0_, ...), custom_call_target="tpu_custom_call" | custom-call | flops 134217728 | bytes 4194304 | tf_op jit(solution)/shard_map/pallas_call | solution.py:243
  37.5 1.7 %collective-permute-done.11 = bf16[4,12,32,128]{3,2,1,0:T(8,128)(2,1)S(1)} collective-permute-done((bf16[4,12,32,128]{3,2,1,0:T(8,128)(2,1)S(1)}, bf16[4,12,32,128]{3,2,1,0:T(8,128)(2,1)S(1)}, u32[]{:S(2)}, u32[]{:S(2)}) %collective-permute-start.11) | collective-permute-done | bytes 393248 | tf_op jit(solution)/shard_map/ppermute | solution.py:23
  39.4 2.6 %collective-permute-start.14 = (bf16[12,32,128]{2,1,0:T(8,128)(2,1)S(1)}, bf16[12,32,128]{2,1,0:T(8,128)(2,1)S(1)}, u32[]{:S(2)}, u32[]{:S(2)}) collective-permute-start(bf16[12,32,128]{2,1,0:T(8,128)(2,1)S(1)} %get-tuple-element.54), channel_id=1, source_target_pairs={{0,24},{4,28},{8,16},{12,20},{16,8},{20,12},{24,0},{28,4},{1,25},{... | collective-permute-start | bytes 294920 | tf_op jit(solution)/shard_map/ppermute | solution.py:23
  42.9 1.3 %collective-permute-done.12 = bf16[12,32,128]{2,1,0:T(8,128)(2,1)S(1)} collective-permute-done((bf16[12,32,128]{2,1,0:T(8,128)(2,1)S(1)}, bf16[12,32,128]{2,1,0:T(8,128)(2,1)S(1)}, u32[]{:S(2)}, u32[]{:S(2)}) %collective-permute-start.12) | collective-permute-done | bytes 98336 | tf_op jit(solution)/shard_map/ppermute | solution.py:23
  44.3 3.5 %collective-permute-done.14 = bf16[12,32,128]{2,1,0:T(8,128)(2,1)S(1)} collective-permute-done((bf16[12,32,128]{2,1,0:T(8,128)(2,1)S(1)}, bf16[12,32,128]{2,1,0:T(8,128)(2,1)S(1)}, u32[]{:S(2)}, u32[]{:S(2)}) %collective-permute-start.14) | collective-permute-done | bytes 98336 | tf_op jit(solution)/shard_map/ppermute | solution.py:23
  47.7 4.1 %collective-permute-done.13 = bf16[12,32,128]{2,1,0:T(8,128)(2,1)S(1)} collective-permute-done((bf16[12,32,128]{2,1,0:T(8,128)(2,1)S(1)}, bf16[12,32,128]{2,1,0:T(8,128)(2,1)S(1)}, u32[]{:S(2)}, u32[]{:S(2)}) %collective-permute-start.13) | collective-permute-done | bytes 98336 | tf_op jit(solution)/shard_map/ppermute | solution.py:23
  51.9 2.5 %collective-permute-start.17 = (bf16[12,32,128]{2,1,0:T(8,128)(2,1)S(1)}, bf16[12,32,128]{2,1,0:T(8,128)(2,1)S(1)}, u32[]{:S(2)}, u32[]{:S(2)}) collective-permute-start(bf16[12,32,128]{2,1,0:T(8,128)(2,1)S(1)} %fusion.6.refs_0_.refs_2_), channel_id=1, source_target_pairs={{0,24},{4,28},{8,16},{12,20},{16,8},{20,12},{24,0},{28,4},{1,25},{... | collective-permute-start | bytes 294920 | tf_op jit(solution)/shard_map/ppermute | solution.py:23
  54.4 1.9 %collective-permute-start.15 = (bf16[12,32,128]{2,1,0:T(8,128)(2,1)S(1)}, bf16[12,32,128]{2,1,0:T(8,128)(2,1)S(1)}, u32[]{:S(2)}, u32[]{:S(2)}) collective-permute-start(bf16[12,32,128]{2,1,0:T(8,128)(2,1)S(1)} %fusion.6.refs_0_.refs_2_), channel_id=1, source_target_pairs={{0,8},{4,12},{8,0},{12,4},{16,24},{20,28},{24,16},{28,20},{1,9},{5... | collective-permute-start | bytes 294920 | tf_op jit(solution)/shard_map/ppermute | solution.py:23
  56.3 3.2 %collective-permute-done.17.refs_3_.refs_5_ = bf16[12,32,128]{2,1,0:T(8,128)(2,1)S(1)} collective-permute-done((bf16[12,32,128]{2,1,0:T(8,128)(2,1)S(1)}, bf16[12,32,128]{2,1,0:T(8,128)(2,1)S(1)}, u32[]{:S(2)}, u32[]{:S(2)}) %collective-permute-start.17) | collective-permute-done | bytes 98336 | tf_op jit(solution)/shard_map/ppermute | solution.py:23
  59.6 2.7 %collective-permute-done.16.refs_2_.refs_4_ = bf16[12,32,128]{2,1,0:T(8,128)(2,1)S(1)} collective-permute-done((bf16[12,32,128]{2,1,0:T(8,128)(2,1)S(1)}, bf16[12,32,128]{2,1,0:T(8,128)(2,1)S(1)}, u32[]{:S(2)}, u32[]{:S(2)}) %collective-permute-start.16) | collective-permute-done | bytes 98336 | tf_op jit(solution)/shard_map/ppermute | solution.py:23
  63.7 2.0 %shard_map.86 = (bf16[24,32,128]{2,1,0:T(8,128)(2,1)S(1)}, bf16[24,32,128]{2,1,0:T(8,128)(2,1)S(1)}) custom-call(s32[96]{0:T(128)S(1)} %reshape.18.entry_ref, f32[8]{0:T(128)S(1)} %copy-done.2, s32[3]{0:T(128)S(1)} %pad_add_fusion.place_ref, bf16[12,32,128]{2,1,0:T(8,128)(2,1)S(1)} %fusion.6.refs_0_.refs_2_, ...), custom_call_target="tpu_custom_call" | custom-call | flops 134217728 | bytes 4194304 | tf_op jit(solution)/shard_map/pallas_call | solution.py:243
  65.6 1.6 %collective-permute-start.22 = (bf16[24,32,128]{2,1,0:T(8,128)(2,1)S(1)}, bf16[24,32,128]{2,1,0:T(8,128)(2,1)S(1)}, u32[]{:S(2)}, u32[]{:S(2)}) collective-permute-start(bf16[24,32,128]{2,1,0:T(8,128)(2,1)S(1)} %get-tuple-element.45), channel_id=1, source_target_pairs={{0,1},{1,0},{2,3},{3,2},{4,5},{5,4},{6,7},{7,6},{8,9},{9,8},{10,11... | collective-permute-start | bytes 589832 | tf_op jit(solution)/shard_map/ppermute | solution.py:23
  67.7 5.2 %collective-permute-done.22 = bf16[24,32,128]{2,1,0:T(8,128)(2,1)S(1)} collective-permute-done((bf16[24,32,128]{2,1,0:T(8,128)(2,1)S(1)}, bf16[24,32,128]{2,1,0:T(8,128)(2,1)S(1)}, u32[]{:S(2)}, u32[]{:S(2)}) %collective-permute-start.22) | collective-permute-done | bytes 196640 | tf_op jit(solution)/shard_map/ppermute | solution.py:23
  75.1 4.2 %collective-permute-done.23 = bf16[24,32,128]{2,1,0:T(8,128)(2,1)S(1)} collective-permute-done((bf16[24,32,128]{2,1,0:T(8,128)(2,1)S(1)}, bf16[24,32,128]{2,1,0:T(8,128)(2,1)S(1)}, u32[]{:S(2)}, u32[]{:S(2)}) %collective-permute-start.23) | collective-permute-done | bytes 196640 | tf_op jit(solution)/shard_map/ppermute | solution.py:23
  80.3 1.8 %shard_map.88 = bf16[2,4,4,12288]{3,2,1,0:T(4,128)(2,1)S(1)} custom-call(s32[96]{0:T(128)S(1)} %reshape.18.entry_ref, f32[8]{0:T(128)S(1)} %copy-done.2, s32[3]{0:T(128)S(1)} %pad_add_fusion.place_ref, bf16[24,32,128]{2,1,0:T(8,128)(2,1)S(1)} %add_convert_fusion.3.refs_0_, bf16[24,32,128]{2,1,0:T(8,128)(2,1)S(1)} %add_convert_fusion.1.refs_1_, ...), custom_call_target="tpu_custom_call" | custom-call | flops 134217728 | bytes 4194304 | tf_op jit(solution)/shard_map/pallas_call | solution.py:243
  82.4 1.7 %collective-permute-done.26 = bf16[4,4,12288]{2,1,0:T(4,128)(2,1)S(1)} collective-permute-done((bf16[4,4,12288]{2,1,0:T(4,128)(2,1)S(1)}, bf16[4,4,12288]{2,1,0:T(4,128)(2,1)S(1)}, u32[]{:S(2)}, u32[]{:S(2)}) %collective-permute-start.26) | collective-permute-done | bytes 393248 | tf_op jit(solution)/shard_map/ppermute | solution.py:23
  84.5 2.3 %collective-permute-start.29 = (bf16[4,12288]{1,0:T(4,128)(2,1)S(1)}, bf16[4,12288]{1,0:T(4,128)(2,1)S(1)}, u32[]{:S(2)}, u32[]{:S(2)}) collective-permute-start(bf16[4,12288]{1,0:T(4,128)(2,1)S(1)} %get-tuple-element.51), channel_id=1, source_target_pairs={{0,24},{4,28},{8,16},{12,20},{16,8},{20,12},{24,0},{28,4},{1,25},{... | collective-permute-start | bytes 294920 | tf_op jit(solution)/shard_map/ppermute | solution.py:23
  87.9 1.5 %shard_map.87 = (bf16[8,6144]{1,0:T(8,128)(2,1)}, bf16[4,12288]{1,0:T(4,128)(2,1)}) custom-call(s32[3]{0:T(128)S(1)} %pad_add_fusion.place_ref, bf16[24,32,128]{2,1,0:T(8,128)(2,1)S(1)} %add_convert_fusion.7.refs_0_, bf16[24,32,128]{2,1,0:T(8,128)(2,1)S(1)} %add_convert_fusion.5.refs_1_, bf16[12,32,128]{2,1,0:T(8,128)(2,1)S(1)} %fusion.6.refs_0_.refs_2_, ...), custom_call_target="tpu_custom_call" | custom-call | bytes 393216 | tf_op jit(solution)/shard_map/pallas_call | solution.py:232
  89.5 1.2 %shard_map.89 = bf16[8,6144]{1,0:T(8,128)(2,1)} custom-call(s32[3]{0:T(128)S(1)} %pad_add_fusion.place_ref, bf16[24,32,128]{2,1,0:T(8,128)(2,1)S(1)} %add_convert_fusion.3.refs_0_, bf16[24,32,128]{2,1,0:T(8,128)(2,1)S(1)} %add_convert_fusion.1.refs_1_), custom_call_target="tpu_custom_call" | custom-call | bytes 393216 | tf_op jit(solution)/shard_map/pallas_call | solution.py:232
  90.7 1.7 %collective-permute-done.29 = bf16[4,12288]{1,0:T(4,128)(2,1)S(1)} collective-permute-done((bf16[4,12288]{1,0:T(4,128)(2,1)S(1)}, bf16[4,12288]{1,0:T(4,128)(2,1)S(1)}, u32[]{:S(2)}, u32[]{:S(2)}) %collective-permute-start.29) | collective-permute-done | bytes 98336 | tf_op jit(solution)/shard_map/ppermute | solution.py:23
  92.4 4.3 %collective-permute-done.28 = bf16[4,12288]{1,0:T(4,128)(2,1)S(1)} collective-permute-done((bf16[4,12288]{1,0:T(4,128)(2,1)S(1)}, bf16[4,12288]{1,0:T(4,128)(2,1)S(1)}, u32[]{:S(2)}, u32[]{:S(2)}) %collective-permute-start.28) | collective-permute-done | bytes 98336 | tf_op jit(solution)/shard_map/ppermute | solution.py:23
  (61 shorter events, 14.5 us)
Async XLA Ops:
  0.6 9.0 %collective-permute-start.2 = (bf16[4,12288]{1,0:T(4,128)(2,1)}, bf16[4,12288]{1,0:T(4,128)(2,1)S(1)}, u32[]{:S(2)}, u32[]{:S(2)}) collective-permute-start(bf16[4,12288]{1,0:T(4,128)(2,1)} %refs_0_.1), channel_id=1, source_target_pairs={{0,24},{4,28},{8,16},{12,20},{16,8},{20,12},{24,0},{28,4},{1,25},{... | collective-permute-start | bytes 294920 | tf_op jit(solution)/shard_map/ppermute | solution.py:23
  5.7 8.5 %collective-permute-start.1 = (bf16[4,12288]{1,0:T(4,128)(2,1)}, bf16[4,12288]{1,0:T(4,128)(2,1)S(1)}, u32[]{:S(2)}, u32[]{:S(2)}) collective-permute-start(bf16[4,12288]{1,0:T(4,128)(2,1)} %refs_0_.1), channel_id=1, source_target_pairs={{0,16},{4,20},{8,24},{12,28},{16,0},{20,4},{24,8},{28,12},{1,17},{... | collective-permute-start | bytes 294920 | tf_op jit(solution)/shard_map/ppermute | solution.py:23
  5.7 8.5 %collective-permute-start = (bf16[4,12288]{1,0:T(4,128)(2,1)}, bf16[4,12288]{1,0:T(4,128)(2,1)S(1)}, u32[]{:S(2)}, u32[]{:S(2)}) collective-permute-start(bf16[4,12288]{1,0:T(4,128)(2,1)} %refs_0_.1), channel_id=1, source_target_pairs={{0,8},{4,12},{8,0},{12,4},{16,24},{20,28},{24,16},{28,20},{1,9},{5... | collective-permute-start | bytes 294920 | tf_op jit(solution)/shard_map/ppermute | solution.py:23
  6.4 8.4 %collective-permute-start.3 = (bf16[4,12288]{1,0:T(4,128)(2,1)}, bf16[4,12288]{1,0:T(4,128)(2,1)S(1)}, u32[]{:S(2)}, u32[]{:S(2)}) collective-permute-start(bf16[4,12288]{1,0:T(4,128)(2,1)} %refs_0_.1), channel_id=1, source_target_pairs={{0,4},{4,0},{8,12},{12,8},{16,20},{20,16},{24,28},{28,24},{1,5},{5... | collective-permute-start | bytes 294920 | tf_op jit(solution)/shard_map/ppermute | solution.py:23
  8.1 27.8 %copy-start = (bf16[32,256,256]{2,1,0:T(8,128)(2,1)S(1)}, bf16[32,256,256]{2,1,0:T(8,128)(2,1)}, u32[]{:S(2)}) copy-start(bf16[32,256,256]{2,1,0:T(8,128)(2,1)} %refs_2_.3) | copy-start | bytes 12582916
  9.7 5.2 %collective-permute-start.6 = (bf16[4,12288]{1,0:T(4,128)(2,1)S(1)}, bf16[4,12288]{1,0:T(4,128)(2,1)S(1)}, u32[]{:S(2)}, u32[]{:S(2)}) collective-permute-start(bf16[4,12288]{1,0:T(4,128)(2,1)S(1)} %collective-permute-done.2.refs_3_), channel_id=1, source_target_pairs={{0,4},{4,0},{8,12},{12,8},{16,20},{20,16},{24,28},{28,24},{1,5},{5... | collective-permute-start | bytes 294920 | tf_op jit(solution)/shard_map/ppermute | solution.py:23
  14.2 1.3 %collective-permute-start.5 = (bf16[4,12288]{1,0:T(4,128)(2,1)S(1)}, bf16[4,12288]{1,0:T(4,128)(2,1)S(1)}, u32[]{:S(2)}, u32[]{:S(2)}) collective-permute-start(bf16[4,12288]{1,0:T(4,128)(2,1)S(1)} %collective-permute-done.1.refs_2_), channel_id=1, source_target_pairs={{0,4},{4,0},{8,12},{12,8},{16,20},{20,16},{24,28},{28,24},{1,5},{5... | collective-permute-start | bytes 294920 | tf_op jit(solution)/shard_map/ppermute | solution.py:23
  14.2 1.5 %collective-permute-start.4 = (bf16[4,12288]{1,0:T(4,128)(2,1)S(1)}, bf16[4,12288]{1,0:T(4,128)(2,1)S(1)}, u32[]{:S(2)}, u32[]{:S(2)}) collective-permute-start(bf16[4,12288]{1,0:T(4,128)(2,1)S(1)} %collective-permute-done.refs_1_), channel_id=1, source_target_pairs={{0,4},{4,0},{8,12},{12,8},{16,20},{20,16},{24,28},{28,24},{1,5},{5... | collective-permute-start | bytes 294920 | tf_op jit(solution)/shard_map/ppermute | solution.py:23
  15.7 0.9 copy-start.1
  20.8 7.2 %collective-permute-start.7 = (bf16[24,32,128]{2,1,0:T(8,128)(2,1)S(1)}, bf16[24,32,128]{2,1,0:T(8,128)(2,1)S(1)}, u32[]{:S(2)}, u32[]{:S(2)}) collective-permute-start(bf16[24,32,128]{2,1,0:T(8,128)(2,1)S(1)} %get-tuple-element.27), channel_id=1, source_target_pairs={{0,1},{1,0},{2,3},{3,2},{4,5},{5,4},{6,7},{7,6},{8,9},{9,8},{10,11... | collective-permute-start | bytes 589832 | tf_op jit(solution)/shard_map/ppermute | solution.py:23
  22.4 7.3 %collective-permute-start.9 = (bf16[24,32,128]{2,1,0:T(8,128)(2,1)S(1)}, bf16[24,32,128]{2,1,0:T(8,128)(2,1)S(1)}, u32[]{:S(2)}, u32[]{:S(2)}) collective-permute-start(bf16[24,32,128]{2,1,0:T(8,128)(2,1)S(1)} %get-tuple-element.28), channel_id=1, source_target_pairs={{0,2},{1,3},{2,0},{3,1},{4,6},{5,7},{6,4},{7,5},{8,10},{9,11},{10,... | collective-permute-start | bytes 589832 | tf_op jit(solution)/shard_map/ppermute | solution.py:23
  28.1 6.4 %collective-permute-start.8 = (bf16[24,32,128]{2,1,0:T(8,128)(2,1)S(1)}, bf16[24,32,128]{2,1,0:T(8,128)(2,1)S(1)}, u32[]{:S(2)}, u32[]{:S(2)}) collective-permute-start(bf16[24,32,128]{2,1,0:T(8,128)(2,1)S(1)} %add_convert_fusion.8), channel_id=1, source_target_pairs={{0,2},{1,3},{2,0},{3,1},{4,6},{5,7},{6,4},{7,5},{8,10},{9,11},{10,... | collective-permute-start | bytes 589832 | tf_op jit(solution)/shard_map/ppermute | solution.py:23
  29.7 6.1 %collective-permute-start.10 = (bf16[24,32,128]{2,1,0:T(8,128)(2,1)S(1)}, bf16[24,32,128]{2,1,0:T(8,128)(2,1)S(1)}, u32[]{:S(2)}, u32[]{:S(2)}) collective-permute-start(bf16[24,32,128]{2,1,0:T(8,128)(2,1)S(1)} %add_convert_fusion.6), channel_id=1, source_target_pairs={{0,1},{1,0},{2,3},{3,2},{4,5},{5,4},{6,7},{7,6},{8,9},{9,8},{10,11... | collective-permute-start | bytes 589832 | tf_op jit(solution)/shard_map/ppermute | solution.py:23
  37.4 1.8 %collective-permute-start.11 = (bf16[4,12,32,128]{3,2,1,0:T(8,128)(2,1)S(1)}, bf16[4,12,32,128]{3,2,1,0:T(8,128)(2,1)S(1)}, u32[]{:S(2)}, u32[]{:S(2)}) collective-permute-start(bf16[4,12,32,128]{3,2,1,0:T(8,128)(2,1)S(1)} %get-tuple-element.30), channel_id=1, source_target_pairs={{0,4},{4,0},{8,12},{12,8},{16,20},{20,16},{24,28},{28,24},{1,5},{5... | collective-permute-start | bytes 1179656 | tf_op jit(solution)/shard_map/ppermute | solution.py:23
  39.4 4.9 %collective-permute-start.12 = (bf16[12,32,128]{2,1,0:T(8,128)(2,1)S(1)}, bf16[12,32,128]{2,1,0:T(8,128)(2,1)S(1)}, u32[]{:S(2)}, u32[]{:S(2)}) collective-permute-start(bf16[12,32,128]{2,1,0:T(8,128)(2,1)S(1)} %get-tuple-element.53), channel_id=1, source_target_pairs={{0,8},{4,12},{8,0},{12,4},{16,24},{20,28},{24,16},{28,20},{1,9},{5... | collective-permute-start | bytes 294920 | tf_op jit(solution)/shard_map/ppermute | solution.py:23
  39.4 8.3 %collective-permute-start.14 = (bf16[12,32,128]{2,1,0:T(8,128)(2,1)S(1)}, bf16[12,32,128]{2,1,0:T(8,128)(2,1)S(1)}, u32[]{:S(2)}, u32[]{:S(2)}) collective-permute-start(bf16[12,32,128]{2,1,0:T(8,128)(2,1)S(1)} %get-tuple-element.54), channel_id=1, source_target_pairs={{0,24},{4,28},{8,16},{12,20},{16,8},{20,12},{24,0},{28,4},{1,25},{... | collective-permute-start | bytes 294920 | tf_op jit(solution)/shard_map/ppermute | solution.py:23
  42.0 9.8 %collective-permute-start.13 = (bf16[12,32,128]{2,1,0:T(8,128)(2,1)S(1)}, bf16[12,32,128]{2,1,0:T(8,128)(2,1)S(1)}, u32[]{:S(2)}, u32[]{:S(2)}) collective-permute-start(bf16[12,32,128]{2,1,0:T(8,128)(2,1)S(1)} %get-tuple-element.55), channel_id=1, source_target_pairs={{0,16},{4,20},{8,24},{12,28},{16,0},{20,4},{24,8},{28,12},{1,17},{... | collective-permute-start | bytes 294920 | tf_op jit(solution)/shard_map/ppermute | solution.py:23
  51.9 7.7 %collective-permute-start.17 = (bf16[12,32,128]{2,1,0:T(8,128)(2,1)S(1)}, bf16[12,32,128]{2,1,0:T(8,128)(2,1)S(1)}, u32[]{:S(2)}, u32[]{:S(2)}) collective-permute-start(bf16[12,32,128]{2,1,0:T(8,128)(2,1)S(1)} %fusion.6.refs_0_.refs_2_), channel_id=1, source_target_pairs={{0,24},{4,28},{8,16},{12,20},{16,8},{20,12},{24,0},{28,4},{1,25},{... | collective-permute-start | bytes 294920 | tf_op jit(solution)/shard_map/ppermute | solution.py:23
  54.4 7.8 %collective-permute-start.16 = (bf16[12,32,128]{2,1,0:T(8,128)(2,1)S(1)}, bf16[12,32,128]{2,1,0:T(8,128)(2,1)S(1)}, u32[]{:S(2)}, u32[]{:S(2)}) collective-permute-start(bf16[12,32,128]{2,1,0:T(8,128)(2,1)S(1)} %fusion.6.refs_0_.refs_2_), channel_id=1, source_target_pairs={{0,16},{4,20},{8,24},{12,28},{16,0},{20,4},{24,8},{28,12},{1,17},{... | collective-permute-start | bytes 294920 | tf_op jit(solution)/shard_map/ppermute | solution.py:23
  54.4 7.8 %collective-permute-start.15 = (bf16[12,32,128]{2,1,0:T(8,128)(2,1)S(1)}, bf16[12,32,128]{2,1,0:T(8,128)(2,1)S(1)}, u32[]{:S(2)}, u32[]{:S(2)}) collective-permute-start(bf16[12,32,128]{2,1,0:T(8,128)(2,1)S(1)} %fusion.6.refs_0_.refs_2_), channel_id=1, source_target_pairs={{0,8},{4,12},{8,0},{12,4},{16,24},{20,28},{24,16},{28,20},{1,9},{5... | collective-permute-start | bytes 294920 | tf_op jit(solution)/shard_map/ppermute | solution.py:23
  56.3 6.4 %collective-permute-start.18 = (bf16[12,32,128]{2,1,0:T(8,128)(2,1)S(1)}, bf16[12,32,128]{2,1,0:T(8,128)(2,1)S(1)}, u32[]{:S(2)}, u32[]{:S(2)}) collective-permute-start(bf16[12,32,128]{2,1,0:T(8,128)(2,1)S(1)} %fusion.6.refs_0_.refs_2_), channel_id=1, source_target_pairs={{0,4},{4,0},{8,12},{12,8},{16,20},{20,16},{24,28},{28,24},{1,5},{5... | collective-permute-start | bytes 294920 | tf_op jit(solution)/shard_map/ppermute | solution.py:23
  59.6 3.2 %collective-permute-start.21 = (bf16[12,32,128]{2,1,0:T(8,128)(2,1)S(1)}, bf16[12,32,128]{2,1,0:T(8,128)(2,1)S(1)}, u32[]{:S(2)}, u32[]{:S(2)}) collective-permute-start(bf16[12,32,128]{2,1,0:T(8,128)(2,1)S(1)} %collective-permute-done.17.refs_3_.refs_5_), channel_id=1, source_target_pairs={{0,4},{4,0},{8,12},{12,8},{16,20},{20,16},{24,28},{28,24},{1,5},{5... | collective-permute-start | bytes 294920 | tf_op jit(solution)/shard_map/ppermute | solution.py:23
  62.2 1.3 %collective-permute-start.20 = (bf16[12,32,128]{2,1,0:T(8,128)(2,1)S(1)}, bf16[12,32,128]{2,1,0:T(8,128)(2,1)S(1)}, u32[]{:S(2)}, u32[]{:S(2)}) collective-permute-start(bf16[12,32,128]{2,1,0:T(8,128)(2,1)S(1)} %collective-permute-done.16.refs_2_.refs_4_), channel_id=1, source_target_pairs={{0,4},{4,0},{8,12},{12,8},{16,20},{20,16},{24,28},{28,24},{1,5},{5... | collective-permute-start | bytes 294920 | tf_op jit(solution)/shard_map/ppermute | solution.py:23
  62.2 1.5 %collective-permute-start.19 = (bf16[12,32,128]{2,1,0:T(8,128)(2,1)S(1)}, bf16[12,32,128]{2,1,0:T(8,128)(2,1)S(1)}, u32[]{:S(2)}, u32[]{:S(2)}) collective-permute-start(bf16[12,32,128]{2,1,0:T(8,128)(2,1)S(1)} %collective-permute-done.15.refs_1_.refs_3_), channel_id=1, source_target_pairs={{0,4},{4,0},{8,12},{12,8},{16,20},{20,16},{24,28},{28,24},{1,5},{5... | collective-permute-start | bytes 294920 | tf_op jit(solution)/shard_map/ppermute | solution.py:23
  65.6 7.2 %collective-permute-start.22 = (bf16[24,32,128]{2,1,0:T(8,128)(2,1)S(1)}, bf16[24,32,128]{2,1,0:T(8,128)(2,1)S(1)}, u32[]{:S(2)}, u32[]{:S(2)}) collective-permute-start(bf16[24,32,128]{2,1,0:T(8,128)(2,1)S(1)} %get-tuple-element.45), channel_id=1, source_target_pairs={{0,1},{1,0},{2,3},{3,2},{4,5},{5,4},{6,7},{7,6},{8,9},{9,8},{10,11... | collective-permute-start | bytes 589832 | tf_op jit(solution)/shard_map/ppermute | solution.py:23
  67.2 6.9 %collective-permute-start.24 = (bf16[24,32,128]{2,1,0:T(8,128)(2,1)S(1)}, bf16[24,32,128]{2,1,0:T(8,128)(2,1)S(1)}, u32[]{:S(2)}, u32[]{:S(2)}) collective-permute-start(bf16[24,32,128]{2,1,0:T(8,128)(2,1)S(1)} %get-tuple-element.46), channel_id=1, source_target_pairs={{0,2},{1,3},{2,0},{3,1},{4,6},{5,7},{6,4},{7,5},{8,10},{9,11},{10,... | collective-permute-start | bytes 589832 | tf_op jit(solution)/shard_map/ppermute | solution.py:23
  72.9 6.4 %collective-permute-start.23 = (bf16[24,32,128]{2,1,0:T(8,128)(2,1)S(1)}, bf16[24,32,128]{2,1,0:T(8,128)(2,1)S(1)}, u32[]{:S(2)}, u32[]{:S(2)}) collective-permute-start(bf16[24,32,128]{2,1,0:T(8,128)(2,1)S(1)} %add_convert_fusion.4), channel_id=1, source_target_pairs={{0,2},{1,3},{2,0},{3,1},{4,6},{5,7},{6,4},{7,5},{8,10},{9,11},{10,... | collective-permute-start | bytes 589832 | tf_op jit(solution)/shard_map/ppermute | solution.py:23
  74.1 6.1 %collective-permute-start.25 = (bf16[24,32,128]{2,1,0:T(8,128)(2,1)S(1)}, bf16[24,32,128]{2,1,0:T(8,128)(2,1)S(1)}, u32[]{:S(2)}, u32[]{:S(2)}) collective-permute-start(bf16[24,32,128]{2,1,0:T(8,128)(2,1)S(1)} %add_convert_fusion.2), channel_id=1, source_target_pairs={{0,1},{1,0},{2,3},{3,2},{4,5},{5,4},{6,7},{7,6},{8,9},{9,8},{10,11... | collective-permute-start | bytes 589832 | tf_op jit(solution)/shard_map/ppermute | solution.py:23
  82.3 1.8 %collective-permute-start.26 = (bf16[4,4,12288]{2,1,0:T(4,128)(2,1)S(1)}, bf16[4,4,12288]{2,1,0:T(4,128)(2,1)S(1)}, u32[]{:S(2)}, u32[]{:S(2)}) collective-permute-start(bf16[4,4,12288]{2,1,0:T(4,128)(2,1)S(1)} %slice_bitcast_fusion), channel_id=1, source_target_pairs={{0,4},{4,0},{8,12},{12,8},{16,20},{20,16},{24,28},{28,24},{1,5},{5... | collective-permute-start | bytes 1179656 | tf_op jit(solution)/shard_map/ppermute | solution.py:23
  84.4 6.3 %collective-permute-start.27 = (bf16[4,12288]{1,0:T(4,128)(2,1)S(1)}, bf16[4,12288]{1,0:T(4,128)(2,1)S(1)}, u32[]{:S(2)}, u32[]{:S(2)}) collective-permute-start(bf16[4,12288]{1,0:T(4,128)(2,1)S(1)} %get-tuple-element.50), channel_id=1, source_target_pairs={{0,8},{4,12},{8,0},{12,4},{16,24},{20,28},{24,16},{28,20},{1,9},{5... | collective-permute-start | bytes 294920 | tf_op jit(solution)/shard_map/ppermute | solution.py:23
  84.5 8.0 %collective-permute-start.29 = (bf16[4,12288]{1,0:T(4,128)(2,1)S(1)}, bf16[4,12288]{1,0:T(4,128)(2,1)S(1)}, u32[]{:S(2)}, u32[]{:S(2)}) collective-permute-start(bf16[4,12288]{1,0:T(4,128)(2,1)S(1)} %get-tuple-element.51), channel_id=1, source_target_pairs={{0,24},{4,28},{8,16},{12,20},{16,8},{20,12},{24,0},{28,4},{1,25},{... | collective-permute-start | bytes 294920 | tf_op jit(solution)/shard_map/ppermute | solution.py:23
  86.7 10.1 %collective-permute-start.28 = (bf16[4,12288]{1,0:T(4,128)(2,1)S(1)}, bf16[4,12288]{1,0:T(4,128)(2,1)S(1)}, u32[]{:S(2)}, u32[]{:S(2)}) collective-permute-start(bf16[4,12288]{1,0:T(4,128)(2,1)S(1)} %get-tuple-element.52), channel_id=1, source_target_pairs={{0,16},{4,20},{8,24},{12,28},{16,0},{20,4},{24,8},{28,12},{1,17},{... | collective-permute-start | bytes 294920 | tf_op jit(solution)/shard_map/ppermute | solution.py:23
  (1 other events, 0.7 us)

commit v11 on v10

--- a/solution.py
+++ b/solution.py
@@ -11,9 +11,10 @@
 B = 256
 LANES = 128
 PER = B // LANES
-COPIES = 4
+COPIES = 8
 ROW_PARTS = 2
-CHUNK = 768
+CHUNK = 512
+UNROLL = 16
 VMEM_LIMIT = 12 * 1024 * 1024
 FIRST_LIMIT = 50 * 1024 * 1024
 
@@ -80,7 +81,7 @@
     cut_rows(place_ref, refs[:-1], refs[-1])
 
 
-def add_products(entry_ref, gain_ref, load, block_refs, total, adjoint, copies=()):
+def add_products(entry_ref, scale_ref, load, block_refs, total, adjoint, copies=()):
     total[...] = jnp.zeros_like(total)
     at = 0
     for block_ref in block_refs:
@@ -88,9 +89,8 @@
             for start, copy in copies:
                 if start == slot:
                     copy.wait()
-            row, col, level = entry_ref[at], entry_ref[at + 1], entry_ref[at + 2]
-            at += 3
-            scale = jnp.where(level >= 0, gain_ref[jnp.maximum(level, 0)], jnp.float32(0.0))
+            row, col, scale = entry_ref[2 * at], entry_ref[2 * at + 1], scale_ref[at]
+            at += 1
             source, target = (row, col) if adjoint else (col, row)
             term = lax.dot_general(
                 load(source),
@@ -126,7 +126,7 @@
         at += size
 
 
-def first_kernel(ways, entry_ref, gain_ref, place_ref, *refs):
+def first_kernel(ways, entry_ref, scale_ref, place_ref, *refs):
     count = 2 * ways
     pieces, blocks_ref, outs = refs[:count], refs[count], refs[count + 1 : -5]
     total, wide, x, held_ref, sems = refs[-5:]
@@ -155,11 +155,11 @@
     def load(block):
         return x[:, pl.ds(pl.multiple_of(block * B, B), B)]
 
-    add_products(entry_ref, gain_ref, load, [held_ref], total, False, copies)
+    add_products(entry_ref, scale_ref, load, [held_ref], total, False, copies)
     write_parts(total, outs)
 
 
-def forward_kernel(ways, entry_ref, gain_ref, place_ref, *refs):
+def forward_kernel(ways, entry_ref, scale_ref, place_ref, *refs):
     count = 2 * ways
     pieces, block_refs, outs = refs[:count], refs[count : count + 1], refs[count + 1 : -2]
     total, x = refs[-2:]
@@ -169,16 +169,16 @@
         for way in range(ways):
             at = ((core ^ side) * ways + (along ^ way)) * size
             x[pl.ds(at, size)] = pieces[side * ways + way][...]
-    add_products(entry_ref, gain_ref, load_from(x), block_refs, total, False)
+    add_products(entry_ref, scale_ref, load_from(x), block_refs, total, False)
     write_parts(total, outs)
 
 
-def adjoint_kernel(ways, entry_ref, gain_ref, place_ref, *refs):
+def adjoint_kernel(ways, entry_ref, scale_ref, place_ref, *refs):
     parts, block_refs = refs[:ROW_PARTS], refs[ROW_PARTS : ROW_PARTS + 1]
     outs = refs[ROW_PARTS + 1 : -2]
     total, x = refs[-2:]
     join_parts(x, parts)
-    add_products(entry_ref, gain_ref, load_from(x), block_refs, total, True)
+    add_products(entry_ref, scale_ref, load_from(x), block_refs, total, True)
     core, along = place_ref[0], place_ref[1]
     size = outs[0].shape[1]
     for side, out_ref in enumerate(outs):
@@ -187,18 +187,26 @@
             out_ref[way] = total[pl.ds(at, size)].astype(out_ref.dtype)
 
 
-def last_kernel(ways, entry_ref, gain_ref, place_ref, *refs):
+def last_kernel(ways, entry_ref, scale_ref, place_ref, *refs):
     parts, block_refs = refs[:ROW_PARTS], refs[ROW_PARTS : ROW_PARTS + 1]
     out_ref, total, x = refs[ROW_PARTS + 1 :]
     join_parts(x, parts)
-    add_products(entry_ref, gain_ref, load_from(x), block_refs, total, True)
+    add_products(entry_ref, scale_ref, load_from(x), block_refs, total, True)
     core, along = place_ref[0], place_ref[1]
     share = out_ref.shape[2]
-    for group in range(total.shape[0]):
-        values = total[group].astype(out_ref.dtype)
-        for index in range(2 * ways):
-            piece = values[index * share : (index + 1) * share]
-            out_ref[core ^ (index % 2), along ^ (index // 2), :, group * LANES : (group + 1) * LANES] = piece
+    groups = math.gcd(total.shape[0], UNROLL)
+
+    def write(step, carry):
+        for i in range(groups):
+            group = step * groups + i
+            lanes = pl.ds(pl.multiple_of(group * LANES, LANES), LANES)
+            values = total[group].astype(out_ref.dtype)
+            for index in range(2 * ways):
+                piece = values[index * share : (index + 1) * share]
+                out_ref[core ^ (index % 2), along ^ (index // 2), :, lanes] = piece
+        return carry
+
+    lax.fori_loop(0, total.shape[0] // groups, write, 0)
 
 
 def shards(strengths, blocks, pattern, level_gain):
@@ -221,8 +229,10 @@
     part_size = col_groups // n_panel
 
     place = jnp.stack([core, along, case]).astype(jnp.int32)
-    first = jnp.stack([panel * row_blocks, case * col_blocks, 0]).astype(jnp.int32)
-    entry = jnp.where(pattern[:, 2:3] < 0, jnp.array([0, 0, -1], jnp.int32), pattern - first).reshape(-1)
+    first = jnp.stack([panel * row_blocks, case * col_blocks]).astype(jnp.int32)
+    entry = jnp.where(pattern[:, 2:] >= 0, pattern[:, :2] - first, 0).reshape(-1)
+    level_ids = jnp.arange(level_gain.shape[0], dtype=jnp.int32)
+    scale = jnp.sum(jnp.where(pattern[:, 2:] == level_ids, level_gain, jnp.float32(0.0)), axis=1)
 
     smem = pl.BlockSpec(memory_space=pltpu.SMEM)
     vmem = pl.BlockSpec(memory_space=pltpu.VMEM)
@@ -238,12 +248,12 @@
             cost_estimate=pl.CostEstimate(flops=0, bytes_accessed=8 * share * width, transcendentals=0),
         )(place, *vectors)
 
-    def product(kernel, vectors, outs, scratch, limit=VMEM_LIMIT, space=pltpu.VMEM):
-        small = (entry, level_gain, place)
+    def product(kernel, vectors, outs, scratch, limit=VMEM_LIMIT, space=None):
+        small = (entry, scale, place)
         return pl.pallas_call(
             functools.partial(kernel, ways),
             out_shape=[jax.ShapeDtypeStruct(shape, value) for shape in outs],
-            in_specs=[smem] * len(small) + [vmem] * len(vectors) + [pl.BlockSpec(memory_space=space)],
+            in_specs=[smem] * len(small) + [vmem] * len(vectors) + [space or vmem],
             out_specs=[vmem] * len(outs),
             scratch_shapes=scratch,
             compiler_params=pltpu.CompilerParams(vmem_limit_bytes=limit),
@@ -284,10 +294,11 @@
         same = [part, *along_swaps(lambda way: part)]
         return same + [swap(one, "panel", 1) for one in same]
 
+    mine = jnp.where(core >= 0, strengths, 0)
     own_copy = [pltpu.VMEM(blocks.shape, blocks.dtype), pltpu.SemaphoreType.DMA((COPIES,))]
     scratches = [rows_total, *flat, *own_copy]
     first_sums = over_case(
-        product(first_kernel, gather_panel(strengths), row_shapes, scratches, FIRST_LIMIT, pl.ANY)
+        product(first_kernel, [mine, *gather_panel(strengths)[1:]], row_shapes, scratches, FIRST_LIMIT, pl.BlockSpec(memory_space=pl.ANY))
     )
     outs = [(ways, part_size, cases, LANES)] * 2
     pieces = gather_panel(scatter_panel(*product(adjoint_kernel, first_sums, outs, [cols_total, rows_held])))

time: 97.7 us -> 97.1 us (level)
  waiting for transfers between devices: 51.1 us -> 47.4 us
  other arithmetic: 3.15 us -> 4.98 us
  Pallas kernels: 11.6 us -> 12.6 us
  starting transfers between devices: 28.9 us -> 29.9 us
    ppermute x30, waiting for transfers between devices: 51.1 us -> 47.4 us  [swap(): return lax.ppermute(value, axis, [(i, i ^ offset) for i in range(count)])]
    unnamed x6 -> x2, local copies, waits for them, and re-layouts: 1.55 us -> 0.01 us
    ppermute x30, starting transfers between devices: 28.9 us -> 29.9 us  [swap(): return lax.ppermute(value, axis, [(i, i ^ offset) for i in range(count)])]
    pallas_call x4, Pallas kernels: 8.82 us -> 9.8 us  [product(): pl.pallas_call(functools.partial(kernel, ways), out_shape=[jax.ShapeDtype...]
  transfers between devices with their start and end apart: 30 -> 30, of which waited for: 21 -> 19; matrix products, arithmetic and copies ran while one was open for 2% -> 5% of each run, Pallas kernels for 3% -> 3%
where the time goes in v11:
time: 97.1 us; the launch traced here: 96.9 us
  waiting for transfers between devices  47.4 us (49%)
  starting transfers between devices  29.9 us (31%)
  Pallas kernels  12.6 us (13%)
  other arithmetic  4.98 us (5%)
  local copies, waits for them, and re-layouts  1.15 us (1%)
    ppermute x30, waiting for transfers between devices, swap(): return lax.ppermute(value, axis, [(i, i ^ offset) for i in range(count)])  47.4 us
    ppermute x30, starting transfers between devices, swap(): return lax.ppermute(value, axis, [(i, i ^ offset) for i in range(count)])  29.9 us
    pallas_call x4, Pallas kernels, product(): pl.pallas_call(functools.partial(kernel, ways), out_shape=[jax.ShapeDtype...  9.8 us
    pallas_call x2, Pallas kernels, cut(): pl.pallas_call(functools.partial(kernel, ways), out_shape=[jax.ShapeDtype...  2.77 us
  transfers between devices with their start and end apart: 30, of which 19 were waited for; matrix products, arithmetic and copies ran while one was open for 5% of the time, Pallas kernels for 3%

profile of v11, /device:TPU:0, one launch (start us, length us, event | category | flops | bytes accessed | tf_op | source)
XLA Modules:
  0.0 96.9 jit_solution(608690796979616665)
XLA Ops:
  0.6 4.1 %collective-permute-start.1 = (bf16[4,12288]{1,0:T(4,128)(2,1)}, bf16[4,12288]{1,0:T(4,128)(2,1)S(1)}, u32[]{:S(2)}, u32[]{:S(2)}) collective-permute-start(bf16[4,12288]{1,0:T(4,128)(2,1)} %param.4), channel_id=1, source_target_pairs={{0,16},{4,20},{8,24},{12,28},{16,0},{20,4},{24,8},{28,12},{1,17},{... | collective-permute-start | bytes 294920 | tf_op jit(solution)/shard_map/ppermute | solution.py:24
  4.7 1.6 %collective-permute-start = (bf16[4,12288]{1,0:T(4,128)(2,1)}, bf16[4,12288]{1,0:T(4,128)(2,1)S(1)}, u32[]{:S(2)}, u32[]{:S(2)}) collective-permute-start(bf16[4,12288]{1,0:T(4,128)(2,1)} %param.4), channel_id=1, source_target_pairs={{0,8},{4,12},{8,0},{12,4},{16,24},{20,28},{24,16},{28,20},{1,9},{5... | collective-permute-start | bytes 294920 | tf_op jit(solution)/shard_map/ppermute | solution.py:24
  11.2 2.4 %collective-permute-done.2.refs_3_ = bf16[4,12288]{1,0:T(4,128)(2,1)S(1)} collective-permute-done((bf16[4,12288]{1,0:T(4,128)(2,1)}, bf16[4,12288]{1,0:T(4,128)(2,1)S(1)}, u32[]{:S(2)}, u32[]{:S(2)}) %collective-permute-start.2) | collective-permute-done | bytes 98336 | tf_op jit(solution)/shard_map/ppermute | solution.py:24
  14.9 3.9 %shard_map.75 = (bf16[24,32,128]{2,1,0:T(8,128)(2,1)S(1)}, bf16[24,32,128]{2,1,0:T(8,128)(2,1)S(1)}) custom-call(s32[64]{0:T(128)S(1)} %reshape.18.entry_ref, f32[32]{0:T(128)S(1)} %select_reduce_fusion.scale_ref, s32[3]{0:T(128)S(1)} %pad_add_fusion.place_ref, bf16[4,12288]{1,0:T(4,128)(2,1)S(1)} %broadcast_select_fusion.refs_0_, ...), custom_call_target="tpu_custom_call" | custom-call | flops 134217728 | bytes 4194304 | tf_op jit(solution)/shard_map/pallas_call | solution.py:253
  18.8 1.6 %collective-permute-start.7 = (bf16[24,32,128]{2,1,0:T(8,128)(2,1)S(1)}, bf16[24,32,128]{2,1,0:T(8,128)(2,1)S(1)}, u32[]{:S(2)}, u32[]{:S(2)}) collective-permute-start(bf16[24,32,128]{2,1,0:T(8,128)(2,1)S(1)} %get-tuple-element.27), channel_id=1, source_target_pairs={{0,1},{1,0},{2,3},{3,2},{4,5},{5,4},{6,7},{7,6},{8,9},{9,8},{10,11... | collective-permute-start | bytes 589832 | tf_op jit(solution)/shard_map/ppermute | solution.py:24
  20.4 1.5 %collective-permute-start.9 = (bf16[24,32,128]{2,1,0:T(8,128)(2,1)S(1)}, bf16[24,32,128]{2,1,0:T(8,128)(2,1)S(1)}, u32[]{:S(2)}, u32[]{:S(2)}) collective-permute-start(bf16[24,32,128]{2,1,0:T(8,128)(2,1)S(1)} %get-tuple-element.28), channel_id=1, source_target_pairs={{0,2},{1,3},{2,0},{3,1},{4,6},{5,7},{6,4},{7,5},{8,10},{9,11},{10,... | collective-permute-start | bytes 589832 | tf_op jit(solution)/shard_map/ppermute | solution.py:24
  21.9 3.9 %collective-permute-done.7 = bf16[24,32,128]{2,1,0:T(8,128)(2,1)S(1)} collective-permute-done((bf16[24,32,128]{2,1,0:T(8,128)(2,1)S(1)}, bf16[24,32,128]{2,1,0:T(8,128)(2,1)S(1)}, u32[]{:S(2)}, u32[]{:S(2)}) %collective-permute-start.7) | collective-permute-done | bytes 196640 | tf_op jit(solution)/shard_map/ppermute | solution.py:24
  25.9 1.6 %collective-permute-start.8 = (bf16[24,32,128]{2,1,0:T(8,128)(2,1)S(1)}, bf16[24,32,128]{2,1,0:T(8,128)(2,1)S(1)}, u32[]{:S(2)}, u32[]{:S(2)}) collective-permute-start(bf16[24,32,128]{2,1,0:T(8,128)(2,1)S(1)} %add_convert_fusion.8), channel_id=1, source_target_pairs={{0,2},{1,3},{2,0},{3,1},{4,6},{5,7},{6,4},{7,5},{8,10},{9,11},{10,... | collective-permute-start | bytes 589832 | tf_op jit(solution)/shard_map/ppermute | solution.py:24
  27.6 1.6 %collective-permute-start.10 = (bf16[24,32,128]{2,1,0:T(8,128)(2,1)S(1)}, bf16[24,32,128]{2,1,0:T(8,128)(2,1)S(1)}, u32[]{:S(2)}, u32[]{:S(2)}) collective-permute-start(bf16[24,32,128]{2,1,0:T(8,128)(2,1)S(1)} %add_convert_fusion.6), channel_id=1, source_target_pairs={{0,1},{1,0},{2,3},{3,2},{4,5},{5,4},{6,7},{7,6},{8,9},{9,8},{10,11... | collective-permute-start | bytes 589832 | tf_op jit(solution)/shard_map/ppermute | solution.py:24
  29.1 3.0 %collective-permute-done.8 = bf16[24,32,128]{2,1,0:T(8,128)(2,1)S(1)} collective-permute-done((bf16[24,32,128]{2,1,0:T(8,128)(2,1)S(1)}, bf16[24,32,128]{2,1,0:T(8,128)(2,1)S(1)}, u32[]{:S(2)}, u32[]{:S(2)}) %collective-permute-start.8) | collective-permute-done | bytes 196640 | tf_op jit(solution)/shard_map/ppermute | solution.py:24
  32.2 1.3 %collective-permute-done.10 = bf16[24,32,128]{2,1,0:T(8,128)(2,1)S(1)} collective-permute-done((bf16[24,32,128]{2,1,0:T(8,128)(2,1)S(1)}, bf16[24,32,128]{2,1,0:T(8,128)(2,1)S(1)}, u32[]{:S(2)}, u32[]{:S(2)}) %collective-permute-start.10) | collective-permute-done | bytes 196640 | tf_op jit(solution)/shard_map/ppermute | solution.py:24
  33.6 1.5 %shard_map.76 = (bf16[4,12,32,128]{3,2,1,0:T(8,128)(2,1)S(1)}, bf16[4,12,32,128]{3,2,1,0:T(8,128)(2,1)S(1)}) custom-call(s32[64]{0:T(128)S(1)} %reshape.18.entry_ref, f32[32]{0:T(128)S(1)} %select_reduce_fusion.scale_ref, s32[3]{0:T(128)S(1)} %pad_add_fusion.place_ref, bf16[24,32,128]{2,1,0:T(8,128)(2,1)S(1)} %add_convert_fusion.7.refs_0_, ...), custom_call_target="tpu_custom_call" | custom-call | flops 134217728 | bytes 4194304 | tf_op jit(solution)/shard_map/pallas_call | solution.py:253
  35.1 1.7 %collective-permute-done.11 = bf16[4,12,32,128]{3,2,1,0:T(8,128)(2,1)S(1)} collective-permute-done((bf16[4,12,32,128]{3,2,1,0:T(8,128)(2,1)S(1)}, bf16[4,12,32,128]{3,2,1,0:T(8,128)(2,1)S(1)}, u32[]{:S(2)}, u32[]{:S(2)}) %collective-permute-start.11) | collective-permute-done | bytes 393248 | tf_op jit(solution)/shard_map/ppermute | solution.py:24
  37.0 1.3 %collective-permute-start.12 = (bf16[12,32,128]{2,1,0:T(8,128)(2,1)S(1)}, bf16[12,32,128]{2,1,0:T(8,128)(2,1)S(1)}, u32[]{:S(2)}, u32[]{:S(2)}) collective-permute-start(bf16[12,32,128]{2,1,0:T(8,128)(2,1)S(1)} %get-tuple-element.53), channel_id=1, source_target_pairs={{0,8},{4,12},{8,0},{12,4},{16,24},{20,28},{24,16},{28,20},{1,9},{5... | collective-permute-start | bytes 294920 | tf_op jit(solution)/shard_map/ppermute | solution.py:24
  38.3 3.3 %collective-permute-start.14 = (bf16[12,32,128]{2,1,0:T(8,128)(2,1)S(1)}, bf16[12,32,128]{2,1,0:T(8,128)(2,1)S(1)}, u32[]{:S(2)}, u32[]{:S(2)}) collective-permute-start(bf16[12,32,128]{2,1,0:T(8,128)(2,1)S(1)} %get-tuple-element.54), channel_id=1, source_target_pairs={{0,24},{4,28},{8,16},{12,20},{16,8},{20,12},{24,0},{28,4},{1,25},{... | collective-permute-start | bytes 294920 | tf_op jit(solution)/shard_map/ppermute | solution.py:24
  41.9 5.5 %collective-permute-done.14 = bf16[12,32,128]{2,1,0:T(8,128)(2,1)S(1)} collective-permute-done((bf16[12,32,128]{2,1,0:T(8,128)(2,1)S(1)}, bf16[12,32,128]{2,1,0:T(8,128)(2,1)S(1)}, u32[]{:S(2)}, u32[]{:S(2)}) %collective-permute-start.14) | collective-permute-done | bytes 98336 | tf_op jit(solution)/shard_map/ppermute | solution.py:24
  47.4 3.0 %collective-permute-done.13 = bf16[12,32,128]{2,1,0:T(8,128)(2,1)S(1)} collective-permute-done((bf16[12,32,128]{2,1,0:T(8,128)(2,1)S(1)}, bf16[12,32,128]{2,1,0:T(8,128)(2,1)S(1)}, u32[]{:S(2)}, u32[]{:S(2)}) %collective-permute-start.13) | collective-permute-done | bytes 98336 | tf_op jit(solution)/shard_map/ppermute | solution.py:24
  50.5 1.9 %collective-permute-start.17 = (bf16[12,32,128]{2,1,0:T(8,128)(2,1)S(1)}, bf16[12,32,128]{2,1,0:T(8,128)(2,1)S(1)}, u32[]{:S(2)}, u32[]{:S(2)}) collective-permute-start(bf16[12,32,128]{2,1,0:T(8,128)(2,1)S(1)} %fusion.6.refs_0_.refs_2_), channel_id=1, source_target_pairs={{0,24},{4,28},{8,16},{12,20},{16,8},{20,12},{24,0},{28,4},{1,25},{... | collective-permute-start | bytes 294920 | tf_op jit(solution)/shard_map/ppermute | solution.py:24
  52.4 2.6 %collective-permute-start.15 = (bf16[12,32,128]{2,1,0:T(8,128)(2,1)S(1)}, bf16[12,32,128]{2,1,0:T(8,128)(2,1)S(1)}, u32[]{:S(2)}, u32[]{:S(2)}) collective-permute-start(bf16[12,32,128]{2,1,0:T(8,128)(2,1)S(1)} %fusion.6.refs_0_.refs_2_), channel_id=1, source_target_pairs={{0,8},{4,12},{8,0},{12,4},{16,24},{20,28},{24,16},{28,20},{1,9},{5... | collective-permute-start | bytes 294920 | tf_op jit(solution)/shard_map/ppermute | solution.py:24
  54.9 3.2 %collective-permute-done.17.refs_3_.refs_5_ = bf16[12,32,128]{2,1,0:T(8,128)(2,1)S(1)} collective-permute-done((bf16[12,32,128]{2,1,0:T(8,128)(2,1)S(1)}, bf16[12,32,128]{2,1,0:T(8,128)(2,1)S(1)}, u32[]{:S(2)}, u32[]{:S(2)}) %collective-permute-start.17) | collective-permute-done | bytes 98336 | tf_op jit(solution)/shard_map/ppermute | solution.py:24
  58.1 2.8 %collective-permute-done.16.refs_2_.refs_4_ = bf16[12,32,128]{2,1,0:T(8,128)(2,1)S(1)} collective-permute-done((bf16[12,32,128]{2,1,0:T(8,128)(2,1)S(1)}, bf16[12,32,128]{2,1,0:T(8,128)(2,1)S(1)}, u32[]{:S(2)}, u32[]{:S(2)}) %collective-permute-start.16) | collective-permute-done | bytes 98336 | tf_op jit(solution)/shard_map/ppermute | solution.py:24
  62.4 2.0 %shard_map.77 = (bf16[24,32,128]{2,1,0:T(8,128)(2,1)S(1)}, bf16[24,32,128]{2,1,0:T(8,128)(2,1)S(1)}) custom-call(s32[64]{0:T(128)S(1)} %reshape.18.entry_ref, f32[32]{0:T(128)S(1)} %select_reduce_fusion.scale_ref, s32[3]{0:T(128)S(1)} %pad_add_fusion.place_ref, bf16[12,32,128]{2,1,0:T(8,128)(2,1)S(1)} %fusion.6.refs_0_.refs_2_, ...), custom_call_target="tpu_custom_call" | custom-call | flops 134217728 | bytes 4194304 | tf_op jit(solution)/shard_map/pallas_call | solution.py:253
  64.4 1.6 %collective-permute-start.22 = (bf16[24,32,128]{2,1,0:T(8,128)(2,1)S(1)}, bf16[24,32,128]{2,1,0:T(8,128)(2,1)S(1)}, u32[]{:S(2)}, u32[]{:S(2)}) collective-permute-start(bf16[24,32,128]{2,1,0:T(8,128)(2,1)S(1)} %get-tuple-element.45), channel_id=1, source_target_pairs={{0,1},{1,0},{2,3},{3,2},{4,5},{5,4},{6,7},{7,6},{8,9},{9,8},{10,11... | collective-permute-start | bytes 589832 | tf_op jit(solution)/shard_map/ppermute | solution.py:24
  66.4 5.2 %collective-permute-done.22 = bf16[24,32,128]{2,1,0:T(8,128)(2,1)S(1)} collective-permute-done((bf16[24,32,128]{2,1,0:T(8,128)(2,1)S(1)}, bf16[24,32,128]{2,1,0:T(8,128)(2,1)S(1)}, u32[]{:S(2)}, u32[]{:S(2)}) %collective-permute-start.22) | collective-permute-done | bytes 196640 | tf_op jit(solution)/shard_map/ppermute | solution.py:24
  73.8 4.2 %collective-permute-done.23 = bf16[24,32,128]{2,1,0:T(8,128)(2,1)S(1)} collective-permute-done((bf16[24,32,128]{2,1,0:T(8,128)(2,1)S(1)}, bf16[24,32,128]{2,1,0:T(8,128)(2,1)S(1)}, u32[]{:S(2)}, u32[]{:S(2)}) %collective-permute-start.23) | collective-permute-done | bytes 196640 | tf_op jit(solution)/shard_map/ppermute | solution.py:24
  79.0 2.4 %shard_map.79 = bf16[2,4,4,12288]{3,2,1,0:T(4,128)(2,1)S(1)} custom-call(s32[64]{0:T(128)S(1)} %reshape.18.entry_ref, f32[32]{0:T(128)S(1)} %select_reduce_fusion.scale_ref, s32[3]{0:T(128)S(1)} %pad_add_fusion.place_ref, bf16[24,32,128]{2,1,0:T(8,128)(2,1)S(1)} %add_convert_fusion.3.refs_0_, bf16[24,32,128]{2,1,0:T(8,128)(2,1)S(1)} %add_convert_fusion.1.refs_1_, ...), custom_call_target="tpu_custom_call" | custom-call | flops 134217728 | bytes 4194304 | tf_op jit(solution)/shard_map/pallas_call | solution.py:253
  81.7 1.7 %collective-permute-done.26 = bf16[4,4,12288]{2,1,0:T(4,128)(2,1)S(1)} collective-permute-done((bf16[4,4,12288]{2,1,0:T(4,128)(2,1)S(1)}, bf16[4,4,12288]{2,1,0:T(4,128)(2,1)S(1)}, u32[]{:S(2)}, u32[]{:S(2)}) %collective-permute-start.26) | collective-permute-done | bytes 393248 | tf_op jit(solution)/shard_map/ppermute | solution.py:24
  83.8 1.6 %collective-permute-start.29 = (bf16[4,12288]{1,0:T(4,128)(2,1)S(1)}, bf16[4,12288]{1,0:T(4,128)(2,1)S(1)}, u32[]{:S(2)}, u32[]{:S(2)}) collective-permute-start(bf16[4,12288]{1,0:T(4,128)(2,1)S(1)} %get-tuple-element.51), channel_id=1, source_target_pairs={{0,24},{4,28},{8,16},{12,20},{16,8},{20,12},{24,0},{28,4},{1,25},{... | collective-permute-start | bytes 294920 | tf_op jit(solution)/shard_map/ppermute | solution.py:24
  85.4 1.9 %collective-permute-start.28 = (bf16[4,12288]{1,0:T(4,128)(2,1)S(1)}, bf16[4,12288]{1,0:T(4,128)(2,1)S(1)}, u32[]{:S(2)}, u32[]{:S(2)}) collective-permute-start(bf16[4,12288]{1,0:T(4,128)(2,1)S(1)} %get-tuple-element.52), channel_id=1, source_target_pairs={{0,16},{4,20},{8,24},{12,28},{16,0},{20,4},{24,8},{28,12},{1,17},{... | collective-permute-start | bytes 294920 | tf_op jit(solution)/shard_map/ppermute | solution.py:24
  87.3 1.5 %shard_map.78 = (bf16[8,6144]{1,0:T(8,128)(2,1)}, bf16[4,12288]{1,0:T(4,128)(2,1)}) custom-call(s32[3]{0:T(128)S(1)} %pad_add_fusion.place_ref, bf16[24,32,128]{2,1,0:T(8,128)(2,1)S(1)} %add_convert_fusion.7.refs_0_, bf16[24,32,128]{2,1,0:T(8,128)(2,1)S(1)} %add_convert_fusion.5.refs_1_, bf16[12,32,128]{2,1,0:T(8,128)(2,1)S(1)} %fusion.6.refs_0_.refs_2_, ...), custom_call_target="tpu_custom_call" | custom-call | bytes 393216 | tf_op jit(solution)/shard_map/pallas_call | solution.py:242
  90.1 1.3 %collective-permute-done.29 = bf16[4,12288]{1,0:T(4,128)(2,1)S(1)} collective-permute-done((bf16[4,12288]{1,0:T(4,128)(2,1)S(1)}, bf16[4,12288]{1,0:T(4,128)(2,1)S(1)}, u32[]{:S(2)}, u32[]{:S(2)}) %collective-permute-start.29) | collective-permute-done | bytes 98336 | tf_op jit(solution)/shard_map/ppermute | solution.py:24
  91.4 4.7 %collective-permute-done.28 = bf16[4,12288]{1,0:T(4,128)(2,1)S(1)} collective-permute-done((bf16[4,12288]{1,0:T(4,128)(2,1)S(1)}, bf16[4,12288]{1,0:T(4,128)(2,1)S(1)}, u32[]{:S(2)}, u32[]{:S(2)}) %collective-permute-start.28) | collective-permute-done | bytes 98336 | tf_op jit(solution)/shard_map/ppermute | solution.py:24
  (60 shorter events, 14.7 us)
Async XLA Ops:
  0.6 9.9 %collective-permute-start.1 = (bf16[4,12288]{1,0:T(4,128)(2,1)}, bf16[4,12288]{1,0:T(4,128)(2,1)S(1)}, u32[]{:S(2)}, u32[]{:S(2)}) collective-permute-start(bf16[4,12288]{1,0:T(4,128)(2,1)} %param.4), channel_id=1, source_target_pairs={{0,16},{4,20},{8,24},{12,28},{16,0},{20,4},{24,8},{28,12},{1,17},{... | collective-permute-start | bytes 294920 | tf_op jit(solution)/shard_map/ppermute | solution.py:24
  4.7 6.4 %collective-permute-start = (bf16[4,12288]{1,0:T(4,128)(2,1)}, bf16[4,12288]{1,0:T(4,128)(2,1)S(1)}, u32[]{:S(2)}, u32[]{:S(2)}) collective-permute-start(bf16[4,12288]{1,0:T(4,128)(2,1)} %param.4), channel_id=1, source_target_pairs={{0,8},{4,12},{8,0},{12,4},{16,24},{20,28},{24,16},{28,20},{1,9},{5... | collective-permute-start | bytes 294920 | tf_op jit(solution)/shard_map/ppermute | solution.py:24
  6.3 7.4 %collective-permute-start.3 = (bf16[4,12288]{1,0:T(4,128)(2,1)}, bf16[4,12288]{1,0:T(4,128)(2,1)S(1)}, u32[]{:S(2)}, u32[]{:S(2)}) collective-permute-start(bf16[4,12288]{1,0:T(4,128)(2,1)} %param.4), channel_id=1, source_target_pairs={{0,4},{4,0},{8,12},{12,8},{16,20},{20,16},{24,28},{28,24},{1,5},{5... | collective-permute-start | bytes 294920 | tf_op jit(solution)/shard_map/ppermute | solution.py:24
  6.3 7.3 %collective-permute-start.2 = (bf16[4,12288]{1,0:T(4,128)(2,1)}, bf16[4,12288]{1,0:T(4,128)(2,1)S(1)}, u32[]{:S(2)}, u32[]{:S(2)}) collective-permute-start(bf16[4,12288]{1,0:T(4,128)(2,1)} %param.4), channel_id=1, source_target_pairs={{0,24},{4,28},{8,16},{12,20},{16,8},{20,12},{24,0},{28,4},{1,25},{... | collective-permute-start | bytes 294920 | tf_op jit(solution)/shard_map/ppermute | solution.py:24
  9.7 23.9 %copy-start = (bf16[32,256,256]{2,1,0:T(8,128)(2,1)S(1)}, bf16[32,256,256]{2,1,0:T(8,128)(2,1)}, u32[]{:S(2)}) copy-start(bf16[32,256,256]{2,1,0:T(8,128)(2,1)} %refs_2_.3) | copy-start | bytes 12582916
  10.6 3.1 %collective-permute-start.5 = (bf16[4,12288]{1,0:T(4,128)(2,1)S(1)}, bf16[4,12288]{1,0:T(4,128)(2,1)S(1)}, u32[]{:S(2)}, u32[]{:S(2)}) collective-permute-start(bf16[4,12288]{1,0:T(4,128)(2,1)S(1)} %collective-permute-done.1.refs_2_), channel_id=1, source_target_pairs={{0,4},{4,0},{8,12},{12,8},{16,20},{20,16},{24,28},{28,24},{1,5},{5... | collective-permute-start | bytes 294920 | tf_op jit(solution)/shard_map/ppermute | solution.py:24
  11.1 2.6 %collective-permute-start.4 = (bf16[4,12288]{1,0:T(4,128)(2,1)S(1)}, bf16[4,12288]{1,0:T(4,128)(2,1)S(1)}, u32[]{:S(2)}, u32[]{:S(2)}) collective-permute-start(bf16[4,12288]{1,0:T(4,128)(2,1)S(1)} %collective-permute-done.refs_1_), channel_id=1, source_target_pairs={{0,4},{4,0},{8,12},{12,8},{16,20},{20,16},{24,28},{28,24},{1,5},{5... | collective-permute-start | bytes 294920 | tf_op jit(solution)/shard_map/ppermute | solution.py:24
  13.6 1.3 %collective-permute-start.6 = (bf16[4,12288]{1,0:T(4,128)(2,1)S(1)}, bf16[4,12288]{1,0:T(4,128)(2,1)S(1)}, u32[]{:S(2)}, u32[]{:S(2)}) collective-permute-start(bf16[4,12288]{1,0:T(4,128)(2,1)S(1)} %collective-permute-done.2.refs_3_), channel_id=1, source_target_pairs={{0,4},{4,0},{8,12},{12,8},{16,20},{20,16},{24,28},{28,24},{1,5},{5... | collective-permute-start | bytes 294920 | tf_op jit(solution)/shard_map/ppermute | solution.py:24
  18.8 7.0 %collective-permute-start.7 = (bf16[24,32,128]{2,1,0:T(8,128)(2,1)S(1)}, bf16[24,32,128]{2,1,0:T(8,128)(2,1)S(1)}, u32[]{:S(2)}, u32[]{:S(2)}) collective-permute-start(bf16[24,32,128]{2,1,0:T(8,128)(2,1)S(1)} %get-tuple-element.27), channel_id=1, source_target_pairs={{0,1},{1,0},{2,3},{3,2},{4,5},{5,4},{6,7},{7,6},{8,9},{9,8},{10,11... | collective-permute-start | bytes 589832 | tf_op jit(solution)/shard_map/ppermute | solution.py:24
  20.4 7.1 %collective-permute-start.9 = (bf16[24,32,128]{2,1,0:T(8,128)(2,1)S(1)}, bf16[24,32,128]{2,1,0:T(8,128)(2,1)S(1)}, u32[]{:S(2)}, u32[]{:S(2)}) collective-permute-start(bf16[24,32,128]{2,1,0:T(8,128)(2,1)S(1)} %get-tuple-element.28), channel_id=1, source_target_pairs={{0,2},{1,3},{2,0},{3,1},{4,6},{5,7},{6,4},{7,5},{8,10},{9,11},{10,... | collective-permute-start | bytes 589832 | tf_op jit(solution)/shard_map/ppermute | solution.py:24
  25.9 6.2 %collective-permute-start.8 = (bf16[24,32,128]{2,1,0:T(8,128)(2,1)S(1)}, bf16[24,32,128]{2,1,0:T(8,128)(2,1)S(1)}, u32[]{:S(2)}, u32[]{:S(2)}) collective-permute-start(bf16[24,32,128]{2,1,0:T(8,128)(2,1)S(1)} %add_convert_fusion.8), channel_id=1, source_target_pairs={{0,2},{1,3},{2,0},{3,1},{4,6},{5,7},{6,4},{7,5},{8,10},{9,11},{10,... | collective-permute-start | bytes 589832 | tf_op jit(solution)/shard_map/ppermute | solution.py:24
  27.6 5.9 %collective-permute-start.10 = (bf16[24,32,128]{2,1,0:T(8,128)(2,1)S(1)}, bf16[24,32,128]{2,1,0:T(8,128)(2,1)S(1)}, u32[]{:S(2)}, u32[]{:S(2)}) collective-permute-start(bf16[24,32,128]{2,1,0:T(8,128)(2,1)S(1)} %add_convert_fusion.6), channel_id=1, source_target_pairs={{0,1},{1,0},{2,3},{3,2},{4,5},{5,4},{6,7},{7,6},{8,9},{9,8},{10,11... | collective-permute-start | bytes 589832 | tf_op jit(solution)/shard_map/ppermute | solution.py:24
  35.0 1.8 %collective-permute-start.11 = (bf16[4,12,32,128]{3,2,1,0:T(8,128)(2,1)S(1)}, bf16[4,12,32,128]{3,2,1,0:T(8,128)(2,1)S(1)}, u32[]{:S(2)}, u32[]{:S(2)}) collective-permute-start(bf16[4,12,32,128]{3,2,1,0:T(8,128)(2,1)S(1)} %get-tuple-element.30), channel_id=1, source_target_pairs={{0,4},{4,0},{8,12},{12,8},{16,20},{20,16},{24,28},{28,24},{1,5},{5... | collective-permute-start | bytes 1179656 | tf_op jit(solution)/shard_map/ppermute | solution.py:24
  37.0 4.9 %collective-permute-start.12 = (bf16[12,32,128]{2,1,0:T(8,128)(2,1)S(1)}, bf16[12,32,128]{2,1,0:T(8,128)(2,1)S(1)}, u32[]{:S(2)}, u32[]{:S(2)}) collective-permute-start(bf16[12,32,128]{2,1,0:T(8,128)(2,1)S(1)} %get-tuple-element.53), channel_id=1, source_target_pairs={{0,8},{4,12},{8,0},{12,4},{16,24},{20,28},{24,16},{28,20},{1,9},{5... | collective-permute-start | bytes 294920 | tf_op jit(solution)/shard_map/ppermute | solution.py:24
  38.3 9.1 %collective-permute-start.14 = (bf16[12,32,128]{2,1,0:T(8,128)(2,1)S(1)}, bf16[12,32,128]{2,1,0:T(8,128)(2,1)S(1)}, u32[]{:S(2)}, u32[]{:S(2)}) collective-permute-start(bf16[12,32,128]{2,1,0:T(8,128)(2,1)S(1)} %get-tuple-element.54), channel_id=1, source_target_pairs={{0,24},{4,28},{8,16},{12,20},{16,8},{20,12},{24,0},{28,4},{1,25},{... | collective-permute-start | bytes 294920 | tf_op jit(solution)/shard_map/ppermute | solution.py:24
  41.6 8.9 %collective-permute-start.13 = (bf16[12,32,128]{2,1,0:T(8,128)(2,1)S(1)}, bf16[12,32,128]{2,1,0:T(8,128)(2,1)S(1)}, u32[]{:S(2)}, u32[]{:S(2)}) collective-permute-start(bf16[12,32,128]{2,1,0:T(8,128)(2,1)S(1)} %get-tuple-element.55), channel_id=1, source_target_pairs={{0,16},{4,20},{8,24},{12,28},{16,0},{20,4},{24,8},{28,12},{1,17},{... | collective-permute-start | bytes 294920 | tf_op jit(solution)/shard_map/ppermute | solution.py:24
  50.5 7.7 %collective-permute-start.17 = (bf16[12,32,128]{2,1,0:T(8,128)(2,1)S(1)}, bf16[12,32,128]{2,1,0:T(8,128)(2,1)S(1)}, u32[]{:S(2)}, u32[]{:S(2)}) collective-permute-start(bf16[12,32,128]{2,1,0:T(8,128)(2,1)S(1)} %fusion.6.refs_0_.refs_2_), channel_id=1, source_target_pairs={{0,24},{4,28},{8,16},{12,20},{16,8},{20,12},{24,0},{28,4},{1,25},{... | collective-permute-start | bytes 294920 | tf_op jit(solution)/shard_map/ppermute | solution.py:24
  52.4 8.6 %collective-permute-start.16 = (bf16[12,32,128]{2,1,0:T(8,128)(2,1)S(1)}, bf16[12,32,128]{2,1,0:T(8,128)(2,1)S(1)}, u32[]{:S(2)}, u32[]{:S(2)}) collective-permute-start(bf16[12,32,128]{2,1,0:T(8,128)(2,1)S(1)} %fusion.6.refs_0_.refs_2_), channel_id=1, source_target_pairs={{0,16},{4,20},{8,24},{12,28},{16,0},{20,4},{24,8},{28,12},{1,17},{... | collective-permute-start | bytes 294920 | tf_op jit(solution)/shard_map/ppermute | solution.py:24
  52.4 8.6 %collective-permute-start.15 = (bf16[12,32,128]{2,1,0:T(8,128)(2,1)S(1)}, bf16[12,32,128]{2,1,0:T(8,128)(2,1)S(1)}, u32[]{:S(2)}, u32[]{:S(2)}) collective-permute-start(bf16[12,32,128]{2,1,0:T(8,128)(2,1)S(1)} %fusion.6.refs_0_.refs_2_), channel_id=1, source_target_pairs={{0,8},{4,12},{8,0},{12,4},{16,24},{20,28},{24,16},{28,20},{1,9},{5... | collective-permute-start | bytes 294920 | tf_op jit(solution)/shard_map/ppermute | solution.py:24
  54.9 6.5 %collective-permute-start.18 = (bf16[12,32,128]{2,1,0:T(8,128)(2,1)S(1)}, bf16[12,32,128]{2,1,0:T(8,128)(2,1)S(1)}, u32[]{:S(2)}, u32[]{:S(2)}) collective-permute-start(bf16[12,32,128]{2,1,0:T(8,128)(2,1)S(1)} %fusion.6.refs_0_.refs_2_), channel_id=1, source_target_pairs={{0,4},{4,0},{8,12},{12,8},{16,20},{20,16},{24,28},{28,24},{1,5},{5... | collective-permute-start | bytes 294920 | tf_op jit(solution)/shard_map/ppermute | solution.py:24
  58.1 3.3 %collective-permute-start.21 = (bf16[12,32,128]{2,1,0:T(8,128)(2,1)S(1)}, bf16[12,32,128]{2,1,0:T(8,128)(2,1)S(1)}, u32[]{:S(2)}, u32[]{:S(2)}) collective-permute-start(bf16[12,32,128]{2,1,0:T(8,128)(2,1)S(1)} %collective-permute-done.17.refs_3_.refs_5_), channel_id=1, source_target_pairs={{0,4},{4,0},{8,12},{12,8},{16,20},{20,16},{24,28},{28,24},{1,5},{5... | collective-permute-start | bytes 294920 | tf_op jit(solution)/shard_map/ppermute | solution.py:24
  60.9 1.3 %collective-permute-start.20 = (bf16[12,32,128]{2,1,0:T(8,128)(2,1)S(1)}, bf16[12,32,128]{2,1,0:T(8,128)(2,1)S(1)}, u32[]{:S(2)}, u32[]{:S(2)}) collective-permute-start(bf16[12,32,128]{2,1,0:T(8,128)(2,1)S(1)} %collective-permute-done.16.refs_2_.refs_4_), channel_id=1, source_target_pairs={{0,4},{4,0},{8,12},{12,8},{16,20},{20,16},{24,28},{28,24},{1,5},{5... | collective-permute-start | bytes 294920 | tf_op jit(solution)/shard_map/ppermute | solution.py:24
  61.0 1.4 %collective-permute-start.19 = (bf16[12,32,128]{2,1,0:T(8,128)(2,1)S(1)}, bf16[12,32,128]{2,1,0:T(8,128)(2,1)S(1)}, u32[]{:S(2)}, u32[]{:S(2)}) collective-permute-start(bf16[12,32,128]{2,1,0:T(8,128)(2,1)S(1)} %collective-permute-done.15.refs_1_.refs_3_), channel_id=1, source_target_pairs={{0,4},{4,0},{8,12},{12,8},{16,20},{20,16},{24,28},{28,24},{1,5},{5... | collective-permute-start | bytes 294920 | tf_op jit(solution)/shard_map/ppermute | solution.py:24
  64.4 7.2 %collective-permute-start.22 = (bf16[24,32,128]{2,1,0:T(8,128)(2,1)S(1)}, bf16[24,32,128]{2,1,0:T(8,128)(2,1)S(1)}, u32[]{:S(2)}, u32[]{:S(2)}) collective-permute-start(bf16[24,32,128]{2,1,0:T(8,128)(2,1)S(1)} %get-tuple-element.45), channel_id=1, source_target_pairs={{0,1},{1,0},{2,3},{3,2},{4,5},{5,4},{6,7},{7,6},{8,9},{9,8},{10,11... | collective-permute-start | bytes 589832 | tf_op jit(solution)/shard_map/ppermute | solution.py:24
  65.9 6.9 %collective-permute-start.24 = (bf16[24,32,128]{2,1,0:T(8,128)(2,1)S(1)}, bf16[24,32,128]{2,1,0:T(8,128)(2,1)S(1)}, u32[]{:S(2)}, u32[]{:S(2)}) collective-permute-start(bf16[24,32,128]{2,1,0:T(8,128)(2,1)S(1)} %get-tuple-element.46), channel_id=1, source_target_pairs={{0,2},{1,3},{2,0},{3,1},{4,6},{5,7},{6,4},{7,5},{8,10},{9,11},{10,... | collective-permute-start | bytes 589832 | tf_op jit(solution)/shard_map/ppermute | solution.py:24
  71.7 6.4 %collective-permute-start.23 = (bf16[24,32,128]{2,1,0:T(8,128)(2,1)S(1)}, bf16[24,32,128]{2,1,0:T(8,128)(2,1)S(1)}, u32[]{:S(2)}, u32[]{:S(2)}) collective-permute-start(bf16[24,32,128]{2,1,0:T(8,128)(2,1)S(1)} %add_convert_fusion.4), channel_id=1, source_target_pairs={{0,2},{1,3},{2,0},{3,1},{4,6},{5,7},{6,4},{7,5},{8,10},{9,11},{10,... | collective-permute-start | bytes 589832 | tf_op jit(solution)/shard_map/ppermute | solution.py:24
  72.9 6.1 %collective-permute-start.25 = (bf16[24,32,128]{2,1,0:T(8,128)(2,1)S(1)}, bf16[24,32,128]{2,1,0:T(8,128)(2,1)S(1)}, u32[]{:S(2)}, u32[]{:S(2)}) collective-permute-start(bf16[24,32,128]{2,1,0:T(8,128)(2,1)S(1)} %add_convert_fusion.2), channel_id=1, source_target_pairs={{0,1},{1,0},{2,3},{3,2},{4,5},{5,4},{6,7},{7,6},{8,9},{9,8},{10,11... | collective-permute-start | bytes 589832 | tf_op jit(solution)/shard_map/ppermute | solution.py:24
  81.6 1.8 %collective-permute-start.26 = (bf16[4,4,12288]{2,1,0:T(4,128)(2,1)S(1)}, bf16[4,4,12288]{2,1,0:T(4,128)(2,1)S(1)}, u32[]{:S(2)}, u32[]{:S(2)}) collective-permute-start(bf16[4,4,12288]{2,1,0:T(4,128)(2,1)S(1)} %slice_bitcast_fusion), channel_id=1, source_target_pairs={{0,4},{4,0},{8,12},{12,8},{16,20},{20,16},{24,28},{28,24},{1,5},{5... | collective-permute-start | bytes 1179656 | tf_op jit(solution)/shard_map/ppermute | solution.py:24
  83.8 6.3 %collective-permute-start.27 = (bf16[4,12288]{1,0:T(4,128)(2,1)S(1)}, bf16[4,12288]{1,0:T(4,128)(2,1)S(1)}, u32[]{:S(2)}, u32[]{:S(2)}) collective-permute-start(bf16[4,12288]{1,0:T(4,128)(2,1)S(1)} %get-tuple-element.50), channel_id=1, source_target_pairs={{0,8},{4,12},{8,0},{12,4},{16,24},{20,28},{24,16},{28,20},{1,9},{5... | collective-permute-start | bytes 294920 | tf_op jit(solution)/shard_map/ppermute | solution.py:24
  83.8 7.6 %collective-permute-start.29 = (bf16[4,12288]{1,0:T(4,128)(2,1)S(1)}, bf16[4,12288]{1,0:T(4,128)(2,1)S(1)}, u32[]{:S(2)}, u32[]{:S(2)}) collective-permute-start(bf16[4,12288]{1,0:T(4,128)(2,1)S(1)} %get-tuple-element.51), channel_id=1, source_target_pairs={{0,24},{4,28},{8,16},{12,20},{16,8},{20,12},{24,0},{28,4},{1,25},{... | collective-permute-start | bytes 294920 | tf_op jit(solution)/shard_map/ppermute | solution.py:24
  85.4 10.8 %collective-permute-start.28 = (bf16[4,12288]{1,0:T(4,128)(2,1)S(1)}, bf16[4,12288]{1,0:T(4,128)(2,1)S(1)}, u32[]{:S(2)}, u32[]{:S(2)}) collective-permute-start(bf16[4,12288]{1,0:T(4,128)(2,1)S(1)} %get-tuple-element.52), channel_id=1, source_target_pairs={{0,16},{4,20},{8,24},{12,28},{16,0},{20,4},{24,8},{28,12},{1,17},{... | collective-permute-start | bytes 294920 | tf_op jit(solution)/shard_map/ppermute | solution.py:24

commit v12 on v11

--- a/solution.py
+++ b/solution.py
@@ -11,10 +11,10 @@
 B = 256
 LANES = 128
 PER = B // LANES
-COPIES = 8
+COPIES = 4
 ROW_PARTS = 2
-CHUNK = 512
-UNROLL = 16
+CHUNK = 1024
+UNROLL = 48
 VMEM_LIMIT = 12 * 1024 * 1024
 FIRST_LIMIT = 50 * 1024 * 1024
 
@@ -37,12 +37,15 @@
 
 
 def start_hold(blocks_ref, held_ref, sems):
+    size = held_ref.shape[0]
+    before = blocks_ref.shape[0] - size
     copies = []
-    for i, (start, size) in enumerate(spans(blocks_ref.shape[0], COPIES)):
-        span = pl.ds(start, size)
-        copies.append(pltpu.make_async_copy(blocks_ref.at[span], held_ref.at[span], sems.at[i]))
-        copies[-1].start()
-    return [(start, copy) for (start, _), copy in zip(spans(blocks_ref.shape[0], COPIES), copies)]
+    for i, (start, count) in enumerate(spans(size, COPIES)):
+        source = blocks_ref.at[pl.ds(before + start, count)]
+        copy = pltpu.make_async_copy(source, held_ref.at[pl.ds(start, count)], sems.at[i])
+        copy.start()
+        copies.append((before + start, copy))
+    return copies
 
 
 def pick_rows(values, index, size):
@@ -87,7 +90,7 @@
     for block_ref in block_refs:
         for slot in range(block_ref.shape[0]):
             for start, copy in copies:
-                if start == slot:
+                if start == at:
                     copy.wait()
             row, col, scale = entry_ref[2 * at], entry_ref[2 * at + 1], scale_ref[at]
             at += 1
@@ -128,7 +131,7 @@
 
 def first_kernel(ways, entry_ref, scale_ref, place_ref, *refs):
     count = 2 * ways
-    pieces, blocks_ref, outs = refs[:count], refs[count], refs[count + 1 : -5]
+    pieces, ready_ref, blocks_ref, outs = refs[:count], refs[count], refs[count + 1], refs[count + 2 : -5]
     total, wide, x, held_ref, sems = refs[-5:]
     copies = start_hold(blocks_ref, held_ref, sems)
     core, along = place_ref[0], place_ref[1]
@@ -155,7 +158,7 @@
     def load(block):
         return x[:, pl.ds(pl.multiple_of(block * B, B), B)]
 
-    add_products(entry_ref, scale_ref, load, [held_ref], total, False, copies)
+    add_products(entry_ref, scale_ref, load, [ready_ref, held_ref], total, False, copies)
     write_parts(total, outs)
 
 
@@ -295,10 +298,11 @@
         return same + [swap(one, "panel", 1) for one in same]
 
     mine = jnp.where(core >= 0, strengths, 0)
-    own_copy = [pltpu.VMEM(blocks.shape, blocks.dtype), pltpu.SemaphoreType.DMA((COPIES,))]
+    ready = jnp.where(core >= 0, blocks[: slots // 2], 0)
+    own_copy = [pltpu.VMEM((slots - slots // 2, B, B), blocks.dtype), pltpu.SemaphoreType.DMA((COPIES,))]
     scratches = [rows_total, *flat, *own_copy]
     first_sums = over_case(
-        product(first_kernel, [mine, *gather_panel(strengths)[1:]], row_shapes, scratches, FIRST_LIMIT, pl.BlockSpec(memory_space=pl.ANY))
+        product(first_kernel, [mine, *gather_panel(strengths)[1:], ready], row_shapes, scratches, FIRST_LIMIT, pl.BlockSpec(memory_space=pl.ANY))
     )
     outs = [(ways, part_size, cases, LANES)] * 2
     pieces = gather_panel(scatter_panel(*product(adjoint_kernel, first_sums, outs, [cols_total, rows_held])))

time: 97.1 us -> 96 us (0.989)
  Pallas kernels: 12.6 us -> 11.4 us
    select_n x0 -> x1, other arithmetic: none -> 1.74 us  [shards(): ready = jnp.where(core >= 0, blocks[:slots // 2], 0)]
    pallas_call x4, Pallas kernels: 9.8 us -> 8.66 us  [product(): pl.pallas_call(functools.partial(kernel, ways), out_shape=[jax.ShapeDtype...]
    ppermute x30, waiting for transfers between devices: 47.4 us -> 46.5 us  [swap(): return lax.ppermute(value, axis, [(i, i ^ offset) for i in range(count)])]
  transfers between devices with their start and end apart: 30 -> 30, of which waited for: 19 -> 19; matrix products, arithmetic and copies ran while one was open for 5% -> 6% of each run, Pallas kernels for 3% -> 3%
where the time goes in v12:
time: 96 us; the launch traced here: 95.8 us
  waiting for transfers between devices  46.5 us (48%)
  starting transfers between devices  30 us (31%)
  Pallas kernels  11.4 us (12%)
  other arithmetic  5.9 us (6%)
  local copies, waits for them, and re-layouts  1.15 us (1%)
    ppermute x30, waiting for transfers between devices, swap(): return lax.ppermute(value, axis, [(i, i ^ offset) for i in range(count)])  46.5 us
    ppermute x30, starting transfers between devices, swap(): return lax.ppermute(value, axis, [(i, i ^ offset) for i in range(count)])  30 us
    pallas_call x4, Pallas kernels, product(): pl.pallas_call(functools.partial(kernel, ways), out_shape=[jax.ShapeDtype...  8.66 us
    pallas_call x2, Pallas kernels, cut(): pl.pallas_call(functools.partial(kernel, ways), out_shape=[jax.ShapeDtype...  2.77 us
  transfers between devices with their start and end apart: 30, of which 19 were waited for; matrix products, arithmetic and copies ran while one was open for 6% of the time, Pallas kernels for 3%

profile of v12, /device:TPU:0, one launch (start us, length us, event | category | flops | bytes accessed | tf_op | source)
XLA Modules:
  0.0 95.8 jit_solution(16913164589855790383)
XLA Ops:
  0.6 4.1 %collective-permute-start.1 = (bf16[4,12288]{1,0:T(4,128)(2,1)}, bf16[4,12288]{1,0:T(4,128)(2,1)S(1)}, u32[]{:S(2)}, u32[]{:S(2)}) collective-permute-start(bf16[4,12288]{1,0:T(4,128)(2,1)} %param.4), channel_id=1, source_target_pairs={{0,16},{4,20},{8,24},{12,28},{16,0},{20,4},{24,8},{28,12},{1,17},{... | collective-permute-start | bytes 294920 | tf_op jit(solution)/shard_map/ppermute | solution.py:24
  4.7 1.6 %collective-permute-start = (bf16[4,12288]{1,0:T(4,128)(2,1)}, bf16[4,12288]{1,0:T(4,128)(2,1)S(1)}, u32[]{:S(2)}, u32[]{:S(2)}) collective-permute-start(bf16[4,12288]{1,0:T(4,128)(2,1)} %param.4), channel_id=1, source_target_pairs={{0,8},{4,12},{8,0},{12,4},{16,24},{20,28},{24,16},{28,20},{1,9},{5... | collective-permute-start | bytes 294920 | tf_op jit(solution)/shard_map/ppermute | solution.py:24
  9.7 1.7 %slice_select_fusion.refs_8_ = bf16[16,256,256]{2,1,0:T(8,128)(2,1)S(1)} fusion(bf16[32,256,256]{2,1,0:T(8,128)(2,1)} %refs_2_.3, pred[]{:T(512)S(6)} %ge.12), kind=kLoop, calls=%fused_computation | loop fusion | flops 1048576 | bytes 4194305 | tf_op jit(solution)/shard_map/jit(_where)/select_n | solution.py:301
  12.2 1.5 %collective-permute-done.2.refs_3_ = bf16[4,12288]{1,0:T(4,128)(2,1)S(1)} collective-permute-done((bf16[4,12288]{1,0:T(4,128)(2,1)}, bf16[4,12288]{1,0:T(4,128)(2,1)S(1)}, u32[]{:S(2)}, u32[]{:S(2)}) %collective-permute-start.2) | collective-permute-done | bytes 98336 | tf_op jit(solution)/shard_map/ppermute | solution.py:24
  14.9 3.0 %shard_map.75 = (bf16[24,32,128]{2,1,0:T(8,128)(2,1)S(1)}, bf16[24,32,128]{2,1,0:T(8,128)(2,1)S(1)}) custom-call(s32[64]{0:T(128)S(1)} %reshape.18.entry_ref, f32[32]{0:T(128)S(1)} %select_reduce_fusion.scale_ref, s32[3]{0:T(128)S(1)} %pad_add_fusion.place_ref, bf16[4,12288]{1,0:T(4,128)(2,1)S(1)} %broadcast_select_fusion.refs_0_, ...), custom_call_target="tpu_custom_call" | custom-call | flops 134217728 | bytes 4194304 | tf_op jit(solution)/shard_map/pallas_call | solution.py:256
  18.0 1.6 %collective-permute-start.7 = (bf16[24,32,128]{2,1,0:T(8,128)(2,1)S(1)}, bf16[24,32,128]{2,1,0:T(8,128)(2,1)S(1)}, u32[]{:S(2)}, u32[]{:S(2)}) collective-permute-start(bf16[24,32,128]{2,1,0:T(8,128)(2,1)S(1)} %get-tuple-element.27), channel_id=1, source_target_pairs={{0,1},{1,0},{2,3},{3,2},{4,5},{5,4},{6,7},{7,6},{8,9},{9,8},{10,11... | collective-permute-start | bytes 589832 | tf_op jit(solution)/shard_map/ppermute | solution.py:24
  19.5 1.5 %collective-permute-start.9 = (bf16[24,32,128]{2,1,0:T(8,128)(2,1)S(1)}, bf16[24,32,128]{2,1,0:T(8,128)(2,1)S(1)}, u32[]{:S(2)}, u32[]{:S(2)}) collective-permute-start(bf16[24,32,128]{2,1,0:T(8,128)(2,1)S(1)} %get-tuple-element.28), channel_id=1, source_target_pairs={{0,2},{1,3},{2,0},{3,1},{4,6},{5,7},{6,4},{7,5},{8,10},{9,11},{10,... | collective-permute-start | bytes 589832 | tf_op jit(solution)/shard_map/ppermute | solution.py:24
  21.1 3.9 %collective-permute-done.7 = bf16[24,32,128]{2,1,0:T(8,128)(2,1)S(1)} collective-permute-done((bf16[24,32,128]{2,1,0:T(8,128)(2,1)S(1)}, bf16[24,32,128]{2,1,0:T(8,128)(2,1)S(1)}, u32[]{:S(2)}, u32[]{:S(2)}) %collective-permute-start.7) | collective-permute-done | bytes 196640 | tf_op jit(solution)/shard_map/ppermute | solution.py:24
  25.1 1.6 %collective-permute-start.8 = (bf16[24,32,128]{2,1,0:T(8,128)(2,1)S(1)}, bf16[24,32,128]{2,1,0:T(8,128)(2,1)S(1)}, u32[]{:S(2)}, u32[]{:S(2)}) collective-permute-start(bf16[24,32,128]{2,1,0:T(8,128)(2,1)S(1)} %add_convert_fusion.8), channel_id=1, source_target_pairs={{0,2},{1,3},{2,0},{3,1},{4,6},{5,7},{6,4},{7,5},{8,10},{9,11},{10,... | collective-permute-start | bytes 589832 | tf_op jit(solution)/shard_map/ppermute | solution.py:24
  26.7 1.6 %collective-permute-start.10 = (bf16[24,32,128]{2,1,0:T(8,128)(2,1)S(1)}, bf16[24,32,128]{2,1,0:T(8,128)(2,1)S(1)}, u32[]{:S(2)}, u32[]{:S(2)}) collective-permute-start(bf16[24,32,128]{2,1,0:T(8,128)(2,1)S(1)} %add_convert_fusion.6), channel_id=1, source_target_pairs={{0,1},{1,0},{2,3},{3,2},{4,5},{5,4},{6,7},{7,6},{8,9},{9,8},{10,11... | collective-permute-start | bytes 589832 | tf_op jit(solution)/shard_map/ppermute | solution.py:24
  28.3 3.0 %collective-permute-done.8 = bf16[24,32,128]{2,1,0:T(8,128)(2,1)S(1)} collective-permute-done((bf16[24,32,128]{2,1,0:T(8,128)(2,1)S(1)}, bf16[24,32,128]{2,1,0:T(8,128)(2,1)S(1)}, u32[]{:S(2)}, u32[]{:S(2)}) %collective-permute-start.8) | collective-permute-done | bytes 196640 | tf_op jit(solution)/shard_map/ppermute | solution.py:24
  32.7 1.5 %shard_map.76 = (bf16[4,12,32,128]{3,2,1,0:T(8,128)(2,1)S(1)}, bf16[4,12,32,128]{3,2,1,0:T(8,128)(2,1)S(1)}) custom-call(s32[64]{0:T(128)S(1)} %reshape.18.entry_ref, f32[32]{0:T(128)S(1)} %select_reduce_fusion.scale_ref, s32[3]{0:T(128)S(1)} %pad_add_fusion.place_ref, bf16[24,32,128]{2,1,0:T(8,128)(2,1)S(1)} %add_convert_fusion.7.refs_0_, ...), custom_call_target="tpu_custom_call" | custom-call | flops 134217728 | bytes 4194304 | tf_op jit(solution)/shard_map/pallas_call | solution.py:256
  34.3 1.7 %collective-permute-done.11 = bf16[4,12,32,128]{3,2,1,0:T(8,128)(2,1)S(1)} collective-permute-done((bf16[4,12,32,128]{3,2,1,0:T(8,128)(2,1)S(1)}, bf16[4,12,32,128]{3,2,1,0:T(8,128)(2,1)S(1)}, u32[]{:S(2)}, u32[]{:S(2)}) %collective-permute-start.11) | collective-permute-done | bytes 393248 | tf_op jit(solution)/shard_map/ppermute | solution.py:24
  36.1 1.3 %collective-permute-start.12 = (bf16[12,32,128]{2,1,0:T(8,128)(2,1)S(1)}, bf16[12,32,128]{2,1,0:T(8,128)(2,1)S(1)}, u32[]{:S(2)}, u32[]{:S(2)}) collective-permute-start(bf16[12,32,128]{2,1,0:T(8,128)(2,1)S(1)} %get-tuple-element.53), channel_id=1, source_target_pairs={{0,8},{4,12},{8,0},{12,4},{16,24},{20,28},{24,16},{28,20},{1,9},{5... | collective-permute-start | bytes 294920 | tf_op jit(solution)/shard_map/ppermute | solution.py:24
  37.4 3.3 %collective-permute-start.14 = (bf16[12,32,128]{2,1,0:T(8,128)(2,1)S(1)}, bf16[12,32,128]{2,1,0:T(8,128)(2,1)S(1)}, u32[]{:S(2)}, u32[]{:S(2)}) collective-permute-start(bf16[12,32,128]{2,1,0:T(8,128)(2,1)S(1)} %get-tuple-element.54), channel_id=1, source_target_pairs={{0,24},{4,28},{8,16},{12,20},{16,8},{20,12},{24,0},{28,4},{1,25},{... | collective-permute-start | bytes 294920 | tf_op jit(solution)/shard_map/ppermute | solution.py:24
  41.0 5.5 %collective-permute-done.14 = bf16[12,32,128]{2,1,0:T(8,128)(2,1)S(1)} collective-permute-done((bf16[12,32,128]{2,1,0:T(8,128)(2,1)S(1)}, bf16[12,32,128]{2,1,0:T(8,128)(2,1)S(1)}, u32[]{:S(2)}, u32[]{:S(2)}) %collective-permute-start.14) | collective-permute-done | bytes 98336 | tf_op jit(solution)/shard_map/ppermute | solution.py:24
  46.5 3.0 %collective-permute-done.13 = bf16[12,32,128]{2,1,0:T(8,128)(2,1)S(1)} collective-permute-done((bf16[12,32,128]{2,1,0:T(8,128)(2,1)S(1)}, bf16[12,32,128]{2,1,0:T(8,128)(2,1)S(1)}, u32[]{:S(2)}, u32[]{:S(2)}) %collective-permute-start.13) | collective-permute-done | bytes 98336 | tf_op jit(solution)/shard_map/ppermute | solution.py:24
  49.6 1.9 %collective-permute-start.17 = (bf16[12,32,128]{2,1,0:T(8,128)(2,1)S(1)}, bf16[12,32,128]{2,1,0:T(8,128)(2,1)S(1)}, u32[]{:S(2)}, u32[]{:S(2)}) collective-permute-start(bf16[12,32,128]{2,1,0:T(8,128)(2,1)S(1)} %fusion.6.refs_0_.refs_2_), channel_id=1, source_target_pairs={{0,24},{4,28},{8,16},{12,20},{16,8},{20,12},{24,0},{28,4},{1,25},{... | collective-permute-start | bytes 294920 | tf_op jit(solution)/shard_map/ppermute | solution.py:24
  51.5 2.6 %collective-permute-start.15 = (bf16[12,32,128]{2,1,0:T(8,128)(2,1)S(1)}, bf16[12,32,128]{2,1,0:T(8,128)(2,1)S(1)}, u32[]{:S(2)}, u32[]{:S(2)}) collective-permute-start(bf16[12,32,128]{2,1,0:T(8,128)(2,1)S(1)} %fusion.6.refs_0_.refs_2_), channel_id=1, source_target_pairs={{0,8},{4,12},{8,0},{12,4},{16,24},{20,28},{24,16},{28,20},{1,9},{5... | collective-permute-start | bytes 294920 | tf_op jit(solution)/shard_map/ppermute | solution.py:24
  54.1 3.2 %collective-permute-done.17.refs_3_.refs_5_ = bf16[12,32,128]{2,1,0:T(8,128)(2,1)S(1)} collective-permute-done((bf16[12,32,128]{2,1,0:T(8,128)(2,1)S(1)}, bf16[12,32,128]{2,1,0:T(8,128)(2,1)S(1)}, u32[]{:S(2)}, u32[]{:S(2)}) %collective-permute-start.17) | collective-permute-done | bytes 98336 | tf_op jit(solution)/shard_map/ppermute | solution.py:24
  57.3 2.8 %collective-permute-done.16.refs_2_.refs_4_ = bf16[12,32,128]{2,1,0:T(8,128)(2,1)S(1)} collective-permute-done((bf16[12,32,128]{2,1,0:T(8,128)(2,1)S(1)}, bf16[12,32,128]{2,1,0:T(8,128)(2,1)S(1)}, u32[]{:S(2)}, u32[]{:S(2)}) %collective-permute-start.16) | collective-permute-done | bytes 98336 | tf_op jit(solution)/shard_map/ppermute | solution.py:24
  61.5 2.0 %shard_map.77 = (bf16[24,32,128]{2,1,0:T(8,128)(2,1)S(1)}, bf16[24,32,128]{2,1,0:T(8,128)(2,1)S(1)}) custom-call(s32[64]{0:T(128)S(1)} %reshape.18.entry_ref, f32[32]{0:T(128)S(1)} %select_reduce_fusion.scale_ref, s32[3]{0:T(128)S(1)} %pad_add_fusion.place_ref, bf16[12,32,128]{2,1,0:T(8,128)(2,1)S(1)} %fusion.6.refs_0_.refs_2_, ...), custom_call_target="tpu_custom_call" | custom-call | flops 134217728 | bytes 4194304 | tf_op jit(solution)/shard_map/pallas_call | solution.py:256
  63.5 1.6 %collective-permute-start.22 = (bf16[24,32,128]{2,1,0:T(8,128)(2,1)S(1)}, bf16[24,32,128]{2,1,0:T(8,128)(2,1)S(1)}, u32[]{:S(2)}, u32[]{:S(2)}) collective-permute-start(bf16[24,32,128]{2,1,0:T(8,128)(2,1)S(1)} %get-tuple-element.45), channel_id=1, source_target_pairs={{0,1},{1,0},{2,3},{3,2},{4,5},{5,4},{6,7},{7,6},{8,9},{9,8},{10,11... | collective-permute-start | bytes 589832 | tf_op jit(solution)/shard_map/ppermute | solution.py:24
  65.6 5.1 %collective-permute-done.22 = bf16[24,32,128]{2,1,0:T(8,128)(2,1)S(1)} collective-permute-done((bf16[24,32,128]{2,1,0:T(8,128)(2,1)S(1)}, bf16[24,32,128]{2,1,0:T(8,128)(2,1)S(1)}, u32[]{:S(2)}, u32[]{:S(2)}) %collective-permute-start.22) | collective-permute-done | bytes 196640 | tf_op jit(solution)/shard_map/ppermute | solution.py:24
  73.0 4.2 %collective-permute-done.23 = bf16[24,32,128]{2,1,0:T(8,128)(2,1)S(1)} collective-permute-done((bf16[24,32,128]{2,1,0:T(8,128)(2,1)S(1)}, bf16[24,32,128]{2,1,0:T(8,128)(2,1)S(1)}, u32[]{:S(2)}, u32[]{:S(2)}) %collective-permute-start.23) | collective-permute-done | bytes 196640 | tf_op jit(solution)/shard_map/ppermute | solution.py:24
  78.2 2.2 %shard_map.79 = bf16[2,4,4,12288]{3,2,1,0:T(4,128)(2,1)S(1)} custom-call(s32[64]{0:T(128)S(1)} %reshape.18.entry_ref, f32[32]{0:T(128)S(1)} %select_reduce_fusion.scale_ref, s32[3]{0:T(128)S(1)} %pad_add_fusion.place_ref, bf16[24,32,128]{2,1,0:T(8,128)(2,1)S(1)} %add_convert_fusion.3.refs_0_, bf16[24,32,128]{2,1,0:T(8,128)(2,1)S(1)} %add_convert_fusion.1.refs_1_, ...), custom_call_target="tpu_custom_call" | custom-call | flops 134217728 | bytes 4194304 | tf_op jit(solution)/shard_map/pallas_call | solution.py:256
  80.6 1.7 %collective-permute-done.26 = bf16[4,4,12288]{2,1,0:T(4,128)(2,1)S(1)} collective-permute-done((bf16[4,4,12288]{2,1,0:T(4,128)(2,1)S(1)}, bf16[4,4,12288]{2,1,0:T(4,128)(2,1)S(1)}, u32[]{:S(2)}, u32[]{:S(2)}) %collective-permute-start.26) | collective-permute-done | bytes 393248 | tf_op jit(solution)/shard_map/ppermute | solution.py:24
  82.7 1.6 %collective-permute-start.29 = (bf16[4,12288]{1,0:T(4,128)(2,1)S(1)}, bf16[4,12288]{1,0:T(4,128)(2,1)S(1)}, u32[]{:S(2)}, u32[]{:S(2)}) collective-permute-start(bf16[4,12288]{1,0:T(4,128)(2,1)S(1)} %get-tuple-element.51), channel_id=1, source_target_pairs={{0,24},{4,28},{8,16},{12,20},{16,8},{20,12},{24,0},{28,4},{1,25},{... | collective-permute-start | bytes 294920 | tf_op jit(solution)/shard_map/ppermute | solution.py:24
  84.3 1.9 %collective-permute-start.28 = (bf16[4,12288]{1,0:T(4,128)(2,1)S(1)}, bf16[4,12288]{1,0:T(4,128)(2,1)S(1)}, u32[]{:S(2)}, u32[]{:S(2)}) collective-permute-start(bf16[4,12288]{1,0:T(4,128)(2,1)S(1)} %get-tuple-element.52), channel_id=1, source_target_pairs={{0,16},{4,20},{8,24},{12,28},{16,0},{20,4},{24,8},{28,12},{1,17},{... | collective-permute-start | bytes 294920 | tf_op jit(solution)/shard_map/ppermute | solution.py:24
  86.2 1.5 %shard_map.78 = (bf16[8,6144]{1,0:T(8,128)(2,1)}, bf16[4,12288]{1,0:T(4,128)(2,1)}) custom-call(s32[3]{0:T(128)S(1)} %pad_add_fusion.place_ref, bf16[24,32,128]{2,1,0:T(8,128)(2,1)S(1)} %add_convert_fusion.7.refs_0_, bf16[24,32,128]{2,1,0:T(8,128)(2,1)S(1)} %add_convert_fusion.5.refs_1_, bf16[12,32,128]{2,1,0:T(8,128)(2,1)S(1)} %fusion.6.refs_0_.refs_2_, ...), custom_call_target="tpu_custom_call" | custom-call | bytes 393216 | tf_op jit(solution)/shard_map/pallas_call | solution.py:245
  89.0 1.3 %collective-permute-done.29 = bf16[4,12288]{1,0:T(4,128)(2,1)S(1)} collective-permute-done((bf16[4,12288]{1,0:T(4,128)(2,1)S(1)}, bf16[4,12288]{1,0:T(4,128)(2,1)S(1)}, u32[]{:S(2)}, u32[]{:S(2)}) %collective-permute-start.29) | collective-permute-done | bytes 98336 | tf_op jit(solution)/shard_map/ppermute | solution.py:24
  90.3 4.7 %collective-permute-done.28 = bf16[4,12288]{1,0:T(4,128)(2,1)S(1)} collective-permute-done((bf16[4,12288]{1,0:T(4,128)(2,1)S(1)}, bf16[4,12288]{1,0:T(4,128)(2,1)S(1)}, u32[]{:S(2)}, u32[]{:S(2)}) %collective-permute-start.28) | collective-permute-done | bytes 98336 | tf_op jit(solution)/shard_map/ppermute | solution.py:24
  (63 shorter events, 15.2 us)
Async XLA Ops:
  0.6 10.9 %collective-permute-start.1 = (bf16[4,12288]{1,0:T(4,128)(2,1)}, bf16[4,12288]{1,0:T(4,128)(2,1)S(1)}, u32[]{:S(2)}, u32[]{:S(2)}) collective-permute-start(bf16[4,12288]{1,0:T(4,128)(2,1)} %param.4), channel_id=1, source_target_pairs={{0,16},{4,20},{8,24},{12,28},{16,0},{20,4},{24,8},{28,12},{1,17},{... | collective-permute-start | bytes 294920 | tf_op jit(solution)/shard_map/ppermute | solution.py:24
  4.7 7.4 %collective-permute-start = (bf16[4,12288]{1,0:T(4,128)(2,1)}, bf16[4,12288]{1,0:T(4,128)(2,1)S(1)}, u32[]{:S(2)}, u32[]{:S(2)}) collective-permute-start(bf16[4,12288]{1,0:T(4,128)(2,1)} %param.4), channel_id=1, source_target_pairs={{0,8},{4,12},{8,0},{12,4},{16,24},{20,28},{24,16},{28,20},{1,9},{5... | collective-permute-start | bytes 294920 | tf_op jit(solution)/shard_map/ppermute | solution.py:24
  6.3 7.4 %collective-permute-start.3 = (bf16[4,12288]{1,0:T(4,128)(2,1)}, bf16[4,12288]{1,0:T(4,128)(2,1)S(1)}, u32[]{:S(2)}, u32[]{:S(2)}) collective-permute-start(bf16[4,12288]{1,0:T(4,128)(2,1)} %param.4), channel_id=1, source_target_pairs={{0,4},{4,0},{8,12},{12,8},{16,20},{20,16},{24,28},{28,24},{1,5},{5... | collective-permute-start | bytes 294920 | tf_op jit(solution)/shard_map/ppermute | solution.py:24
  6.3 7.3 %collective-permute-start.2 = (bf16[4,12288]{1,0:T(4,128)(2,1)}, bf16[4,12288]{1,0:T(4,128)(2,1)S(1)}, u32[]{:S(2)}, u32[]{:S(2)}) collective-permute-start(bf16[4,12288]{1,0:T(4,128)(2,1)} %param.4), channel_id=1, source_target_pairs={{0,24},{4,28},{8,16},{12,20},{16,8},{20,12},{24,0},{28,4},{1,25},{... | collective-permute-start | bytes 294920 | tf_op jit(solution)/shard_map/ppermute | solution.py:24
  9.7 1.8 %copy-start.1 = (f32[8]{0:T(128)S(1)}, f32[8]{0:T(128)}, u32[]{:S(2)}) copy-start(f32[8]{0:T(128)} %param.7) | copy-start | bytes 100
  11.5 2.2 %collective-permute-start.5 = (bf16[4,12288]{1,0:T(4,128)(2,1)S(1)}, bf16[4,12288]{1,0:T(4,128)(2,1)S(1)}, u32[]{:S(2)}, u32[]{:S(2)}) collective-permute-start(bf16[4,12288]{1,0:T(4,128)(2,1)S(1)} %collective-permute-done.1.refs_2_), channel_id=1, source_target_pairs={{0,4},{4,0},{8,12},{12,8},{16,20},{20,16},{24,28},{28,24},{1,5},{5... | collective-permute-start | bytes 294920 | tf_op jit(solution)/shard_map/ppermute | solution.py:24
  12.1 1.6 %collective-permute-start.4 = (bf16[4,12288]{1,0:T(4,128)(2,1)S(1)}, bf16[4,12288]{1,0:T(4,128)(2,1)S(1)}, u32[]{:S(2)}, u32[]{:S(2)}) collective-permute-start(bf16[4,12288]{1,0:T(4,128)(2,1)S(1)} %collective-permute-done.refs_1_), channel_id=1, source_target_pairs={{0,4},{4,0},{8,12},{12,8},{16,20},{20,16},{24,28},{28,24},{1,5},{5... | collective-permute-start | bytes 294920 | tf_op jit(solution)/shard_map/ppermute | solution.py:24
  13.6 1.3 %collective-permute-start.6 = (bf16[4,12288]{1,0:T(4,128)(2,1)S(1)}, bf16[4,12288]{1,0:T(4,128)(2,1)S(1)}, u32[]{:S(2)}, u32[]{:S(2)}) collective-permute-start(bf16[4,12288]{1,0:T(4,128)(2,1)S(1)} %collective-permute-done.2.refs_3_), channel_id=1, source_target_pairs={{0,4},{4,0},{8,12},{12,8},{16,20},{20,16},{24,28},{28,24},{1,5},{5... | collective-permute-start | bytes 294920 | tf_op jit(solution)/shard_map/ppermute | solution.py:24
  14.9 17.8 %copy-start = (bf16[32,256,256]{2,1,0:T(8,128)(2,1)S(1)}, bf16[32,256,256]{2,1,0:T(8,128)(2,1)}, u32[]{:S(2)}) copy-start(bf16[32,256,256]{2,1,0:T(8,128)(2,1)} %refs_2_.3) | copy-start | bytes 12582916
  18.0 7.0 %collective-permute-start.7 = (bf16[24,32,128]{2,1,0:T(8,128)(2,1)S(1)}, bf16[24,32,128]{2,1,0:T(8,128)(2,1)S(1)}, u32[]{:S(2)}, u32[]{:S(2)}) collective-permute-start(bf16[24,32,128]{2,1,0:T(8,128)(2,1)S(1)} %get-tuple-element.27), channel_id=1, source_target_pairs={{0,1},{1,0},{2,3},{3,2},{4,5},{5,4},{6,7},{7,6},{8,9},{9,8},{10,11... | collective-permute-start | bytes 589832 | tf_op jit(solution)/shard_map/ppermute | solution.py:24
  19.5 7.1 %collective-permute-start.9 = (bf16[24,32,128]{2,1,0:T(8,128)(2,1)S(1)}, bf16[24,32,128]{2,1,0:T(8,128)(2,1)S(1)}, u32[]{:S(2)}, u32[]{:S(2)}) collective-permute-start(bf16[24,32,128]{2,1,0:T(8,128)(2,1)S(1)} %get-tuple-element.28), channel_id=1, source_target_pairs={{0,2},{1,3},{2,0},{3,1},{4,6},{5,7},{6,4},{7,5},{8,10},{9,11},{10,... | collective-permute-start | bytes 589832 | tf_op jit(solution)/shard_map/ppermute | solution.py:24
  25.1 6.2 %collective-permute-start.8 = (bf16[24,32,128]{2,1,0:T(8,128)(2,1)S(1)}, bf16[24,32,128]{2,1,0:T(8,128)(2,1)S(1)}, u32[]{:S(2)}, u32[]{:S(2)}) collective-permute-start(bf16[24,32,128]{2,1,0:T(8,128)(2,1)S(1)} %add_convert_fusion.8), channel_id=1, source_target_pairs={{0,2},{1,3},{2,0},{3,1},{4,6},{5,7},{6,4},{7,5},{8,10},{9,11},{10,... | collective-permute-start | bytes 589832 | tf_op jit(solution)/shard_map/ppermute | solution.py:24
  26.7 5.9 %collective-permute-start.10 = (bf16[24,32,128]{2,1,0:T(8,128)(2,1)S(1)}, bf16[24,32,128]{2,1,0:T(8,128)(2,1)S(1)}, u32[]{:S(2)}, u32[]{:S(2)}) collective-permute-start(bf16[24,32,128]{2,1,0:T(8,128)(2,1)S(1)} %add_convert_fusion.6), channel_id=1, source_target_pairs={{0,1},{1,0},{2,3},{3,2},{4,5},{5,4},{6,7},{7,6},{8,9},{9,8},{10,11... | collective-permute-start | bytes 589832 | tf_op jit(solution)/shard_map/ppermute | solution.py:24
  34.2 1.8 %collective-permute-start.11 = (bf16[4,12,32,128]{3,2,1,0:T(8,128)(2,1)S(1)}, bf16[4,12,32,128]{3,2,1,0:T(8,128)(2,1)S(1)}, u32[]{:S(2)}, u32[]{:S(2)}) collective-permute-start(bf16[4,12,32,128]{3,2,1,0:T(8,128)(2,1)S(1)} %get-tuple-element.30), channel_id=1, source_target_pairs={{0,4},{4,0},{8,12},{12,8},{16,20},{20,16},{24,28},{28,24},{1,5},{5... | collective-permute-start | bytes 1179656 | tf_op jit(solution)/shard_map/ppermute | solution.py:24
  36.1 4.9 %collective-permute-start.12 = (bf16[12,32,128]{2,1,0:T(8,128)(2,1)S(1)}, bf16[12,32,128]{2,1,0:T(8,128)(2,1)S(1)}, u32[]{:S(2)}, u32[]{:S(2)}) collective-permute-start(bf16[12,32,128]{2,1,0:T(8,128)(2,1)S(1)} %get-tuple-element.53), channel_id=1, source_target_pairs={{0,8},{4,12},{8,0},{12,4},{16,24},{20,28},{24,16},{28,20},{1,9},{5... | collective-permute-start | bytes 294920 | tf_op jit(solution)/shard_map/ppermute | solution.py:24
  37.4 9.1 %collective-permute-start.14 = (bf16[12,32,128]{2,1,0:T(8,128)(2,1)S(1)}, bf16[12,32,128]{2,1,0:T(8,128)(2,1)S(1)}, u32[]{:S(2)}, u32[]{:S(2)}) collective-permute-start(bf16[12,32,128]{2,1,0:T(8,128)(2,1)S(1)} %get-tuple-element.54), channel_id=1, source_target_pairs={{0,24},{4,28},{8,16},{12,20},{16,8},{20,12},{24,0},{28,4},{1,25},{... | collective-permute-start | bytes 294920 | tf_op jit(solution)/shard_map/ppermute | solution.py:24
  40.7 8.9 %collective-permute-start.13 = (bf16[12,32,128]{2,1,0:T(8,128)(2,1)S(1)}, bf16[12,32,128]{2,1,0:T(8,128)(2,1)S(1)}, u32[]{:S(2)}, u32[]{:S(2)}) collective-permute-start(bf16[12,32,128]{2,1,0:T(8,128)(2,1)S(1)} %get-tuple-element.55), channel_id=1, source_target_pairs={{0,16},{4,20},{8,24},{12,28},{16,0},{20,4},{24,8},{28,12},{1,17},{... | collective-permute-start | bytes 294920 | tf_op jit(solution)/shard_map/ppermute | solution.py:24
  49.6 7.7 %collective-permute-start.17 = (bf16[12,32,128]{2,1,0:T(8,128)(2,1)S(1)}, bf16[12,32,128]{2,1,0:T(8,128)(2,1)S(1)}, u32[]{:S(2)}, u32[]{:S(2)}) collective-permute-start(bf16[12,32,128]{2,1,0:T(8,128)(2,1)S(1)} %fusion.6.refs_0_.refs_2_), channel_id=1, source_target_pairs={{0,24},{4,28},{8,16},{12,20},{16,8},{20,12},{24,0},{28,4},{1,25},{... | collective-permute-start | bytes 294920 | tf_op jit(solution)/shard_map/ppermute | solution.py:24
  51.5 8.6 %collective-permute-start.16 = (bf16[12,32,128]{2,1,0:T(8,128)(2,1)S(1)}, bf16[12,32,128]{2,1,0:T(8,128)(2,1)S(1)}, u32[]{:S(2)}, u32[]{:S(2)}) collective-permute-start(bf16[12,32,128]{2,1,0:T(8,128)(2,1)S(1)} %fusion.6.refs_0_.refs_2_), channel_id=1, source_target_pairs={{0,16},{4,20},{8,24},{12,28},{16,0},{20,4},{24,8},{28,12},{1,17},{... | collective-permute-start | bytes 294920 | tf_op jit(solution)/shard_map/ppermute | solution.py:24
  51.5 8.6 %collective-permute-start.15 = (bf16[12,32,128]{2,1,0:T(8,128)(2,1)S(1)}, bf16[12,32,128]{2,1,0:T(8,128)(2,1)S(1)}, u32[]{:S(2)}, u32[]{:S(2)}) collective-permute-start(bf16[12,32,128]{2,1,0:T(8,128)(2,1)S(1)} %fusion.6.refs_0_.refs_2_), channel_id=1, source_target_pairs={{0,8},{4,12},{8,0},{12,4},{16,24},{20,28},{24,16},{28,20},{1,9},{5... | collective-permute-start | bytes 294920 | tf_op jit(solution)/shard_map/ppermute | solution.py:24
  54.1 6.5 %collective-permute-start.18 = (bf16[12,32,128]{2,1,0:T(8,128)(2,1)S(1)}, bf16[12,32,128]{2,1,0:T(8,128)(2,1)S(1)}, u32[]{:S(2)}, u32[]{:S(2)}) collective-permute-start(bf16[12,32,128]{2,1,0:T(8,128)(2,1)S(1)} %fusion.6.refs_0_.refs_2_), channel_id=1, source_target_pairs={{0,4},{4,0},{8,12},{12,8},{16,20},{20,16},{24,28},{28,24},{1,5},{5... | collective-permute-start | bytes 294920 | tf_op jit(solution)/shard_map/ppermute | solution.py:24
  57.3 3.3 %collective-permute-start.21 = (bf16[12,32,128]{2,1,0:T(8,128)(2,1)S(1)}, bf16[12,32,128]{2,1,0:T(8,128)(2,1)S(1)}, u32[]{:S(2)}, u32[]{:S(2)}) collective-permute-start(bf16[12,32,128]{2,1,0:T(8,128)(2,1)S(1)} %collective-permute-done.17.refs_3_.refs_5_), channel_id=1, source_target_pairs={{0,4},{4,0},{8,12},{12,8},{16,20},{20,16},{24,28},{28,24},{1,5},{5... | collective-permute-start | bytes 294920 | tf_op jit(solution)/shard_map/ppermute | solution.py:24
  60.1 1.3 %collective-permute-start.20 = (bf16[12,32,128]{2,1,0:T(8,128)(2,1)S(1)}, bf16[12,32,128]{2,1,0:T(8,128)(2,1)S(1)}, u32[]{:S(2)}, u32[]{:S(2)}) collective-permute-start(bf16[12,32,128]{2,1,0:T(8,128)(2,1)S(1)} %collective-permute-done.16.refs_2_.refs_4_), channel_id=1, source_target_pairs={{0,4},{4,0},{8,12},{12,8},{16,20},{20,16},{24,28},{28,24},{1,5},{5... | collective-permute-start | bytes 294920 | tf_op jit(solution)/shard_map/ppermute | solution.py:24
  60.1 1.4 %collective-permute-start.19 = (bf16[12,32,128]{2,1,0:T(8,128)(2,1)S(1)}, bf16[12,32,128]{2,1,0:T(8,128)(2,1)S(1)}, u32[]{:S(2)}, u32[]{:S(2)}) collective-permute-start(bf16[12,32,128]{2,1,0:T(8,128)(2,1)S(1)} %collective-permute-done.15.refs_1_.refs_3_), channel_id=1, source_target_pairs={{0,4},{4,0},{8,12},{12,8},{16,20},{20,16},{24,28},{28,24},{1,5},{5... | collective-permute-start | bytes 294920 | tf_op jit(solution)/shard_map/ppermute | solution.py:24
  63.5 7.2 %collective-permute-start.22 = (bf16[24,32,128]{2,1,0:T(8,128)(2,1)S(1)}, bf16[24,32,128]{2,1,0:T(8,128)(2,1)S(1)}, u32[]{:S(2)}, u32[]{:S(2)}) collective-permute-start(bf16[24,32,128]{2,1,0:T(8,128)(2,1)S(1)} %get-tuple-element.45), channel_id=1, source_target_pairs={{0,1},{1,0},{2,3},{3,2},{4,5},{5,4},{6,7},{7,6},{8,9},{9,8},{10,11... | collective-permute-start | bytes 589832 | tf_op jit(solution)/shard_map/ppermute | solution.py:24
  65.1 6.9 %collective-permute-start.24 = (bf16[24,32,128]{2,1,0:T(8,128)(2,1)S(1)}, bf16[24,32,128]{2,1,0:T(8,128)(2,1)S(1)}, u32[]{:S(2)}, u32[]{:S(2)}) collective-permute-start(bf16[24,32,128]{2,1,0:T(8,128)(2,1)S(1)} %get-tuple-element.46), channel_id=1, source_target_pairs={{0,2},{1,3},{2,0},{3,1},{4,6},{5,7},{6,4},{7,5},{8,10},{9,11},{10,... | collective-permute-start | bytes 589832 | tf_op jit(solution)/shard_map/ppermute | solution.py:24
  70.8 6.4 %collective-permute-start.23 = (bf16[24,32,128]{2,1,0:T(8,128)(2,1)S(1)}, bf16[24,32,128]{2,1,0:T(8,128)(2,1)S(1)}, u32[]{:S(2)}, u32[]{:S(2)}) collective-permute-start(bf16[24,32,128]{2,1,0:T(8,128)(2,1)S(1)} %add_convert_fusion.4), channel_id=1, source_target_pairs={{0,2},{1,3},{2,0},{3,1},{4,6},{5,7},{6,4},{7,5},{8,10},{9,11},{10,... | collective-permute-start | bytes 589832 | tf_op jit(solution)/shard_map/ppermute | solution.py:24
  72.0 6.1 %collective-permute-start.25 = (bf16[24,32,128]{2,1,0:T(8,128)(2,1)S(1)}, bf16[24,32,128]{2,1,0:T(8,128)(2,1)S(1)}, u32[]{:S(2)}, u32[]{:S(2)}) collective-permute-start(bf16[24,32,128]{2,1,0:T(8,128)(2,1)S(1)} %add_convert_fusion.2), channel_id=1, source_target_pairs={{0,1},{1,0},{2,3},{3,2},{4,5},{5,4},{6,7},{7,6},{8,9},{9,8},{10,11... | collective-permute-start | bytes 589832 | tf_op jit(solution)/shard_map/ppermute | solution.py:24
  80.5 1.8 %collective-permute-start.26 = (bf16[4,4,12288]{2,1,0:T(4,128)(2,1)S(1)}, bf16[4,4,12288]{2,1,0:T(4,128)(2,1)S(1)}, u32[]{:S(2)}, u32[]{:S(2)}) collective-permute-start(bf16[4,4,12288]{2,1,0:T(4,128)(2,1)S(1)} %slice_bitcast_fusion), channel_id=1, source_target_pairs={{0,4},{4,0},{8,12},{12,8},{16,20},{20,16},{24,28},{28,24},{1,5},{5... | collective-permute-start | bytes 1179656 | tf_op jit(solution)/shard_map/ppermute | solution.py:24
  82.6 6.3 %collective-permute-start.27 = (bf16[4,12288]{1,0:T(4,128)(2,1)S(1)}, bf16[4,12288]{1,0:T(4,128)(2,1)S(1)}, u32[]{:S(2)}, u32[]{:S(2)}) collective-permute-start(bf16[4,12288]{1,0:T(4,128)(2,1)S(1)} %get-tuple-element.50), channel_id=1, source_target_pairs={{0,8},{4,12},{8,0},{12,4},{16,24},{20,28},{24,16},{28,20},{1,9},{5... | collective-permute-start | bytes 294920 | tf_op jit(solution)/shard_map/ppermute | solution.py:24
  82.7 7.6 %collective-permute-start.29 = (bf16[4,12288]{1,0:T(4,128)(2,1)S(1)}, bf16[4,12288]{1,0:T(4,128)(2,1)S(1)}, u32[]{:S(2)}, u32[]{:S(2)}) collective-permute-start(bf16[4,12288]{1,0:T(4,128)(2,1)S(1)} %get-tuple-element.51), channel_id=1, source_target_pairs={{0,24},{4,28},{8,16},{12,20},{16,8},{20,12},{24,0},{28,4},{1,25},{... | collective-permute-start | bytes 294920 | tf_op jit(solution)/shard_map/ppermute | solution.py:24
  84.3 10.8 %collective-permute-start.28 = (bf16[4,12288]{1,0:T(4,128)(2,1)S(1)}, bf16[4,12288]{1,0:T(4,128)(2,1)S(1)}, u32[]{:S(2)}, u32[]{:S(2)}) collective-permute-start(bf16[4,12288]{1,0:T(4,128)(2,1)S(1)} %get-tuple-element.52), channel_id=1, source_target_pairs={{0,16},{4,20},{8,24},{12,28},{16,0},{20,4},{24,8},{28,12},{1,17},{... | collective-permute-start | bytes 294920 | tf_op jit(solution)/shard_map/ppermute | solution.py:24

commit v13 on v12

--- a/solution.py
+++ b/solution.py
@@ -12,9 +12,9 @@
 LANES = 128
 PER = B // LANES
 COPIES = 4
-ROW_PARTS = 2
+ROW_PARTS = 1
 CHUNK = 1024
-UNROLL = 48
+UNROLL = 96
 VMEM_LIMIT = 12 * 1024 * 1024
 FIRST_LIMIT = 50 * 1024 * 1024
 
@@ -275,10 +275,12 @@
 
     def over_case(parts):
         bits = [1 << b for b in range(n_case.bit_length() - 1)]
-        parts = list(parts)
         for step in range(len(bits)):
-            arrived = [swap(part, "case", bits[(step + i) % len(bits)]) for i, part in enumerate(parts)]
-            parts = [add_up(part, one) for part, one in zip(parts, arrived)]
+            by_core = [bits[(step + side) % len(bits)] for side in range(2)]
+            pairs = [
+                (p * n_case + c, p * n_case + (c ^ by_core[p % 2])) for p in range(n_panel) for c in range(n_case)
+            ]
+            parts = [add_up(part, lax.ppermute(part, ("panel", "case"), pairs)) for part in parts]
         return parts
 
     def scatter_panel(mine, theirs):

time: 96 us -> 98.1 us (1.022)
  waiting for transfers between devices: 46.5 us -> 53.1 us
  starting transfers between devices: 30 us -> 25.8 us
    ppermute x0 -> x4, waiting for transfers between devices: none -> 25.1 us  [over_case(): lax.ppermute(part, ('panel', 'case'), pairs)]
    ppermute x30 -> x22, waiting for transfers between devices: 46.5 us -> 28 us  [swap(): return lax.ppermute(value, axis, [(i, i ^ offset) for i in range(count)])]
    ppermute x30 -> x22, starting transfers between devices: 30 us -> 19.6 us  [swap(): return lax.ppermute(value, axis, [(i, i ^ offset) for i in range(count)])]
    ppermute x0 -> x4, starting transfers between devices: none -> 6.28 us  [over_case(): lax.ppermute(part, ('panel', 'case'), pairs)]
  transfers between devices with their start and end apart: 30 -> 26, of which waited for: 19 -> 17; matrix products, arithmetic and copies ran while one was open for 6% -> 5% of each run, Pallas kernels for 3% -> 3%
where the time goes in v13:
time: 98.1 us; the launch traced here: 97.8 us
  waiting for transfers between devices  53.1 us (54%)
  starting transfers between devices  25.8 us (26%)
  Pallas kernels  11.1 us (11%)
  other arithmetic  5.89 us (6%)
  local copies, waits for them, and re-layouts  1.15 us (1%)
    ppermute x22, waiting for transfers between devices, swap(): return lax.ppermute(value, axis, [(i, i ^ offset) for i in range(count)])  28 us
    ppermute x4, waiting for transfers between devices, over_case(): lax.ppermute(part, ('panel', 'case'), pairs)  25.1 us
    ppermute x22, starting transfers between devices, swap(): return lax.ppermute(value, axis, [(i, i ^ offset) for i in range(count)])  19.6 us
    pallas_call x4, Pallas kernels, product(): pl.pallas_call(functools.partial(kernel, ways), out_shape=[jax.ShapeDtype...  8.32 us
    ppermute x4, starting transfers between devices, over_case(): lax.ppermute(part, ('panel', 'case'), pairs)  6.28 us
    pallas_call x2, Pallas kernels, cut(): pl.pallas_call(functools.partial(kernel, ways), out_shape=[jax.ShapeDtype...  2.77 us
  transfers between devices with their start and end apart: 26, of which 17 were waited for; matrix products, arithmetic and copies ran while one was open for 5% of the time, Pallas kernels for 3%

profile of v13, /device:TPU:0, one launch (start us, length us, event | category | flops | bytes accessed | tf_op | source)
XLA Modules:
  0.0 97.8 jit_solution(8047806304952782236)
XLA Ops:
  0.6 4.1 %collective-permute-start.1 = (bf16[4,12288]{1,0:T(4,128)(2,1)}, bf16[4,12288]{1,0:T(4,128)(2,1)S(1)}, u32[]{:S(2)}, u32[]{:S(2)}) collective-permute-start(bf16[4,12288]{1,0:T(4,128)(2,1)} %param.4), channel_id=1, source_target_pairs={{0,16},{4,20},{8,24},{12,28},{16,0},{20,4},{24,8},{28,12},{1,17},{... | collective-permute-start | bytes 294920 | tf_op jit(solution)/shard_map/ppermute | solution.py:24
  4.7 1.6 %collective-permute-start = (bf16[4,12288]{1,0:T(4,128)(2,1)}, bf16[4,12288]{1,0:T(4,128)(2,1)S(1)}, u32[]{:S(2)}, u32[]{:S(2)}) collective-permute-start(bf16[4,12288]{1,0:T(4,128)(2,1)} %param.4), channel_id=1, source_target_pairs={{0,8},{4,12},{8,0},{12,4},{16,24},{20,28},{24,16},{28,20},{1,9},{5... | collective-permute-start | bytes 294920 | tf_op jit(solution)/shard_map/ppermute | solution.py:24
  9.7 1.7 %slice_select_fusion.refs_8_ = bf16[16,256,256]{2,1,0:T(8,128)(2,1)S(1)} fusion(bf16[32,256,256]{2,1,0:T(8,128)(2,1)} %refs_1_.3, pred[]{:T(512)S(6)} %ge.12), kind=kLoop, calls=%fused_computation | loop fusion | flops 1048576 | bytes 4194305 | tf_op jit(solution)/shard_map/jit(_where)/select_n | solution.py:303
  12.2 1.5 %collective-permute-done.2.refs_3_ = bf16[4,12288]{1,0:T(4,128)(2,1)S(1)} collective-permute-done((bf16[4,12288]{1,0:T(4,128)(2,1)}, bf16[4,12288]{1,0:T(4,128)(2,1)S(1)}, u32[]{:S(2)}, u32[]{:S(2)}) %collective-permute-start.2) | collective-permute-done | bytes 98336 | tf_op jit(solution)/shard_map/ppermute | solution.py:24
  14.9 3.0 %shard_map.75 = bf16[48,32,128]{2,1,0:T(8,128)(2,1)S(1)} custom-call(s32[64]{0:T(128)S(1)} %reshape.18.entry_ref, f32[32]{0:T(128)S(1)} %select_reduce_fusion.scale_ref, s32[3]{0:T(128)S(1)} %pad_add_fusion.place_ref, bf16[4,12288]{1,0:T(4,128)(2,1)S(1)} %broadcast_select_fusion.refs_0_, bf16[4,12288]{1,0:T(4,128)(2,1)S(1)} %collective-permute-done.refs_1_, ...), custom_call_target="tpu_custom_call" | custom-call | flops 134217728 | bytes 4194304 | tf_op jit(solution)/shard_map/pallas_call | solution.py:256
  18.0 1.6 %collective-permute-start.7 = (bf16[48,32,128]{2,1,0:T(8,128)(2,1)S(1)}, bf16[48,32,128]{2,1,0:T(8,128)(2,1)S(1)}, u32[]{:S(2)}, u32[]{:S(2)}) collective-permute-start(bf16[48,32,128]{2,1,0:T(8,128)(2,1)S(1)} %shard_map.75), channel_id=1, source_target_pairs={{0,1},{1,0},{2,3},{3,2},{4,6},{5,7},{6,4},{7,5},{8,9},{9,8},{10,11... | collective-permute-start | bytes 1179656 | tf_op jit(solution)/shard_map/ppermute | solution.py:283
  19.5 6.3 %collective-permute-done.7 = bf16[48,32,128]{2,1,0:T(8,128)(2,1)S(1)} collective-permute-done((bf16[48,32,128]{2,1,0:T(8,128)(2,1)S(1)}, bf16[48,32,128]{2,1,0:T(8,128)(2,1)S(1)}, u32[]{:S(2)}, u32[]{:S(2)}) %collective-permute-start.7) | collective-permute-done | bytes 393248 | tf_op jit(solution)/shard_map/ppermute | solution.py:283
  25.9 1.6 %collective-permute-start.8 = (bf16[48,32,128]{2,1,0:T(8,128)(2,1)S(1)}, bf16[48,32,128]{2,1,0:T(8,128)(2,1)S(1)}, u32[]{:S(2)}, u32[]{:S(2)}) collective-permute-start(bf16[48,32,128]{2,1,0:T(8,128)(2,1)S(1)} %add_convert_fusion.4), channel_id=1, source_target_pairs={{0,2},{1,3},{2,0},{3,1},{4,5},{5,4},{6,7},{7,6},{8,10},{9,11},{10,... | collective-permute-start | bytes 1179656 | tf_op jit(solution)/shard_map/ppermute | solution.py:283
  27.5 6.3 %collective-permute-done.8 = bf16[48,32,128]{2,1,0:T(8,128)(2,1)S(1)} collective-permute-done((bf16[48,32,128]{2,1,0:T(8,128)(2,1)S(1)}, bf16[48,32,128]{2,1,0:T(8,128)(2,1)S(1)}, u32[]{:S(2)}, u32[]{:S(2)}) %collective-permute-start.8) | collective-permute-done | bytes 393248 | tf_op jit(solution)/shard_map/ppermute | solution.py:283
  33.9 1.5 %shard_map.76 = (bf16[4,12,32,128]{3,2,1,0:T(8,128)(2,1)S(1)}, bf16[4,12,32,128]{3,2,1,0:T(8,128)(2,1)S(1)}) custom-call(s32[64]{0:T(128)S(1)} %reshape.18.entry_ref, f32[32]{0:T(128)S(1)} %select_reduce_fusion.scale_ref, s32[3]{0:T(128)S(1)} %pad_add_fusion.place_ref, bf16[48,32,128]{2,1,0:T(8,128)(2,1)S(1)} %add_convert_fusion.3.refs_0_, ...), custom_call_target="tpu_custom_call" | custom-call | flops 134217728 | bytes 4194304 | tf_op jit(solution)/shard_map/pallas_call | solution.py:256
  35.5 1.7 %collective-permute-done.9 = bf16[4,12,32,128]{3,2,1,0:T(8,128)(2,1)S(1)} collective-permute-done((bf16[4,12,32,128]{3,2,1,0:T(8,128)(2,1)S(1)}, bf16[4,12,32,128]{3,2,1,0:T(8,128)(2,1)S(1)}, u32[]{:S(2)}, u32[]{:S(2)}) %collective-permute-start.9) | collective-permute-done | bytes 393248 | tf_op jit(solution)/shard_map/ppermute | solution.py:24
  37.3 1.3 %collective-permute-start.10 = (bf16[12,32,128]{2,1,0:T(8,128)(2,1)S(1)}, bf16[12,32,128]{2,1,0:T(8,128)(2,1)S(1)}, u32[]{:S(2)}, u32[]{:S(2)}) collective-permute-start(bf16[12,32,128]{2,1,0:T(8,128)(2,1)S(1)} %get-tuple-element.39), channel_id=1, source_target_pairs={{0,8},{4,12},{8,0},{12,4},{16,24},{20,28},{24,16},{28,20},{1,9},{5... | collective-permute-start | bytes 294920 | tf_op jit(solution)/shard_map/ppermute | solution.py:24
  38.6 3.3 %collective-permute-start.12 = (bf16[12,32,128]{2,1,0:T(8,128)(2,1)S(1)}, bf16[12,32,128]{2,1,0:T(8,128)(2,1)S(1)}, u32[]{:S(2)}, u32[]{:S(2)}) collective-permute-start(bf16[12,32,128]{2,1,0:T(8,128)(2,1)S(1)} %get-tuple-element.40), channel_id=1, source_target_pairs={{0,24},{4,28},{8,16},{12,20},{16,8},{20,12},{24,0},{28,4},{1,25},{... | collective-permute-start | bytes 294920 | tf_op jit(solution)/shard_map/ppermute | solution.py:24
  42.2 5.5 %collective-permute-done.12 = bf16[12,32,128]{2,1,0:T(8,128)(2,1)S(1)} collective-permute-done((bf16[12,32,128]{2,1,0:T(8,128)(2,1)S(1)}, bf16[12,32,128]{2,1,0:T(8,128)(2,1)S(1)}, u32[]{:S(2)}, u32[]{:S(2)}) %collective-permute-start.12) | collective-permute-done | bytes 98336 | tf_op jit(solution)/shard_map/ppermute | solution.py:24
  47.7 3.0 %collective-permute-done.11 = bf16[12,32,128]{2,1,0:T(8,128)(2,1)S(1)} collective-permute-done((bf16[12,32,128]{2,1,0:T(8,128)(2,1)S(1)}, bf16[12,32,128]{2,1,0:T(8,128)(2,1)S(1)}, u32[]{:S(2)}, u32[]{:S(2)}) %collective-permute-start.11) | collective-permute-done | bytes 98336 | tf_op jit(solution)/shard_map/ppermute | solution.py:24
  50.8 1.9 %collective-permute-start.15 = (bf16[12,32,128]{2,1,0:T(8,128)(2,1)S(1)}, bf16[12,32,128]{2,1,0:T(8,128)(2,1)S(1)}, u32[]{:S(2)}, u32[]{:S(2)}) collective-permute-start(bf16[12,32,128]{2,1,0:T(8,128)(2,1)S(1)} %fusion.6.refs_0_.refs_1_), channel_id=1, source_target_pairs={{0,24},{4,28},{8,16},{12,20},{16,8},{20,12},{24,0},{28,4},{1,25},{... | collective-permute-start | bytes 294920 | tf_op jit(solution)/shard_map/ppermute | solution.py:24
  52.7 2.6 %collective-permute-start.13 = (bf16[12,32,128]{2,1,0:T(8,128)(2,1)S(1)}, bf16[12,32,128]{2,1,0:T(8,128)(2,1)S(1)}, u32[]{:S(2)}, u32[]{:S(2)}) collective-permute-start(bf16[12,32,128]{2,1,0:T(8,128)(2,1)S(1)} %fusion.6.refs_0_.refs_1_), channel_id=1, source_target_pairs={{0,8},{4,12},{8,0},{12,4},{16,24},{20,28},{24,16},{28,20},{1,9},{5... | collective-permute-start | bytes 294920 | tf_op jit(solution)/shard_map/ppermute | solution.py:24
  55.3 3.2 %collective-permute-done.15.refs_3_.refs_4_ = bf16[12,32,128]{2,1,0:T(8,128)(2,1)S(1)} collective-permute-done((bf16[12,32,128]{2,1,0:T(8,128)(2,1)S(1)}, bf16[12,32,128]{2,1,0:T(8,128)(2,1)S(1)}, u32[]{:S(2)}, u32[]{:S(2)}) %collective-permute-start.15) | collective-permute-done | bytes 98336 | tf_op jit(solution)/shard_map/ppermute | solution.py:24
  58.5 2.8 %collective-permute-done.14.refs_2_.refs_3_ = bf16[12,32,128]{2,1,0:T(8,128)(2,1)S(1)} collective-permute-done((bf16[12,32,128]{2,1,0:T(8,128)(2,1)S(1)}, bf16[12,32,128]{2,1,0:T(8,128)(2,1)S(1)}, u32[]{:S(2)}, u32[]{:S(2)}) %collective-permute-start.14) | collective-permute-done | bytes 98336 | tf_op jit(solution)/shard_map/ppermute | solution.py:24
  62.7 2.0 %shard_map.77 = bf16[48,32,128]{2,1,0:T(8,128)(2,1)S(1)} custom-call(s32[64]{0:T(128)S(1)} %reshape.18.entry_ref, f32[32]{0:T(128)S(1)} %select_reduce_fusion.scale_ref, s32[3]{0:T(128)S(1)} %pad_add_fusion.place_ref, bf16[12,32,128]{2,1,0:T(8,128)(2,1)S(1)} %fusion.6.refs_0_.refs_1_, bf16[12,32,128]{2,1,0:T(8,128)(2,1)S(1)} %collective-permute-done.13.refs_1_.refs_2_, ...), custom_call_target="tpu_custom_call" | custom-call | flops 134217728 | bytes 4194304 | tf_op jit(solution)/shard_map/pallas_call | solution.py:256
  64.7 1.6 %collective-permute-start.20 = (bf16[48,32,128]{2,1,0:T(8,128)(2,1)S(1)}, bf16[48,32,128]{2,1,0:T(8,128)(2,1)S(1)}, u32[]{:S(2)}, u32[]{:S(2)}) collective-permute-start(bf16[48,32,128]{2,1,0:T(8,128)(2,1)S(1)} %shard_map.77), channel_id=1, source_target_pairs={{0,1},{1,0},{2,3},{3,2},{4,6},{5,7},{6,4},{7,5},{8,9},{9,8},{10,11... | collective-permute-start | bytes 1179656 | tf_op jit(solution)/shard_map/ppermute | solution.py:283
  66.3 6.3 %collective-permute-done.20 = bf16[48,32,128]{2,1,0:T(8,128)(2,1)S(1)} collective-permute-done((bf16[48,32,128]{2,1,0:T(8,128)(2,1)S(1)}, bf16[48,32,128]{2,1,0:T(8,128)(2,1)S(1)}, u32[]{:S(2)}, u32[]{:S(2)}) %collective-permute-start.20) | collective-permute-done | bytes 393248 | tf_op jit(solution)/shard_map/ppermute | solution.py:283
  72.7 1.6 %collective-permute-start.21 = (bf16[48,32,128]{2,1,0:T(8,128)(2,1)S(1)}, bf16[48,32,128]{2,1,0:T(8,128)(2,1)S(1)}, u32[]{:S(2)}, u32[]{:S(2)}) collective-permute-start(bf16[48,32,128]{2,1,0:T(8,128)(2,1)S(1)} %add_convert_fusion.1), channel_id=1, source_target_pairs={{0,2},{1,3},{2,0},{3,1},{4,5},{5,4},{6,7},{7,6},{8,10},{9,11},{10,... | collective-permute-start | bytes 1179656 | tf_op jit(solution)/shard_map/ppermute | solution.py:283
  74.3 6.2 %collective-permute-done.21 = bf16[48,32,128]{2,1,0:T(8,128)(2,1)S(1)} collective-permute-done((bf16[48,32,128]{2,1,0:T(8,128)(2,1)S(1)}, bf16[48,32,128]{2,1,0:T(8,128)(2,1)S(1)}, u32[]{:S(2)}, u32[]{:S(2)}) %collective-permute-start.21) | collective-permute-done | bytes 393248 | tf_op jit(solution)/shard_map/ppermute | solution.py:283
  80.6 1.8 %shard_map.79 = bf16[2,4,4,12288]{3,2,1,0:T(4,128)(2,1)S(1)} custom-call(s32[64]{0:T(128)S(1)} %reshape.18.entry_ref, f32[32]{0:T(128)S(1)} %select_reduce_fusion.scale_ref, s32[3]{0:T(128)S(1)} %pad_add_fusion.place_ref, bf16[48,32,128]{2,1,0:T(8,128)(2,1)S(1)} %add_convert_fusion.refs_0_, bf16[32,256,256]{2,1,0:T(8,128)(2,1)S(1)} %copy-done), custom_call_target="tpu_custom_call" | custom-call | flops 134217728 | bytes 4194304 | tf_op jit(solution)/shard_map/pallas_call | solution.py:256
  82.7 1.7 %collective-permute-done.22 = bf16[4,4,12288]{2,1,0:T(4,128)(2,1)S(1)} collective-permute-done((bf16[4,4,12288]{2,1,0:T(4,128)(2,1)S(1)}, bf16[4,4,12288]{2,1,0:T(4,128)(2,1)S(1)}, u32[]{:S(2)}, u32[]{:S(2)}) %collective-permute-start.22) | collective-permute-done | bytes 393248 | tf_op jit(solution)/shard_map/ppermute | solution.py:24
  84.8 1.9 %collective-permute-start.25 = (bf16[4,12288]{1,0:T(4,128)(2,1)S(1)}, bf16[4,12288]{1,0:T(4,128)(2,1)S(1)}, u32[]{:S(2)}, u32[]{:S(2)}) collective-permute-start(bf16[4,12288]{1,0:T(4,128)(2,1)S(1)} %get-tuple-element.37), channel_id=1, source_target_pairs={{0,24},{4,28},{8,16},{12,20},{16,8},{20,12},{24,0},{28,4},{1,25},{... | collective-permute-start | bytes 294920 | tf_op jit(solution)/shard_map/ppermute | solution.py:24
  86.6 1.6 %collective-permute-start.24 = (bf16[4,12288]{1,0:T(4,128)(2,1)S(1)}, bf16[4,12288]{1,0:T(4,128)(2,1)S(1)}, u32[]{:S(2)}, u32[]{:S(2)}) collective-permute-start(bf16[4,12288]{1,0:T(4,128)(2,1)S(1)} %get-tuple-element.38), channel_id=1, source_target_pairs={{0,16},{4,20},{8,24},{12,28},{16,0},{20,4},{24,8},{28,12},{1,17},{... | collective-permute-start | bytes 294920 | tf_op jit(solution)/shard_map/ppermute | solution.py:24
  88.2 1.5 %shard_map.78 = (bf16[8,6144]{1,0:T(8,128)(2,1)}, bf16[4,12288]{1,0:T(4,128)(2,1)}) custom-call(s32[3]{0:T(128)S(1)} %pad_add_fusion.place_ref, bf16[48,32,128]{2,1,0:T(8,128)(2,1)S(1)} %add_convert_fusion.3.refs_0_, bf16[12,32,128]{2,1,0:T(8,128)(2,1)S(1)} %fusion.6.refs_0_.refs_1_, bf16[12,32,128]{2,1,0:T(8,128)(2,1)S(1)} %collective-permute-done.13.refs_1_.refs_2_, ...), custom_call_target="tpu_custom_call" | custom-call | bytes 393216 | tf_op jit(solution)/shard_map/pallas_call | solution.py:245
  89.8 1.2 %shard_map.80 = bf16[8,6144]{1,0:T(8,128)(2,1)} custom-call(s32[3]{0:T(128)S(1)} %pad_add_fusion.place_ref, bf16[48,32,128]{2,1,0:T(8,128)(2,1)S(1)} %add_convert_fusion.refs_0_), custom_call_target="tpu_custom_call" | custom-call | bytes 393216 | tf_op jit(solution)/shard_map/pallas_call | solution.py:245
  91.0 1.3 %collective-permute-done.25 = bf16[4,12288]{1,0:T(4,128)(2,1)S(1)} collective-permute-done((bf16[4,12288]{1,0:T(4,128)(2,1)S(1)}, bf16[4,12288]{1,0:T(4,128)(2,1)S(1)}, u32[]{:S(2)}, u32[]{:S(2)}) %collective-permute-start.25) | collective-permute-done | bytes 98336 | tf_op jit(solution)/shard_map/ppermute | solution.py:24
  92.4 4.7 %collective-permute-done.24 = bf16[4,12288]{1,0:T(4,128)(2,1)S(1)} collective-permute-done((bf16[4,12288]{1,0:T(4,128)(2,1)S(1)}, bf16[4,12288]{1,0:T(4,128)(2,1)S(1)}, u32[]{:S(2)}, u32[]{:S(2)}) %collective-permute-start.24) | collective-permute-done | bytes 98336 | tf_op jit(solution)/shard_map/ppermute | solution.py:24
  (51 shorter events, 9.2 us)
Async XLA Ops:
  0.6 10.9 %collective-permute-start.1 = (bf16[4,12288]{1,0:T(4,128)(2,1)}, bf16[4,12288]{1,0:T(4,128)(2,1)S(1)}, u32[]{:S(2)}, u32[]{:S(2)}) collective-permute-start(bf16[4,12288]{1,0:T(4,128)(2,1)} %param.4), channel_id=1, source_target_pairs={{0,16},{4,20},{8,24},{12,28},{16,0},{20,4},{24,8},{28,12},{1,17},{... | collective-permute-start | bytes 294920 | tf_op jit(solution)/shard_map/ppermute | solution.py:24
  4.7 7.4 %collective-permute-start = (bf16[4,12288]{1,0:T(4,128)(2,1)}, bf16[4,12288]{1,0:T(4,128)(2,1)S(1)}, u32[]{:S(2)}, u32[]{:S(2)}) collective-permute-start(bf16[4,12288]{1,0:T(4,128)(2,1)} %param.4), channel_id=1, source_target_pairs={{0,8},{4,12},{8,0},{12,4},{16,24},{20,28},{24,16},{28,20},{1,9},{5... | collective-permute-start | bytes 294920 | tf_op jit(solution)/shard_map/ppermute | solution.py:24
  6.3 7.4 %collective-permute-start.3 = (bf16[4,12288]{1,0:T(4,128)(2,1)}, bf16[4,12288]{1,0:T(4,128)(2,1)S(1)}, u32[]{:S(2)}, u32[]{:S(2)}) collective-permute-start(bf16[4,12288]{1,0:T(4,128)(2,1)} %param.4), channel_id=1, source_target_pairs={{0,4},{4,0},{8,12},{12,8},{16,20},{20,16},{24,28},{28,24},{1,5},{5... | collective-permute-start | bytes 294920 | tf_op jit(solution)/shard_map/ppermute | solution.py:24
  6.3 7.3 %collective-permute-start.2 = (bf16[4,12288]{1,0:T(4,128)(2,1)}, bf16[4,12288]{1,0:T(4,128)(2,1)S(1)}, u32[]{:S(2)}, u32[]{:S(2)}) collective-permute-start(bf16[4,12288]{1,0:T(4,128)(2,1)} %param.4), channel_id=1, source_target_pairs={{0,24},{4,28},{8,16},{12,20},{16,8},{20,12},{24,0},{28,4},{1,25},{... | collective-permute-start | bytes 294920 | tf_op jit(solution)/shard_map/ppermute | solution.py:24
  9.7 1.8 %copy-start.1 = (f32[8]{0:T(128)S(1)}, f32[8]{0:T(128)}, u32[]{:S(2)}) copy-start(f32[8]{0:T(128)} %param.7) | copy-start | bytes 100
  11.5 2.2 %collective-permute-start.5 = (bf16[4,12288]{1,0:T(4,128)(2,1)S(1)}, bf16[4,12288]{1,0:T(4,128)(2,1)S(1)}, u32[]{:S(2)}, u32[]{:S(2)}) collective-permute-start(bf16[4,12288]{1,0:T(4,128)(2,1)S(1)} %collective-permute-done.1.refs_2_), channel_id=1, source_target_pairs={{0,4},{4,0},{8,12},{12,8},{16,20},{20,16},{24,28},{28,24},{1,5},{5... | collective-permute-start | bytes 294920 | tf_op jit(solution)/shard_map/ppermute | solution.py:24
  12.1 1.6 %collective-permute-start.4 = (bf16[4,12288]{1,0:T(4,128)(2,1)S(1)}, bf16[4,12288]{1,0:T(4,128)(2,1)S(1)}, u32[]{:S(2)}, u32[]{:S(2)}) collective-permute-start(bf16[4,12288]{1,0:T(4,128)(2,1)S(1)} %collective-permute-done.refs_1_), channel_id=1, source_target_pairs={{0,4},{4,0},{8,12},{12,8},{16,20},{20,16},{24,28},{28,24},{1,5},{5... | collective-permute-start | bytes 294920 | tf_op jit(solution)/shard_map/ppermute | solution.py:24
  13.6 1.3 %collective-permute-start.6 = (bf16[4,12288]{1,0:T(4,128)(2,1)S(1)}, bf16[4,12288]{1,0:T(4,128)(2,1)S(1)}, u32[]{:S(2)}, u32[]{:S(2)}) collective-permute-start(bf16[4,12288]{1,0:T(4,128)(2,1)S(1)} %collective-permute-done.2.refs_3_), channel_id=1, source_target_pairs={{0,4},{4,0},{8,12},{12,8},{16,20},{20,16},{24,28},{28,24},{1,5},{5... | collective-permute-start | bytes 294920 | tf_op jit(solution)/shard_map/ppermute | solution.py:24
  14.9 19.0 %copy-start = (bf16[32,256,256]{2,1,0:T(8,128)(2,1)S(1)}, bf16[32,256,256]{2,1,0:T(8,128)(2,1)}, u32[]{:S(2)}) copy-start(bf16[32,256,256]{2,1,0:T(8,128)(2,1)} %refs_1_.3) | copy-start | bytes 12582916
  18.0 7.8 %collective-permute-start.7 = (bf16[48,32,128]{2,1,0:T(8,128)(2,1)S(1)}, bf16[48,32,128]{2,1,0:T(8,128)(2,1)S(1)}, u32[]{:S(2)}, u32[]{:S(2)}) collective-permute-start(bf16[48,32,128]{2,1,0:T(8,128)(2,1)S(1)} %shard_map.75), channel_id=1, source_target_pairs={{0,1},{1,0},{2,3},{3,2},{4,6},{5,7},{6,4},{7,5},{8,9},{9,8},{10,11... | collective-permute-start | bytes 1179656 | tf_op jit(solution)/shard_map/ppermute | solution.py:283
  25.9 7.8 %collective-permute-start.8 = (bf16[48,32,128]{2,1,0:T(8,128)(2,1)S(1)}, bf16[48,32,128]{2,1,0:T(8,128)(2,1)S(1)}, u32[]{:S(2)}, u32[]{:S(2)}) collective-permute-start(bf16[48,32,128]{2,1,0:T(8,128)(2,1)S(1)} %add_convert_fusion.4), channel_id=1, source_target_pairs={{0,2},{1,3},{2,0},{3,1},{4,5},{5,4},{6,7},{7,6},{8,10},{9,11},{10,... | collective-permute-start | bytes 1179656 | tf_op jit(solution)/shard_map/ppermute | solution.py:283
  35.4 1.8 %collective-permute-start.9 = (bf16[4,12,32,128]{3,2,1,0:T(8,128)(2,1)S(1)}, bf16[4,12,32,128]{3,2,1,0:T(8,128)(2,1)S(1)}, u32[]{:S(2)}, u32[]{:S(2)}) collective-permute-start(bf16[4,12,32,128]{3,2,1,0:T(8,128)(2,1)S(1)} %get-tuple-element.21), channel_id=1, source_target_pairs={{0,4},{4,0},{8,12},{12,8},{16,20},{20,16},{24,28},{28,24},{1,5},{5... | collective-permute-start | bytes 1179656 | tf_op jit(solution)/shard_map/ppermute | solution.py:24
  37.3 4.9 %collective-permute-start.10 = (bf16[12,32,128]{2,1,0:T(8,128)(2,1)S(1)}, bf16[12,32,128]{2,1,0:T(8,128)(2,1)S(1)}, u32[]{:S(2)}, u32[]{:S(2)}) collective-permute-start(bf16[12,32,128]{2,1,0:T(8,128)(2,1)S(1)} %get-tuple-element.39), channel_id=1, source_target_pairs={{0,8},{4,12},{8,0},{12,4},{16,24},{20,28},{24,16},{28,20},{1,9},{5... | collective-permute-start | bytes 294920 | tf_op jit(solution)/shard_map/ppermute | solution.py:24
  38.6 9.1 %collective-permute-start.12 = (bf16[12,32,128]{2,1,0:T(8,128)(2,1)S(1)}, bf16[12,32,128]{2,1,0:T(8,128)(2,1)S(1)}, u32[]{:S(2)}, u32[]{:S(2)}) collective-permute-start(bf16[12,32,128]{2,1,0:T(8,128)(2,1)S(1)} %get-tuple-element.40), channel_id=1, source_target_pairs={{0,24},{4,28},{8,16},{12,20},{16,8},{20,12},{24,0},{28,4},{1,25},{... | collective-permute-start | bytes 294920 | tf_op jit(solution)/shard_map/ppermute | solution.py:24
  41.9 8.9 %collective-permute-start.11 = (bf16[12,32,128]{2,1,0:T(8,128)(2,1)S(1)}, bf16[12,32,128]{2,1,0:T(8,128)(2,1)S(1)}, u32[]{:S(2)}, u32[]{:S(2)}) collective-permute-start(bf16[12,32,128]{2,1,0:T(8,128)(2,1)S(1)} %get-tuple-element.41), channel_id=1, source_target_pairs={{0,16},{4,20},{8,24},{12,28},{16,0},{20,4},{24,8},{28,12},{1,17},{... | collective-permute-start | bytes 294920 | tf_op jit(solution)/shard_map/ppermute | solution.py:24
  50.8 7.7 %collective-permute-start.15 = (bf16[12,32,128]{2,1,0:T(8,128)(2,1)S(1)}, bf16[12,32,128]{2,1,0:T(8,128)(2,1)S(1)}, u32[]{:S(2)}, u32[]{:S(2)}) collective-permute-start(bf16[12,32,128]{2,1,0:T(8,128)(2,1)S(1)} %fusion.6.refs_0_.refs_1_), channel_id=1, source_target_pairs={{0,24},{4,28},{8,16},{12,20},{16,8},{20,12},{24,0},{28,4},{1,25},{... | collective-permute-start | bytes 294920 | tf_op jit(solution)/shard_map/ppermute | solution.py:24
  52.7 8.6 %collective-permute-start.14 = (bf16[12,32,128]{2,1,0:T(8,128)(2,1)S(1)}, bf16[12,32,128]{2,1,0:T(8,128)(2,1)S(1)}, u32[]{:S(2)}, u32[]{:S(2)}) collective-permute-start(bf16[12,32,128]{2,1,0:T(8,128)(2,1)S(1)} %fusion.6.refs_0_.refs_1_), channel_id=1, source_target_pairs={{0,16},{4,20},{8,24},{12,28},{16,0},{20,4},{24,8},{28,12},{1,17},{... | collective-permute-start | bytes 294920 | tf_op jit(solution)/shard_map/ppermute | solution.py:24
  52.7 8.6 %collective-permute-start.13 = (bf16[12,32,128]{2,1,0:T(8,128)(2,1)S(1)}, bf16[12,32,128]{2,1,0:T(8,128)(2,1)S(1)}, u32[]{:S(2)}, u32[]{:S(2)}) collective-permute-start(bf16[12,32,128]{2,1,0:T(8,128)(2,1)S(1)} %fusion.6.refs_0_.refs_1_), channel_id=1, source_target_pairs={{0,8},{4,12},{8,0},{12,4},{16,24},{20,28},{24,16},{28,20},{1,9},{5... | collective-permute-start | bytes 294920 | tf_op jit(solution)/shard_map/ppermute | solution.py:24
  55.3 6.5 %collective-permute-start.16 = (bf16[12,32,128]{2,1,0:T(8,128)(2,1)S(1)}, bf16[12,32,128]{2,1,0:T(8,128)(2,1)S(1)}, u32[]{:S(2)}, u32[]{:S(2)}) collective-permute-start(bf16[12,32,128]{2,1,0:T(8,128)(2,1)S(1)} %fusion.6.refs_0_.refs_1_), channel_id=1, source_target_pairs={{0,4},{4,0},{8,12},{12,8},{16,20},{20,16},{24,28},{28,24},{1,5},{5... | collective-permute-start | bytes 294920 | tf_op jit(solution)/shard_map/ppermute | solution.py:24
  58.5 3.3 %collective-permute-start.19 = (bf16[12,32,128]{2,1,0:T(8,128)(2,1)S(1)}, bf16[12,32,128]{2,1,0:T(8,128)(2,1)S(1)}, u32[]{:S(2)}, u32[]{:S(2)}) collective-permute-start(bf16[12,32,128]{2,1,0:T(8,128)(2,1)S(1)} %collective-permute-done.15.refs_3_.refs_4_), channel_id=1, source_target_pairs={{0,4},{4,0},{8,12},{12,8},{16,20},{20,16},{24,28},{28,24},{1,5},{5... | collective-permute-start | bytes 294920 | tf_op jit(solution)/shard_map/ppermute | solution.py:24
  61.3 1.3 %collective-permute-start.18 = (bf16[12,32,128]{2,1,0:T(8,128)(2,1)S(1)}, bf16[12,32,128]{2,1,0:T(8,128)(2,1)S(1)}, u32[]{:S(2)}, u32[]{:S(2)}) collective-permute-start(bf16[12,32,128]{2,1,0:T(8,128)(2,1)S(1)} %collective-permute-done.14.refs_2_.refs_3_), channel_id=1, source_target_pairs={{0,4},{4,0},{8,12},{12,8},{16,20},{20,16},{24,28},{28,24},{1,5},{5... | collective-permute-start | bytes 294920 | tf_op jit(solution)/shard_map/ppermute | solution.py:24
  61.3 1.4 %collective-permute-start.17 = (bf16[12,32,128]{2,1,0:T(8,128)(2,1)S(1)}, bf16[12,32,128]{2,1,0:T(8,128)(2,1)S(1)}, u32[]{:S(2)}, u32[]{:S(2)}) collective-permute-start(bf16[12,32,128]{2,1,0:T(8,128)(2,1)S(1)} %collective-permute-done.13.refs_1_.refs_2_), channel_id=1, source_target_pairs={{0,4},{4,0},{8,12},{12,8},{16,20},{20,16},{24,28},{28,24},{1,5},{5... | collective-permute-start | bytes 294920 | tf_op jit(solution)/shard_map/ppermute | solution.py:24
  64.7 7.8 %collective-permute-start.20 = (bf16[48,32,128]{2,1,0:T(8,128)(2,1)S(1)}, bf16[48,32,128]{2,1,0:T(8,128)(2,1)S(1)}, u32[]{:S(2)}, u32[]{:S(2)}) collective-permute-start(bf16[48,32,128]{2,1,0:T(8,128)(2,1)S(1)} %shard_map.77), channel_id=1, source_target_pairs={{0,1},{1,0},{2,3},{3,2},{4,6},{5,7},{6,4},{7,5},{8,9},{9,8},{10,11... | collective-permute-start | bytes 1179656 | tf_op jit(solution)/shard_map/ppermute | solution.py:283
  72.7 7.8 %collective-permute-start.21 = (bf16[48,32,128]{2,1,0:T(8,128)(2,1)S(1)}, bf16[48,32,128]{2,1,0:T(8,128)(2,1)S(1)}, u32[]{:S(2)}, u32[]{:S(2)}) collective-permute-start(bf16[48,32,128]{2,1,0:T(8,128)(2,1)S(1)} %add_convert_fusion.1), channel_id=1, source_target_pairs={{0,2},{1,3},{2,0},{3,1},{4,5},{5,4},{6,7},{7,6},{8,10},{9,11},{10,... | collective-permute-start | bytes 1179656 | tf_op jit(solution)/shard_map/ppermute | solution.py:283
  82.6 1.8 %collective-permute-start.22 = (bf16[4,4,12288]{2,1,0:T(4,128)(2,1)S(1)}, bf16[4,4,12288]{2,1,0:T(4,128)(2,1)S(1)}, u32[]{:S(2)}, u32[]{:S(2)}) collective-permute-start(bf16[4,4,12288]{2,1,0:T(4,128)(2,1)S(1)} %slice_bitcast_fusion), channel_id=1, source_target_pairs={{0,4},{4,0},{8,12},{12,8},{16,20},{20,16},{24,28},{28,24},{1,5},{5... | collective-permute-start | bytes 1179656 | tf_op jit(solution)/shard_map/ppermute | solution.py:24
  84.7 6.3 %collective-permute-start.23 = (bf16[4,12288]{1,0:T(4,128)(2,1)S(1)}, bf16[4,12288]{1,0:T(4,128)(2,1)S(1)}, u32[]{:S(2)}, u32[]{:S(2)}) collective-permute-start(bf16[4,12288]{1,0:T(4,128)(2,1)S(1)} %get-tuple-element.36), channel_id=1, source_target_pairs={{0,8},{4,12},{8,0},{12,4},{16,24},{20,28},{24,16},{28,20},{1,9},{5... | collective-permute-start | bytes 294920 | tf_op jit(solution)/shard_map/ppermute | solution.py:24
  84.8 7.6 %collective-permute-start.25 = (bf16[4,12288]{1,0:T(4,128)(2,1)S(1)}, bf16[4,12288]{1,0:T(4,128)(2,1)S(1)}, u32[]{:S(2)}, u32[]{:S(2)}) collective-permute-start(bf16[4,12288]{1,0:T(4,128)(2,1)S(1)} %get-tuple-element.37), channel_id=1, source_target_pairs={{0,24},{4,28},{8,16},{12,20},{16,8},{20,12},{24,0},{28,4},{1,25},{... | collective-permute-start | bytes 294920 | tf_op jit(solution)/shard_map/ppermute | solution.py:24
  86.6 10.5 %collective-permute-start.24 = (bf16[4,12288]{1,0:T(4,128)(2,1)S(1)}, bf16[4,12288]{1,0:T(4,128)(2,1)S(1)}, u32[]{:S(2)}, u32[]{:S(2)}) collective-permute-start(bf16[4,12288]{1,0:T(4,128)(2,1)S(1)} %get-tuple-element.38), channel_id=1, source_target_pairs={{0,16},{4,20},{8,24},{12,28},{16,0},{20,4},{24,8},{28,12},{1,17},{... | collective-permute-start | bytes 294920 | tf_op jit(solution)/shard_map/ppermute | solution.py:24

commit v14 on v12

--- a/solution.py
+++ b/solution.py
@@ -14,7 +14,7 @@
 COPIES = 4
 ROW_PARTS = 2
 CHUNK = 1024
-UNROLL = 48
+UNROLL = 96
 VMEM_LIMIT = 12 * 1024 * 1024
 FIRST_LIMIT = 50 * 1024 * 1024
 
@@ -298,8 +298,9 @@
         return same + [swap(one, "panel", 1) for one in same]
 
     mine = jnp.where(core >= 0, strengths, 0)
-    ready = jnp.where(core >= 0, blocks[: slots // 2], 0)
-    own_copy = [pltpu.VMEM((slots - slots // 2, B, B), blocks.dtype), pltpu.SemaphoreType.DMA((COPIES,))]
+    at_hand = slots * 3 // 4
+    ready = jnp.where(core >= 0, blocks[:at_hand], 0)
+    own_copy = [pltpu.VMEM((slots - at_hand, B, B), blocks.dtype), pltpu.SemaphoreType.DMA((COPIES,))]
     scratches = [rows_total, *flat, *own_copy]
     first_sums = over_case(
         product(first_kernel, [mine, *gather_panel(strengths)[1:], ready], row_shapes, scratches, FIRST_LIMIT, pl.BlockSpec(memory_space=pl.ANY))

time: 96 us -> 97.9 us (1.020)
  other arithmetic: 5.9 us -> 7.9 us
  waiting for transfers between devices: 46.5 us -> 45.3 us
  Pallas kernels: 11.4 us -> 12.5 us
    select_n x1, other arithmetic: 1.74 us -> 3.73 us  [shards(): ready = jnp.where(core >= 0, blocks[:at_hand], 0)]
    ppermute x30, waiting for transfers between devices: 46.5 us -> 45.3 us  [swap(): return lax.ppermute(value, axis, [(i, i ^ offset) for i in range(count)])]
    pallas_call x4, Pallas kernels: 8.66 us -> 9.74 us  [product(): pl.pallas_call(functools.partial(kernel, ways), out_shape=[jax.ShapeDtype...]
  transfers between devices with their start and end apart: 30 -> 30, of which waited for: 19 -> 20; matrix products, arithmetic and copies ran while one was open for 6% -> 8% of each run, Pallas kernels for 3% -> 3%
where the time goes in v14:
time: 97.9 us; the launch traced here: 97.6 us
  waiting for transfers between devices  45.3 us (46%)
  starting transfers between devices  30 us (31%)
  Pallas kernels  12.5 us (13%)
  other arithmetic  7.9 us (8%)
  local copies, waits for them, and re-layouts  1.15 us (1%)
    ppermute x30, waiting for transfers between devices, swap(): return lax.ppermute(value, axis, [(i, i ^ offset) for i in range(count)])  45.3 us
    ppermute x30, starting transfers between devices, swap(): return lax.ppermute(value, axis, [(i, i ^ offset) for i in range(count)])  30 us
    pallas_call x4, Pallas kernels, product(): pl.pallas_call(functools.partial(kernel, ways), out_shape=[jax.ShapeDtype...  9.74 us
    select_n x1, other arithmetic, shards(): ready = jnp.where(core >= 0, blocks[:at_hand], 0)  3.73 us
    pallas_call x2, Pallas kernels, cut(): pl.pallas_call(functools.partial(kernel, ways), out_shape=[jax.ShapeDtype...  2.77 us
  transfers between devices with their start and end apart: 30, of which 20 were waited for; matrix products, arithmetic and copies ran while one was open for 8% of the time, Pallas kernels for 3%

profile of v14, /device:TPU:0, one launch (start us, length us, event | category | flops | bytes accessed | tf_op | source)
XLA Modules:
  0.0 97.6 jit_solution(13947620066783627809)
XLA Ops:
  0.6 4.1 %collective-permute-start.1 = (bf16[4,12288]{1,0:T(4,128)(2,1)}, bf16[4,12288]{1,0:T(4,128)(2,1)S(1)}, u32[]{:S(2)}, u32[]{:S(2)}) collective-permute-start(bf16[4,12288]{1,0:T(4,128)(2,1)} %param.4), channel_id=1, source_target_pairs={{0,16},{4,20},{8,24},{12,28},{16,0},{20,4},{24,8},{28,12},{1,17},{... | collective-permute-start | bytes 294920 | tf_op jit(solution)/shard_map/ppermute | solution.py:24
  4.7 1.6 %collective-permute-start = (bf16[4,12288]{1,0:T(4,128)(2,1)}, bf16[4,12288]{1,0:T(4,128)(2,1)S(1)}, u32[]{:S(2)}, u32[]{:S(2)}) collective-permute-start(bf16[4,12288]{1,0:T(4,128)(2,1)} %param.4), channel_id=1, source_target_pairs={{0,8},{4,12},{8,0},{12,4},{16,24},{20,28},{24,16},{28,20},{1,9},{5... | collective-permute-start | bytes 294920 | tf_op jit(solution)/shard_map/ppermute | solution.py:24
  9.7 3.7 %slice_select_fusion.refs_8_ = bf16[24,256,256]{2,1,0:T(8,128)(2,1)} fusion(bf16[32,256,256]{2,1,0:T(8,128)(2,1)} %refs_2_.3, pred[]{:T(512)S(6)} %ge.12), kind=kLoop, calls=%fused_computation | loop fusion | flops 1572864 | bytes 6291457 | tf_op jit(solution)/shard_map/jit(_where)/select_n | solution.py:302
  15.5 4.5 %shard_map.75 = (bf16[24,32,128]{2,1,0:T(8,128)(2,1)S(1)}, bf16[24,32,128]{2,1,0:T(8,128)(2,1)S(1)}) custom-call(s32[64]{0:T(128)S(1)} %reshape.18.entry_ref, f32[32]{0:T(128)S(1)} %select_reduce_fusion.scale_ref, s32[3]{0:T(128)S(1)} %pad_add_fusion.place_ref, bf16[4,12288]{1,0:T(4,128)(2,1)S(1)} %broadcast_select_fusion.refs_0_, ...), custom_call_target="tpu_custom_call" | custom-call | flops 134217728 | bytes 4194304 | tf_op jit(solution)/shard_map/pallas_call | solution.py:256
  20.0 1.6 %collective-permute-start.7 = (bf16[24,32,128]{2,1,0:T(8,128)(2,1)S(1)}, bf16[24,32,128]{2,1,0:T(8,128)(2,1)S(1)}, u32[]{:S(2)}, u32[]{:S(2)}) collective-permute-start(bf16[24,32,128]{2,1,0:T(8,128)(2,1)S(1)} %get-tuple-element.27), channel_id=1, source_target_pairs={{0,1},{1,0},{2,3},{3,2},{4,5},{5,4},{6,7},{7,6},{8,9},{9,8},{10,11... | collective-permute-start | bytes 589832 | tf_op jit(solution)/shard_map/ppermute | solution.py:24
  21.6 1.5 %collective-permute-start.9 = (bf16[24,32,128]{2,1,0:T(8,128)(2,1)S(1)}, bf16[24,32,128]{2,1,0:T(8,128)(2,1)S(1)}, u32[]{:S(2)}, u32[]{:S(2)}) collective-permute-start(bf16[24,32,128]{2,1,0:T(8,128)(2,1)S(1)} %get-tuple-element.28), channel_id=1, source_target_pairs={{0,2},{1,3},{2,0},{3,1},{4,6},{5,7},{6,4},{7,5},{8,10},{9,11},{10,... | collective-permute-start | bytes 589832 | tf_op jit(solution)/shard_map/ppermute | solution.py:24
  23.2 4.1 %collective-permute-done.7 = bf16[24,32,128]{2,1,0:T(8,128)(2,1)S(1)} collective-permute-done((bf16[24,32,128]{2,1,0:T(8,128)(2,1)S(1)}, bf16[24,32,128]{2,1,0:T(8,128)(2,1)S(1)}, u32[]{:S(2)}, u32[]{:S(2)}) %collective-permute-start.7) | collective-permute-done | bytes 196640 | tf_op jit(solution)/shard_map/ppermute | solution.py:24
  27.3 1.6 %collective-permute-start.8 = (bf16[24,32,128]{2,1,0:T(8,128)(2,1)S(1)}, bf16[24,32,128]{2,1,0:T(8,128)(2,1)S(1)}, u32[]{:S(2)}, u32[]{:S(2)}) collective-permute-start(bf16[24,32,128]{2,1,0:T(8,128)(2,1)S(1)} %add_convert_fusion.8), channel_id=1, source_target_pairs={{0,2},{1,3},{2,0},{3,1},{4,6},{5,7},{6,4},{7,5},{8,10},{9,11},{10,... | collective-permute-start | bytes 589832 | tf_op jit(solution)/shard_map/ppermute | solution.py:24
  28.9 1.6 %collective-permute-start.10 = (bf16[24,32,128]{2,1,0:T(8,128)(2,1)S(1)}, bf16[24,32,128]{2,1,0:T(8,128)(2,1)S(1)}, u32[]{:S(2)}, u32[]{:S(2)}) collective-permute-start(bf16[24,32,128]{2,1,0:T(8,128)(2,1)S(1)} %add_convert_fusion.6), channel_id=1, source_target_pairs={{0,1},{1,0},{2,3},{3,2},{4,5},{5,4},{6,7},{7,6},{8,9},{9,8},{10,11... | collective-permute-start | bytes 589832 | tf_op jit(solution)/shard_map/ppermute | solution.py:24
  30.5 3.2 %collective-permute-done.8 = bf16[24,32,128]{2,1,0:T(8,128)(2,1)S(1)} collective-permute-done((bf16[24,32,128]{2,1,0:T(8,128)(2,1)S(1)}, bf16[24,32,128]{2,1,0:T(8,128)(2,1)S(1)}, u32[]{:S(2)}, u32[]{:S(2)}) %collective-permute-start.8) | collective-permute-done | bytes 196640 | tf_op jit(solution)/shard_map/ppermute | solution.py:24
  33.8 1.2 %collective-permute-done.10 = bf16[24,32,128]{2,1,0:T(8,128)(2,1)S(1)} collective-permute-done((bf16[24,32,128]{2,1,0:T(8,128)(2,1)S(1)}, bf16[24,32,128]{2,1,0:T(8,128)(2,1)S(1)}, u32[]{:S(2)}, u32[]{:S(2)}) %collective-permute-start.10) | collective-permute-done | bytes 196640 | tf_op jit(solution)/shard_map/ppermute | solution.py:24
  35.1 1.5 %shard_map.76 = (bf16[4,12,32,128]{3,2,1,0:T(8,128)(2,1)S(1)}, bf16[4,12,32,128]{3,2,1,0:T(8,128)(2,1)S(1)}) custom-call(s32[64]{0:T(128)S(1)} %reshape.18.entry_ref, f32[32]{0:T(128)S(1)} %select_reduce_fusion.scale_ref, s32[3]{0:T(128)S(1)} %pad_add_fusion.place_ref, bf16[24,32,128]{2,1,0:T(8,128)(2,1)S(1)} %add_convert_fusion.7.refs_0_, ...), custom_call_target="tpu_custom_call" | custom-call | flops 134217728 | bytes 4194304 | tf_op jit(solution)/shard_map/pallas_call | solution.py:256
  36.7 1.7 %collective-permute-done.11 = bf16[4,12,32,128]{3,2,1,0:T(8,128)(2,1)S(1)} collective-permute-done((bf16[4,12,32,128]{3,2,1,0:T(8,128)(2,1)S(1)}, bf16[4,12,32,128]{3,2,1,0:T(8,128)(2,1)S(1)}, u32[]{:S(2)}, u32[]{:S(2)}) %collective-permute-start.11) | collective-permute-done | bytes 393248 | tf_op jit(solution)/shard_map/ppermute | solution.py:24
  39.1 3.0 %collective-permute-start.14 = (bf16[12,32,128]{2,1,0:T(8,128)(2,1)S(1)}, bf16[12,32,128]{2,1,0:T(8,128)(2,1)S(1)}, u32[]{:S(2)}, u32[]{:S(2)}) collective-permute-start(bf16[12,32,128]{2,1,0:T(8,128)(2,1)S(1)} %get-tuple-element.54), channel_id=1, source_target_pairs={{0,24},{4,28},{8,16},{12,20},{16,8},{20,12},{24,0},{28,4},{1,25},{... | collective-permute-start | bytes 294920 | tf_op jit(solution)/shard_map/ppermute | solution.py:24
  43.4 4.5 %collective-permute-done.14 = bf16[12,32,128]{2,1,0:T(8,128)(2,1)S(1)} collective-permute-done((bf16[12,32,128]{2,1,0:T(8,128)(2,1)S(1)}, bf16[12,32,128]{2,1,0:T(8,128)(2,1)S(1)}, u32[]{:S(2)}, u32[]{:S(2)}) %collective-permute-start.14) | collective-permute-done | bytes 98336 | tf_op jit(solution)/shard_map/ppermute | solution.py:24
  47.9 3.8 %collective-permute-done.13 = bf16[12,32,128]{2,1,0:T(8,128)(2,1)S(1)} collective-permute-done((bf16[12,32,128]{2,1,0:T(8,128)(2,1)S(1)}, bf16[12,32,128]{2,1,0:T(8,128)(2,1)S(1)}, u32[]{:S(2)}, u32[]{:S(2)}) %collective-permute-start.13) | collective-permute-done | bytes 98336 | tf_op jit(solution)/shard_map/ppermute | solution.py:24
  51.8 2.7 %collective-permute-start.17 = (bf16[12,32,128]{2,1,0:T(8,128)(2,1)S(1)}, bf16[12,32,128]{2,1,0:T(8,128)(2,1)S(1)}, u32[]{:S(2)}, u32[]{:S(2)}) collective-permute-start(bf16[12,32,128]{2,1,0:T(8,128)(2,1)S(1)} %fusion.6.refs_0_.refs_2_), channel_id=1, source_target_pairs={{0,24},{4,28},{8,16},{12,20},{16,8},{20,12},{24,0},{28,4},{1,25},{... | collective-permute-start | bytes 294920 | tf_op jit(solution)/shard_map/ppermute | solution.py:24
  54.5 1.7 %collective-permute-start.15 = (bf16[12,32,128]{2,1,0:T(8,128)(2,1)S(1)}, bf16[12,32,128]{2,1,0:T(8,128)(2,1)S(1)}, u32[]{:S(2)}, u32[]{:S(2)}) collective-permute-start(bf16[12,32,128]{2,1,0:T(8,128)(2,1)S(1)} %fusion.6.refs_0_.refs_2_), channel_id=1, source_target_pairs={{0,8},{4,12},{8,0},{12,4},{16,24},{20,28},{24,16},{28,20},{1,9},{5... | collective-permute-start | bytes 294920 | tf_op jit(solution)/shard_map/ppermute | solution.py:24
  56.3 3.2 %collective-permute-done.17.refs_3_.refs_5_ = bf16[12,32,128]{2,1,0:T(8,128)(2,1)S(1)} collective-permute-done((bf16[12,32,128]{2,1,0:T(8,128)(2,1)S(1)}, bf16[12,32,128]{2,1,0:T(8,128)(2,1)S(1)}, u32[]{:S(2)}, u32[]{:S(2)}) %collective-permute-start.17) | collective-permute-done | bytes 98336 | tf_op jit(solution)/shard_map/ppermute | solution.py:24
  59.4 2.9 %collective-permute-done.16.refs_2_.refs_4_ = bf16[12,32,128]{2,1,0:T(8,128)(2,1)S(1)} collective-permute-done((bf16[12,32,128]{2,1,0:T(8,128)(2,1)S(1)}, bf16[12,32,128]{2,1,0:T(8,128)(2,1)S(1)}, u32[]{:S(2)}, u32[]{:S(2)}) %collective-permute-start.16) | collective-permute-done | bytes 98336 | tf_op jit(solution)/shard_map/ppermute | solution.py:24
  63.8 2.0 %shard_map.77 = (bf16[24,32,128]{2,1,0:T(8,128)(2,1)S(1)}, bf16[24,32,128]{2,1,0:T(8,128)(2,1)S(1)}) custom-call(s32[64]{0:T(128)S(1)} %reshape.18.entry_ref, f32[32]{0:T(128)S(1)} %select_reduce_fusion.scale_ref, s32[3]{0:T(128)S(1)} %pad_add_fusion.place_ref, bf16[12,32,128]{2,1,0:T(8,128)(2,1)S(1)} %fusion.6.refs_0_.refs_2_, ...), custom_call_target="tpu_custom_call" | custom-call | flops 134217728 | bytes 4194304 | tf_op jit(solution)/shard_map/pallas_call | solution.py:256
  65.8 1.5 %collective-permute-start.22 = (bf16[24,32,128]{2,1,0:T(8,128)(2,1)S(1)}, bf16[24,32,128]{2,1,0:T(8,128)(2,1)S(1)}, u32[]{:S(2)}, u32[]{:S(2)}) collective-permute-start(bf16[24,32,128]{2,1,0:T(8,128)(2,1)S(1)} %get-tuple-element.45), channel_id=1, source_target_pairs={{0,1},{1,0},{2,3},{3,2},{4,5},{5,4},{6,7},{7,6},{8,9},{9,8},{10,11... | collective-permute-start | bytes 589832 | tf_op jit(solution)/shard_map/ppermute | solution.py:24
  67.8 5.2 %collective-permute-done.22 = bf16[24,32,128]{2,1,0:T(8,128)(2,1)S(1)} collective-permute-done((bf16[24,32,128]{2,1,0:T(8,128)(2,1)S(1)}, bf16[24,32,128]{2,1,0:T(8,128)(2,1)S(1)}, u32[]{:S(2)}, u32[]{:S(2)}) %collective-permute-start.22) | collective-permute-done | bytes 196640 | tf_op jit(solution)/shard_map/ppermute | solution.py:24
  75.2 4.2 %collective-permute-done.23 = bf16[24,32,128]{2,1,0:T(8,128)(2,1)S(1)} collective-permute-done((bf16[24,32,128]{2,1,0:T(8,128)(2,1)S(1)}, bf16[24,32,128]{2,1,0:T(8,128)(2,1)S(1)}, u32[]{:S(2)}, u32[]{:S(2)}) %collective-permute-start.23) | collective-permute-done | bytes 196640 | tf_op jit(solution)/shard_map/ppermute | solution.py:24
  80.4 1.8 %shard_map.79 = bf16[2,4,4,12288]{3,2,1,0:T(4,128)(2,1)S(1)} custom-call(s32[64]{0:T(128)S(1)} %reshape.18.entry_ref, f32[32]{0:T(128)S(1)} %select_reduce_fusion.scale_ref, s32[3]{0:T(128)S(1)} %pad_add_fusion.place_ref, bf16[24,32,128]{2,1,0:T(8,128)(2,1)S(1)} %add_convert_fusion.3.refs_0_, bf16[24,32,128]{2,1,0:T(8,128)(2,1)S(1)} %add_convert_fusion.1.refs_1_, ...), custom_call_target="tpu_custom_call" | custom-call | flops 134217728 | bytes 4194304 | tf_op jit(solution)/shard_map/pallas_call | solution.py:256
  82.4 1.7 %collective-permute-done.26 = bf16[4,4,12288]{2,1,0:T(4,128)(2,1)S(1)} collective-permute-done((bf16[4,4,12288]{2,1,0:T(4,128)(2,1)S(1)}, bf16[4,4,12288]{2,1,0:T(4,128)(2,1)S(1)}, u32[]{:S(2)}, u32[]{:S(2)}) %collective-permute-start.26) | collective-permute-done | bytes 393248 | tf_op jit(solution)/shard_map/ppermute | solution.py:24
  84.6 2.3 %collective-permute-start.29 = (bf16[4,12288]{1,0:T(4,128)(2,1)S(1)}, bf16[4,12288]{1,0:T(4,128)(2,1)S(1)}, u32[]{:S(2)}, u32[]{:S(2)}) collective-permute-start(bf16[4,12288]{1,0:T(4,128)(2,1)S(1)} %get-tuple-element.51), channel_id=1, source_target_pairs={{0,24},{4,28},{8,16},{12,20},{16,8},{20,12},{24,0},{28,4},{1,25},{... | collective-permute-start | bytes 294920 | tf_op jit(solution)/shard_map/ppermute | solution.py:24
  86.9 1.2 %collective-permute-start.28 = (bf16[4,12288]{1,0:T(4,128)(2,1)S(1)}, bf16[4,12288]{1,0:T(4,128)(2,1)S(1)}, u32[]{:S(2)}, u32[]{:S(2)}) collective-permute-start(bf16[4,12288]{1,0:T(4,128)(2,1)S(1)} %get-tuple-element.52), channel_id=1, source_target_pairs={{0,16},{4,20},{8,24},{12,28},{16,0},{20,4},{24,8},{28,12},{1,17},{... | collective-permute-start | bytes 294920 | tf_op jit(solution)/shard_map/ppermute | solution.py:24
  88.0 1.5 %shard_map.78 = (bf16[8,6144]{1,0:T(8,128)(2,1)}, bf16[4,12288]{1,0:T(4,128)(2,1)}) custom-call(s32[3]{0:T(128)S(1)} %pad_add_fusion.place_ref, bf16[24,32,128]{2,1,0:T(8,128)(2,1)S(1)} %add_convert_fusion.7.refs_0_, bf16[24,32,128]{2,1,0:T(8,128)(2,1)S(1)} %add_convert_fusion.5.refs_1_, bf16[12,32,128]{2,1,0:T(8,128)(2,1)S(1)} %fusion.6.refs_0_.refs_2_, ...), custom_call_target="tpu_custom_call" | custom-call | bytes 393216 | tf_op jit(solution)/shard_map/pallas_call | solution.py:245
  89.6 1.2 %shard_map.80 = bf16[8,6144]{1,0:T(8,128)(2,1)} custom-call(s32[3]{0:T(128)S(1)} %pad_add_fusion.place_ref, bf16[24,32,128]{2,1,0:T(8,128)(2,1)S(1)} %add_convert_fusion.3.refs_0_, bf16[24,32,128]{2,1,0:T(8,128)(2,1)S(1)} %add_convert_fusion.1.refs_1_), custom_call_target="tpu_custom_call" | custom-call | bytes 393216 | tf_op jit(solution)/shard_map/pallas_call | solution.py:245
  90.8 1.8 %collective-permute-done.29 = bf16[4,12288]{1,0:T(4,128)(2,1)S(1)} collective-permute-done((bf16[4,12288]{1,0:T(4,128)(2,1)S(1)}, bf16[4,12288]{1,0:T(4,128)(2,1)S(1)}, u32[]{:S(2)}, u32[]{:S(2)}) %collective-permute-start.29) | collective-permute-done | bytes 98336 | tf_op jit(solution)/shard_map/ppermute | solution.py:24
  92.6 4.3 %collective-permute-done.28 = bf16[4,12288]{1,0:T(4,128)(2,1)S(1)} collective-permute-done((bf16[4,12288]{1,0:T(4,128)(2,1)S(1)}, bf16[4,12288]{1,0:T(4,128)(2,1)S(1)}, u32[]{:S(2)}, u32[]{:S(2)}) %collective-permute-start.28) | collective-permute-done | bytes 98336 | tf_op jit(solution)/shard_map/ppermute | solution.py:24
  (63 shorter events, 14.3 us)
Async XLA Ops:
  0.6 12.9 %collective-permute-start.1 = (bf16[4,12288]{1,0:T(4,128)(2,1)}, bf16[4,12288]{1,0:T(4,128)(2,1)S(1)}, u32[]{:S(2)}, u32[]{:S(2)}) collective-permute-start(bf16[4,12288]{1,0:T(4,128)(2,1)} %param.4), channel_id=1, source_target_pairs={{0,16},{4,20},{8,24},{12,28},{16,0},{20,4},{24,8},{28,12},{1,17},{... | collective-permute-start | bytes 294920 | tf_op jit(solution)/shard_map/ppermute | solution.py:24
  4.7 9.3 %collective-permute-start = (bf16[4,12288]{1,0:T(4,128)(2,1)}, bf16[4,12288]{1,0:T(4,128)(2,1)S(1)}, u32[]{:S(2)}, u32[]{:S(2)}) collective-permute-start(bf16[4,12288]{1,0:T(4,128)(2,1)} %param.4), channel_id=1, source_target_pairs={{0,8},{4,12},{8,0},{12,4},{16,24},{20,28},{24,16},{28,20},{1,9},{5... | collective-permute-start | bytes 294920 | tf_op jit(solution)/shard_map/ppermute | solution.py:24
  6.3 8.3 %collective-permute-start.3 = (bf16[4,12288]{1,0:T(4,128)(2,1)}, bf16[4,12288]{1,0:T(4,128)(2,1)S(1)}, u32[]{:S(2)}, u32[]{:S(2)}) collective-permute-start(bf16[4,12288]{1,0:T(4,128)(2,1)} %param.4), channel_id=1, source_target_pairs={{0,4},{4,0},{8,12},{12,8},{16,20},{20,16},{24,28},{28,24},{1,5},{5... | collective-permute-start | bytes 294920 | tf_op jit(solution)/shard_map/ppermute | solution.py:24
  6.3 7.8 %collective-permute-start.2 = (bf16[4,12288]{1,0:T(4,128)(2,1)}, bf16[4,12288]{1,0:T(4,128)(2,1)S(1)}, u32[]{:S(2)}, u32[]{:S(2)}) collective-permute-start(bf16[4,12288]{1,0:T(4,128)(2,1)} %param.4), channel_id=1, source_target_pairs={{0,24},{4,28},{8,16},{12,20},{16,8},{20,12},{24,0},{28,4},{1,25},{... | collective-permute-start | bytes 294920 | tf_op jit(solution)/shard_map/ppermute | solution.py:24
  9.7 3.7 %copy-start.1 = (f32[8]{0:T(128)S(1)}, f32[8]{0:T(128)}, u32[]{:S(2)}) copy-start(f32[8]{0:T(128)} %param.7) | copy-start | bytes 100
  13.5 1.5 %collective-permute-start.5 = (bf16[4,12288]{1,0:T(4,128)(2,1)S(1)}, bf16[4,12288]{1,0:T(4,128)(2,1)S(1)}, u32[]{:S(2)}, u32[]{:S(2)}) collective-permute-start(bf16[4,12288]{1,0:T(4,128)(2,1)S(1)} %collective-permute-done.1.refs_2_), channel_id=1, source_target_pairs={{0,4},{4,0},{8,12},{12,8},{16,20},{20,16},{24,28},{28,24},{1,5},{5... | collective-permute-start | bytes 294920 | tf_op jit(solution)/shard_map/ppermute | solution.py:24
  14.1 1.3 %collective-permute-start.4 = (bf16[4,12288]{1,0:T(4,128)(2,1)S(1)}, bf16[4,12288]{1,0:T(4,128)(2,1)S(1)}, u32[]{:S(2)}, u32[]{:S(2)}) collective-permute-start(bf16[4,12288]{1,0:T(4,128)(2,1)S(1)} %collective-permute-done.refs_1_), channel_id=1, source_target_pairs={{0,4},{4,0},{8,12},{12,8},{16,20},{20,16},{24,28},{28,24},{1,5},{5... | collective-permute-start | bytes 294920 | tf_op jit(solution)/shard_map/ppermute | solution.py:24
  14.1 1.4 %collective-permute-start.6 = (bf16[4,12288]{1,0:T(4,128)(2,1)S(1)}, bf16[4,12288]{1,0:T(4,128)(2,1)S(1)}, u32[]{:S(2)}, u32[]{:S(2)}) collective-permute-start(bf16[4,12288]{1,0:T(4,128)(2,1)S(1)} %collective-permute-done.2.refs_3_), channel_id=1, source_target_pairs={{0,4},{4,0},{8,12},{12,8},{16,20},{20,16},{24,28},{28,24},{1,5},{5... | collective-permute-start | bytes 294920 | tf_op jit(solution)/shard_map/ppermute | solution.py:24
  15.5 19.6 %copy-start = (bf16[32,256,256]{2,1,0:T(8,128)(2,1)S(1)}, bf16[32,256,256]{2,1,0:T(8,128)(2,1)}, u32[]{:S(2)}) copy-start(bf16[32,256,256]{2,1,0:T(8,128)(2,1)} %refs_2_.3) | copy-start | bytes 12582916
  20.0 7.2 %collective-permute-start.7 = (bf16[24,32,128]{2,1,0:T(8,128)(2,1)S(1)}, bf16[24,32,128]{2,1,0:T(8,128)(2,1)S(1)}, u32[]{:S(2)}, u32[]{:S(2)}) collective-permute-start(bf16[24,32,128]{2,1,0:T(8,128)(2,1)S(1)} %get-tuple-element.27), channel_id=1, source_target_pairs={{0,1},{1,0},{2,3},{3,2},{4,5},{5,4},{6,7},{7,6},{8,9},{9,8},{10,11... | collective-permute-start | bytes 589832 | tf_op jit(solution)/shard_map/ppermute | solution.py:24
  21.6 7.3 %collective-permute-start.9 = (bf16[24,32,128]{2,1,0:T(8,128)(2,1)S(1)}, bf16[24,32,128]{2,1,0:T(8,128)(2,1)S(1)}, u32[]{:S(2)}, u32[]{:S(2)}) collective-permute-start(bf16[24,32,128]{2,1,0:T(8,128)(2,1)S(1)} %get-tuple-element.28), channel_id=1, source_target_pairs={{0,2},{1,3},{2,0},{3,1},{4,6},{5,7},{6,4},{7,5},{8,10},{9,11},{10,... | collective-permute-start | bytes 589832 | tf_op jit(solution)/shard_map/ppermute | solution.py:24
  27.3 6.4 %collective-permute-start.8 = (bf16[24,32,128]{2,1,0:T(8,128)(2,1)S(1)}, bf16[24,32,128]{2,1,0:T(8,128)(2,1)S(1)}, u32[]{:S(2)}, u32[]{:S(2)}) collective-permute-start(bf16[24,32,128]{2,1,0:T(8,128)(2,1)S(1)} %add_convert_fusion.8), channel_id=1, source_target_pairs={{0,2},{1,3},{2,0},{3,1},{4,6},{5,7},{6,4},{7,5},{8,10},{9,11},{10,... | collective-permute-start | bytes 589832 | tf_op jit(solution)/shard_map/ppermute | solution.py:24
  28.9 6.1 %collective-permute-start.10 = (bf16[24,32,128]{2,1,0:T(8,128)(2,1)S(1)}, bf16[24,32,128]{2,1,0:T(8,128)(2,1)S(1)}, u32[]{:S(2)}, u32[]{:S(2)}) collective-permute-start(bf16[24,32,128]{2,1,0:T(8,128)(2,1)S(1)} %add_convert_fusion.6), channel_id=1, source_target_pairs={{0,1},{1,0},{2,3},{3,2},{4,5},{5,4},{6,7},{7,6},{8,9},{9,8},{10,11... | collective-permute-start | bytes 589832 | tf_op jit(solution)/shard_map/ppermute | solution.py:24
  36.6 1.8 %collective-permute-start.11 = (bf16[4,12,32,128]{3,2,1,0:T(8,128)(2,1)S(1)}, bf16[4,12,32,128]{3,2,1,0:T(8,128)(2,1)S(1)}, u32[]{:S(2)}, u32[]{:S(2)}) collective-permute-start(bf16[4,12,32,128]{3,2,1,0:T(8,128)(2,1)S(1)} %get-tuple-element.30), channel_id=1, source_target_pairs={{0,4},{4,0},{8,12},{12,8},{16,20},{20,16},{24,28},{28,24},{1,5},{5... | collective-permute-start | bytes 1179656 | tf_op jit(solution)/shard_map/ppermute | solution.py:24
  38.5 4.9 %collective-permute-start.12 = (bf16[12,32,128]{2,1,0:T(8,128)(2,1)S(1)}, bf16[12,32,128]{2,1,0:T(8,128)(2,1)S(1)}, u32[]{:S(2)}, u32[]{:S(2)}) collective-permute-start(bf16[12,32,128]{2,1,0:T(8,128)(2,1)S(1)} %get-tuple-element.53), channel_id=1, source_target_pairs={{0,8},{4,12},{8,0},{12,4},{16,24},{20,28},{24,16},{28,20},{1,9},{5... | collective-permute-start | bytes 294920 | tf_op jit(solution)/shard_map/ppermute | solution.py:24
  39.1 8.8 %collective-permute-start.14 = (bf16[12,32,128]{2,1,0:T(8,128)(2,1)S(1)}, bf16[12,32,128]{2,1,0:T(8,128)(2,1)S(1)}, u32[]{:S(2)}, u32[]{:S(2)}) collective-permute-start(bf16[12,32,128]{2,1,0:T(8,128)(2,1)S(1)} %get-tuple-element.54), channel_id=1, source_target_pairs={{0,24},{4,28},{8,16},{12,20},{16,8},{20,12},{24,0},{28,4},{1,25},{... | collective-permute-start | bytes 294920 | tf_op jit(solution)/shard_map/ppermute | solution.py:24
  42.1 9.6 %collective-permute-start.13 = (bf16[12,32,128]{2,1,0:T(8,128)(2,1)S(1)}, bf16[12,32,128]{2,1,0:T(8,128)(2,1)S(1)}, u32[]{:S(2)}, u32[]{:S(2)}) collective-permute-start(bf16[12,32,128]{2,1,0:T(8,128)(2,1)S(1)} %get-tuple-element.55), channel_id=1, source_target_pairs={{0,16},{4,20},{8,24},{12,28},{16,0},{20,4},{24,8},{28,12},{1,17},{... | collective-permute-start | bytes 294920 | tf_op jit(solution)/shard_map/ppermute | solution.py:24
  51.8 7.6 %collective-permute-start.17 = (bf16[12,32,128]{2,1,0:T(8,128)(2,1)S(1)}, bf16[12,32,128]{2,1,0:T(8,128)(2,1)S(1)}, u32[]{:S(2)}, u32[]{:S(2)}) collective-permute-start(bf16[12,32,128]{2,1,0:T(8,128)(2,1)S(1)} %fusion.6.refs_0_.refs_2_), channel_id=1, source_target_pairs={{0,24},{4,28},{8,16},{12,20},{16,8},{20,12},{24,0},{28,4},{1,25},{... | collective-permute-start | bytes 294920 | tf_op jit(solution)/shard_map/ppermute | solution.py:24
  54.5 7.8 %collective-permute-start.16 = (bf16[12,32,128]{2,1,0:T(8,128)(2,1)S(1)}, bf16[12,32,128]{2,1,0:T(8,128)(2,1)S(1)}, u32[]{:S(2)}, u32[]{:S(2)}) collective-permute-start(bf16[12,32,128]{2,1,0:T(8,128)(2,1)S(1)} %fusion.6.refs_0_.refs_2_), channel_id=1, source_target_pairs={{0,16},{4,20},{8,24},{12,28},{16,0},{20,4},{24,8},{28,12},{1,17},{... | collective-permute-start | bytes 294920 | tf_op jit(solution)/shard_map/ppermute | solution.py:24
  54.5 7.8 %collective-permute-start.15 = (bf16[12,32,128]{2,1,0:T(8,128)(2,1)S(1)}, bf16[12,32,128]{2,1,0:T(8,128)(2,1)S(1)}, u32[]{:S(2)}, u32[]{:S(2)}) collective-permute-start(bf16[12,32,128]{2,1,0:T(8,128)(2,1)S(1)} %fusion.6.refs_0_.refs_2_), channel_id=1, source_target_pairs={{0,8},{4,12},{8,0},{12,4},{16,24},{20,28},{24,16},{28,20},{1,9},{5... | collective-permute-start | bytes 294920 | tf_op jit(solution)/shard_map/ppermute | solution.py:24
  56.3 6.6 %collective-permute-start.18 = (bf16[12,32,128]{2,1,0:T(8,128)(2,1)S(1)}, bf16[12,32,128]{2,1,0:T(8,128)(2,1)S(1)}, u32[]{:S(2)}, u32[]{:S(2)}) collective-permute-start(bf16[12,32,128]{2,1,0:T(8,128)(2,1)S(1)} %fusion.6.refs_0_.refs_2_), channel_id=1, source_target_pairs={{0,4},{4,0},{8,12},{12,8},{16,20},{20,16},{24,28},{28,24},{1,5},{5... | collective-permute-start | bytes 294920 | tf_op jit(solution)/shard_map/ppermute | solution.py:24
  59.4 3.4 %collective-permute-start.21 = (bf16[12,32,128]{2,1,0:T(8,128)(2,1)S(1)}, bf16[12,32,128]{2,1,0:T(8,128)(2,1)S(1)}, u32[]{:S(2)}, u32[]{:S(2)}) collective-permute-start(bf16[12,32,128]{2,1,0:T(8,128)(2,1)S(1)} %collective-permute-done.17.refs_3_.refs_5_), channel_id=1, source_target_pairs={{0,4},{4,0},{8,12},{12,8},{16,20},{20,16},{24,28},{28,24},{1,5},{5... | collective-permute-start | bytes 294920 | tf_op jit(solution)/shard_map/ppermute | solution.py:24
  62.3 1.3 %collective-permute-start.20 = (bf16[12,32,128]{2,1,0:T(8,128)(2,1)S(1)}, bf16[12,32,128]{2,1,0:T(8,128)(2,1)S(1)}, u32[]{:S(2)}, u32[]{:S(2)}) collective-permute-start(bf16[12,32,128]{2,1,0:T(8,128)(2,1)S(1)} %collective-permute-done.16.refs_2_.refs_4_), channel_id=1, source_target_pairs={{0,4},{4,0},{8,12},{12,8},{16,20},{20,16},{24,28},{28,24},{1,5},{5... | collective-permute-start | bytes 294920 | tf_op jit(solution)/shard_map/ppermute | solution.py:24
  62.4 1.4 %collective-permute-start.19 = (bf16[12,32,128]{2,1,0:T(8,128)(2,1)S(1)}, bf16[12,32,128]{2,1,0:T(8,128)(2,1)S(1)}, u32[]{:S(2)}, u32[]{:S(2)}) collective-permute-start(bf16[12,32,128]{2,1,0:T(8,128)(2,1)S(1)} %collective-permute-done.15.refs_1_.refs_3_), channel_id=1, source_target_pairs={{0,4},{4,0},{8,12},{12,8},{16,20},{20,16},{24,28},{28,24},{1,5},{5... | collective-permute-start | bytes 294920 | tf_op jit(solution)/shard_map/ppermute | solution.py:24
  65.8 7.2 %collective-permute-start.22 = (bf16[24,32,128]{2,1,0:T(8,128)(2,1)S(1)}, bf16[24,32,128]{2,1,0:T(8,128)(2,1)S(1)}, u32[]{:S(2)}, u32[]{:S(2)}) collective-permute-start(bf16[24,32,128]{2,1,0:T(8,128)(2,1)S(1)} %get-tuple-element.45), channel_id=1, source_target_pairs={{0,1},{1,0},{2,3},{3,2},{4,5},{5,4},{6,7},{7,6},{8,9},{9,8},{10,11... | collective-permute-start | bytes 589832 | tf_op jit(solution)/shard_map/ppermute | solution.py:24
  67.3 6.9 %collective-permute-start.24 = (bf16[24,32,128]{2,1,0:T(8,128)(2,1)S(1)}, bf16[24,32,128]{2,1,0:T(8,128)(2,1)S(1)}, u32[]{:S(2)}, u32[]{:S(2)}) collective-permute-start(bf16[24,32,128]{2,1,0:T(8,128)(2,1)S(1)} %get-tuple-element.46), channel_id=1, source_target_pairs={{0,2},{1,3},{2,0},{3,1},{4,6},{5,7},{6,4},{7,5},{8,10},{9,11},{10,... | collective-permute-start | bytes 589832 | tf_op jit(solution)/shard_map/ppermute | solution.py:24
  73.1 6.4 %collective-permute-start.23 = (bf16[24,32,128]{2,1,0:T(8,128)(2,1)S(1)}, bf16[24,32,128]{2,1,0:T(8,128)(2,1)S(1)}, u32[]{:S(2)}, u32[]{:S(2)}) collective-permute-start(bf16[24,32,128]{2,1,0:T(8,128)(2,1)S(1)} %add_convert_fusion.4), channel_id=1, source_target_pairs={{0,2},{1,3},{2,0},{3,1},{4,6},{5,7},{6,4},{7,5},{8,10},{9,11},{10,... | collective-permute-start | bytes 589832 | tf_op jit(solution)/shard_map/ppermute | solution.py:24
  74.2 6.1 %collective-permute-start.25 = (bf16[24,32,128]{2,1,0:T(8,128)(2,1)S(1)}, bf16[24,32,128]{2,1,0:T(8,128)(2,1)S(1)}, u32[]{:S(2)}, u32[]{:S(2)}) collective-permute-start(bf16[24,32,128]{2,1,0:T(8,128)(2,1)S(1)} %add_convert_fusion.2), channel_id=1, source_target_pairs={{0,1},{1,0},{2,3},{3,2},{4,5},{5,4},{6,7},{7,6},{8,9},{9,8},{10,11... | collective-permute-start | bytes 589832 | tf_op jit(solution)/shard_map/ppermute | solution.py:24
  82.4 1.8 %collective-permute-start.26 = (bf16[4,4,12288]{2,1,0:T(4,128)(2,1)S(1)}, bf16[4,4,12288]{2,1,0:T(4,128)(2,1)S(1)}, u32[]{:S(2)}, u32[]{:S(2)}) collective-permute-start(bf16[4,4,12288]{2,1,0:T(4,128)(2,1)S(1)} %slice_bitcast_fusion), channel_id=1, source_target_pairs={{0,4},{4,0},{8,12},{12,8},{16,20},{20,16},{24,28},{28,24},{1,5},{5... | collective-permute-start | bytes 1179656 | tf_op jit(solution)/shard_map/ppermute | solution.py:24
  84.5 6.3 %collective-permute-start.27 = (bf16[4,12288]{1,0:T(4,128)(2,1)S(1)}, bf16[4,12288]{1,0:T(4,128)(2,1)S(1)}, u32[]{:S(2)}, u32[]{:S(2)}) collective-permute-start(bf16[4,12288]{1,0:T(4,128)(2,1)S(1)} %get-tuple-element.50), channel_id=1, source_target_pairs={{0,8},{4,12},{8,0},{12,4},{16,24},{20,28},{24,16},{28,20},{1,9},{5... | collective-permute-start | bytes 294920 | tf_op jit(solution)/shard_map/ppermute | solution.py:24
  84.6 8.0 %collective-permute-start.29 = (bf16[4,12288]{1,0:T(4,128)(2,1)S(1)}, bf16[4,12288]{1,0:T(4,128)(2,1)S(1)}, u32[]{:S(2)}, u32[]{:S(2)}) collective-permute-start(bf16[4,12288]{1,0:T(4,128)(2,1)S(1)} %get-tuple-element.51), channel_id=1, source_target_pairs={{0,24},{4,28},{8,16},{12,20},{16,8},{20,12},{24,0},{28,4},{1,25},{... | collective-permute-start | bytes 294920 | tf_op jit(solution)/shard_map/ppermute | solution.py:24
  86.9 10.0 %collective-permute-start.28 = (bf16[4,12288]{1,0:T(4,128)(2,1)S(1)}, bf16[4,12288]{1,0:T(4,128)(2,1)S(1)}, u32[]{:S(2)}, u32[]{:S(2)}) collective-permute-start(bf16[4,12288]{1,0:T(4,128)(2,1)S(1)} %get-tuple-element.52), channel_id=1, source_target_pairs={{0,16},{4,20},{8,24},{12,28},{16,0},{20,4},{24,8},{28,12},{1,17},{... | collective-permute-start | bytes 294920 | tf_op jit(solution)/shard_map/ppermute | solution.py:24

commit v15 on v14

--- a/solution.py
+++ b/solution.py
@@ -16,7 +16,7 @@
 CHUNK = 1024
 UNROLL = 96
 VMEM_LIMIT = 12 * 1024 * 1024
-FIRST_LIMIT = 50 * 1024 * 1024
+FIRST_LIMIT = 48 * 1024 * 1024
 
 
 def swap(value, axis, offset):

time: 97.9 us -> 96.4 us (0.985)
  other arithmetic: 7.9 us -> 6.27 us
  waiting for transfers between devices: 45.3 us -> 46.5 us
  Pallas kernels: 12.5 us -> 11.5 us
    select_n x1, other arithmetic: 3.73 us -> 2.1 us  [shards(): ready = jnp.where(core >= 0, blocks[:at_hand], 0)]
    ppermute x30, waiting for transfers between devices: 45.3 us -> 46.5 us  [swap(): return lax.ppermute(value, axis, [(i, i ^ offset) for i in range(count)])]
    pallas_call x4, Pallas kernels: 9.74 us -> 8.75 us  [product(): pl.pallas_call(functools.partial(kernel, ways), out_shape=[jax.ShapeDtype...]
  transfers between devices with their start and end apart: 30 -> 30, of which waited for: 20 -> 19; matrix products, arithmetic and copies ran while one was open for 8% -> 6% of each run, Pallas kernels for 3% -> 3%
where the time goes in v15:
time: 96.4 us; the launch traced here: 96.2 us
  waiting for transfers between devices  46.5 us (48%)
  starting transfers between devices  29.9 us (31%)
  Pallas kernels  11.5 us (12%)
  other arithmetic  6.27 us (7%)
  local copies, waits for them, and re-layouts  1.15 us (1%)
    ppermute x30, waiting for transfers between devices, swap(): return lax.ppermute(value, axis, [(i, i ^ offset) for i in range(count)])  46.5 us
    ppermute x30, starting transfers between devices, swap(): return lax.ppermute(value, axis, [(i, i ^ offset) for i in range(count)])  29.9 us
    pallas_call x4, Pallas kernels, product(): pl.pallas_call(functools.partial(kernel, ways), out_shape=[jax.ShapeDtype...  8.75 us
    pallas_call x2, Pallas kernels, cut(): pl.pallas_call(functools.partial(kernel, ways), out_shape=[jax.ShapeDtype...  2.77 us
    select_n x1, other arithmetic, shards(): ready = jnp.where(core >= 0, blocks[:at_hand], 0)  2.1 us
  transfers between devices with their start and end apart: 30, of which 19 were waited for; matrix products, arithmetic and copies ran while one was open for 6% of the time, Pallas kernels for 3%

profile of v15, /device:TPU:0, one launch (start us, length us, event | category | flops | bytes accessed | tf_op | source)
XLA Modules:
  0.0 96.2 jit_solution(18053076741134816642)
XLA Ops:
  0.6 4.1 %collective-permute-start.1 = (bf16[4,12288]{1,0:T(4,128)(2,1)}, bf16[4,12288]{1,0:T(4,128)(2,1)S(1)}, u32[]{:S(2)}, u32[]{:S(2)}) collective-permute-start(bf16[4,12288]{1,0:T(4,128)(2,1)} %param.4), channel_id=1, source_target_pairs={{0,16},{4,20},{8,24},{12,28},{16,0},{20,4},{24,8},{28,12},{1,17},{... | collective-permute-start | bytes 294920 | tf_op jit(solution)/shard_map/ppermute | solution.py:24
  4.7 1.6 %collective-permute-start = (bf16[4,12288]{1,0:T(4,128)(2,1)}, bf16[4,12288]{1,0:T(4,128)(2,1)S(1)}, u32[]{:S(2)}, u32[]{:S(2)}) collective-permute-start(bf16[4,12288]{1,0:T(4,128)(2,1)} %param.4), channel_id=1, source_target_pairs={{0,8},{4,12},{8,0},{12,4},{16,24},{20,28},{24,16},{28,20},{1,9},{5... | collective-permute-start | bytes 294920 | tf_op jit(solution)/shard_map/ppermute | solution.py:24
  9.7 2.1 %slice_select_fusion.refs_8_ = bf16[24,256,256]{2,1,0:T(8,128)(2,1)S(1)} fusion(bf16[32,256,256]{2,1,0:T(8,128)(2,1)} %refs_2_.3, pred[]{:T(512)S(6)} %ge.12), kind=kLoop, calls=%fused_computation | loop fusion | flops 1572864 | bytes 6291457 | tf_op jit(solution)/shard_map/jit(_where)/select_n | solution.py:302
  13.8 1.4 %collective-permute-done.6.refs_7_ = bf16[4,12288]{1,0:T(4,128)(2,1)S(1)} collective-permute-done((bf16[4,12288]{1,0:T(4,128)(2,1)}, bf16[4,12288]{1,0:T(4,128)(2,1)S(1)}, u32[]{:S(2)}, u32[]{:S(2)}) %collective-permute-start.6) | collective-permute-done | bytes 98336 | tf_op jit(solution)/shard_map/ppermute | solution.py:24
  15.3 3.5 %shard_map.75 = (bf16[24,32,128]{2,1,0:T(8,128)(2,1)S(1)}, bf16[24,32,128]{2,1,0:T(8,128)(2,1)S(1)}) custom-call(s32[64]{0:T(128)S(1)} %reshape.18.entry_ref, f32[32]{0:T(128)S(1)} %select_reduce_fusion.scale_ref, s32[3]{0:T(128)S(1)} %pad_add_fusion.place_ref, bf16[4,12288]{1,0:T(4,128)(2,1)S(1)} %broadcast_select_fusion.refs_0_, ...), custom_call_target="tpu_custom_call" | custom-call | flops 134217728 | bytes 4194304 | tf_op jit(solution)/shard_map/pallas_call | solution.py:256
  18.8 1.6 %collective-permute-start.7 = (bf16[24,32,128]{2,1,0:T(8,128)(2,1)S(1)}, bf16[24,32,128]{2,1,0:T(8,128)(2,1)S(1)}, u32[]{:S(2)}, u32[]{:S(2)}) collective-permute-start(bf16[24,32,128]{2,1,0:T(8,128)(2,1)S(1)} %get-tuple-element.27), channel_id=1, source_target_pairs={{0,1},{1,0},{2,3},{3,2},{4,5},{5,4},{6,7},{7,6},{8,9},{9,8},{10,11... | collective-permute-start | bytes 589832 | tf_op jit(solution)/shard_map/ppermute | solution.py:24
  20.3 1.5 %collective-permute-start.9 = (bf16[24,32,128]{2,1,0:T(8,128)(2,1)S(1)}, bf16[24,32,128]{2,1,0:T(8,128)(2,1)S(1)}, u32[]{:S(2)}, u32[]{:S(2)}) collective-permute-start(bf16[24,32,128]{2,1,0:T(8,128)(2,1)S(1)} %get-tuple-element.28), channel_id=1, source_target_pairs={{0,2},{1,3},{2,0},{3,1},{4,6},{5,7},{6,4},{7,5},{8,10},{9,11},{10,... | collective-permute-start | bytes 589832 | tf_op jit(solution)/shard_map/ppermute | solution.py:24
  21.8 4.0 %collective-permute-done.7 = bf16[24,32,128]{2,1,0:T(8,128)(2,1)S(1)} collective-permute-done((bf16[24,32,128]{2,1,0:T(8,128)(2,1)S(1)}, bf16[24,32,128]{2,1,0:T(8,128)(2,1)S(1)}, u32[]{:S(2)}, u32[]{:S(2)}) %collective-permute-start.7) | collective-permute-done | bytes 196640 | tf_op jit(solution)/shard_map/ppermute | solution.py:24
  25.8 1.6 %collective-permute-start.8 = (bf16[24,32,128]{2,1,0:T(8,128)(2,1)S(1)}, bf16[24,32,128]{2,1,0:T(8,128)(2,1)S(1)}, u32[]{:S(2)}, u32[]{:S(2)}) collective-permute-start(bf16[24,32,128]{2,1,0:T(8,128)(2,1)S(1)} %add_convert_fusion.8), channel_id=1, source_target_pairs={{0,2},{1,3},{2,0},{3,1},{4,6},{5,7},{6,4},{7,5},{8,10},{9,11},{10,... | collective-permute-start | bytes 589832 | tf_op jit(solution)/shard_map/ppermute | solution.py:24
  27.5 1.6 %collective-permute-start.10 = (bf16[24,32,128]{2,1,0:T(8,128)(2,1)S(1)}, bf16[24,32,128]{2,1,0:T(8,128)(2,1)S(1)}, u32[]{:S(2)}, u32[]{:S(2)}) collective-permute-start(bf16[24,32,128]{2,1,0:T(8,128)(2,1)S(1)} %add_convert_fusion.6), channel_id=1, source_target_pairs={{0,1},{1,0},{2,3},{3,2},{4,5},{5,4},{6,7},{7,6},{8,9},{9,8},{10,11... | collective-permute-start | bytes 589832 | tf_op jit(solution)/shard_map/ppermute | solution.py:24
  29.0 3.0 %collective-permute-done.8 = bf16[24,32,128]{2,1,0:T(8,128)(2,1)S(1)} collective-permute-done((bf16[24,32,128]{2,1,0:T(8,128)(2,1)S(1)}, bf16[24,32,128]{2,1,0:T(8,128)(2,1)S(1)}, u32[]{:S(2)}, u32[]{:S(2)}) %collective-permute-start.8) | collective-permute-done | bytes 196640 | tf_op jit(solution)/shard_map/ppermute | solution.py:24
  32.1 1.3 %collective-permute-done.10 = bf16[24,32,128]{2,1,0:T(8,128)(2,1)S(1)} collective-permute-done((bf16[24,32,128]{2,1,0:T(8,128)(2,1)S(1)}, bf16[24,32,128]{2,1,0:T(8,128)(2,1)S(1)}, u32[]{:S(2)}, u32[]{:S(2)}) %collective-permute-start.10) | collective-permute-done | bytes 196640 | tf_op jit(solution)/shard_map/ppermute | solution.py:24
  33.5 1.5 %shard_map.76 = (bf16[4,12,32,128]{3,2,1,0:T(8,128)(2,1)S(1)}, bf16[4,12,32,128]{3,2,1,0:T(8,128)(2,1)S(1)}) custom-call(s32[64]{0:T(128)S(1)} %reshape.18.entry_ref, f32[32]{0:T(128)S(1)} %select_reduce_fusion.scale_ref, s32[3]{0:T(128)S(1)} %pad_add_fusion.place_ref, bf16[24,32,128]{2,1,0:T(8,128)(2,1)S(1)} %add_convert_fusion.7.refs_0_, ...), custom_call_target="tpu_custom_call" | custom-call | flops 134217728 | bytes 4194304 | tf_op jit(solution)/shard_map/pallas_call | solution.py:256
  35.0 1.7 %collective-permute-done.11 = bf16[4,12,32,128]{3,2,1,0:T(8,128)(2,1)S(1)} collective-permute-done((bf16[4,12,32,128]{3,2,1,0:T(8,128)(2,1)S(1)}, bf16[4,12,32,128]{3,2,1,0:T(8,128)(2,1)S(1)}, u32[]{:S(2)}, u32[]{:S(2)}) %collective-permute-start.11) | collective-permute-done | bytes 393248 | tf_op jit(solution)/shard_map/ppermute | solution.py:24
  38.1 3.4 %collective-permute-start.14 = (bf16[12,32,128]{2,1,0:T(8,128)(2,1)S(1)}, bf16[12,32,128]{2,1,0:T(8,128)(2,1)S(1)}, u32[]{:S(2)}, u32[]{:S(2)}) collective-permute-start(bf16[12,32,128]{2,1,0:T(8,128)(2,1)S(1)} %get-tuple-element.54), channel_id=1, source_target_pairs={{0,24},{4,28},{8,16},{12,20},{16,8},{20,12},{24,0},{28,4},{1,25},{... | collective-permute-start | bytes 294920 | tf_op jit(solution)/shard_map/ppermute | solution.py:24
  41.8 5.5 %collective-permute-done.14 = bf16[12,32,128]{2,1,0:T(8,128)(2,1)S(1)} collective-permute-done((bf16[12,32,128]{2,1,0:T(8,128)(2,1)S(1)}, bf16[12,32,128]{2,1,0:T(8,128)(2,1)S(1)}, u32[]{:S(2)}, u32[]{:S(2)}) %collective-permute-start.14) | collective-permute-done | bytes 98336 | tf_op jit(solution)/shard_map/ppermute | solution.py:24
  47.3 3.0 %collective-permute-done.13 = bf16[12,32,128]{2,1,0:T(8,128)(2,1)S(1)} collective-permute-done((bf16[12,32,128]{2,1,0:T(8,128)(2,1)S(1)}, bf16[12,32,128]{2,1,0:T(8,128)(2,1)S(1)}, u32[]{:S(2)}, u32[]{:S(2)}) %collective-permute-start.13) | collective-permute-done | bytes 98336 | tf_op jit(solution)/shard_map/ppermute | solution.py:24
  50.4 1.9 %collective-permute-start.17 = (bf16[12,32,128]{2,1,0:T(8,128)(2,1)S(1)}, bf16[12,32,128]{2,1,0:T(8,128)(2,1)S(1)}, u32[]{:S(2)}, u32[]{:S(2)}) collective-permute-start(bf16[12,32,128]{2,1,0:T(8,128)(2,1)S(1)} %fusion.6.refs_0_.refs_2_), channel_id=1, source_target_pairs={{0,24},{4,28},{8,16},{12,20},{16,8},{20,12},{24,0},{28,4},{1,25},{... | collective-permute-start | bytes 294920 | tf_op jit(solution)/shard_map/ppermute | solution.py:24
  52.3 2.6 %collective-permute-start.15 = (bf16[12,32,128]{2,1,0:T(8,128)(2,1)S(1)}, bf16[12,32,128]{2,1,0:T(8,128)(2,1)S(1)}, u32[]{:S(2)}, u32[]{:S(2)}) collective-permute-start(bf16[12,32,128]{2,1,0:T(8,128)(2,1)S(1)} %fusion.6.refs_0_.refs_2_), channel_id=1, source_target_pairs={{0,8},{4,12},{8,0},{12,4},{16,24},{20,28},{24,16},{28,20},{1,9},{5... | collective-permute-start | bytes 294920 | tf_op jit(solution)/shard_map/ppermute | solution.py:24
  54.9 3.2 %collective-permute-done.17.refs_3_.refs_5_ = bf16[12,32,128]{2,1,0:T(8,128)(2,1)S(1)} collective-permute-done((bf16[12,32,128]{2,1,0:T(8,128)(2,1)S(1)}, bf16[12,32,128]{2,1,0:T(8,128)(2,1)S(1)}, u32[]{:S(2)}, u32[]{:S(2)}) %collective-permute-start.17) | collective-permute-done | bytes 98336 | tf_op jit(solution)/shard_map/ppermute | solution.py:24
  58.1 2.8 %collective-permute-done.16.refs_2_.refs_4_ = bf16[12,32,128]{2,1,0:T(8,128)(2,1)S(1)} collective-permute-done((bf16[12,32,128]{2,1,0:T(8,128)(2,1)S(1)}, bf16[12,32,128]{2,1,0:T(8,128)(2,1)S(1)}, u32[]{:S(2)}, u32[]{:S(2)}) %collective-permute-start.16) | collective-permute-done | bytes 98336 | tf_op jit(solution)/shard_map/ppermute | solution.py:24
  62.3 2.0 %shard_map.77 = (bf16[24,32,128]{2,1,0:T(8,128)(2,1)S(1)}, bf16[24,32,128]{2,1,0:T(8,128)(2,1)S(1)}) custom-call(s32[64]{0:T(128)S(1)} %reshape.18.entry_ref, f32[32]{0:T(128)S(1)} %select_reduce_fusion.scale_ref, s32[3]{0:T(128)S(1)} %pad_add_fusion.place_ref, bf16[12,32,128]{2,1,0:T(8,128)(2,1)S(1)} %fusion.6.refs_0_.refs_2_, ...), custom_call_target="tpu_custom_call" | custom-call | flops 134217728 | bytes 4194304 | tf_op jit(solution)/shard_map/pallas_call | solution.py:256
  64.3 1.6 %collective-permute-start.22 = (bf16[24,32,128]{2,1,0:T(8,128)(2,1)S(1)}, bf16[24,32,128]{2,1,0:T(8,128)(2,1)S(1)}, u32[]{:S(2)}, u32[]{:S(2)}) collective-permute-start(bf16[24,32,128]{2,1,0:T(8,128)(2,1)S(1)} %get-tuple-element.45), channel_id=1, source_target_pairs={{0,1},{1,0},{2,3},{3,2},{4,5},{5,4},{6,7},{7,6},{8,9},{9,8},{10,11... | collective-permute-start | bytes 589832 | tf_op jit(solution)/shard_map/ppermute | solution.py:24
  66.4 5.2 %collective-permute-done.22 = bf16[24,32,128]{2,1,0:T(8,128)(2,1)S(1)} collective-permute-done((bf16[24,32,128]{2,1,0:T(8,128)(2,1)S(1)}, bf16[24,32,128]{2,1,0:T(8,128)(2,1)S(1)}, u32[]{:S(2)}, u32[]{:S(2)}) %collective-permute-start.22) | collective-permute-done | bytes 196640 | tf_op jit(solution)/shard_map/ppermute | solution.py:24
  73.8 4.2 %collective-permute-done.23 = bf16[24,32,128]{2,1,0:T(8,128)(2,1)S(1)} collective-permute-done((bf16[24,32,128]{2,1,0:T(8,128)(2,1)S(1)}, bf16[24,32,128]{2,1,0:T(8,128)(2,1)S(1)}, u32[]{:S(2)}, u32[]{:S(2)}) %collective-permute-start.23) | collective-permute-done | bytes 196640 | tf_op jit(solution)/shard_map/ppermute | solution.py:24
  79.0 1.8 %shard_map.79 = bf16[2,4,4,12288]{3,2,1,0:T(4,128)(2,1)S(1)} custom-call(s32[64]{0:T(128)S(1)} %reshape.18.entry_ref, f32[32]{0:T(128)S(1)} %select_reduce_fusion.scale_ref, s32[3]{0:T(128)S(1)} %pad_add_fusion.place_ref, bf16[24,32,128]{2,1,0:T(8,128)(2,1)S(1)} %add_convert_fusion.3.refs_0_, bf16[24,32,128]{2,1,0:T(8,128)(2,1)S(1)} %add_convert_fusion.1.refs_1_, ...), custom_call_target="tpu_custom_call" | custom-call | flops 134217728 | bytes 4194304 | tf_op jit(solution)/shard_map/pallas_call | solution.py:256
  81.0 1.7 %collective-permute-done.26 = bf16[4,4,12288]{2,1,0:T(4,128)(2,1)S(1)} collective-permute-done((bf16[4,4,12288]{2,1,0:T(4,128)(2,1)S(1)}, bf16[4,4,12288]{2,1,0:T(4,128)(2,1)S(1)}, u32[]{:S(2)}, u32[]{:S(2)}) %collective-permute-start.26) | collective-permute-done | bytes 393248 | tf_op jit(solution)/shard_map/ppermute | solution.py:24
  83.1 1.5 %collective-permute-start.29 = (bf16[4,12288]{1,0:T(4,128)(2,1)S(1)}, bf16[4,12288]{1,0:T(4,128)(2,1)S(1)}, u32[]{:S(2)}, u32[]{:S(2)}) collective-permute-start(bf16[4,12288]{1,0:T(4,128)(2,1)S(1)} %get-tuple-element.51), channel_id=1, source_target_pairs={{0,24},{4,28},{8,16},{12,20},{16,8},{20,12},{24,0},{28,4},{1,25},{... | collective-permute-start | bytes 294920 | tf_op jit(solution)/shard_map/ppermute | solution.py:24
  84.6 2.0 %collective-permute-start.28 = (bf16[4,12288]{1,0:T(4,128)(2,1)S(1)}, bf16[4,12288]{1,0:T(4,128)(2,1)S(1)}, u32[]{:S(2)}, u32[]{:S(2)}) collective-permute-start(bf16[4,12288]{1,0:T(4,128)(2,1)S(1)} %get-tuple-element.52), channel_id=1, source_target_pairs={{0,16},{4,20},{8,24},{12,28},{16,0},{20,4},{24,8},{28,12},{1,17},{... | collective-permute-start | bytes 294920 | tf_op jit(solution)/shard_map/ppermute | solution.py:24
  86.6 1.5 %shard_map.78 = (bf16[8,6144]{1,0:T(8,128)(2,1)}, bf16[4,12288]{1,0:T(4,128)(2,1)}) custom-call(s32[3]{0:T(128)S(1)} %pad_add_fusion.place_ref, bf16[24,32,128]{2,1,0:T(8,128)(2,1)S(1)} %add_convert_fusion.7.refs_0_, bf16[24,32,128]{2,1,0:T(8,128)(2,1)S(1)} %add_convert_fusion.5.refs_1_, bf16[12,32,128]{2,1,0:T(8,128)(2,1)S(1)} %fusion.6.refs_0_.refs_2_, ...), custom_call_target="tpu_custom_call" | custom-call | bytes 393216 | tf_op jit(solution)/shard_map/pallas_call | solution.py:245
  89.4 1.3 %collective-permute-done.29 = bf16[4,12288]{1,0:T(4,128)(2,1)S(1)} collective-permute-done((bf16[4,12288]{1,0:T(4,128)(2,1)S(1)}, bf16[4,12288]{1,0:T(4,128)(2,1)S(1)}, u32[]{:S(2)}, u32[]{:S(2)}) %collective-permute-start.29) | collective-permute-done | bytes 98336 | tf_op jit(solution)/shard_map/ppermute | solution.py:24
  90.7 4.7 %collective-permute-done.28 = bf16[4,12288]{1,0:T(4,128)(2,1)S(1)} collective-permute-done((bf16[4,12288]{1,0:T(4,128)(2,1)S(1)}, bf16[4,12288]{1,0:T(4,128)(2,1)S(1)}, u32[]{:S(2)}, u32[]{:S(2)}) %collective-permute-start.28) | collective-permute-done | bytes 98336 | tf_op jit(solution)/shard_map/ppermute | solution.py:24
  (63 shorter events, 15.1 us)
Async XLA Ops:
  0.6 11.3 %collective-permute-start.1 = (bf16[4,12288]{1,0:T(4,128)(2,1)}, bf16[4,12288]{1,0:T(4,128)(2,1)S(1)}, u32[]{:S(2)}, u32[]{:S(2)}) collective-permute-start(bf16[4,12288]{1,0:T(4,128)(2,1)} %param.4), channel_id=1, source_target_pairs={{0,16},{4,20},{8,24},{12,28},{16,0},{20,4},{24,8},{28,12},{1,17},{... | collective-permute-start | bytes 294920 | tf_op jit(solution)/shard_map/ppermute | solution.py:24
  4.7 7.7 %collective-permute-start = (bf16[4,12288]{1,0:T(4,128)(2,1)}, bf16[4,12288]{1,0:T(4,128)(2,1)S(1)}, u32[]{:S(2)}, u32[]{:S(2)}) collective-permute-start(bf16[4,12288]{1,0:T(4,128)(2,1)} %param.4), channel_id=1, source_target_pairs={{0,8},{4,12},{8,0},{12,4},{16,24},{20,28},{24,16},{28,20},{1,9},{5... | collective-permute-start | bytes 294920 | tf_op jit(solution)/shard_map/ppermute | solution.py:24
  6.3 7.5 %collective-permute-start.3 = (bf16[4,12288]{1,0:T(4,128)(2,1)}, bf16[4,12288]{1,0:T(4,128)(2,1)S(1)}, u32[]{:S(2)}, u32[]{:S(2)}) collective-permute-start(bf16[4,12288]{1,0:T(4,128)(2,1)} %param.4), channel_id=1, source_target_pairs={{0,4},{4,0},{8,12},{12,8},{16,20},{20,16},{24,28},{28,24},{1,5},{5... | collective-permute-start | bytes 294920 | tf_op jit(solution)/shard_map/ppermute | solution.py:24
  6.3 7.4 %collective-permute-start.2 = (bf16[4,12288]{1,0:T(4,128)(2,1)}, bf16[4,12288]{1,0:T(4,128)(2,1)}, u32[]{:S(2)}, u32[]{:S(2)}) collective-permute-start(bf16[4,12288]{1,0:T(4,128)(2,1)} %param.4), channel_id=1, source_target_pairs={{0,24},{4,28},{8,16},{12,20},{16,8},{20,12},{24,0},{28,4},{1,25},{... | collective-permute-start | bytes 294920 | tf_op jit(solution)/shard_map/ppermute | solution.py:24
  9.7 2.1 %copy-start.1 = (f32[8]{0:T(128)S(1)}, f32[8]{0:T(128)}, u32[]{:S(2)}) copy-start(f32[8]{0:T(128)} %param.7) | copy-start | bytes 100
  11.9 1.9 %collective-permute-start.5 = (bf16[4,12288]{1,0:T(4,128)(2,1)S(1)}, bf16[4,12288]{1,0:T(4,128)(2,1)S(1)}, u32[]{:S(2)}, u32[]{:S(2)}) collective-permute-start(bf16[4,12288]{1,0:T(4,128)(2,1)S(1)} %collective-permute-done.1.refs_2_), channel_id=1, source_target_pairs={{0,4},{4,0},{8,12},{12,8},{16,20},{20,16},{24,28},{28,24},{1,5},{5... | collective-permute-start | bytes 294920 | tf_op jit(solution)/shard_map/ppermute | solution.py:24
  12.5 1.4 %collective-permute-start.4 = (bf16[4,12288]{1,0:T(4,128)(2,1)S(1)}, bf16[4,12288]{1,0:T(4,128)(2,1)S(1)}, u32[]{:S(2)}, u32[]{:S(2)}) collective-permute-start(bf16[4,12288]{1,0:T(4,128)(2,1)S(1)} %collective-permute-done.refs_1_), channel_id=1, source_target_pairs={{0,4},{4,0},{8,12},{12,8},{16,20},{20,16},{24,28},{28,24},{1,5},{5... | collective-permute-start | bytes 294920 | tf_op jit(solution)/shard_map/ppermute | solution.py:24
  13.7 1.5 %collective-permute-start.6 = (bf16[4,12288]{1,0:T(4,128)(2,1)}, bf16[4,12288]{1,0:T(4,128)(2,1)S(1)}, u32[]{:S(2)}, u32[]{:S(2)}) collective-permute-start(bf16[4,12288]{1,0:T(4,128)(2,1)} %collective-permute-done.2.refs_3_), channel_id=1, source_target_pairs={{0,4},{4,0},{8,12},{12,8},{16,20},{20,16},{24,28},{28,24},{1,5},{5... | collective-permute-start | bytes 294920 | tf_op jit(solution)/shard_map/ppermute | solution.py:24
  15.3 18.2 %copy-start = (bf16[32,256,256]{2,1,0:T(8,128)(2,1)S(1)}, bf16[32,256,256]{2,1,0:T(8,128)(2,1)}, u32[]{:S(2)}) copy-start(bf16[32,256,256]{2,1,0:T(8,128)(2,1)} %refs_2_.3) | copy-start | bytes 12582916
  18.8 7.0 %collective-permute-start.7 = (bf16[24,32,128]{2,1,0:T(8,128)(2,1)S(1)}, bf16[24,32,128]{2,1,0:T(8,128)(2,1)S(1)}, u32[]{:S(2)}, u32[]{:S(2)}) collective-permute-start(bf16[24,32,128]{2,1,0:T(8,128)(2,1)S(1)} %get-tuple-element.27), channel_id=1, source_target_pairs={{0,1},{1,0},{2,3},{3,2},{4,5},{5,4},{6,7},{7,6},{8,9},{9,8},{10,11... | collective-permute-start | bytes 589832 | tf_op jit(solution)/shard_map/ppermute | solution.py:24
  20.3 7.1 %collective-permute-start.9 = (bf16[24,32,128]{2,1,0:T(8,128)(2,1)S(1)}, bf16[24,32,128]{2,1,0:T(8,128)(2,1)S(1)}, u32[]{:S(2)}, u32[]{:S(2)}) collective-permute-start(bf16[24,32,128]{2,1,0:T(8,128)(2,1)S(1)} %get-tuple-element.28), channel_id=1, source_target_pairs={{0,2},{1,3},{2,0},{3,1},{4,6},{5,7},{6,4},{7,5},{8,10},{9,11},{10,... | collective-permute-start | bytes 589832 | tf_op jit(solution)/shard_map/ppermute | solution.py:24
  25.8 6.2 %collective-permute-start.8 = (bf16[24,32,128]{2,1,0:T(8,128)(2,1)S(1)}, bf16[24,32,128]{2,1,0:T(8,128)(2,1)S(1)}, u32[]{:S(2)}, u32[]{:S(2)}) collective-permute-start(bf16[24,32,128]{2,1,0:T(8,128)(2,1)S(1)} %add_convert_fusion.8), channel_id=1, source_target_pairs={{0,2},{1,3},{2,0},{3,1},{4,6},{5,7},{6,4},{7,5},{8,10},{9,11},{10,... | collective-permute-start | bytes 589832 | tf_op jit(solution)/shard_map/ppermute | solution.py:24
  27.5 5.9 %collective-permute-start.10 = (bf16[24,32,128]{2,1,0:T(8,128)(2,1)S(1)}, bf16[24,32,128]{2,1,0:T(8,128)(2,1)S(1)}, u32[]{:S(2)}, u32[]{:S(2)}) collective-permute-start(bf16[24,32,128]{2,1,0:T(8,128)(2,1)S(1)} %add_convert_fusion.6), channel_id=1, source_target_pairs={{0,1},{1,0},{2,3},{3,2},{4,5},{5,4},{6,7},{7,6},{8,9},{9,8},{10,11... | collective-permute-start | bytes 589832 | tf_op jit(solution)/shard_map/ppermute | solution.py:24
  34.9 1.8 %collective-permute-start.11 = (bf16[4,12,32,128]{3,2,1,0:T(8,128)(2,1)S(1)}, bf16[4,12,32,128]{3,2,1,0:T(8,128)(2,1)S(1)}, u32[]{:S(2)}, u32[]{:S(2)}) collective-permute-start(bf16[4,12,32,128]{3,2,1,0:T(8,128)(2,1)S(1)} %get-tuple-element.30), channel_id=1, source_target_pairs={{0,4},{4,0},{8,12},{12,8},{16,20},{20,16},{24,28},{28,24},{1,5},{5... | collective-permute-start | bytes 1179656 | tf_op jit(solution)/shard_map/ppermute | solution.py:24
  36.9 4.9 %collective-permute-start.12 = (bf16[12,32,128]{2,1,0:T(8,128)(2,1)S(1)}, bf16[12,32,128]{2,1,0:T(8,128)(2,1)S(1)}, u32[]{:S(2)}, u32[]{:S(2)}) collective-permute-start(bf16[12,32,128]{2,1,0:T(8,128)(2,1)S(1)} %get-tuple-element.53), channel_id=1, source_target_pairs={{0,8},{4,12},{8,0},{12,4},{16,24},{20,28},{24,16},{28,20},{1,9},{5... | collective-permute-start | bytes 294920 | tf_op jit(solution)/shard_map/ppermute | solution.py:24
  38.1 9.2 %collective-permute-start.14 = (bf16[12,32,128]{2,1,0:T(8,128)(2,1)S(1)}, bf16[12,32,128]{2,1,0:T(8,128)(2,1)S(1)}, u32[]{:S(2)}, u32[]{:S(2)}) collective-permute-start(bf16[12,32,128]{2,1,0:T(8,128)(2,1)S(1)} %get-tuple-element.54), channel_id=1, source_target_pairs={{0,24},{4,28},{8,16},{12,20},{16,8},{20,12},{24,0},{28,4},{1,25},{... | collective-permute-start | bytes 294920 | tf_op jit(solution)/shard_map/ppermute | solution.py:24
  41.5 8.9 %collective-permute-start.13 = (bf16[12,32,128]{2,1,0:T(8,128)(2,1)S(1)}, bf16[12,32,128]{2,1,0:T(8,128)(2,1)S(1)}, u32[]{:S(2)}, u32[]{:S(2)}) collective-permute-start(bf16[12,32,128]{2,1,0:T(8,128)(2,1)S(1)} %get-tuple-element.55), channel_id=1, source_target_pairs={{0,16},{4,20},{8,24},{12,28},{16,0},{20,4},{24,8},{28,12},{1,17},{... | collective-permute-start | bytes 294920 | tf_op jit(solution)/shard_map/ppermute | solution.py:24
  50.4 7.7 %collective-permute-start.17 = (bf16[12,32,128]{2,1,0:T(8,128)(2,1)S(1)}, bf16[12,32,128]{2,1,0:T(8,128)(2,1)S(1)}, u32[]{:S(2)}, u32[]{:S(2)}) collective-permute-start(bf16[12,32,128]{2,1,0:T(8,128)(2,1)S(1)} %fusion.6.refs_0_.refs_2_), channel_id=1, source_target_pairs={{0,24},{4,28},{8,16},{12,20},{16,8},{20,12},{24,0},{28,4},{1,25},{... | collective-permute-start | bytes 294920 | tf_op jit(solution)/shard_map/ppermute | solution.py:24
  52.3 8.6 %collective-permute-start.16 = (bf16[12,32,128]{2,1,0:T(8,128)(2,1)S(1)}, bf16[12,32,128]{2,1,0:T(8,128)(2,1)S(1)}, u32[]{:S(2)}, u32[]{:S(2)}) collective-permute-start(bf16[12,32,128]{2,1,0:T(8,128)(2,1)S(1)} %fusion.6.refs_0_.refs_2_), channel_id=1, source_target_pairs={{0,16},{4,20},{8,24},{12,28},{16,0},{20,4},{24,8},{28,12},{1,17},{... | collective-permute-start | bytes 294920 | tf_op jit(solution)/shard_map/ppermute | solution.py:24
  52.3 8.6 %collective-permute-start.15 = (bf16[12,32,128]{2,1,0:T(8,128)(2,1)S(1)}, bf16[12,32,128]{2,1,0:T(8,128)(2,1)S(1)}, u32[]{:S(2)}, u32[]{:S(2)}) collective-permute-start(bf16[12,32,128]{2,1,0:T(8,128)(2,1)S(1)} %fusion.6.refs_0_.refs_2_), channel_id=1, source_target_pairs={{0,8},{4,12},{8,0},{12,4},{16,24},{20,28},{24,16},{28,20},{1,9},{5... | collective-permute-start | bytes 294920 | tf_op jit(solution)/shard_map/ppermute | solution.py:24
  54.9 6.5 %collective-permute-start.18 = (bf16[12,32,128]{2,1,0:T(8,128)(2,1)S(1)}, bf16[12,32,128]{2,1,0:T(8,128)(2,1)S(1)}, u32[]{:S(2)}, u32[]{:S(2)}) collective-permute-start(bf16[12,32,128]{2,1,0:T(8,128)(2,1)S(1)} %fusion.6.refs_0_.refs_2_), channel_id=1, source_target_pairs={{0,4},{4,0},{8,12},{12,8},{16,20},{20,16},{24,28},{28,24},{1,5},{5... | collective-permute-start | bytes 294920 | tf_op jit(solution)/shard_map/ppermute | solution.py:24
  58.1 3.3 %collective-permute-start.21 = (bf16[12,32,128]{2,1,0:T(8,128)(2,1)S(1)}, bf16[12,32,128]{2,1,0:T(8,128)(2,1)S(1)}, u32[]{:S(2)}, u32[]{:S(2)}) collective-permute-start(bf16[12,32,128]{2,1,0:T(8,128)(2,1)S(1)} %collective-permute-done.17.refs_3_.refs_5_), channel_id=1, source_target_pairs={{0,4},{4,0},{8,12},{12,8},{16,20},{20,16},{24,28},{28,24},{1,5},{5... | collective-permute-start | bytes 294920 | tf_op jit(solution)/shard_map/ppermute | solution.py:24
  60.9 1.3 %collective-permute-start.20 = (bf16[12,32,128]{2,1,0:T(8,128)(2,1)S(1)}, bf16[12,32,128]{2,1,0:T(8,128)(2,1)S(1)}, u32[]{:S(2)}, u32[]{:S(2)}) collective-permute-start(bf16[12,32,128]{2,1,0:T(8,128)(2,1)S(1)} %collective-permute-done.16.refs_2_.refs_4_), channel_id=1, source_target_pairs={{0,4},{4,0},{8,12},{12,8},{16,20},{20,16},{24,28},{28,24},{1,5},{5... | collective-permute-start | bytes 294920 | tf_op jit(solution)/shard_map/ppermute | solution.py:24
  60.9 1.4 %collective-permute-start.19 = (bf16[12,32,128]{2,1,0:T(8,128)(2,1)S(1)}, bf16[12,32,128]{2,1,0:T(8,128)(2,1)S(1)}, u32[]{:S(2)}, u32[]{:S(2)}) collective-permute-start(bf16[12,32,128]{2,1,0:T(8,128)(2,1)S(1)} %collective-permute-done.15.refs_1_.refs_3_), channel_id=1, source_target_pairs={{0,4},{4,0},{8,12},{12,8},{16,20},{20,16},{24,28},{28,24},{1,5},{5... | collective-permute-start | bytes 294920 | tf_op jit(solution)/shard_map/ppermute | solution.py:24
  64.3 7.2 %collective-permute-start.22 = (bf16[24,32,128]{2,1,0:T(8,128)(2,1)S(1)}, bf16[24,32,128]{2,1,0:T(8,128)(2,1)S(1)}, u32[]{:S(2)}, u32[]{:S(2)}) collective-permute-start(bf16[24,32,128]{2,1,0:T(8,128)(2,1)S(1)} %get-tuple-element.45), channel_id=1, source_target_pairs={{0,1},{1,0},{2,3},{3,2},{4,5},{5,4},{6,7},{7,6},{8,9},{9,8},{10,11... | collective-permute-start | bytes 589832 | tf_op jit(solution)/shard_map/ppermute | solution.py:24
  65.9 6.9 %collective-permute-start.24 = (bf16[24,32,128]{2,1,0:T(8,128)(2,1)S(1)}, bf16[24,32,128]{2,1,0:T(8,128)(2,1)S(1)}, u32[]{:S(2)}, u32[]{:S(2)}) collective-permute-start(bf16[24,32,128]{2,1,0:T(8,128)(2,1)S(1)} %get-tuple-element.46), channel_id=1, source_target_pairs={{0,2},{1,3},{2,0},{3,1},{4,6},{5,7},{6,4},{7,5},{8,10},{9,11},{10,... | collective-permute-start | bytes 589832 | tf_op jit(solution)/shard_map/ppermute | solution.py:24
  71.6 6.4 %collective-permute-start.23 = (bf16[24,32,128]{2,1,0:T(8,128)(2,1)S(1)}, bf16[24,32,128]{2,1,0:T(8,128)(2,1)S(1)}, u32[]{:S(2)}, u32[]{:S(2)}) collective-permute-start(bf16[24,32,128]{2,1,0:T(8,128)(2,1)S(1)} %add_convert_fusion.4), channel_id=1, source_target_pairs={{0,2},{1,3},{2,0},{3,1},{4,6},{5,7},{6,4},{7,5},{8,10},{9,11},{10,... | collective-permute-start | bytes 589832 | tf_op jit(solution)/shard_map/ppermute | solution.py:24
  72.8 6.1 %collective-permute-start.25 = (bf16[24,32,128]{2,1,0:T(8,128)(2,1)S(1)}, bf16[24,32,128]{2,1,0:T(8,128)(2,1)S(1)}, u32[]{:S(2)}, u32[]{:S(2)}) collective-permute-start(bf16[24,32,128]{2,1,0:T(8,128)(2,1)S(1)} %add_convert_fusion.2), channel_id=1, source_target_pairs={{0,1},{1,0},{2,3},{3,2},{4,5},{5,4},{6,7},{7,6},{8,9},{9,8},{10,11... | collective-permute-start | bytes 589832 | tf_op jit(solution)/shard_map/ppermute | solution.py:24
  80.9 1.8 %collective-permute-start.26 = (bf16[4,4,12288]{2,1,0:T(4,128)(2,1)S(1)}, bf16[4,4,12288]{2,1,0:T(4,128)(2,1)S(1)}, u32[]{:S(2)}, u32[]{:S(2)}) collective-permute-start(bf16[4,4,12288]{2,1,0:T(4,128)(2,1)S(1)} %slice_bitcast_fusion), channel_id=1, source_target_pairs={{0,4},{4,0},{8,12},{12,8},{16,20},{20,16},{24,28},{28,24},{1,5},{5... | collective-permute-start | bytes 1179656 | tf_op jit(solution)/shard_map/ppermute | solution.py:24
  83.0 6.3 %collective-permute-start.27 = (bf16[4,12288]{1,0:T(4,128)(2,1)S(1)}, bf16[4,12288]{1,0:T(4,128)(2,1)S(1)}, u32[]{:S(2)}, u32[]{:S(2)}) collective-permute-start(bf16[4,12288]{1,0:T(4,128)(2,1)S(1)} %get-tuple-element.50), channel_id=1, source_target_pairs={{0,8},{4,12},{8,0},{12,4},{16,24},{20,28},{24,16},{28,20},{1,9},{5... | collective-permute-start | bytes 294920 | tf_op jit(solution)/shard_map/ppermute | solution.py:24
  83.1 7.6 %collective-permute-start.29 = (bf16[4,12288]{1,0:T(4,128)(2,1)S(1)}, bf16[4,12288]{1,0:T(4,128)(2,1)S(1)}, u32[]{:S(2)}, u32[]{:S(2)}) collective-permute-start(bf16[4,12288]{1,0:T(4,128)(2,1)S(1)} %get-tuple-element.51), channel_id=1, source_target_pairs={{0,24},{4,28},{8,16},{12,20},{16,8},{20,12},{24,0},{28,4},{1,25},{... | collective-permute-start | bytes 294920 | tf_op jit(solution)/shard_map/ppermute | solution.py:24
  84.6 10.8 %collective-permute-start.28 = (bf16[4,12288]{1,0:T(4,128)(2,1)S(1)}, bf16[4,12288]{1,0:T(4,128)(2,1)S(1)}, u32[]{:S(2)}, u32[]{:S(2)}) collective-permute-start(bf16[4,12288]{1,0:T(4,128)(2,1)S(1)} %get-tuple-element.52), channel_id=1, source_target_pairs={{0,16},{4,20},{8,24},{12,28},{16,0},{20,4},{24,8},{28,12},{1,17},{... | collective-permute-start | bytes 294920 | tf_op jit(solution)/shard_map/ppermute | solution.py:24

commit v16 on v12

--- a/solution.py
+++ b/solution.py
@@ -14,7 +14,7 @@
 COPIES = 4
 ROW_PARTS = 2
 CHUNK = 1024
-UNROLL = 48
+UNROLL = 96
 VMEM_LIMIT = 12 * 1024 * 1024
 FIRST_LIMIT = 50 * 1024 * 1024
 

time: 96 us -> 95.7 us (level)
  no operation moved by 1% of the time
where the time goes in v16:
time: 95.7 us; the launch traced here: 95.4 us
  waiting for transfers between devices  46.5 us (49%)
  starting transfers between devices  29.9 us (31%)
  Pallas kernels  11.1 us (12%)
  other arithmetic  5.9 us (6%)
  local copies, waits for them, and re-layouts  1.15 us (1%)
    ppermute x30, waiting for transfers between devices, swap(): return lax.ppermute(value, axis, [(i, i ^ offset) for i in range(count)])  46.5 us
    ppermute x30, starting transfers between devices, swap(): return lax.ppermute(value, axis, [(i, i ^ offset) for i in range(count)])  29.9 us
    pallas_call x4, Pallas kernels, product(): pl.pallas_call(functools.partial(kernel, ways), out_shape=[jax.ShapeDtype...  8.3 us
    pallas_call x2, Pallas kernels, cut(): pl.pallas_call(functools.partial(kernel, ways), out_shape=[jax.ShapeDtype...  2.77 us
  transfers between devices with their start and end apart: 30, of which 19 were waited for; matrix products, arithmetic and copies ran while one was open for 6% of the time, Pallas kernels for 3%

profile of v16, /device:TPU:0, one launch (start us, length us, event | category | flops | bytes accessed | tf_op | source)
XLA Modules:
  0.0 95.4 jit_solution(13412692933360434781)
XLA Ops:
  0.6 4.1 %collective-permute-start.1 = (bf16[4,12288]{1,0:T(4,128)(2,1)}, bf16[4,12288]{1,0:T(4,128)(2,1)S(1)}, u32[]{:S(2)}, u32[]{:S(2)}) collective-permute-start(bf16[4,12288]{1,0:T(4,128)(2,1)} %param.4), channel_id=1, source_target_pairs={{0,16},{4,20},{8,24},{12,28},{16,0},{20,4},{24,8},{28,12},{1,17},{... | collective-permute-start | bytes 294920 | tf_op jit(solution)/shard_map/ppermute | solution.py:24
  4.7 1.6 %collective-permute-start = (bf16[4,12288]{1,0:T(4,128)(2,1)}, bf16[4,12288]{1,0:T(4,128)(2,1)S(1)}, u32[]{:S(2)}, u32[]{:S(2)}) collective-permute-start(bf16[4,12288]{1,0:T(4,128)(2,1)} %param.4), channel_id=1, source_target_pairs={{0,8},{4,12},{8,0},{12,4},{16,24},{20,28},{24,16},{28,20},{1,9},{5... | collective-permute-start | bytes 294920 | tf_op jit(solution)/shard_map/ppermute | solution.py:24
  9.7 1.7 %slice_select_fusion.refs_8_ = bf16[16,256,256]{2,1,0:T(8,128)(2,1)S(1)} fusion(bf16[32,256,256]{2,1,0:T(8,128)(2,1)} %refs_2_.3, pred[]{:T(512)S(6)} %ge.12), kind=kLoop, calls=%fused_computation | loop fusion | flops 1048576 | bytes 4194305 | tf_op jit(solution)/shard_map/jit(_where)/select_n | solution.py:301
  12.2 1.5 %collective-permute-done.2.refs_3_ = bf16[4,12288]{1,0:T(4,128)(2,1)S(1)} collective-permute-done((bf16[4,12288]{1,0:T(4,128)(2,1)}, bf16[4,12288]{1,0:T(4,128)(2,1)S(1)}, u32[]{:S(2)}, u32[]{:S(2)}) %collective-permute-start.2) | collective-permute-done | bytes 98336 | tf_op jit(solution)/shard_map/ppermute | solution.py:24
  14.9 3.0 %shard_map.75 = (bf16[24,32,128]{2,1,0:T(8,128)(2,1)S(1)}, bf16[24,32,128]{2,1,0:T(8,128)(2,1)S(1)}) custom-call(s32[64]{0:T(128)S(1)} %reshape.18.entry_ref, f32[32]{0:T(128)S(1)} %select_reduce_fusion.scale_ref, s32[3]{0:T(128)S(1)} %pad_add_fusion.place_ref, bf16[4,12288]{1,0:T(4,128)(2,1)S(1)} %broadcast_select_fusion.refs_0_, ...), custom_call_target="tpu_custom_call" | custom-call | flops 134217728 | bytes 4194304 | tf_op jit(solution)/shard_map/pallas_call | solution.py:256
  18.0 1.5 %collective-permute-start.7 = (bf16[24,32,128]{2,1,0:T(8,128)(2,1)S(1)}, bf16[24,32,128]{2,1,0:T(8,128)(2,1)S(1)}, u32[]{:S(2)}, u32[]{:S(2)}) collective-permute-start(bf16[24,32,128]{2,1,0:T(8,128)(2,1)S(1)} %get-tuple-element.27), channel_id=1, source_target_pairs={{0,1},{1,0},{2,3},{3,2},{4,5},{5,4},{6,7},{7,6},{8,9},{9,8},{10,11... | collective-permute-start | bytes 589832 | tf_op jit(solution)/shard_map/ppermute | solution.py:24
  19.5 1.5 %collective-permute-start.9 = (bf16[24,32,128]{2,1,0:T(8,128)(2,1)S(1)}, bf16[24,32,128]{2,1,0:T(8,128)(2,1)S(1)}, u32[]{:S(2)}, u32[]{:S(2)}) collective-permute-start(bf16[24,32,128]{2,1,0:T(8,128)(2,1)S(1)} %get-tuple-element.28), channel_id=1, source_target_pairs={{0,2},{1,3},{2,0},{3,1},{4,6},{5,7},{6,4},{7,5},{8,10},{9,11},{10,... | collective-permute-start | bytes 589832 | tf_op jit(solution)/shard_map/ppermute | solution.py:24
  21.1 3.9 %collective-permute-done.7 = bf16[24,32,128]{2,1,0:T(8,128)(2,1)S(1)} collective-permute-done((bf16[24,32,128]{2,1,0:T(8,128)(2,1)S(1)}, bf16[24,32,128]{2,1,0:T(8,128)(2,1)S(1)}, u32[]{:S(2)}, u32[]{:S(2)}) %collective-permute-start.7) | collective-permute-done | bytes 196640 | tf_op jit(solution)/shard_map/ppermute | solution.py:24
  25.1 1.6 %collective-permute-start.8 = (bf16[24,32,128]{2,1,0:T(8,128)(2,1)S(1)}, bf16[24,32,128]{2,1,0:T(8,128)(2,1)S(1)}, u32[]{:S(2)}, u32[]{:S(2)}) collective-permute-start(bf16[24,32,128]{2,1,0:T(8,128)(2,1)S(1)} %add_convert_fusion.8), channel_id=1, source_target_pairs={{0,2},{1,3},{2,0},{3,1},{4,6},{5,7},{6,4},{7,5},{8,10},{9,11},{10,... | collective-permute-start | bytes 589832 | tf_op jit(solution)/shard_map/ppermute | solution.py:24
  26.7 1.6 %collective-permute-start.10 = (bf16[24,32,128]{2,1,0:T(8,128)(2,1)S(1)}, bf16[24,32,128]{2,1,0:T(8,128)(2,1)S(1)}, u32[]{:S(2)}, u32[]{:S(2)}) collective-permute-start(bf16[24,32,128]{2,1,0:T(8,128)(2,1)S(1)} %add_convert_fusion.6), channel_id=1, source_target_pairs={{0,1},{1,0},{2,3},{3,2},{4,5},{5,4},{6,7},{7,6},{8,9},{9,8},{10,11... | collective-permute-start | bytes 589832 | tf_op jit(solution)/shard_map/ppermute | solution.py:24
  28.3 3.0 %collective-permute-done.8 = bf16[24,32,128]{2,1,0:T(8,128)(2,1)S(1)} collective-permute-done((bf16[24,32,128]{2,1,0:T(8,128)(2,1)S(1)}, bf16[24,32,128]{2,1,0:T(8,128)(2,1)S(1)}, u32[]{:S(2)}, u32[]{:S(2)}) %collective-permute-start.8) | collective-permute-done | bytes 196640 | tf_op jit(solution)/shard_map/ppermute | solution.py:24
  31.3 1.3 %collective-permute-done.10 = bf16[24,32,128]{2,1,0:T(8,128)(2,1)S(1)} collective-permute-done((bf16[24,32,128]{2,1,0:T(8,128)(2,1)S(1)}, bf16[24,32,128]{2,1,0:T(8,128)(2,1)S(1)}, u32[]{:S(2)}, u32[]{:S(2)}) %collective-permute-start.10) | collective-permute-done | bytes 196640 | tf_op jit(solution)/shard_map/ppermute | solution.py:24
  32.7 1.5 %shard_map.76 = (bf16[4,12,32,128]{3,2,1,0:T(8,128)(2,1)S(1)}, bf16[4,12,32,128]{3,2,1,0:T(8,128)(2,1)S(1)}) custom-call(s32[64]{0:T(128)S(1)} %reshape.18.entry_ref, f32[32]{0:T(128)S(1)} %select_reduce_fusion.scale_ref, s32[3]{0:T(128)S(1)} %pad_add_fusion.place_ref, bf16[24,32,128]{2,1,0:T(8,128)(2,1)S(1)} %add_convert_fusion.7.refs_0_, ...), custom_call_target="tpu_custom_call" | custom-call | flops 134217728 | bytes 4194304 | tf_op jit(solution)/shard_map/pallas_call | solution.py:256
  34.3 1.7 %collective-permute-done.11 = bf16[4,12,32,128]{3,2,1,0:T(8,128)(2,1)S(1)} collective-permute-done((bf16[4,12,32,128]{3,2,1,0:T(8,128)(2,1)S(1)}, bf16[4,12,32,128]{3,2,1,0:T(8,128)(2,1)S(1)}, u32[]{:S(2)}, u32[]{:S(2)}) %collective-permute-start.11) | collective-permute-done | bytes 393248 | tf_op jit(solution)/shard_map/ppermute | solution.py:24
  37.4 3.3 %collective-permute-start.14 = (bf16[12,32,128]{2,1,0:T(8,128)(2,1)S(1)}, bf16[12,32,128]{2,1,0:T(8,128)(2,1)S(1)}, u32[]{:S(2)}, u32[]{:S(2)}) collective-permute-start(bf16[12,32,128]{2,1,0:T(8,128)(2,1)S(1)} %get-tuple-element.54), channel_id=1, source_target_pairs={{0,24},{4,28},{8,16},{12,20},{16,8},{20,12},{24,0},{28,4},{1,25},{... | collective-permute-start | bytes 294920 | tf_op jit(solution)/shard_map/ppermute | solution.py:24
  41.0 5.5 %collective-permute-done.14 = bf16[12,32,128]{2,1,0:T(8,128)(2,1)S(1)} collective-permute-done((bf16[12,32,128]{2,1,0:T(8,128)(2,1)S(1)}, bf16[12,32,128]{2,1,0:T(8,128)(2,1)S(1)}, u32[]{:S(2)}, u32[]{:S(2)}) %collective-permute-start.14) | collective-permute-done | bytes 98336 | tf_op jit(solution)/shard_map/ppermute | solution.py:24
  46.5 3.0 %collective-permute-done.13 = bf16[12,32,128]{2,1,0:T(8,128)(2,1)S(1)} collective-permute-done((bf16[12,32,128]{2,1,0:T(8,128)(2,1)S(1)}, bf16[12,32,128]{2,1,0:T(8,128)(2,1)S(1)}, u32[]{:S(2)}, u32[]{:S(2)}) %collective-permute-start.13) | collective-permute-done | bytes 98336 | tf_op jit(solution)/shard_map/ppermute | solution.py:24
  49.6 1.9 %collective-permute-start.17 = (bf16[12,32,128]{2,1,0:T(8,128)(2,1)S(1)}, bf16[12,32,128]{2,1,0:T(8,128)(2,1)S(1)}, u32[]{:S(2)}, u32[]{:S(2)}) collective-permute-start(bf16[12,32,128]{2,1,0:T(8,128)(2,1)S(1)} %fusion.6.refs_0_.refs_2_), channel_id=1, source_target_pairs={{0,24},{4,28},{8,16},{12,20},{16,8},{20,12},{24,0},{28,4},{1,25},{... | collective-permute-start | bytes 294920 | tf_op jit(solution)/shard_map/ppermute | solution.py:24
  51.5 2.6 %collective-permute-start.15 = (bf16[12,32,128]{2,1,0:T(8,128)(2,1)S(1)}, bf16[12,32,128]{2,1,0:T(8,128)(2,1)S(1)}, u32[]{:S(2)}, u32[]{:S(2)}) collective-permute-start(bf16[12,32,128]{2,1,0:T(8,128)(2,1)S(1)} %fusion.6.refs_0_.refs_2_), channel_id=1, source_target_pairs={{0,8},{4,12},{8,0},{12,4},{16,24},{20,28},{24,16},{28,20},{1,9},{5... | collective-permute-start | bytes 294920 | tf_op jit(solution)/shard_map/ppermute | solution.py:24
  54.1 3.2 %collective-permute-done.17.refs_3_.refs_5_ = bf16[12,32,128]{2,1,0:T(8,128)(2,1)S(1)} collective-permute-done((bf16[12,32,128]{2,1,0:T(8,128)(2,1)S(1)}, bf16[12,32,128]{2,1,0:T(8,128)(2,1)S(1)}, u32[]{:S(2)}, u32[]{:S(2)}) %collective-permute-start.17) | collective-permute-done | bytes 98336 | tf_op jit(solution)/shard_map/ppermute | solution.py:24
  57.3 2.8 %collective-permute-done.16.refs_2_.refs_4_ = bf16[12,32,128]{2,1,0:T(8,128)(2,1)S(1)} collective-permute-done((bf16[12,32,128]{2,1,0:T(8,128)(2,1)S(1)}, bf16[12,32,128]{2,1,0:T(8,128)(2,1)S(1)}, u32[]{:S(2)}, u32[]{:S(2)}) %collective-permute-start.16) | collective-permute-done | bytes 98336 | tf_op jit(solution)/shard_map/ppermute | solution.py:24
  61.5 2.0 %shard_map.77 = (bf16[24,32,128]{2,1,0:T(8,128)(2,1)S(1)}, bf16[24,32,128]{2,1,0:T(8,128)(2,1)S(1)}) custom-call(s32[64]{0:T(128)S(1)} %reshape.18.entry_ref, f32[32]{0:T(128)S(1)} %select_reduce_fusion.scale_ref, s32[3]{0:T(128)S(1)} %pad_add_fusion.place_ref, bf16[12,32,128]{2,1,0:T(8,128)(2,1)S(1)} %fusion.6.refs_0_.refs_2_, ...), custom_call_target="tpu_custom_call" | custom-call | flops 134217728 | bytes 4194304 | tf_op jit(solution)/shard_map/pallas_call | solution.py:256
  63.5 1.6 %collective-permute-start.22 = (bf16[24,32,128]{2,1,0:T(8,128)(2,1)S(1)}, bf16[24,32,128]{2,1,0:T(8,128)(2,1)S(1)}, u32[]{:S(2)}, u32[]{:S(2)}) collective-permute-start(bf16[24,32,128]{2,1,0:T(8,128)(2,1)S(1)} %get-tuple-element.45), channel_id=1, source_target_pairs={{0,1},{1,0},{2,3},{3,2},{4,5},{5,4},{6,7},{7,6},{8,9},{9,8},{10,11... | collective-permute-start | bytes 589832 | tf_op jit(solution)/shard_map/ppermute | solution.py:24
  65.6 5.2 %collective-permute-done.22 = bf16[24,32,128]{2,1,0:T(8,128)(2,1)S(1)} collective-permute-done((bf16[24,32,128]{2,1,0:T(8,128)(2,1)S(1)}, bf16[24,32,128]{2,1,0:T(8,128)(2,1)S(1)}, u32[]{:S(2)}, u32[]{:S(2)}) %collective-permute-start.22) | collective-permute-done | bytes 196640 | tf_op jit(solution)/shard_map/ppermute | solution.py:24
  73.0 4.2 %collective-permute-done.23 = bf16[24,32,128]{2,1,0:T(8,128)(2,1)S(1)} collective-permute-done((bf16[24,32,128]{2,1,0:T(8,128)(2,1)S(1)}, bf16[24,32,128]{2,1,0:T(8,128)(2,1)S(1)}, u32[]{:S(2)}, u32[]{:S(2)}) %collective-permute-start.23) | collective-permute-done | bytes 196640 | tf_op jit(solution)/shard_map/ppermute | solution.py:24
  78.2 1.8 %shard_map.79 = bf16[2,4,4,12288]{3,2,1,0:T(4,128)(2,1)S(1)} custom-call(s32[64]{0:T(128)S(1)} %reshape.18.entry_ref, f32[32]{0:T(128)S(1)} %select_reduce_fusion.scale_ref, s32[3]{0:T(128)S(1)} %pad_add_fusion.place_ref, bf16[24,32,128]{2,1,0:T(8,128)(2,1)S(1)} %add_convert_fusion.3.refs_0_, bf16[24,32,128]{2,1,0:T(8,128)(2,1)S(1)} %add_convert_fusion.1.refs_1_, ...), custom_call_target="tpu_custom_call" | custom-call | flops 134217728 | bytes 4194304 | tf_op jit(solution)/shard_map/pallas_call | solution.py:256
  80.2 1.7 %collective-permute-done.26 = bf16[4,4,12288]{2,1,0:T(4,128)(2,1)S(1)} collective-permute-done((bf16[4,4,12288]{2,1,0:T(4,128)(2,1)S(1)}, bf16[4,4,12288]{2,1,0:T(4,128)(2,1)S(1)}, u32[]{:S(2)}, u32[]{:S(2)}) %collective-permute-start.26) | collective-permute-done | bytes 393248 | tf_op jit(solution)/shard_map/ppermute | solution.py:24
  82.3 1.6 %collective-permute-start.29 = (bf16[4,12288]{1,0:T(4,128)(2,1)S(1)}, bf16[4,12288]{1,0:T(4,128)(2,1)S(1)}, u32[]{:S(2)}, u32[]{:S(2)}) collective-permute-start(bf16[4,12288]{1,0:T(4,128)(2,1)S(1)} %get-tuple-element.51), channel_id=1, source_target_pairs={{0,24},{4,28},{8,16},{12,20},{16,8},{20,12},{24,0},{28,4},{1,25},{... | collective-permute-start | bytes 294920 | tf_op jit(solution)/shard_map/ppermute | solution.py:24
  83.9 1.9 %collective-permute-start.28 = (bf16[4,12288]{1,0:T(4,128)(2,1)S(1)}, bf16[4,12288]{1,0:T(4,128)(2,1)S(1)}, u32[]{:S(2)}, u32[]{:S(2)}) collective-permute-start(bf16[4,12288]{1,0:T(4,128)(2,1)S(1)} %get-tuple-element.52), channel_id=1, source_target_pairs={{0,16},{4,20},{8,24},{12,28},{16,0},{20,4},{24,8},{28,12},{1,17},{... | collective-permute-start | bytes 294920 | tf_op jit(solution)/shard_map/ppermute | solution.py:24
  85.8 1.5 %shard_map.78 = (bf16[8,6144]{1,0:T(8,128)(2,1)}, bf16[4,12288]{1,0:T(4,128)(2,1)}) custom-call(s32[3]{0:T(128)S(1)} %pad_add_fusion.place_ref, bf16[24,32,128]{2,1,0:T(8,128)(2,1)S(1)} %add_convert_fusion.7.refs_0_, bf16[24,32,128]{2,1,0:T(8,128)(2,1)S(1)} %add_convert_fusion.5.refs_1_, bf16[12,32,128]{2,1,0:T(8,128)(2,1)S(1)} %fusion.6.refs_0_.refs_2_, ...), custom_call_target="tpu_custom_call" | custom-call | bytes 393216 | tf_op jit(solution)/shard_map/pallas_call | solution.py:245
  88.6 1.3 %collective-permute-done.29 = bf16[4,12288]{1,0:T(4,128)(2,1)S(1)} collective-permute-done((bf16[4,12288]{1,0:T(4,128)(2,1)S(1)}, bf16[4,12288]{1,0:T(4,128)(2,1)S(1)}, u32[]{:S(2)}, u32[]{:S(2)}) %collective-permute-start.29) | collective-permute-done | bytes 98336 | tf_op jit(solution)/shard_map/ppermute | solution.py:24
  89.9 4.7 %collective-permute-done.28 = bf16[4,12288]{1,0:T(4,128)(2,1)S(1)} collective-permute-done((bf16[4,12288]{1,0:T(4,128)(2,1)S(1)}, bf16[4,12288]{1,0:T(4,128)(2,1)S(1)}, u32[]{:S(2)}, u32[]{:S(2)}) %collective-permute-start.28) | collective-permute-done | bytes 98336 | tf_op jit(solution)/shard_map/ppermute | solution.py:24
  (63 shorter events, 15.2 us)
Async XLA Ops:
  0.6 10.9 %collective-permute-start.1 = (bf16[4,12288]{1,0:T(4,128)(2,1)}, bf16[4,12288]{1,0:T(4,128)(2,1)S(1)}, u32[]{:S(2)}, u32[]{:S(2)}) collective-permute-start(bf16[4,12288]{1,0:T(4,128)(2,1)} %param.4), channel_id=1, source_target_pairs={{0,16},{4,20},{8,24},{12,28},{16,0},{20,4},{24,8},{28,12},{1,17},{... | collective-permute-start | bytes 294920 | tf_op jit(solution)/shard_map/ppermute | solution.py:24
  4.7 7.4 %collective-permute-start = (bf16[4,12288]{1,0:T(4,128)(2,1)}, bf16[4,12288]{1,0:T(4,128)(2,1)S(1)}, u32[]{:S(2)}, u32[]{:S(2)}) collective-permute-start(bf16[4,12288]{1,0:T(4,128)(2,1)} %param.4), channel_id=1, source_target_pairs={{0,8},{4,12},{8,0},{12,4},{16,24},{20,28},{24,16},{28,20},{1,9},{5... | collective-permute-start | bytes 294920 | tf_op jit(solution)/shard_map/ppermute | solution.py:24
  6.3 7.4 %collective-permute-start.3 = (bf16[4,12288]{1,0:T(4,128)(2,1)}, bf16[4,12288]{1,0:T(4,128)(2,1)S(1)}, u32[]{:S(2)}, u32[]{:S(2)}) collective-permute-start(bf16[4,12288]{1,0:T(4,128)(2,1)} %param.4), channel_id=1, source_target_pairs={{0,4},{4,0},{8,12},{12,8},{16,20},{20,16},{24,28},{28,24},{1,5},{5... | collective-permute-start | bytes 294920 | tf_op jit(solution)/shard_map/ppermute | solution.py:24
  6.3 7.3 %collective-permute-start.2 = (bf16[4,12288]{1,0:T(4,128)(2,1)}, bf16[4,12288]{1,0:T(4,128)(2,1)S(1)}, u32[]{:S(2)}, u32[]{:S(2)}) collective-permute-start(bf16[4,12288]{1,0:T(4,128)(2,1)} %param.4), channel_id=1, source_target_pairs={{0,24},{4,28},{8,16},{12,20},{16,8},{20,12},{24,0},{28,4},{1,25},{... | collective-permute-start | bytes 294920 | tf_op jit(solution)/shard_map/ppermute | solution.py:24
  9.7 1.8 %copy-start.1 = (f32[8]{0:T(128)S(1)}, f32[8]{0:T(128)}, u32[]{:S(2)}) copy-start(f32[8]{0:T(128)} %param.7) | copy-start | bytes 100
  11.5 2.2 %collective-permute-start.5 = (bf16[4,12288]{1,0:T(4,128)(2,1)S(1)}, bf16[4,12288]{1,0:T(4,128)(2,1)S(1)}, u32[]{:S(2)}, u32[]{:S(2)}) collective-permute-start(bf16[4,12288]{1,0:T(4,128)(2,1)S(1)} %collective-permute-done.1.refs_2_), channel_id=1, source_target_pairs={{0,4},{4,0},{8,12},{12,8},{16,20},{20,16},{24,28},{28,24},{1,5},{5... | collective-permute-start | bytes 294920 | tf_op jit(solution)/shard_map/ppermute | solution.py:24
  12.1 1.6 %collective-permute-start.4 = (bf16[4,12288]{1,0:T(4,128)(2,1)S(1)}, bf16[4,12288]{1,0:T(4,128)(2,1)S(1)}, u32[]{:S(2)}, u32[]{:S(2)}) collective-permute-start(bf16[4,12288]{1,0:T(4,128)(2,1)S(1)} %collective-permute-done.refs_1_), channel_id=1, source_target_pairs={{0,4},{4,0},{8,12},{12,8},{16,20},{20,16},{24,28},{28,24},{1,5},{5... | collective-permute-start | bytes 294920 | tf_op jit(solution)/shard_map/ppermute | solution.py:24
  13.6 1.3 %collective-permute-start.6 = (bf16[4,12288]{1,0:T(4,128)(2,1)S(1)}, bf16[4,12288]{1,0:T(4,128)(2,1)S(1)}, u32[]{:S(2)}, u32[]{:S(2)}) collective-permute-start(bf16[4,12288]{1,0:T(4,128)(2,1)S(1)} %collective-permute-done.2.refs_3_), channel_id=1, source_target_pairs={{0,4},{4,0},{8,12},{12,8},{16,20},{20,16},{24,28},{28,24},{1,5},{5... | collective-permute-start | bytes 294920 | tf_op jit(solution)/shard_map/ppermute | solution.py:24
  14.9 17.8 %copy-start = (bf16[32,256,256]{2,1,0:T(8,128)(2,1)S(1)}, bf16[32,256,256]{2,1,0:T(8,128)(2,1)}, u32[]{:S(2)}) copy-start(bf16[32,256,256]{2,1,0:T(8,128)(2,1)} %refs_2_.3) | copy-start | bytes 12582916
  18.0 7.0 %collective-permute-start.7 = (bf16[24,32,128]{2,1,0:T(8,128)(2,1)S(1)}, bf16[24,32,128]{2,1,0:T(8,128)(2,1)S(1)}, u32[]{:S(2)}, u32[]{:S(2)}) collective-permute-start(bf16[24,32,128]{2,1,0:T(8,128)(2,1)S(1)} %get-tuple-element.27), channel_id=1, source_target_pairs={{0,1},{1,0},{2,3},{3,2},{4,5},{5,4},{6,7},{7,6},{8,9},{9,8},{10,11... | collective-permute-start | bytes 589832 | tf_op jit(solution)/shard_map/ppermute | solution.py:24
  19.5 7.1 %collective-permute-start.9 = (bf16[24,32,128]{2,1,0:T(8,128)(2,1)S(1)}, bf16[24,32,128]{2,1,0:T(8,128)(2,1)S(1)}, u32[]{:S(2)}, u32[]{:S(2)}) collective-permute-start(bf16[24,32,128]{2,1,0:T(8,128)(2,1)S(1)} %get-tuple-element.28), channel_id=1, source_target_pairs={{0,2},{1,3},{2,0},{3,1},{4,6},{5,7},{6,4},{7,5},{8,10},{9,11},{10,... | collective-permute-start | bytes 589832 | tf_op jit(solution)/shard_map/ppermute | solution.py:24
  25.1 6.2 %collective-permute-start.8 = (bf16[24,32,128]{2,1,0:T(8,128)(2,1)S(1)}, bf16[24,32,128]{2,1,0:T(8,128)(2,1)S(1)}, u32[]{:S(2)}, u32[]{:S(2)}) collective-permute-start(bf16[24,32,128]{2,1,0:T(8,128)(2,1)S(1)} %add_convert_fusion.8), channel_id=1, source_target_pairs={{0,2},{1,3},{2,0},{3,1},{4,6},{5,7},{6,4},{7,5},{8,10},{9,11},{10,... | collective-permute-start | bytes 589832 | tf_op jit(solution)/shard_map/ppermute | solution.py:24
  26.7 5.9 %collective-permute-start.10 = (bf16[24,32,128]{2,1,0:T(8,128)(2,1)S(1)}, bf16[24,32,128]{2,1,0:T(8,128)(2,1)S(1)}, u32[]{:S(2)}, u32[]{:S(2)}) collective-permute-start(bf16[24,32,128]{2,1,0:T(8,128)(2,1)S(1)} %add_convert_fusion.6), channel_id=1, source_target_pairs={{0,1},{1,0},{2,3},{3,2},{4,5},{5,4},{6,7},{7,6},{8,9},{9,8},{10,11... | collective-permute-start | bytes 589832 | tf_op jit(solution)/shard_map/ppermute | solution.py:24
  34.2 1.8 %collective-permute-start.11 = (bf16[4,12,32,128]{3,2,1,0:T(8,128)(2,1)S(1)}, bf16[4,12,32,128]{3,2,1,0:T(8,128)(2,1)S(1)}, u32[]{:S(2)}, u32[]{:S(2)}) collective-permute-start(bf16[4,12,32,128]{3,2,1,0:T(8,128)(2,1)S(1)} %get-tuple-element.30), channel_id=1, source_target_pairs={{0,4},{4,0},{8,12},{12,8},{16,20},{20,16},{24,28},{28,24},{1,5},{5... | collective-permute-start | bytes 1179656 | tf_op jit(solution)/shard_map/ppermute | solution.py:24
  36.1 4.9 %collective-permute-start.12 = (bf16[12,32,128]{2,1,0:T(8,128)(2,1)S(1)}, bf16[12,32,128]{2,1,0:T(8,128)(2,1)S(1)}, u32[]{:S(2)}, u32[]{:S(2)}) collective-permute-start(bf16[12,32,128]{2,1,0:T(8,128)(2,1)S(1)} %get-tuple-element.53), channel_id=1, source_target_pairs={{0,8},{4,12},{8,0},{12,4},{16,24},{20,28},{24,16},{28,20},{1,9},{5... | collective-permute-start | bytes 294920 | tf_op jit(solution)/shard_map/ppermute | solution.py:24
  37.4 9.1 %collective-permute-start.14 = (bf16[12,32,128]{2,1,0:T(8,128)(2,1)S(1)}, bf16[12,32,128]{2,1,0:T(8,128)(2,1)S(1)}, u32[]{:S(2)}, u32[]{:S(2)}) collective-permute-start(bf16[12,32,128]{2,1,0:T(8,128)(2,1)S(1)} %get-tuple-element.54), channel_id=1, source_target_pairs={{0,24},{4,28},{8,16},{12,20},{16,8},{20,12},{24,0},{28,4},{1,25},{... | collective-permute-start | bytes 294920 | tf_op jit(solution)/shard_map/ppermute | solution.py:24
  40.7 8.9 %collective-permute-start.13 = (bf16[12,32,128]{2,1,0:T(8,128)(2,1)S(1)}, bf16[12,32,128]{2,1,0:T(8,128)(2,1)S(1)}, u32[]{:S(2)}, u32[]{:S(2)}) collective-permute-start(bf16[12,32,128]{2,1,0:T(8,128)(2,1)S(1)} %get-tuple-element.55), channel_id=1, source_target_pairs={{0,16},{4,20},{8,24},{12,28},{16,0},{20,4},{24,8},{28,12},{1,17},{... | collective-permute-start | bytes 294920 | tf_op jit(solution)/shard_map/ppermute | solution.py:24
  49.6 7.7 %collective-permute-start.17 = (bf16[12,32,128]{2,1,0:T(8,128)(2,1)S(1)}, bf16[12,32,128]{2,1,0:T(8,128)(2,1)S(1)}, u32[]{:S(2)}, u32[]{:S(2)}) collective-permute-start(bf16[12,32,128]{2,1,0:T(8,128)(2,1)S(1)} %fusion.6.refs_0_.refs_2_), channel_id=1, source_target_pairs={{0,24},{4,28},{8,16},{12,20},{16,8},{20,12},{24,0},{28,4},{1,25},{... | collective-permute-start | bytes 294920 | tf_op jit(solution)/shard_map/ppermute | solution.py:24
  51.5 8.6 %collective-permute-start.16 = (bf16[12,32,128]{2,1,0:T(8,128)(2,1)S(1)}, bf16[12,32,128]{2,1,0:T(8,128)(2,1)S(1)}, u32[]{:S(2)}, u32[]{:S(2)}) collective-permute-start(bf16[12,32,128]{2,1,0:T(8,128)(2,1)S(1)} %fusion.6.refs_0_.refs_2_), channel_id=1, source_target_pairs={{0,16},{4,20},{8,24},{12,28},{16,0},{20,4},{24,8},{28,12},{1,17},{... | collective-permute-start | bytes 294920 | tf_op jit(solution)/shard_map/ppermute | solution.py:24
  51.5 8.6 %collective-permute-start.15 = (bf16[12,32,128]{2,1,0:T(8,128)(2,1)S(1)}, bf16[12,32,128]{2,1,0:T(8,128)(2,1)S(1)}, u32[]{:S(2)}, u32[]{:S(2)}) collective-permute-start(bf16[12,32,128]{2,1,0:T(8,128)(2,1)S(1)} %fusion.6.refs_0_.refs_2_), channel_id=1, source_target_pairs={{0,8},{4,12},{8,0},{12,4},{16,24},{20,28},{24,16},{28,20},{1,9},{5... | collective-permute-start | bytes 294920 | tf_op jit(solution)/shard_map/ppermute | solution.py:24
  54.1 6.5 %collective-permute-start.18 = (bf16[12,32,128]{2,1,0:T(8,128)(2,1)S(1)}, bf16[12,32,128]{2,1,0:T(8,128)(2,1)S(1)}, u32[]{:S(2)}, u32[]{:S(2)}) collective-permute-start(bf16[12,32,128]{2,1,0:T(8,128)(2,1)S(1)} %fusion.6.refs_0_.refs_2_), channel_id=1, source_target_pairs={{0,4},{4,0},{8,12},{12,8},{16,20},{20,16},{24,28},{28,24},{1,5},{5... | collective-permute-start | bytes 294920 | tf_op jit(solution)/shard_map/ppermute | solution.py:24
  57.3 3.3 %collective-permute-start.21 = (bf16[12,32,128]{2,1,0:T(8,128)(2,1)S(1)}, bf16[12,32,128]{2,1,0:T(8,128)(2,1)S(1)}, u32[]{:S(2)}, u32[]{:S(2)}) collective-permute-start(bf16[12,32,128]{2,1,0:T(8,128)(2,1)S(1)} %collective-permute-done.17.refs_3_.refs_5_), channel_id=1, source_target_pairs={{0,4},{4,0},{8,12},{12,8},{16,20},{20,16},{24,28},{28,24},{1,5},{5... | collective-permute-start | bytes 294920 | tf_op jit(solution)/shard_map/ppermute | solution.py:24
  60.1 1.3 %collective-permute-start.20 = (bf16[12,32,128]{2,1,0:T(8,128)(2,1)S(1)}, bf16[12,32,128]{2,1,0:T(8,128)(2,1)S(1)}, u32[]{:S(2)}, u32[]{:S(2)}) collective-permute-start(bf16[12,32,128]{2,1,0:T(8,128)(2,1)S(1)} %collective-permute-done.16.refs_2_.refs_4_), channel_id=1, source_target_pairs={{0,4},{4,0},{8,12},{12,8},{16,20},{20,16},{24,28},{28,24},{1,5},{5... | collective-permute-start | bytes 294920 | tf_op jit(solution)/shard_map/ppermute | solution.py:24
  60.1 1.4 %collective-permute-start.19 = (bf16[12,32,128]{2,1,0:T(8,128)(2,1)S(1)}, bf16[12,32,128]{2,1,0:T(8,128)(2,1)S(1)}, u32[]{:S(2)}, u32[]{:S(2)}) collective-permute-start(bf16[12,32,128]{2,1,0:T(8,128)(2,1)S(1)} %collective-permute-done.15.refs_1_.refs_3_), channel_id=1, source_target_pairs={{0,4},{4,0},{8,12},{12,8},{16,20},{20,16},{24,28},{28,24},{1,5},{5... | collective-permute-start | bytes 294920 | tf_op jit(solution)/shard_map/ppermute | solution.py:24
  63.5 7.2 %collective-permute-start.22 = (bf16[24,32,128]{2,1,0:T(8,128)(2,1)S(1)}, bf16[24,32,128]{2,1,0:T(8,128)(2,1)S(1)}, u32[]{:S(2)}, u32[]{:S(2)}) collective-permute-start(bf16[24,32,128]{2,1,0:T(8,128)(2,1)S(1)} %get-tuple-element.45), channel_id=1, source_target_pairs={{0,1},{1,0},{2,3},{3,2},{4,5},{5,4},{6,7},{7,6},{8,9},{9,8},{10,11... | collective-permute-start | bytes 589832 | tf_op jit(solution)/shard_map/ppermute | solution.py:24
  65.1 6.9 %collective-permute-start.24 = (bf16[24,32,128]{2,1,0:T(8,128)(2,1)S(1)}, bf16[24,32,128]{2,1,0:T(8,128)(2,1)S(1)}, u32[]{:S(2)}, u32[]{:S(2)}) collective-permute-start(bf16[24,32,128]{2,1,0:T(8,128)(2,1)S(1)} %get-tuple-element.46), channel_id=1, source_target_pairs={{0,2},{1,3},{2,0},{3,1},{4,6},{5,7},{6,4},{7,5},{8,10},{9,11},{10,... | collective-permute-start | bytes 589832 | tf_op jit(solution)/shard_map/ppermute | solution.py:24
  70.8 6.4 %collective-permute-start.23 = (bf16[24,32,128]{2,1,0:T(8,128)(2,1)S(1)}, bf16[24,32,128]{2,1,0:T(8,128)(2,1)S(1)}, u32[]{:S(2)}, u32[]{:S(2)}) collective-permute-start(bf16[24,32,128]{2,1,0:T(8,128)(2,1)S(1)} %add_convert_fusion.4), channel_id=1, source_target_pairs={{0,2},{1,3},{2,0},{3,1},{4,6},{5,7},{6,4},{7,5},{8,10},{9,11},{10,... | collective-permute-start | bytes 589832 | tf_op jit(solution)/shard_map/ppermute | solution.py:24
  72.0 6.1 %collective-permute-start.25 = (bf16[24,32,128]{2,1,0:T(8,128)(2,1)S(1)}, bf16[24,32,128]{2,1,0:T(8,128)(2,1)S(1)}, u32[]{:S(2)}, u32[]{:S(2)}) collective-permute-start(bf16[24,32,128]{2,1,0:T(8,128)(2,1)S(1)} %add_convert_fusion.2), channel_id=1, source_target_pairs={{0,1},{1,0},{2,3},{3,2},{4,5},{5,4},{6,7},{7,6},{8,9},{9,8},{10,11... | collective-permute-start | bytes 589832 | tf_op jit(solution)/shard_map/ppermute | solution.py:24
  80.2 1.8 %collective-permute-start.26 = (bf16[4,4,12288]{2,1,0:T(4,128)(2,1)S(1)}, bf16[4,4,12288]{2,1,0:T(4,128)(2,1)S(1)}, u32[]{:S(2)}, u32[]{:S(2)}) collective-permute-start(bf16[4,4,12288]{2,1,0:T(4,128)(2,1)S(1)} %slice_bitcast_fusion), channel_id=1, source_target_pairs={{0,4},{4,0},{8,12},{12,8},{16,20},{20,16},{24,28},{28,24},{1,5},{5... | collective-permute-start | bytes 1179656 | tf_op jit(solution)/shard_map/ppermute | solution.py:24
  82.3 6.3 %collective-permute-start.27 = (bf16[4,12288]{1,0:T(4,128)(2,1)S(1)}, bf16[4,12288]{1,0:T(4,128)(2,1)S(1)}, u32[]{:S(2)}, u32[]{:S(2)}) collective-permute-start(bf16[4,12288]{1,0:T(4,128)(2,1)S(1)} %get-tuple-element.50), channel_id=1, source_target_pairs={{0,8},{4,12},{8,0},{12,4},{16,24},{20,28},{24,16},{28,20},{1,9},{5... | collective-permute-start | bytes 294920 | tf_op jit(solution)/shard_map/ppermute | solution.py:24
  82.3 7.6 %collective-permute-start.29 = (bf16[4,12288]{1,0:T(4,128)(2,1)S(1)}, bf16[4,12288]{1,0:T(4,128)(2,1)S(1)}, u32[]{:S(2)}, u32[]{:S(2)}) collective-permute-start(bf16[4,12288]{1,0:T(4,128)(2,1)S(1)} %get-tuple-element.51), channel_id=1, source_target_pairs={{0,24},{4,28},{8,16},{12,20},{16,8},{20,12},{24,0},{28,4},{1,25},{... | collective-permute-start | bytes 294920 | tf_op jit(solution)/shard_map/ppermute | solution.py:24
  83.9 10.8 %collective-permute-start.28 = (bf16[4,12288]{1,0:T(4,128)(2,1)S(1)}, bf16[4,12288]{1,0:T(4,128)(2,1)S(1)}, u32[]{:S(2)}, u32[]{:S(2)}) collective-permute-start(bf16[4,12288]{1,0:T(4,128)(2,1)S(1)} %get-tuple-element.52), channel_id=1, source_target_pairs={{0,16},{4,20},{8,24},{12,28},{16,0},{20,4},{24,8},{28,12},{1,17},{... | collective-permute-start | bytes 294920 | tf_op jit(solution)/shard_map/ppermute | solution.py:24
